TPU v7x, 32 devices: a whole 2x2x4 slice. The times are simulated.
32 devices in a mesh: dp: 16 (over z, y, core), tensor: 2 (over x).
Axes of the slice: x: 2, y: 2, z: 4, core: 2. Of those that a mesh axis runs over, the one named last changes fastest.
Arguments:
- block_input: bfloat16 [2, 16, 576, 1280], P(None, 'dp', 'tensor'), may hold values from -6 to 6
- out_cotangent: bfloat16 [2, 16, 576, 1280], P(None, 'dp', 'tensor'), may hold values from -6 to 6
- picture_ids: int32 [2, 16, 576], P(None, 'dp'), may hold values from 0 to 3, as said below
- patch_positions: int32 [2, 2, 16, 576], P(None, None, 'dp'), may hold values from 0 to 23, as said below
- picture_lengths: int32 [2, 16, 4], P(None, 'dp'), may hold values from 0 to 576, as said below
- pad_mask: int32 [2, 16, 576], P(None, 'dp'), may hold values from 0 to 1, as said below
- qkv_weight: float32 [1280, 3, 1280], P('dp', None, 'tensor')
- proj_weight: float32 [1280, 1280], P('tensor', 'dp')
- fc1_weight: float32 [1280, 5120], P('dp', 'tensor')
- fc2_weight: float32 [5120, 1280], P('tensor', 'dp')
- qkv_bias: float32 [3, 1280], P(None, 'tensor'), may hold values from -3 to 3
- fc1_bias: float32 [5120], P('tensor'), may hold values from -3 to 3
- vectors: float32 [6, 1280], replicated
- qkv_moments: float32 [2, 1280, 3, 1280], P(None, 'dp', None, 'tensor')
- proj_moments: float32 [2, 1280, 1280], P(None, 'tensor', 'dp')
- fc1_moments: float32 [2, 1280, 5120], P(None, 'dp', 'tensor')
- fc2_moments: float32 [2, 5120, 1280], P(None, 'tensor', 'dp')
- qkv_bias_moments: float32 [2, 3, 1280], P(None, None, 'tensor')
- fc1_bias_moments: float32 [2, 5120], P(None, 'tensor')
- vector_moments: float32 [2, 6, 1280], replicated
Outputs:
- block_output: bfloat16 [2, 16, 576, 1280], P(None, 'dp', 'tensor')
- input_grad: bfloat16 [2, 16, 576, 1280], P(None, 'dp', 'tensor')
- qkv_new: float32 [1280, 3, 1280], P('dp', None, 'tensor')
- proj_new: float32 [1280, 1280], P('tensor', 'dp')
- fc1_new: float32 [1280, 5120], P('dp', 'tensor')
- fc2_new: float32 [5120, 1280], P('tensor', 'dp')
- qkv_bias_new: float32 [3, 1280], P(None, 'tensor')
- fc1_bias_new: float32 [5120], P('tensor')
- vectors_new: float32 [6, 1280], replicated
- qkv_moments_new: float32 [2, 1280, 3, 1280], P(None, 'dp', None, 'tensor')
- proj_moments_new: float32 [2, 1280, 1280], P(None, 'tensor', 'dp')
- fc1_moments_new: float32 [2, 1280, 5120], P(None, 'dp', 'tensor')
- fc2_moments_new: float32 [2, 5120, 1280], P(None, 'tensor', 'dp')
- qkv_bias_moments_new: float32 [2, 3, 1280], P(None, None, 'tensor')
- fc1_bias_moments_new: float32 [2, 5120], P(None, 'tensor')
- vector_moments_new: float32 [2, 6, 1280], replicated
- qkv_copy: bfloat16 [1280, 3, 1280], P('dp', None, 'tensor')
- proj_copy: bfloat16 [1280, 1280], P('tensor', 'dp')
- fc1_copy: bfloat16 [1280, 5120], P('dp', 'tensor')
- fc2_copy: bfloat16 [5120, 1280], P('tensor', 'dp')
- norms: float32 [2, 7], replicated
- trust: float32 [7], replicated
Inputs may be any that keep to these rules, and one draw needn't show every extreme that they name: `picture_ids`: within a row the picture number never falls; the patches after a row's last picture are padding and carry that picture's number. `patch_positions`: A picture of height h and width w, both from 10 to 24, lists its h * w patches row by row; [0] is the row and [1] the column inside it; padding has 0 and 0. `picture_lengths`: the pictures fill a row's first patches in slot order; a used slot holds h * w, unused slots at the end hold 0; a row's lengths sum to at most 576. `pad_mask`: 1 exactly on a row's first (sum of its picture_lengths) patches.
All inputs are finite; a program needn't handle non-finite values.
Results may differ from a plain program's by a relative error of at most 0.013.
The roundings to bfloat16 on the way count: a program that leaves them out, or rounds other values in their place, can miss the bound.
Values may be sent and summed in bfloat16 or wider, within the bound.
No kernel may reach another device: no remote copies, remote signals or barrier semaphores. Data moves between devices by JAX's collectives and lax.ppermute only.
A program may use at most 256 MiB of HBM per device.

v0:
```python
import jax
import jax.numpy as jnp
from jax import lax
from jax.sharding import PartitionSpec as P

HD = 80
SLOTS = 4
LEN = 576


NEGATIVE = -1e30
EPS_NORM = 1e-06
EPS_ADAM = 1e-06
WEIGHT_DECAY = 0.01
LEARN_RATE = 0.5
GELU_SLOPE = 1.702


def norm_parts(values):
    center = values - jnp.mean(values, -1, keepdims=True)
    inverse = lax.rsqrt(jnp.mean(center * center, -1, keepdims=True) + EPS_NORM)
    return (center * inverse, inverse)


def norm_back(out_grad, normed, inverse, gain):
    scaled = out_grad * gain
    return inverse * (
        scaled
        - jnp.mean(scaled, -1, keepdims=True)
        - normed * jnp.mean(scaled * normed, -1, keepdims=True)
    )


def rotary_tables(rows_at, cols_at):
    quarter = HD // 4
    frequency = 10000.0 ** (-jnp.arange(quarter, dtype=jnp.float32) / quarter)
    halves = jnp.concatenate(
        [
            rows_at.astype(jnp.float32)[:, None] * frequency,
            cols_at.astype(jnp.float32)[:, None] * frequency,
        ],
        -1,
    )
    angles = jnp.concatenate([halves, halves], -1)
    return (jnp.cos(angles), jnp.sin(angles))


def rotate_pairs(values, cosine, sine):
    middle = values.shape[-1] // 2
    turned = jnp.concatenate([-values[..., middle:], values[..., :middle]], -1)
    return values * cosine[:, None, :] + turned * sine[:, None, :]


def rotate_back(grads, cosine, sine):
    middle = grads.shape[-1] // 2
    weighted = grads * sine[:, None, :]
    return grads * cosine[:, None, :] + jnp.concatenate(
        [weighted[..., middle:], -weighted[..., :middle]], -1
    )


def attend(queries, keys_rot, values, allowed):
    score_scale = HD ** (-0.5)
    raw_scores = jnp.einsum("qhd,khd->hqk", queries, keys_rot, preferred_element_type=jnp.float32)
    logits = jnp.where(allowed[None], raw_scores * score_scale, NEGATIVE)
    row_top = jnp.max(logits, -1, keepdims=True)
    exponent = jnp.exp(logits - row_top)
    row_total = jnp.sum(exponent, -1, keepdims=True)
    prob_rows = (exponent / row_total).astype(jnp.bfloat16)
    mixed = jnp.einsum("hqk,khd->qhd", prob_rows, values, preferred_element_type=jnp.float32)
    return (mixed, row_top + jnp.log(row_total))


def attend_back(queries, keys_rot, values, allowed, log_total, grad_out):
    score_scale = HD ** (-0.5)
    raw_scores = jnp.einsum("qhd,khd->hqk", queries, keys_rot, preferred_element_type=jnp.float32)
    logits = jnp.where(allowed[None], raw_scores * score_scale, NEGATIVE)
    prob_rows = jnp.exp(logits - log_total)
    prob_grad = jnp.einsum("qhd,khd->hqk", grad_out, values, preferred_element_type=jnp.float32)
    inner_sum = jnp.sum(prob_rows * prob_grad, -1, keepdims=True)
    score_grad = (score_scale * prob_rows * (prob_grad - inner_sum)).astype(jnp.bfloat16)
    query_grad = jnp.einsum(
        "hqk,khd->qhd", score_grad, keys_rot, preferred_element_type=jnp.float32
    )
    key_grad = jnp.einsum("hqk,qhd->khd", score_grad, queries, preferred_element_type=jnp.float32)
    value_grad = jnp.einsum(
        "hqk,qhd->khd", prob_rows.astype(jnp.bfloat16), grad_out, preferred_element_type=jnp.float32
    )
    return (query_grad, key_grad, value_grad)


def collect_rows(rows_low):
    return lax.all_gather(rows_low, "tensor", axis=0, tiled=True)


def spread_rows(source, weight_low, contract):
    return lax.psum_scatter(
        lax.dot_general(
            source, weight_low, (contract, ((), ())), preferred_element_type=jnp.float32
        ),
        "tensor",
        scatter_dimension=0,
        tiled=True,
    )


def outer_term(left, right):
    return lax.dot_general(
        left, right, (((0,), (0,)), ((), ())), preferred_element_type=jnp.float32
    )


def owner_grad(left, right):
    return lax.psum_scatter(outer_term(left, right), "dp", scatter_dimension=0, tiled=True)


def flat_rows(stacked):
    return stacked.reshape((-1,) + stacked.shape[2:])


def lamb_parts(master, moments, gradient):
    first = 0.5 * moments[0] + 0.5 * gradient
    second = 0.5 * moments[1] + 0.5 * gradient * gradient
    update = first / (jnp.sqrt(second) + EPS_ADAM) + WEIGHT_DECAY * master
    return (first, second, update)


def body(
    block_input,
    out_cotangent,
    picture_ids,
    patch_positions,
    picture_lengths,
    pad_mask,
    qkv_weight,
    proj_weight,
    fc1_weight,
    fc2_weight,
    qkv_bias,
    fc1_bias,
    vectors,
    qkv_moments,
    proj_moments,
    fc1_moments,
    fc2_moments,
    qkv_bias_moments,
    fc1_bias_moments,
    vector_moments,
):
    tensor_slot = lax.axis_index("tensor")
    lead_dp = (lax.axis_index("dp") == 0).astype(jnp.float32)
    lead_all = lead_dp * (tensor_slot == 0).astype(jnp.float32)
    local_rows = block_input.shape[2]
    heads_here = qkv_weight.shape[2] // HD
    grad_factor = float(
        block_input.shape[0] * block_input.shape[1] * lax.axis_size("dp") * LEN
    ) ** (-0.5)
    params = (qkv_weight, proj_weight, fc1_weight, fc2_weight, qkv_bias, fc1_bias, vectors)
    moment_list = (
        qkv_moments,
        proj_moments,
        fc1_moments,
        fc2_moments,
        qkv_bias_moments,
        fc1_bias_moments,
        vector_moments,
    )
    shares = (1.0, 1.0, 1.0, 1.0, lead_dp, lead_dp, lead_all)
    low_weights = (
        qkv_weight.astype(jnp.bfloat16),
        proj_weight.astype(jnp.bfloat16),
        fc1_weight.astype(jnp.bfloat16),
        fc2_weight.astype(jnp.bfloat16),
    )
    gathered = (
        lax.all_gather(low_weights[0], "dp", axis=0, tiled=True),
        lax.all_gather(low_weights[1], "dp", axis=1, tiled=True),
        lax.all_gather(low_weights[2], "dp", axis=0, tiled=True),
        lax.all_gather(low_weights[3], "dp", axis=1, tiled=True),
    )

    def own_slice(row_array):
        return lax.dynamic_slice_in_dim(row_array, tensor_slot * local_rows, local_rows, 0)

    def forward_step(carry, inputs):
        rows_in, ids_row, rows_at, cols_at, mask_row = inputs
        w_qkv, w_proj, w_up, w_down = gathered
        row_values = rows_in.astype(jnp.float32)
        normed1, inverse1 = norm_parts(row_values)
        first_in = collect_rows((normed1 * vectors[0] + vectors[1]).astype(jnp.bfloat16))
        mixed = (
            jnp.einsum("td,dcf->tcf", first_in, w_qkv, preferred_element_type=jnp.float32)
            + qkv_bias[None]
        )
        cosine, sine = rotary_tables(rows_at, cols_at)
        queries = rotate_pairs(mixed[:, 0].reshape(LEN, heads_here, HD), cosine, sine).astype(
            jnp.bfloat16
        )
        keys_rot = rotate_pairs(mixed[:, 1].reshape(LEN, heads_here, HD), cosine, sine).astype(
            jnp.bfloat16
        )
        head_values = mixed[:, 2].reshape(LEN, heads_here, HD).astype(jnp.bfloat16)
        allowed = (ids_row[:, None] == ids_row[None, :]) & (mask_row[None, :] == 1)
        attended, log_total = attend(queries, keys_rot, head_values, allowed)
        attended_low = attended.reshape(LEN, -1).astype(jnp.bfloat16)
        hidden1 = row_values + (spread_rows(attended_low, w_proj, ((1,), (0,))) + vectors[2])
        normed2, inverse2 = norm_parts(hidden1)
        second_in = collect_rows((normed2 * vectors[3] + vectors[4]).astype(jnp.bfloat16))
        upward = jnp.dot(second_in, w_up, preferred_element_type=jnp.float32) + fc1_bias
        activated = (upward * jax.nn.sigmoid(GELU_SLOPE * upward)).astype(jnp.bfloat16)
        result = hidden1 + (spread_rows(activated, w_down, ((1,), (0,))) + vectors[5])
        saved = (
            first_in,
            queries,
            keys_rot,
            head_values,
            log_total,
            attended_low,
            hidden1,
            second_in,
            upward,
            activated,
        )
        return (carry, (result.astype(jnp.bfloat16), saved))

    forward_inputs = (
        block_input[:, 0],
        picture_ids[:, 0],
        patch_positions[0][:, 0],
        patch_positions[1][:, 0],
        pad_mask[:, 0],
    )
    unused, (outputs, saved_all) = lax.scan(forward_step, 0, forward_inputs)
    back_weights = (
        lax.all_gather(low_weights[0], "dp", axis=0, tiled=True),
        lax.all_gather(low_weights[1], "dp", axis=1, tiled=True),
        lax.all_gather(low_weights[2], "dp", axis=0, tiled=True),
        lax.all_gather(low_weights[3], "dp", axis=1, tiled=True),
    )

    def backward_step(sums, inputs):
        rows_in, cot_rows, ids_row, rows_at, cols_at, mask_row, length_row, saved = inputs
        (
            first_in,
            queries,
            keys_rot,
            head_values,
            log_total,
            attended_low,
            hidden1,
            second_in,
            upward,
            activated,
        ) = saved
        w_qkv, w_proj, w_up, w_down = back_weights
        sum_qkv_bias, sum_up_bias, sum_vectors, owner_sums = sums
        own_ids = own_slice(ids_row)
        own_mask = own_slice(mask_row)
        slot_hit = (own_ids[:, None] == jnp.arange(SLOTS, dtype=jnp.int32)[None, :]).astype(
            jnp.float32
        )
        picture_size = jnp.sum(slot_hit * length_row.astype(jnp.float32)[None, :], -1)
        token_weight = own_mask.astype(jnp.float32) * jnp.sqrt(LEN / picture_size)
        grad_y = cot_rows.astype(jnp.float32) * token_weight[:, None]
        down_grad = grad_y.astype(jnp.bfloat16)
        down_all = collect_rows(down_grad)
        act_grad = lax.dot_general(
            down_all, w_down, (((1,), (1,)), ((), ())), preferred_element_type=jnp.float32
        )
        sigma = jax.nn.sigmoid(GELU_SLOPE * upward)
        up_grad = (act_grad * (sigma + GELU_SLOPE * upward * sigma * (1.0 - sigma))).astype(
            jnp.bfloat16
        )
        sum_up_bias = sum_up_bias + jnp.sum(up_grad.astype(jnp.float32), 0)
        norm2_grad = spread_rows(up_grad, w_up, ((1,), (1,)))
        normed2, inverse2 = norm_parts(hidden1)
        hidden1_grad = grad_y + norm_back(norm2_grad, normed2, inverse2, vectors[3])
        branch_grad = hidden1_grad.astype(jnp.bfloat16)
        branch_all = collect_rows(branch_grad)
        attn_grad = lax.dot_general(
            branch_all, w_proj, (((1,), (1,)), ((), ())), preferred_element_type=jnp.float32
        )
        attn_grad = attn_grad.astype(jnp.bfloat16).reshape(LEN, heads_here, HD)
        allowed = (ids_row[:, None] == ids_row[None, :]) & (mask_row[None, :] == 1)
        query_grad, key_grad, value_grad = attend_back(
            queries, keys_rot, head_values, allowed, log_total, attn_grad
        )
        cosine, sine = rotary_tables(rows_at, cols_at)
        mixed_grad = jnp.stack(
            [
                rotate_back(query_grad, cosine, sine).reshape(LEN, -1),
                rotate_back(key_grad, cosine, sine).reshape(LEN, -1),
                value_grad.reshape(LEN, -1),
            ],
            1,
        ).astype(jnp.bfloat16)
        sum_qkv_bias = sum_qkv_bias + jnp.sum(mixed_grad.astype(jnp.float32), 0)
        norm1_grad = spread_rows(mixed_grad, w_qkv, ((1, 2), (1, 2)))
        normed1, inverse1 = norm_parts(rows_in.astype(jnp.float32))
        input_rows = hidden1_grad + norm_back(norm1_grad, normed1, inverse1, vectors[0])
        vector_terms = jnp.stack(
            [
                jnp.sum(norm1_grad * normed1, 0),
                jnp.sum(norm1_grad, 0),
                jnp.sum(branch_grad.astype(jnp.float32), 0),
                jnp.sum(norm2_grad * normed2, 0),
                jnp.sum(norm2_grad, 0),
                jnp.sum(down_grad.astype(jnp.float32), 0),
            ]
        )
        sum_vectors = sum_vectors + vector_terms
        kept_grads = (down_all, branch_all, mixed_grad, up_grad)
        return (
            (sum_qkv_bias, sum_up_bias, sum_vectors, owner_sums),
            (input_rows.astype(jnp.bfloat16), kept_grads),
        )

    zero_owner = ()
    zero_sums = (
        jnp.zeros(qkv_bias.shape, jnp.float32),
        jnp.zeros(fc1_bias.shape, jnp.float32),
        jnp.zeros(vectors.shape, jnp.float32),
        zero_owner,
    )
    backward_inputs = (
        block_input[:, 0],
        out_cotangent[:, 0],
        picture_ids[:, 0],
        patch_positions[0][:, 0],
        patch_positions[1][:, 0],
        pad_mask[:, 0],
        picture_lengths[:, 0],
        saved_all,
    )
    final_sums, (input_rows_all, kept_all) = lax.scan(
        backward_step, zero_sums, backward_inputs, reverse=True
    )
    sum_qkv_bias, sum_up_bias, sum_vectors, owner_sums = final_sums
    down_stack, branch_stack, mixed_stack, up_stack = kept_all
    first_stack = saved_all[0]
    attended_stack = saved_all[5]
    second_stack = saved_all[7]
    activated_stack = saved_all[9]
    grad_qkv = owner_grad(flat_rows(first_stack), flat_rows(mixed_stack))
    grad_proj = owner_grad(flat_rows(branch_stack), flat_rows(attended_stack)).T
    grad_up = owner_grad(flat_rows(second_stack), flat_rows(up_stack))
    grad_down = owner_grad(flat_rows(down_stack), flat_rows(activated_stack)).T
    grad_qkv_bias, grad_up_bias = lax.psum((sum_qkv_bias, sum_up_bias), "dp")
    grad_vectors = lax.psum(sum_vectors, ("dp", "tensor"))
    summed = (grad_qkv, grad_proj, grad_up, grad_down, grad_qkv_bias, grad_up_bias, grad_vectors)
    gradients = tuple((gradient * grad_factor for gradient in summed))
    new_moments = []
    updates = []
    update_terms = []
    for master, moments, gradient, factor in zip(params, moment_list, gradients, shares):
        first, second, update = lamb_parts(master, moments, gradient)
        new_moments.append(jnp.stack([first, second]))
        updates.append(update)
        update_terms.append(jnp.sum(update * update) * factor)
    update_terms = jnp.stack(update_terms)
    weight_sq, update_sq = lax.psum(
        (
            jnp.stack(
                [jnp.sum(master * master) * factor for master, factor in zip(params, shares)]
            ),
            update_terms,
        ),
        ("dp", "tensor"),
    )
    trust = jnp.sqrt(weight_sq) / jnp.sqrt(update_sq + 1e-12)
    new_params = [params[index] - LEARN_RATE * trust[index] * updates[index] for index in range(7)]
    norms = jnp.stack([jnp.sqrt(weight_sq), jnp.sqrt(update_sq)])
    block_output = outputs[:, None]
    input_grad = input_rows_all[:, None]
    return (
        block_output,
        input_grad,
        new_params[0],
        new_params[1],
        new_params[2],
        new_params[3],
        new_params[4],
        new_params[5],
        new_params[6],
        new_moments[0],
        new_moments[1],
        new_moments[2],
        new_moments[3],
        new_moments[4],
        new_moments[5],
        new_moments[6],
        new_params[0].astype(jnp.bfloat16),
        new_params[1].astype(jnp.bfloat16),
        new_params[2].astype(jnp.bfloat16),
        new_params[3].astype(jnp.bfloat16),
        norms,
        trust,
    )


def solution(mesh):
    in_specs = (
        P(None, "dp", "tensor", None),
        P(None, "dp", "tensor", None),
        P(None, "dp", None),
        P(None, None, "dp", None),
        P(None, "dp", None),
        P(None, "dp", None),
        P("dp", None, "tensor"),
        P("tensor", "dp"),
        P("dp", "tensor"),
        P("tensor", "dp"),
        P(None, "tensor"),
        P("tensor"),
        P(),
        P(None, "dp", None, "tensor"),
        P(None, "tensor", "dp"),
        P(None, "dp", "tensor"),
        P(None, "tensor", "dp"),
        P(None, None, "tensor"),
        P(None, "tensor"),
        P(),
    )
    out_specs = (
        P(None, "dp", "tensor", None),
        P(None, "dp", "tensor", None),
        P("dp", None, "tensor"),
        P("tensor", "dp"),
        P("dp", "tensor"),
        P("tensor", "dp"),
        P(None, "tensor"),
        P("tensor"),
        P(),
        P(None, "dp", None, "tensor"),
        P(None, "tensor", "dp"),
        P(None, "dp", "tensor"),
        P(None, "tensor", "dp"),
        P(None, None, "tensor"),
        P(None, "tensor"),
        P(),
        P("dp", None, "tensor"),
        P("tensor", "dp"),
        P("dp", "tensor"),
        P("tensor", "dp"),
        P(),
        P(),
    )
    return jax.shard_map(body, mesh=mesh, in_specs=in_specs, out_specs=out_specs, check_vma=False)
```

profile of v0, /device:TPU:0, one launch (start us, length us, event | category | flops | bytes accessed | tf_op | source)
XLA Modules:
  0.0 1638.6 jit_solution(13775843257738431195)
XLA Ops:
  14.1 39.4 %all-gather.11.cloned.1.call-done = bf16[640,1280]{0,1:T(8,128)(2,1)} async-done(((bf16[640,80]{0,1:T(8,128)(2,1)}), bf16[640,1280]{0,1:T(8,128)(2,1)}) %all-gather.11.cloned.1.call-update) | async-done | bytes 1638416 | tf_op jit(solution)/shard_map/all_gather | solution.py:177
  57.0 61.6 %all-gather.15.cloned.1.call-done = bf16[2560,1280]{0,1:T(8,128)(2,1)} async-done(((bf16[2560,80]{0,1:T(8,128)(2,1)}), bf16[2560,1280]{0,1:T(8,128)(2,1)}) %all-gather.15.cloned.1.call-update) | async-done | bytes 6553616 | tf_op jit(solution)/shard_map/all_gather | solution.py:179
  128.1 46.3 %all-gather.9.cloned.1.call-done = bf16[1280,3,640]{2,0,1:T(8,128)(2,1)} async-done(((bf16[80,3,640]{2,0,1:T(8,128)(2,1)}), bf16[1280,3,640]{2,0,1:T(8,128)(2,1)}) %all-gather.9.cloned.1.call-update) | async-done | bytes 4915216 | tf_op jit(solution)/shard_map/all_gather | solution.py:176
  174.4 64.7 %all-gather.13.cloned.1.call-done = bf16[1280,2560]{1,0:T(8,128)(2,1)} async-done(((bf16[80,2560]{1,0:T(8,128)(2,1)}), bf16[1280,2560]{1,0:T(8,128)(2,1)}) %all-gather.13.cloned.1.call-update) | async-done | bytes 6553616 | tf_op jit(solution)/shard_map/all_gather | solution.py:178
  246.8 381.4 %while.60 = (s32[]{:T(128)}, bf16[2,288,1280]{2,1,0:T(8,128)(2,1)}, bf16[2,576,1280]{2,1,0:T(8,128)(2,1)}, bf16[2,576,8,80]{1,3,2,0:T(8,128)(2,1)}, bf16[2,576,8...) while((s32[]{:T(128)}, bf16[2,288,1280]{2,1,0:T(8,128)(2,1)}, ...), condition=%wide.region_9.10_spmd, body=%wide.region_0.9_spmd.sunk | while | flops 12237604864 | bytes 285456864 | solution.py:233
  255.2 19.3 %all-gather.17.cloned.1.call-done = bf16[576,1280]{1,0:T(8,128)(2,1)} async-done(((bf16[288,1280]{1,0:T(8,128)(2,1)}), bf16[576,1280]{1,0:T(8,128)(2,1)}) %all-gather.17.cloned.1.call-update) | async-done | bytes 1474576 | tf_op jit(solution)/shard_map/while/body/eval_jaxpr/all_gather | solution.py:93
  301.0 41.3 %reduce-scatter.17.cloned.1.call-done = f32[288,1280]{1,0:T(8,128)} async-done(((f32[576,1280]{1,0:T(8,128)}), f32[288,1280]{1,0:T(8,128)}) %reduce-scatter.17.cloned.1.call-update) | async-done | bytes 1474576 | tf_op jit(solution)/shard_map/while/body/eval_jaxpr/reduce_scatter | solution.py:97
  347.0 26.2 %all-gather.19.cloned.1.call-done = bf16[576,1280]{1,0:T(8,128)(2,1)} async-done(((bf16[288,1280]{1,0:T(8,128)(2,1)}), bf16[576,1280]{1,0:T(8,128)(2,1)}) %all-gather.19.cloned.1.call-update) | async-done | bytes 1474576 | tf_op jit(solution)/shard_map/while/body/eval_jaxpr/all_gather | solution.py:93
  406.9 27.2 %reduce-scatter.19.cloned.1.call-done = f32[288,1280]{1,0:T(8,128)} async-done(((f32[576,1280]{1,0:T(8,128)}), f32[288,1280]{1,0:T(8,128)}) %reduce-scatter.19.cloned.1.call-update) | async-done | bytes 1474576 | tf_op jit(solution)/shard_map/while/body/eval_jaxpr/reduce_scatter | solution.py:97
  445.1 20.8 %all-gather.17.cloned.1.call-done = bf16[576,1280]{1,0:T(8,128)(2,1)} async-done(((bf16[288,1280]{1,0:T(8,128)(2,1)}), bf16[576,1280]{1,0:T(8,128)(2,1)}) %all-gather.17.cloned.1.call-update) | async-done | bytes 1474576 | tf_op jit(solution)/shard_map/while/body/eval_jaxpr/all_gather | solution.py:93
  492.4 41.3 %reduce-scatter.17.cloned.1.call-done = f32[288,1280]{1,0:T(8,128)} async-done(((f32[576,1280]{1,0:T(8,128)}), f32[288,1280]{1,0:T(8,128)}) %reduce-scatter.17.cloned.1.call-update) | async-done | bytes 1474576 | tf_op jit(solution)/shard_map/while/body/eval_jaxpr/reduce_scatter | solution.py:97
  538.4 26.2 %all-gather.19.cloned.1.call-done = bf16[576,1280]{1,0:T(8,128)(2,1)} async-done(((bf16[288,1280]{1,0:T(8,128)(2,1)}), bf16[576,1280]{1,0:T(8,128)(2,1)}) %all-gather.19.cloned.1.call-update) | async-done | bytes 1474576 | tf_op jit(solution)/shard_map/while/body/eval_jaxpr/all_gather | solution.py:93
  564.6 11.2 bitcast_dynamic-update-slice_fusion.19
  598.5 27.1 %reduce-scatter.19.cloned.1.call-done = f32[288,1280]{1,0:T(8,128)} async-done(((f32[576,1280]{1,0:T(8,128)}), f32[288,1280]{1,0:T(8,128)}) %reduce-scatter.19.cloned.1.call-update) | async-done | bytes 1474576 | tf_op jit(solution)/shard_map/while/body/eval_jaxpr/reduce_scatter | solution.py:97
  638.6 444.1 %while.61 = (s32[]{:T(128)}, f32[3,640]{1,0:T(4,128)S(1)}, f32[2560]{0:T(1024)S(1)}, f32[6,1280]{1,0:T(8,128)S(1)}, bf16[2,288,1280]{2,1,0:T(8,128)(2,1)}, /*ind...) while((s32[]{:T(128)}, f32[3,640]{1,0:T(4,128)S(1)}, ...), condition=%wide.region_31.32_spmd.clone, body=%wide.region_10.31_spmd.clone.sunk | while | flops 13548062720 | bytes 386946240 | solution.py:335
  662.2 26.2 %all-gather.21.cloned.1.call-done = bf16[576,1280]{1,0:T(8,128)(2,1)} async-done(((bf16[288,1280]{1,0:T(8,128)(2,1)}), bf16[576,1280]{1,0:T(8,128)(2,1)}) %all-gather.21.cloned.1.call-update) | async-done | bytes 1474576 | tf_op jit(solution)/shard_map/while/body/eval_jaxpr/all_gather | solution.py:93
  712.0 38.1 %reduce-scatter.21.cloned.1.call-done = f32[288,1280]{1,0:T(8,128)} async-done(((f32[576,1280]{1,0:T(8,128)}), f32[288,1280]{1,0:T(8,128)}) %reduce-scatter.21.cloned.1.call-update) | async-done | bytes 1474576 | tf_op jit(solution)/shard_map/while/body/eval_jaxpr/reduce_scatter | solution.py:97
  767.7 14.1 all-gather.23.cloned.1.call-done
  830.9 30.6 %reduce-scatter.23.cloned.1.call-done = f32[288,1280]{1,0:T(8,128)} async-done(((f32[576,1280]{1,0:T(8,128)}), f32[288,1280]{1,0:T(8,128)}) %reduce-scatter.23.cloned.1.call-update) | async-done | bytes 1474576 | tf_op jit(solution)/shard_map/while/body/eval_jaxpr/reduce_scatter | solution.py:97
  870.6 26.2 %all-gather.21.cloned.1.call-done = bf16[576,1280]{1,0:T(8,128)(2,1)} async-done(((bf16[288,1280]{1,0:T(8,128)(2,1)}), bf16[576,1280]{1,0:T(8,128)(2,1)}) %all-gather.21.cloned.1.call-update) | async-done | bytes 1474576 | tf_op jit(solution)/shard_map/while/body/eval_jaxpr/all_gather | solution.py:93
  920.5 38.1 %reduce-scatter.21.cloned.1.call-done = f32[288,1280]{1,0:T(8,128)} async-done(((f32[576,1280]{1,0:T(8,128)}), f32[288,1280]{1,0:T(8,128)}) %reduce-scatter.21.cloned.1.call-update) | async-done | bytes 1474576 | tf_op jit(solution)/shard_map/while/body/eval_jaxpr/reduce_scatter | solution.py:97
  976.1 14.1 all-gather.23.cloned.1.call-done
  1039.3 30.7 %reduce-scatter.23.cloned.1.call-done = f32[288,1280]{1,0:T(8,128)} async-done(((f32[576,1280]{1,0:T(8,128)}), f32[288,1280]{1,0:T(8,128)}) %reduce-scatter.23.cloned.1.call-update) | async-done | bytes 1474576 | tf_op jit(solution)/shard_map/while/body/eval_jaxpr/reduce_scatter | solution.py:97
  1091.4 11.9 convolution_bitcast_fusion.3
  1105.3 13.8 convolution_bitcast_fusion.2
  1121.0 13.8 convolution_bitcast_fusion.1
  1135.7 61.7 %all-reduce.1 = (f32[3,640]{1,0:T(4,128)S(1)}, f32[2560]{0:T(1024)S(1)}) all-reduce(f32[3,640]{1,0:T(4,128)S(1)} %get-tuple-element.805, f32[2560]{0:T(1024)S(1)} %get-tuple-element.806), channel_id=1, replica_groups=mesh['dp'=16,'tensor'=2] {'dp'}, use_global_device_ids=true, to_apply=%region_48.49 | all-reduce | flops 4480 | bytes 35840 | tf_op jit(solution)/shard_map/psum | solution.py:348
  1202.5 41.7 %psum.38 = f32[6,1280]{1,0:T(8,128)S(1)} all-reduce(f32[6,1280]{1,0:T(8,128)S(1)} %get-tuple-element.807), channel_id=1, replica_groups=mesh['dp'=16,'tensor'=2] {'dp','tensor'}, use_global_device_ids=true, to_apply=%region_52.53 | all-reduce | flops 7680 | bytes 61440 | tf_op jit(solution)/shard_map/psum | solution.py:349
  1250.8 26.6 %reduce-scatter.9.cloned.1.call-done = f32[80,3,640]{2,0,1:T(8,128)} async-done(((f32[1280,3,640]{2,0,1:T(8,128)}), f32[80,3,640]{2,0,1:T(8,128)}) %reduce-scatter.9.cloned.1.call-update) | async-done | bytes 614416 | tf_op jit(solution)/shard_map/reduce_scatter | solution.py:114
  1281.0 139.2 %reduce-scatter.13.cloned.1.call-done = f32[80,2560]{1,0:T(8,128)} async-done(((f32[1280,2560]{1,0:T(8,128)}), f32[80,2560]{1,0:T(8,128)}) %reduce-scatter.13.cloned.1.call-update) | async-done | bytes 819216 | tf_op jit(solution)/shard_map/reduce_scatter | solution.py:114
  1424.2 137.5 %reduce-scatter.15.cloned.1.call-done = f32[80,2560]{1,0:T(8,128)} async-done(((f32[1280,2560]{1,0:T(8,128)}), f32[80,2560]{1,0:T(8,128)}) %reduce-scatter.15.cloned.1.call-update) | async-done | bytes 819216 | tf_op jit(solution)/shard_map/reduce_scatter | solution.py:114
  1574.5 39.6 %all-reduce = (f32[7]{0:T(128)S(1)}, f32[7]{0:T(128)S(1)}) all-reduce(f32[7]{0:T(128)} %stack.224, f32[7]{0:T(128)} %stack.216), channel_id=1, replica_groups=mesh['dp'=16,'tensor'=2] {'dp','tensor'}, use_global_device_ids=true, to_apply=%region_54.55 | all-reduce | flops 14 | bytes 112 | tf_op jit(solution)/shard_map/psum | solution.py:361
  (552 shorter events, 429.9 us)
Async XLA Ops:
  7.2 46.2 %all-gather.11.cloned.1.call-start = ((), (), s32[]{:S(2)}) async-start(), calls=%async_computation.9 | async-start | bytes 1740800 | tf_op jit(solution)/shard_map/all_gather | solution.py:177
  9.0 109.7 %all-gather.15.cloned.1.call-start = ((), (), s32[]{:S(2)}) async-start(), calls=%async_computation.11 | async-start | bytes 6963200 | tf_op jit(solution)/shard_map/all_gather | solution.py:179
  11.0 163.4 %all-gather.9.cloned.1.call-start = ((), (), s32[]{:S(2)}) async-start(), calls=%async_computation.8 | async-start | bytes 5222400 | tf_op jit(solution)/shard_map/all_gather | solution.py:176
  11.8 227.2 %all-gather.13.cloned.1.call-start = ((), (), s32[]{:S(2)}) async-start(), calls=%async_computation.10 | async-start | bytes 6963200 | tf_op jit(solution)/shard_map/all_gather | solution.py:178
  246.8 27.7 %all-gather.17.cloned.1.call-start = ((), (), s32[]{:S(2)}) async-start(), calls=%async_computation.16 | async-start | bytes 2211840 | tf_op jit(solution)/shard_map/while/body/eval_jaxpr/all_gather | solution.py:93
  249.7 92.6 %reduce-scatter.17.cloned.1.call-start = ((), (), s32[]{:S(2)}) async-start(), calls=%async_computation.17 | async-start | bytes 4423680 | tf_op jit(solution)/shard_map/while/body/eval_jaxpr/reduce_scatter | solution.py:97
  301.0 72.2 %all-gather.19.cloned.1.call-start = ((), (), s32[]{:S(2)}) async-start(), calls=%async_computation.18 | async-start | bytes 2211840 | tf_op jit(solution)/shard_map/while/body/eval_jaxpr/all_gather | solution.py:93
  347.0 87.2 %reduce-scatter.19.cloned.1.call-start = ((), (), s32[]{:S(2)}) async-start(), calls=%async_computation.19 | async-start | bytes 4423680 | tf_op jit(solution)/shard_map/while/body/eval_jaxpr/reduce_scatter | solution.py:97
  436.7 29.2 %all-gather.17.cloned.1.call-start = ((), (), s32[]{:S(2)}) async-start(), calls=%async_computation.16 | async-start | bytes 2211840 | tf_op jit(solution)/shard_map/while/body/eval_jaxpr/all_gather | solution.py:93
  439.6 94.1 %reduce-scatter.17.cloned.1.call-start = ((), (), s32[]{:S(2)}) async-start(), calls=%async_computation.17 | async-start | bytes 4423680 | tf_op jit(solution)/shard_map/while/body/eval_jaxpr/reduce_scatter | solution.py:97
  492.3 72.3 %all-gather.19.cloned.1.call-start = ((), (), s32[]{:S(2)}) async-start(), calls=%async_computation.18 | async-start | bytes 2211840 | tf_op jit(solution)/shard_map/while/body/eval_jaxpr/all_gather | solution.py:93
  538.4 87.3 %reduce-scatter.19.cloned.1.call-start = ((), (), s32[]{:S(2)}) async-start(), calls=%async_computation.19 | async-start | bytes 4423680 | tf_op jit(solution)/shard_map/while/body/eval_jaxpr/reduce_scatter | solution.py:97
  658.1 40.5 %copy-start.4 = (bf16[2,288,1280]{2,1,0:T(8,128)(2,1)}, bf16[2,288,1280]{2,1,0:T(8,128)(2,1)S(1)}, u32[]{:S(2)}) copy-start(bf16[2,288,1280]{2,1,0:T(8,128)(2,1)S(1)} %get-tuple-element.1974) | copy-start | bytes 4423684 | tf_op jit(solution)/shard_map/while
  658.1 30.3 %all-gather.21.cloned.1.call-start = ((), (), s32[]{:S(2)}) async-start(), calls=%async_computation.20 | async-start | bytes 2211840 | tf_op jit(solution)/shard_map/while/body/eval_jaxpr/all_gather | solution.py:93
  662.1 88.0 %reduce-scatter.21.cloned.1.call-start = ((), (), s32[]{:S(2)}) async-start(), calls=%async_computation.21 | async-start | bytes 4423680 | tf_op jit(solution)/shard_map/while/body/eval_jaxpr/reduce_scatter | solution.py:97
  708.8 72.9 %all-gather.23.cloned.1.call-start = ((), (), s32[]{:S(2)}) async-start(), calls=%async_computation.22 | async-start | bytes 2211840 | tf_op jit(solution)/shard_map/while/body/eval_jaxpr/all_gather | solution.py:93
  755.5 106.0 %reduce-scatter.23.cloned.1.call-start = ((), (), s32[]{:S(2)}) async-start(), calls=%async_computation.23 | async-start | bytes 4423680 | tf_op jit(solution)/shard_map/while/body/eval_jaxpr/reduce_scatter | solution.py:97
  866.6 30.2 %all-gather.21.cloned.1.call-start = ((), (), s32[]{:S(2)}) async-start(), calls=%async_computation.20 | async-start | bytes 2211840 | tf_op jit(solution)/shard_map/while/body/eval_jaxpr/all_gather | solution.py:93
  870.6 88.0 %reduce-scatter.21.cloned.1.call-start = ((), (), s32[]{:S(2)}) async-start(), calls=%async_computation.21 | async-start | bytes 4423680 | tf_op jit(solution)/shard_map/while/body/eval_jaxpr/reduce_scatter | solution.py:97
  917.3 72.9 %all-gather.23.cloned.1.call-start = ((), (), s32[]{:S(2)}) async-start(), calls=%async_computation.22 | async-start | bytes 2211840 | tf_op jit(solution)/shard_map/while/body/eval_jaxpr/all_gather | solution.py:93
  963.9 106.1 %reduce-scatter.23.cloned.1.call-start = ((), (), s32[]{:S(2)}) async-start(), calls=%async_computation.23 | async-start | bytes 4423680 | tf_op jit(solution)/shard_map/while/body/eval_jaxpr/reduce_scatter | solution.py:97
  1082.7 165.6 %reduce-scatter.11.cloned.1.call-start = ((), (), s32[]{:S(2)}) async-start(), calls=%async_computation.13 | async-start | bytes 3481600 | tf_op jit(solution)/shard_map/reduce_scatter | solution.py:114
  1089.6 187.8 %reduce-scatter.9.cloned.1.call-start = ((), (), s32[]{:S(2)}) async-start(), calls=%async_computation.12 | async-start | bytes 10444800 | tf_op jit(solution)/shard_map/reduce_scatter | solution.py:114
  1103.4 316.8 %reduce-scatter.13.cloned.1.call-start = ((), (), s32[]{:S(2)}) async-start(), calls=%async_computation.14 | async-start | bytes 13926400 | tf_op jit(solution)/shard_map/reduce_scatter | solution.py:114
  1119.2 442.6 %reduce-scatter.15.cloned.1.call-start = ((), (), s32[]{:S(2)}) async-start(), calls=%async_computation.15 | async-start | bytes 13926400 | tf_op jit(solution)/shard_map/reduce_scatter | solution.py:114
  1134.8 62.6 %copy-start.49 = (f32[2560]{0:T(1024)S(1)}, f32[2560]{0:T(1024)}, u32[]{:S(2)}) copy-start(f32[2560]{0:T(1024)} %get-tuple-element.2088) | copy-start | bytes 30724
  1134.8 64.6 %copy-start.59 = (f32[3,640]{1,0:T(4,128)S(1)}, f32[3,640]{1,0:T(4,128)}, u32[]{:S(2)}) copy-start(f32[3,640]{1,0:T(4,128)} %param.34) | copy-start | bytes 23044
  1134.8 113.5 %copy-start.45 = (f32[640,80]{0,1:T(8,128)S(1)}, f32[640,80]{0,1:T(8,128)}, u32[]{:S(2)}) copy-start(f32[640,80]{0,1:T(8,128)} %param.31) | copy-start | bytes 614404
  1134.8 113.5 %copy-start.51 = (f32[2,640,80]{1,2,0:T(8,128)S(1)}, f32[2,640,80]{1,2,0:T(8,128)}, u32[]{:S(2)}) copy-start(f32[2,640,80]{1,2,0:T(8,128)} %param.38) | copy-start | bytes 1228804
  1197.4 80.0 %copy-start.35 = (f32[80,3,640]{2,0,1:T(8,128)S(1)}, f32[80,3,640]{2,0,1:T(8,128)}, u32[]{:S(2)}) copy-start(f32[80,3,640]{2,0,1:T(8,128)} %param.30) | copy-start | bytes 1843204
  1250.8 169.4 %copy-start.33 = (f32[80,2560]{1,0:T(8,128)S(1)}, f32[80,2560]{1,0:T(8,128)}, u32[]{:S(2)}) copy-start(f32[80,2560]{1,0:T(8,128)} %param.32) | copy-start | bytes 2457604
  1281.0 280.7 %copy-start.31 = (f32[2560,80]{0,1:T(8,128)S(1)}, f32[2560,80]{0,1:T(8,128)}, u32[]{:S(2)}) copy-start(f32[2560,80]{0,1:T(8,128)} %param.33) | copy-start | bytes 2457604
  (108 other events, 424.8 us)
Sparse Core Ops, SparseCore 0:
  10.8 42.6 all-gather.10
  56.3 62.2 all-gather.14
  121.4 52.9 all-gather.8
  177.1 61.9 all-gather.12
  249.8 24.6 all-gather.16
  301.1 41.1 reduce-scatter.16
  347.1 26.0 all-gather.18
  392.9 41.1 reduce-scatter.18
  439.7 26.0 all-gather.16
  492.5 41.1 reduce-scatter.16
  538.5 26.0 all-gather.18
  584.4 41.1 reduce-scatter.18
  662.3 26.0 all-gather.20
  709.0 41.1 reduce-scatter.20
  755.6 26.0 all-gather.22
  820.3 41.1 reduce-scatter.22
  870.7 26.0 all-gather.20
  917.4 41.1 reduce-scatter.20
  964.0 26.0 all-gather.22
  1028.7 41.1 reduce-scatter.22
  1089.8 66.8 reduce-scatter.10
  1161.4 116.0 reduce-scatter.8
  1282.1 138.0 reduce-scatter.12
  1424.2 137.4 reduce-scatter.14
where the time goes:
time: 1660 us; the launch traced here: 1640 us
  waiting for transfers between devices  963 us (58%)
  matrix products  229 us (14%)
  blocking collectives  143 us (9%)
  other arithmetic  139 us (8%)
  local copies, waits for them, and re-layouts  112 us (7%)
  loops' own time  28.7 us (2%)
  between operations  23.4 us (1%)
    reduce_scatter x4, waiting for transfers between devices, owner_grad(): lax.psum_scatter(outer_term(left, right), 'dp', scatter_dimension=0, tile...  303 us
    reduce_scatter x8, waiting for transfers between devices, spread_rows(): lax.psum_scatter(lax.dot_general(source, weight_low, (contract, ((), ()))...  275 us
    all_gather x8, waiting for transfers between devices, collect_rows(): return lax.all_gather(rows_low, 'tensor', axis=0, tiled=True)  173 us
    all_gather x1, waiting for transfers between devices, body(): lax.all_gather(low_weights[2], 'dp', axis=0, tiled=True)  64.7 us
    psum x1, blocking collectives, body(): grad_qkv_bias, grad_up_bias = lax.psum((sum_qkv_bias, sum_up_bias), 'dp')  61.7 us
    all_gather x1, waiting for transfers between devices, body(): lax.all_gather(low_weights[3], 'dp', axis=1, tiled=True)  61.6 us
    dot_general x8, matrix products, spread_rows(): lax.dot_general(source, weight_low, (contract, ((), ())), preferred_eleme...  55 us
    dot_general x4, matrix products, outer_term(): lax.dot_general(left, right, (((0,), (0,)), ((), ())), preferred_element_...  46.4 us
  transfers between devices with their start and end apart: 24, of which 23 were waited for; matrix products, arithmetic and copies ran while one was open for 9% of the time, Pallas kernels for 0%

commit v1 on v0

v1 whole, which is shorter than its diff:
```python
import jax
import jax.numpy as jnp
from jax import lax
from jax.sharding import PartitionSpec as P

HD = 80
SLOTS = 4
LEN = 576


NEGATIVE = -1e30
EPS_NORM = 1e-06
EPS_ADAM = 1e-06
WEIGHT_DECAY = 0.01
LEARN_RATE = 0.5
GELU_SLOPE = 1.702
F32 = jnp.float32
LOW = jnp.bfloat16


def norm_parts(values):
    center = values - jnp.mean(values, -1, keepdims=True)
    inverse = lax.rsqrt(jnp.mean(center * center, -1, keepdims=True) + EPS_NORM)
    return (center * inverse, inverse)


def norm_back(out_grad, normed, inverse, gain):
    scaled = out_grad * gain
    return inverse * (
        scaled
        - jnp.mean(scaled, -1, keepdims=True)
        - normed * jnp.mean(scaled * normed, -1, keepdims=True)
    )


def rotary_tables(rows_at, cols_at):
    quarter = HD // 4
    frequency = 10000.0 ** (-jnp.arange(quarter, dtype=F32) / quarter)
    halves = jnp.concatenate(
        [
            rows_at.astype(F32)[:, None] * frequency,
            cols_at.astype(F32)[:, None] * frequency,
        ],
        -1,
    )
    angles = jnp.concatenate([halves, halves], -1)
    return (jnp.cos(angles), jnp.sin(angles))


def rotate_pairs(values, cosine, sine):
    middle = values.shape[-1] // 2
    turned = jnp.concatenate([-values[..., middle:], values[..., :middle]], -1)
    return values * cosine[:, None, :] + turned * sine[:, None, :]


def rotate_back(grads, cosine, sine):
    middle = grads.shape[-1] // 2
    weighted = grads * sine[:, None, :]
    return grads * cosine[:, None, :] + jnp.concatenate(
        [weighted[..., middle:], -weighted[..., :middle]], -1
    )


def attend(queries, keys_rot, values, allowed):
    score_scale = HD ** (-0.5)
    raw_scores = jnp.einsum("qhd,khd->hqk", queries, keys_rot, preferred_element_type=F32)
    logits = jnp.where(allowed[None], raw_scores * score_scale, NEGATIVE)
    row_top = jnp.max(logits, -1, keepdims=True)
    exponent = jnp.exp(logits - row_top)
    row_total = jnp.sum(exponent, -1, keepdims=True)
    prob_rows = (exponent / row_total).astype(LOW)
    mixed = jnp.einsum("hqk,khd->qhd", prob_rows, values, preferred_element_type=F32)
    return (mixed, row_top + jnp.log(row_total))


def attend_back(queries, keys_rot, values, allowed, log_total, grad_out):
    score_scale = HD ** (-0.5)
    raw_scores = jnp.einsum("qhd,khd->hqk", queries, keys_rot, preferred_element_type=F32)
    logits = jnp.where(allowed[None], raw_scores * score_scale, NEGATIVE)
    prob_rows = jnp.exp(logits - log_total)
    prob_grad = jnp.einsum("qhd,khd->hqk", grad_out, values, preferred_element_type=F32)
    inner_sum = jnp.sum(prob_rows * prob_grad, -1, keepdims=True)
    score_grad = (score_scale * prob_rows * (prob_grad - inner_sum)).astype(LOW)
    query_grad = jnp.einsum("hqk,khd->qhd", score_grad, keys_rot, preferred_element_type=F32)
    key_grad = jnp.einsum("hqk,qhd->khd", score_grad, queries, preferred_element_type=F32)
    value_grad = jnp.einsum(
        "hqk,qhd->khd", prob_rows.astype(LOW), grad_out, preferred_element_type=F32
    )
    return (query_grad, key_grad, value_grad)


def dot(left, right):
    return lax.dot_general(left, right, (((1,), (0,)), ((), ())), preferred_element_type=F32)


def dot_t(left, right):
    return lax.dot_general(left, right, (((1,), (1,)), ((), ())), preferred_element_type=F32)


def outer(left, right):
    return lax.dot_general(left, right, (((0,), (0,)), ((), ())), preferred_element_type=F32)


def lamb_parts(master, moments, gradient):
    first = 0.5 * moments[0] + 0.5 * gradient
    second = 0.5 * moments[1] + 0.5 * gradient * gradient
    update = first / (jnp.sqrt(second) + EPS_ADAM) + WEIGHT_DECAY * master
    return (first, second, update)


class Lanes:
    def __init__(self, dp):
        self.dp = dp
        self.ring = dp // 4

    def over_x(self, v):
        return lax.ppermute(v, "tensor", [(0, 1), (1, 0)])

    def over_core(self, v):
        return lax.ppermute(v, "dp", [(i, i ^ 1) for i in range(self.dp)])

    def over_y(self, v):
        return lax.ppermute(v, "dp", [(i, i ^ 2) for i in range(self.dp)])

    def down_z(self, v):
        return lax.ppermute(v, "dp", [(i, (i - 4) % self.dp) for i in range(self.dp)])

    def up_z(self, v):
        return lax.ppermute(v, "dp", [(i, (i + 4) % self.dp) for i in range(self.dp)])

    def order(self):
        i = lax.axis_index("dp")
        z, y, c = i // 4, (i // 2) % 2, i % 2
        blocks = []
        for dc in range(2):
            for dy in range(2):
                for dz in range(self.ring):
                    blocks.append(((z + dz) % self.ring) * 4 + (y ^ dy) * 2 + (c ^ dc))
        return jnp.stack(blocks)

    def ring_down(self, v):
        held = [v]
        for _ in range(self.ring - 1):
            held.append(self.down_z(held[-1]))
        return held

    def gather_a(self, own):
        wide = jnp.concatenate([own, self.over_x(own)], 1)
        held = jnp.concatenate(self.ring_down(wide), 0)
        across = self.over_y(held)
        return [held, across, self.over_core(held), self.over_core(across)]

    def gather_b(self, own):
        pair = jnp.stack([own, self.over_y(own)])
        held = jnp.stack(self.ring_down(pair), 1)
        held = held.reshape((-1,) + own.shape[1:])
        across = self.over_x(held)
        return [held, self.over_core(held)], [across, self.over_core(across)]

    def reduce_a(self, own, other):
        own = own + [self.over_x(total(other))]
        half = own[0].shape[0] // 2
        came = self.over_y(total([v[half:] for v in own]))
        own = [v[:half] for v in own] + [came]
        rows = half // self.ring
        came = None
        for step in range(self.ring - 1, -1, -1):
            part = [v[step * rows : (step + 1) * rows] for v in own]
            if came is not None:
                part = part + [came]
            if step:
                came = self.up_z(total(part))
        return wide_total(part)

    def reduce_b(self, own, other):
        half = own[0].shape[0] // 2
        came = self.over_y(
            jnp.stack([total([v[half:] for v in own]), total([v[half:] for v in other])])
        )
        own = [v[:half] for v in own] + [came[0]]
        other = [v[:half] for v in other] + [came[1]]
        rows = half // self.ring
        came = None
        for step in range(self.ring - 1, -1, -1):
            cut = slice(step * rows, (step + 1) * rows)
            parts = [[v[cut] for v in own], [v[cut] for v in other]]
            if came is not None:
                parts = [parts[0] + [came[0]], parts[1] + [came[1]]]
            if step:
                came = self.up_z(jnp.stack([total(parts[0]), total(parts[1])]))
        return wide_total(parts[0] + [self.over_x(total(parts[1]))])


def wide_total(parts):
    result = parts[0].astype(F32)
    for part in parts[1:]:
        result = result + part.astype(F32)
    return result


def total(parts):
    return wide_total(parts).astype(LOW)


class PlainLanes(Lanes):
    def order(self):
        return jnp.arange(self.dp)

    def gather_a(self, own):
        wide = jnp.concatenate([own, self.over_x(own)], 1)
        return [lax.all_gather(wide, "dp", axis=0, tiled=True)]

    def gather_b(self, own):
        held = lax.all_gather(own, "dp", axis=0, tiled=True)
        return [held], [self.over_x(held)]


def butterfly(value, dp):
    if dp & (dp - 1):
        return lax.psum(value, ("dp", "tensor"))
    value = value + lax.ppermute(value, "tensor", [(0, 1), (1, 0)])
    bit = 1
    while bit < dp:
        value = value + lax.ppermute(value, "dp", [(i, i ^ bit) for i in range(dp)])
        bit *= 2
    return value


def body(
    block_input,
    out_cotangent,
    picture_ids,
    patch_positions,
    picture_lengths,
    pad_mask,
    qkv_weight,
    proj_weight,
    fc1_weight,
    fc2_weight,
    qkv_bias,
    fc1_bias,
    vectors,
    qkv_moments,
    proj_moments,
    fc1_moments,
    fc2_moments,
    qkv_bias_moments,
    fc1_bias_moments,
    vector_moments,
):
    dp = lax.axis_size("dp")
    relative = dp == 16
    lanes = Lanes(dp) if relative else PlainLanes(dp)
    slot = lax.axis_index("tensor")
    lead_dp = (lax.axis_index("dp") == 0).astype(F32)
    lead_all = lead_dp * (slot == 0).astype(F32)
    width = block_input.shape[3]
    rows_own = width // dp
    half_heads = qkv_weight.shape[2] // HD // 2
    quarter = half_heads * HD
    hidden = fc1_weight.shape[1] // 2
    grad_factor = float(block_input.shape[0] * block_input.shape[1] * dp * LEN) ** (-0.5)

    def own_row(both):
        mine = lax.dynamic_index_in_dim(both[:, 0], slot, 0, keepdims=False)
        theirs = lax.dynamic_index_in_dim(both[:, 0], 1 - slot, 0, keepdims=False)
        return jnp.concatenate([mine, lanes.over_x(theirs)], 0)

    local_rows = block_input.shape[2]
    biases = jnp.concatenate([qkv_bias.reshape(-1), fc1_bias])
    other_biases = lanes.over_x(biases)

    def pick(array, axis=0):
        return lax.dynamic_index_in_dim(array, slot, axis, keepdims=False)

    def turn(values):
        return jnp.roll(values, -slot * local_rows, axis=-1)

    ids_row = turn(pick(picture_ids[:, 0]))
    rows_at = turn(pick(patch_positions[0, :, 0]))
    cols_at = turn(pick(patch_positions[1, :, 0]))
    mask_row = turn(pick(pad_mask[:, 0]))
    length_row = pick(picture_lengths[:, 0])

    q_low = qkv_weight.astype(LOW)
    p_low = proj_weight.astype(LOW).T
    group_1 = [
        jnp.concatenate(
            [
                q_low[:, :, k * quarter : (k + 1) * quarter].reshape(rows_own, 3 * quarter),
                p_low[:, k * quarter : (k + 1) * quarter],
            ],
            1,
        )
        for k in range(2)
    ]
    f1_low = fc1_weight.astype(LOW)
    f2_low = fc2_weight.astype(LOW).T
    group_2 = [f1_low[:, k * hidden : (k + 1) * hidden] for k in range(2)]
    group_3 = [f2_low[:, k * hidden : (k + 1) * hidden] for k in range(2)]

    def gather(group):
        wide = lanes.gather_a(group[0])
        own, other = lanes.gather_b(group[1])
        return wide, own, other

    g1, g2, g3 = gather(group_1), gather(group_2), gather(group_3)

    def rows_of(pieces, start, stop):
        return jnp.concatenate([v[:, start:stop] for v in pieces], 0)

    n1 = 4 * quarter
    w_qkv = [
        rows_of(g1[0], 0, 3 * quarter),
        rows_of(g1[0], n1, n1 + 3 * quarter),
        rows_of(g1[1], 0, 3 * quarter),
        rows_of(g1[2], 0, 3 * quarter),
    ]
    w_proj = [
        rows_of(g1[0], 3 * quarter, n1),
        rows_of(g1[0], n1 + 3 * quarter, 2 * n1),
        rows_of(g1[1], 3 * quarter, n1),
        rows_of(g1[2], 3 * quarter, n1),
    ]

    def three(group):
        return [jnp.concatenate(v, 0) for v in group]

    w_up = three(g2)
    w_down = three(g3)

    order = lanes.order()
    column = (order[:, None] * rows_own + jnp.arange(rows_own)[None, :]).reshape(-1)
    shuffle = (jnp.arange(width)[:, None] == column[None, :]).astype(LOW)
    if relative:
        vec = lax.dot_general(
            vectors,
            shuffle.astype(F32),
            (((1,), (0,)), ((), ())),
            precision=lax.Precision.HIGHEST,
            preferred_element_type=F32,
        )
        row_low = dot(own_row(block_input), shuffle).astype(LOW)
        cot_low = dot(own_row(out_cotangent), shuffle).astype(LOW)
    else:
        vec = vectors
        row_low = own_row(block_input)
        cot_low = own_row(out_cotangent)

    def quarters(own, other):
        half = own.shape[-1] // 2
        return [own[..., :half], other[..., :half], own[..., half:], other[..., half:]]

    bq = quarters(
        qkv_bias, other_biases[: qkv_bias.size].reshape(qkv_bias.shape)
    )
    bu = quarters(fc1_bias, other_biases[qkv_bias.size :])

    row_values = row_low.astype(F32)
    normed1, inverse1 = norm_parts(row_values)
    first_in = (normed1 * vec[0] + vec[1]).astype(LOW)
    mixed = [
        (dot(first_in, w) + b.reshape(-1)).reshape(LEN, 3, half_heads, HD)
        for w, b in zip(w_qkv, bq)
    ]
    mixed = jnp.concatenate(mixed, 2)
    heads = 4 * half_heads
    cosine, sine = rotary_tables(rows_at, cols_at)
    queries = rotate_pairs(mixed[:, 0], cosine, sine).astype(LOW)
    keys_rot = rotate_pairs(mixed[:, 1], cosine, sine).astype(LOW)
    head_values = mixed[:, 2].astype(LOW)
    allowed = (ids_row[:, None] == ids_row[None, :]) & (mask_row[None, :] == 1)
    attended, log_total = attend(queries, keys_rot, head_values, allowed)
    attended_low = attended.reshape(LEN, -1).astype(LOW)
    att_parts = [attended_low[:, k * quarter : (k + 1) * quarter] for k in range(4)]
    hidden1 = row_values + (sum(dot_t(a, w) for a, w in zip(att_parts, w_proj)) + vec[2])
    normed2, inverse2 = norm_parts(hidden1)
    second_in = (normed2 * vec[3] + vec[4]).astype(LOW)
    bu3 = [jnp.concatenate(bu[:2]), bu[2], bu[3]]
    upward = [dot(second_in, w) + b for w, b in zip(w_up, bu3)]
    activated = [(u * jax.nn.sigmoid(GELU_SLOPE * u)).astype(LOW) for u in upward]
    result = hidden1 + (sum(dot_t(a, w) for a, w in zip(activated, w_down)) + vec[5])

    def give_back(values_low):
        if relative:
            values_low = dot_t(values_low, shuffle).astype(LOW)
        mine, theirs = values_low[:local_rows], lanes.over_x(values_low[local_rows:])
        swap = slot == 0
        return jnp.stack([jnp.where(swap, mine, theirs), jnp.where(swap, theirs, mine)])[:, None]

    block_output = give_back(result.astype(LOW))

    slot_hit = (ids_row[:, None] == jnp.arange(SLOTS, dtype=jnp.int32)[None, :]).astype(F32)
    picture_size = jnp.sum(slot_hit * length_row.astype(F32)[None, :], -1)
    token_weight = mask_row.astype(F32) * jnp.sqrt(LEN / picture_size)
    grad_y = cot_low.astype(F32) * token_weight[:, None]
    down_grad = grad_y.astype(LOW)

    middle = width // 2

    def weight_grads(left, rights):
        kept = [outer(left[:, :middle], r).astype(LOW) for r in rights]
        sent = [outer(left[:, middle:], r).astype(LOW) for r in rights]
        return [[k, lanes.over_core(s)] for k, s in zip(kept, sent)]

    def columns(addends, start, stop):
        return [v[:, start:stop] for v in addends]

    def reduce_plain(parts):
        own = jnp.concatenate([parts[0], parts[2]], 1).astype(LOW)
        other = jnp.concatenate([parts[1], parts[3]], 1).astype(LOW)
        both = wide_total([own, lanes.over_x(other)])
        return lax.psum_scatter(both, "dp", scatter_dimension=0, tiled=True)

    def reduce_wide(left, rights):
        if not relative:
            a = outer(left, rights[0])
            return reduce_plain(
                [a[:, :hidden], a[:, hidden:], outer(left, rights[1]), outer(left, rights[2])]
            )
        a, b_own, b_other = weight_grads(left, rights)
        first = lanes.reduce_a(columns(a, 0, hidden), columns(a, hidden, 2 * hidden))
        second = lanes.reduce_b(b_own, b_other)
        return jnp.concatenate([first, second], 1)

    grad_down = reduce_wide(down_grad, activated).T
    act_grad = [dot(down_grad, w) for w in w_down]
    up_grad = []
    for g, u in zip(act_grad, upward):
        sigma = jax.nn.sigmoid(GELU_SLOPE * u)
        up_grad.append((g * (sigma + GELU_SLOPE * u * sigma * (1.0 - sigma))).astype(LOW))
    grad_up = reduce_wide(second_in, up_grad)
    sum_up = [jnp.sum(g.astype(F32), 0) for g in up_grad]
    norm2_grad = sum(dot_t(g, w) for g, w in zip(up_grad, w_up))
    hidden1_grad = grad_y + norm_back(norm2_grad, normed2, inverse2, vec[3])
    branch_grad = hidden1_grad.astype(LOW)
    attn_grad = jnp.concatenate([dot(branch_grad, w) for w in w_proj], 1).astype(LOW)
    attn_grad = attn_grad.reshape(LEN, heads, HD)
    query_grad, key_grad, value_grad = attend_back(
        queries, keys_rot, head_values, allowed, log_total, attn_grad
    )
    mixed_grad = jnp.stack(
        [rotate_back(query_grad, cosine, sine), rotate_back(key_grad, cosine, sine), value_grad], 1
    ).astype(LOW)
    mixed_parts = [
        mixed_grad[:, :, k * half_heads : (k + 1) * half_heads].reshape(LEN, 3 * quarter)
        for k in range(4)
    ]
    sum_qkv = [jnp.sum(g.astype(F32), 0).reshape(3, quarter) for g in mixed_parts]
    if relative:
        q_grads = weight_grads(first_in, mixed_parts)
        p_grads = weight_grads(branch_grad, att_parts)
        joined = [
            [jnp.concatenate([a, b], 1) for a, b in zip(q, p)] for q, p in zip(q_grads, p_grads)
        ]
        halves = [lanes.reduce_a(joined[0], joined[1]), lanes.reduce_b(joined[2], joined[3])]
        grad_qkv = jnp.concatenate(
            [h[:, : 3 * quarter].reshape(rows_own, 3, quarter) for h in halves], 2
        )
        grad_proj = jnp.concatenate([h[:, 3 * quarter :] for h in halves], 1).T
    else:
        q_parts = [outer(first_in, g).reshape(width, 3, quarter) for g in mixed_parts]
        own = jnp.concatenate([q_parts[0], q_parts[2]], 2)
        other = jnp.concatenate([q_parts[1], q_parts[3]], 2)
        grad_qkv = lax.psum_scatter(
            own + lanes.over_x(other), "dp", scatter_dimension=0, tiled=True
        )
        grad_proj = reduce_plain([outer(branch_grad, a) for a in att_parts]).T
    norm1_grad = sum(dot_t(g, w) for g, w in zip(mixed_parts, w_qkv))
    input_rows = hidden1_grad + norm_back(norm1_grad, normed1, inverse1, vec[0])
    input_grad = give_back(input_rows.astype(LOW))
    vector_terms = jnp.stack(
        [
            jnp.sum(norm1_grad * normed1, 0),
            jnp.sum(norm1_grad, 0),
            jnp.sum(branch_grad.astype(F32), 0),
            jnp.sum(norm2_grad * normed2, 0),
            jnp.sum(norm2_grad, 0),
            jnp.sum(down_grad.astype(F32), 0),
        ]
    )
    if relative:
        vector_terms = lax.dot_general(
            vector_terms,
            shuffle.astype(F32),
            (((1,), (1,)), ((), ())),
            precision=lax.Precision.HIGHEST,
            preferred_element_type=F32,
        )
    own_small = jnp.concatenate(
        [
            jnp.concatenate([sum_qkv[0], sum_qkv[2]], 1).reshape(-1),
            sum_up[0][:hidden],
            sum_up[1],
        ]
    )
    other_small = jnp.concatenate(
        [
            jnp.concatenate([sum_qkv[1], sum_qkv[3]], 1).reshape(-1),
            sum_up[0][hidden:],
            sum_up[2],
        ]
    )
    first_half = slot == 0
    small = jnp.concatenate(
        [
            jnp.where(first_half, own_small, other_small),
            jnp.where(first_half, other_small, own_small),
            vector_terms.reshape(-1),
        ]
    )
    small = butterfly(small.reshape(-1, 128), dp).reshape(-1)
    size = own_small.shape[0]
    bias_sum = jnp.where(first_half, small[:size], small[size : 2 * size])
    grad_qkv_bias = bias_sum[: qkv_bias.size].reshape(qkv_bias.shape)
    grad_up_bias = bias_sum[qkv_bias.size :]
    grad_vectors = small[2 * size :].reshape(vectors.shape)

    params = (qkv_weight, proj_weight, fc1_weight, fc2_weight, qkv_bias, fc1_bias, vectors)
    moment_list = (
        qkv_moments,
        proj_moments,
        fc1_moments,
        fc2_moments,
        qkv_bias_moments,
        fc1_bias_moments,
        vector_moments,
    )
    shares = (1.0, 1.0, 1.0, 1.0, lead_dp, lead_dp, lead_all)
    summed = (grad_qkv, grad_proj, grad_up, grad_down, grad_qkv_bias, grad_up_bias, grad_vectors)
    new_moments = []
    updates = []
    terms = []
    for master, moments, gradient, factor in zip(params, moment_list, summed, shares):
        first, second, update = lamb_parts(master, moments, gradient * grad_factor)
        new_moments.append(jnp.stack([first, second]))
        updates.append(update)
        terms.append(jnp.sum(update * update) * factor)
    terms = [
        jnp.sum(master * master) * factor for master, factor in zip(params, shares)
    ] + terms
    terms = jnp.pad(jnp.stack(terms), (0, 114)).reshape(1, 128)
    terms = butterfly(terms, dp)[0]
    weight_sq, update_sq = terms[:7], terms[7:14]
    trust = jnp.sqrt(weight_sq) / jnp.sqrt(update_sq + 1e-12)
    new_params = [params[k] - LEARN_RATE * trust[k] * updates[k] for k in range(7)]
    norms = jnp.stack([jnp.sqrt(weight_sq), jnp.sqrt(update_sq)])
    return (
        block_output,
        input_grad,
        *new_params,
        *new_moments,
        *[p.astype(LOW) for p in new_params[:4]],
        norms,
        trust,
    )


def solution(mesh):
    in_specs = (
        P(None, "dp", "tensor", None),
        P(None, "dp", "tensor", None),
        P(None, "dp", None),
        P(None, None, "dp", None),
        P(None, "dp", None),
        P(None, "dp", None),
        P("dp", None, "tensor"),
        P("tensor", "dp"),
        P("dp", "tensor"),
        P("tensor", "dp"),
        P(None, "tensor"),
        P("tensor"),
        P(),
        P(None, "dp", None, "tensor"),
        P(None, "tensor", "dp"),
        P(None, "dp", "tensor"),
        P(None, "tensor", "dp"),
        P(None, None, "tensor"),
        P(None, "tensor"),
        P(),
    )
    out_specs = (
        P(None, "dp", "tensor", None),
        P(None, "dp", "tensor", None),
        P("dp", None, "tensor"),
        P("tensor", "dp"),
        P("dp", "tensor"),
        P("tensor", "dp"),
        P(None, "tensor"),
        P("tensor"),
        P(),
        P(None, "dp", None, "tensor"),
        P(None, "tensor", "dp"),
        P(None, "dp", "tensor"),
        P(None, "tensor", "dp"),
        P(None, None, "tensor"),
        P(None, "tensor"),
        P(),
        P("dp", None, "tensor"),
        P("tensor", "dp"),
        P("dp", "tensor"),
        P("tensor", "dp"),
        P(),
        P(),
    )
    return jax.shard_map(body, mesh=mesh, in_specs=in_specs, out_specs=out_specs, check_vma=False)
```

time: 1660 us -> 1020 us (0.61)
  waiting for transfers between devices: 963 us -> 312 us
  blocking collectives: 143 us -> 0 us
  starting transfers between devices: 0.91 us -> 99.9 us
  local copies, waits for them, and re-layouts: 112 us -> 163 us
  other arithmetic: 139 us -> 173 us
  loops' own time: 28.7 us -> 0 us
  matrix products: 229 us -> 253 us
    reduce_scatter x12 -> x0, waiting for transfers between devices: 578 us -> none  [the longest x4 303 us: owner_grad(): lax.psum_scatter(outer_term(left, right), 'dp', scatter_dimension=0, tile...]
    all_gather x12 -> x0, waiting for transfers between devices: 385 us -> none  [the longest x8 173 us: collect_rows(): return lax.all_gather(rows_low, 'tensor', axis=0, tiled=True)]
    ppermute x0 -> x101, waiting for transfers between devices: none -> 312 us  [the longest x18 85.1 us: down_z(): lax.ppermute(v, 'dp', [(i, (i - 4) % self.dp) for i in range(self.dp)])]
    psum x3 -> x0, blocking collectives: 143 us -> none  [the longest x1 61.7 us: body(): grad_qkv_bias, grad_up_bias = lax.psum((sum_qkv_bias, sum_up_bias), 'dp')]
    ppermute x0 -> x101, starting transfers between devices: none -> 99.9 us  [the longest x18 38.6 us: down_z(): lax.ppermute(v, 'dp', [(i, (i - 4) % self.dp) for i in range(self.dp)])]
    unnamed x67 -> x429, local copies, waits for them, and re-layouts: 8.07 us -> 69.5 us
    another operation x5 -> x41, other arithmetic: 1.08 us -> 45.8 us  [the longest x21 20.9 us: reduce_b(): came = self.up_z(jnp.stack([total(parts[0]), total(parts[1])]))]
    while x170 -> x0, local copies, waits for them, and re-layouts: 35.6 us -> none
  transfers between devices with their start and end apart: 24 -> 101, of which waited for: 23 -> 44; matrix products, arithmetic and copies ran while one was open for 9% -> 54% of each run, Pallas kernels for 0% -> 0%
where the time goes in v1:
time: 1020 us; the launch traced here: 1010 us
  waiting for transfers between devices  312 us (31%)
  matrix products  253 us (25%)
  other arithmetic  173 us (17%)
  local copies, waits for them, and re-layouts  163 us (16%)
  starting transfers between devices  99.9 us (10%)
  between operations  12.1 us (1%)
    ppermute x18, waiting for transfers between devices, down_z(): lax.ppermute(v, 'dp', [(i, (i - 4) % self.dp) for i in range(self.dp)])  85.1 us
    ppermute x12, waiting for transfers between devices, over_y(): return lax.ppermute(v, 'dp', [(i, i ^ 2) for i in range(self.dp)])  74.6 us
    ppermute x18, waiting for transfers between devices, up_z(): lax.ppermute(v, 'dp', [(i, (i + 4) % self.dp) for i in range(self.dp)])  69.6 us
    unnamed x429, local copies, waits for them, and re-layouts  69.5 us
    ppermute x17, waiting for transfers between devices, over_x(): return lax.ppermute(v, 'tensor', [(0, 1), (1, 0)])  67.5 us
    dot_general x15, matrix products, dot_t(): lax.dot_general(left, right, (((1,), (1,)), ((), ())), preferred_element_...  63.5 us
    dot_general x28, matrix products, outer(): lax.dot_general(left, right, (((0,), (0,)), ((), ())), preferred_element_...  59.2 us
    dot_general x16, matrix products, dot(): lax.dot_general(left, right, (((1,), (0,)), ((), ())), preferred_element_...  59.1 us
  transfers between devices with their start and end apart: 101, of which 44 were waited for; matrix products, arithmetic and copies ran while one was open for 54% of the time, Pallas kernels for 0%

profile of v1, /device:TPU:0, one launch (start us, length us, event | category | flops | bytes accessed | tf_op | source)
XLA Modules:
  0.0 1012.1 jit_solution(5348652232921411805)
XLA Ops:
  46.5 6.6 collective-permute-done.10
  79.8 8.5 collective-permute-done.11
  115.9 16.2 %collective-permute-done.4 = bf16[80,2560]{1,0:T(8,128)(2,1)S(1)} collective-permute-done((bf16[80,2560]{1,0:T(8,128)(2,1)S(1)}, bf16[80,2560]{1,0:T(8,128)(2,1)S(1)}, u32[]{:S(2)}, u32[]{:S(2)}) %collective-permute-start.4) | collective-permute-done | bytes 409632 | tf_op jit(solution)/shard_map/ppermute | solution.py:126
  155.2 21.5 %collective-permute-done.14 = bf16[640,1280]{1,0:T(8,128)(2,1)} collective-permute-done((bf16[640,1280]{1,0:T(8,128)(2,1)S(1)}, bf16[640,1280]{1,0:T(8,128)(2,1)}, u32[]{:S(2)}, u32[]{:S(2)}) %collective-permute-start.14) | collective-permute-done | bytes 1638432 | tf_op jit(solution)/shard_map/ppermute | solution.py:117
  191.9 16.1 %collective-permute-done.40 = bf16[640,1280]{1,0:T(8,128)(2,1)} collective-permute-done((bf16[640,1280]{1,0:T(8,128)(2,1)}, bf16[640,1280]{1,0:T(8,128)(2,1)}, u32[]{:S(2)}, u32[]{:S(2)}) %collective-permute-start.40) | collective-permute-done | bytes 1638432 | tf_op jit(solution)/shard_map/ppermute | solution.py:117
  251.4 10.2 %fusion.6 = (f32[16,576]{1,0:T(8,128)S(1)}, f32[16,576,576]{1,2,0:T(8,128)}) fusion(pred[576,576]{0,1:T(8,128)(4,1)S(1)} %compare_and_fusion, bf16[576,16,80]{0,2,1:T(8,128)(2,1)S(1)} %get-tuple-element.161, bf16[576,16,80]{0,2,1:T(8,128)(2,1)S(1)} %get-tuple-element.160), kind=kOutput, calls=%fused_computation.12 | convolution fusion | flops 865262592 | bytes 24551424 | tf_op jit(solution)/shard_map/qhd,khd->hqk/dot_general | solution.py:66
  261.7 10.7 %fusion = f32[16,576]{1,0:T(8,128)S(1)} fusion(f32[16,576]{1,0:T(8,128)S(1)} %get-tuple-element.318, f32[16,576,576]{1,2,0:T(8,128)} %get-tuple-element.319, pred[576,576]{0,1:T(8,128)(4,1)S(1)} %compare_and_fusion), kind=kLoop, calls=%fused_computation.6 | loop fusion | flops 21224448 | bytes 21639168 | tf_op jit(solution)/shard_map/reduce_sum | solution.py:70
  272.4 11.8 %fusion.59 = bf16[16,80,576]{2,1,0:T(8,128)(2,1)S(1)} fusion(f32[16,576]{1,0:T(8,128)S(1)} %fusion, f32[16,576]{1,0:T(8,128)S(1)} %get-tuple-element.318, f32[16,576,576]{1,2,0:T(8,128)} %get-tuple-element.319, pred[576,576]{0,1:T(8,128)(4,1)S(1)} %compare_and_fusion, f32[576,3,16,80]{0,3,2,1:T(8,128)S(1)} %pad_maximum_fusion), kind=kOutput, calls=%fused_computation.152 | convolution fusion | flops 876625920 | bytes 24797184 | tf_op jit(solution)/shard_map/hqk,khd->qhd/dot_general | solution.py:72
  301.6 6.0 multiply_convert_fusion.4
  310.9 6.8 multiply_convert_fusion.2
  331.2 31.3 %collective-permute-done.86 = bf16[2,320,1280]{2,1,0:T(8,128)(2,1)S(1)} collective-permute-done((bf16[2,320,1280]{2,1,0:T(8,128)(2,1)S(1)}, bf16[2,320,1280]{2,1,0:T(8,128)(2,1)S(1)}, u32[]{:S(2)}, u32[]{:S(2)}) %collective-permute-start.86) | collective-permute-done | bytes 1638432 | tf_op jit(solution)/shard_map/ppermute | solution.py:123
  363.2 12.8 %collective-permute-done.87 = bf16[2,80,1280]{2,1,0:T(8,128)(2,1)S(1)} collective-permute-done((bf16[2,80,1280]{2,1,0:T(8,128)(2,1)S(1)}, bf16[2,80,1280]{2,1,0:T(8,128)(2,1)S(1)}, u32[]{:S(2)}, u32[]{:S(2)}) %collective-permute-start.87) | collective-permute-done | bytes 409632 | tf_op jit(solution)/shard_map/ppermute | solution.py:129
  378.2 9.9 collective-permute-done.88
  388.4 7.2 collective-permute-done.80
  398.1 7.5 collective-permute-done.81
  405.7 7.5 collective-permute-done.89
  456.0 6.8 collective-permute-done.37
  473.6 6.8 collective-permute-done.38
  495.3 26.2 %collective-permute-done.42 = bf16[640,1280]{1,0:T(8,128)(2,1)S(1)} collective-permute-done((bf16[640,1280]{1,0:T(8,128)(2,1)S(1)}, bf16[640,1280]{1,0:T(8,128)(2,1)S(1)}, u32[]{:S(2)}, u32[]{:S(2)}) %collective-permute-start.42) | collective-permute-done | bytes 1638432 | tf_op jit(solution)/shard_map/ppermute | solution.py:117
  552.0 7.6 convert_reduce_fusion
  559.6 8.1 multiply_reduce_fusion.1
  580.2 12.4 %fusion.71 = bf16[576,1,16,80]{0,3,2,1:T(8,128)(2,1)} fusion(f32[16,576]{1,0:T(8,128)S(1)} %log_add_fusion, f32[16,576,576]{1,2,0:T(8,128)} %get-tuple-element.319, pred[576,576]{0,1:T(8,128)(4,1)S(1)} %copy-done.15, bf16[576,4,80]{0,2,1:T(8,128)(2,1)S(1)} %bitcast.676, bf16[576,4,80]{0,2,1:T(8,128)(2,1)S(1)} %bitcast.678, ...), kind=kOutput, calls=%fused_computation.205 | convolution fusion | flops 873529344 | bytes 24551424 | tf_op jit(solution)/shard_map/hqk,qhd->khd/dot_general | solution.py:86
  592.6 17.6 %multiply_reduce_fusion = (f32[16,576]{1,0:T(8,128)S(1)}, f32[16,576,576]{1,2,0:T(8,128)}) fusion(f32[16,576]{1,0:T(8,128)} %copy-done.117, f32[16,576,576]{1,2,0:T(8,128)} %get-tuple-element.319, pred[576,576]{0,1:T(8,128)(4,1)S(1)} %copy-done.15, f32[576,3,16,80]{0,3,2,1:T(8,128)} %copy-done, bf16[576,4,80]{0,2,1:T(8,128)(2,1)} %bitcast.677, ...), kind=kOutput, calls=%fused_computation.1 | convolution fusion | flops 878091264 | bytes 48513024 | tf_op jit(solution)/shard_map/qhd,khd->hqk/dot_general | solution.py:81
  610.2 20.3 %multiply_convert_fusion = bf16[16,576,576]{1,2,0:T(8,128)(2,1)} fusion(f32[16,576,576]{1,2,0:T(8,128)} %get-tuple-element.330, f32[16,576]{1,0:T(8,128)S(1)} %get-tuple-element.329, f32[16,576]{1,0:T(8,128)S(1)} %copy-done.118, f32[16,576,576]{1,2,0:T(8,128)} %get-tuple-element.319, pred[576,576]{0,1:T(8,128)(4,1)S(1)} %copy-done.15), kind=kLoop, calls=%fused_computation | loop fusion | flops 37158912 | bytes 53489664 | tf_op jit(solution)/shard_map/convert_element_type | solution.py:83
  630.5 6.5 fusion.308
  637.1 7.4 bitcast_multiply_fusion.2
  676.7 12.6 %fusion.42 = bf16[576,1280]{1,0:T(8,128)(2,1)} fusion(s32[1280]{0:T(1024)S(1)} %copy-done.161, f32[576,1280]{1,0:T(8,128)S(1)} %get-tuple-element.321, f32[576,1280]{1,0:T(8,128)} %fusion.306, f32[576,1280]{1,0:T(8,128)} %fusion.57, bf16[576,2560]{1,0:T(8,128)(2,1)} %copy-done.184, bf16[1280,2560]{1,0:T(8,128)(2,1)} %copy-done.147, f32[1280]{0:T(1024)S(1)} %copy-done.158), kind=kOutput, calls=%fused_computation.95 | convolution fusion | flops 5668372480 | bytes 19834880 | tf_op jit(solution)/shard_map/dot_general | solution.py:97
  692.5 6.0 fusion.21
  793.8 23.4 %collective-permute-done.60 = bf16[2,320,1280]{2,1,0:T(8,128)(2,1)S(1)} collective-permute-done((bf16[2,320,1280]{2,1,0:T(8,128)(2,1)}, bf16[2,320,1280]{2,1,0:T(8,128)(2,1)S(1)}, u32[]{:S(2)}, u32[]{:S(2)}) %collective-permute-start.60) | collective-permute-done | bytes 1638432 | tf_op jit(solution)/shard_map/ppermute | solution.py:123
  845.9 6.5 collective-permute-done.73
  903.5 8.8 collective-permute-done.54
  964.2 6.2 collective-permute-done.70
  (934 shorter events, 626.2 us)
Async XLA Ops:
  27.3 47.5 %collective-permute-start = (bf16[288,1280]{1,0:T(8,128)(2,1)}, bf16[288,1280]{1,0:T(8,128)(2,1)}, u32[]{:S(2)}, u32[]{:S(2)}) collective-permute-start(bf16[288,1280]{1,0:T(8,128)(2,1)} %get-tuple-element.227), channel_id=1, source_target_pairs={{0,1},{1,0},{2,3},{3,2},{4,5},{5,4},{6,7},{7,6},{8,9},{9,8},{10,11... | collective-permute-start | bytes 2211848 | tf_op jit(solution)/shard_map/ppermute | solution.py:117
  38.8 31.7 %collective-permute-start.2 = (bf16[80,2560]{1,0:T(8,128)(2,1)S(1)}, bf16[80,2560]{1,0:T(8,128)(2,1)S(1)}, u32[]{:S(2)}, u32[]{:S(2)}) collective-permute-start(bf16[80,2560]{1,0:T(8,128)(2,1)S(1)} %concatenate.228), channel_id=1, source_target_pairs={{0,24},{2,26},{4,28},{6,30},{8,0},{10,2},{12,4},{14,6},{16,8},{18,... | collective-permute-start | bytes 1228808 | tf_op jit(solution)/shard_map/ppermute | solution.py:126
  44.2 48.4 %collective-permute-start.45 = (bf16[288,1280]{1,0:T(8,128)(2,1)}, bf16[288,1280]{1,0:T(8,128)(2,1)S(1)}, u32[]{:S(2)}, u32[]{:S(2)}) collective-permute-start(bf16[288,1280]{1,0:T(8,128)(2,1)} %get-tuple-element.225), channel_id=1, source_target_pairs={{0,1},{1,0},{2,3},{3,2},{4,5},{5,4},{6,7},{7,6},{8,9},{9,8},{10,11... | collective-permute-start | bytes 2211848 | tf_op jit(solution)/shard_map/ppermute | solution.py:117
  53.1 56.8 %collective-permute-start.18 = (bf16[80,2560]{1,0:T(8,128)(2,1)S(1)}, bf16[80,2560]{1,0:T(8,128)(2,1)S(1)}, u32[]{:S(2)}, u32[]{:S(2)}) collective-permute-start(bf16[80,2560]{1,0:T(8,128)(2,1)S(1)} %collective-permute-done.17), channel_id=1, source_target_pairs={{0,24},{2,26},{4,28},{6,30},{8,0},{10,2},{12,4},{14,6},{16,8},{18,... | collective-permute-start | bytes 1228808 | tf_op jit(solution)/shard_map/ppermute | solution.py:126
  97.4 42.8 %collective-permute-start.33 = (bf16[2,80,1280]{2,1,0:T(8,128)(2,1)S(1)}, bf16[2,80,1280]{2,1,0:T(8,128)(2,1)S(1)}, u32[]{:S(2)}, u32[]{:S(2)}) collective-permute-start(bf16[2,80,1280]{2,1,0:T(8,128)(2,1)S(1)} %collective-permute-done.32), channel_id=1, source_target_pairs={{0,24},{2,26},{4,28},{6,30},{8,0},{10,2},{12,4},{14,6},{16,8},{18,... | collective-permute-start | bytes 1228808 | tf_op jit(solution)/shard_map/ppermute | solution.py:126
  115.8 34.5 %collective-permute-start.13 = (bf16[640,1280]{1,0:T(8,128)(2,1)S(1)}, bf16[640,1280]{1,0:T(8,128)(2,1)S(1)}, u32[]{:S(2)}, u32[]{:S(2)}) collective-permute-start(bf16[640,1280]{1,0:T(8,128)(2,1)S(1)} %bitcast.632), channel_id=1, source_target_pairs={{0,2},{2,0},{4,6},{6,4},{8,10},{10,8},{12,14},{14,12},{16,18},{18,... | collective-permute-start | bytes 4915208 | tf_op jit(solution)/shard_map/ppermute | solution.py:120
  133.3 53.6 %collective-permute-start.5 = (bf16[320,2560]{1,0:T(8,128)(2,1)}, bf16[320,2560]{1,0:T(8,128)(2,1)}, u32[]{:S(2)}, u32[]{:S(2)}) collective-permute-start(bf16[320,2560]{1,0:T(8,128)(2,1)} %pad_maximum_fusion.17), channel_id=1, source_target_pairs={{0,4},{2,6},{4,0},{6,2},{8,12},{10,14},{12,8},{14,10},{16,20},{18,... | collective-permute-start | bytes 4915208 | tf_op jit(solution)/shard_map/ppermute | solution.py:123
  137.9 38.8 %collective-permute-start.14 = (bf16[640,1280]{1,0:T(8,128)(2,1)S(1)}, bf16[640,1280]{1,0:T(8,128)(2,1)}, u32[]{:S(2)}, u32[]{:S(2)}) collective-permute-start(bf16[640,1280]{1,0:T(8,128)(2,1)S(1)} %bitcast.633), channel_id=1, source_target_pairs={{0,1},{1,0},{2,3},{3,2},{4,5},{5,4},{6,7},{7,6},{8,9},{9,8},{10,11... | collective-permute-start | bytes 4915208 | tf_op jit(solution)/shard_map/ppermute | solution.py:117
  146.2 61.8 %collective-permute-start.40 = (bf16[640,1280]{1,0:T(8,128)(2,1)}, bf16[640,1280]{1,0:T(8,128)(2,1)}, u32[]{:S(2)}, u32[]{:S(2)}) collective-permute-start(bf16[640,1280]{1,0:T(8,128)(2,1)} %bitcast.47), channel_id=1, source_target_pairs={{0,1},{1,0},{2,3},{3,2},{4,5},{5,4},{6,7},{7,6},{8,9},{9,8},{10,11... | collective-permute-start | bytes 4915208 | tf_op jit(solution)/shard_map/ppermute | solution.py:117
  150.2 60.5 %collective-permute-start.20 = (bf16[320,2560]{1,0:T(8,128)(2,1)}, bf16[320,2560]{1,0:T(8,128)(2,1)}, u32[]{:S(2)}, u32[]{:S(2)}) collective-permute-start(bf16[320,2560]{1,0:T(8,128)(2,1)} %pad_maximum_fusion.19), channel_id=1, source_target_pairs={{0,4},{2,6},{4,0},{6,2},{8,12},{10,14},{12,8},{14,10},{16,20},{18,... | collective-permute-start | bytes 4915208 | tf_op jit(solution)/shard_map/ppermute | solution.py:123
  155.1 59.0 %collective-permute-start.21 = (bf16[320,2560]{1,0:T(8,128)(2,1)}, bf16[320,2560]{1,0:T(8,128)(2,1)}, u32[]{:S(2)}, u32[]{:S(2)}) collective-permute-start(bf16[320,2560]{1,0:T(8,128)(2,1)} %pad_maximum_fusion.19), channel_id=1, source_target_pairs={{0,2},{2,0},{4,6},{6,4},{8,10},{10,8},{12,14},{14,12},{16,18},{18,... | collective-permute-start | bytes 4915208 | tf_op jit(solution)/shard_map/ppermute | solution.py:120
  176.7 40.0 %collective-permute-start.15 = (bf16[640,1280]{1,0:T(8,128)(2,1)}, bf16[640,1280]{1,0:T(8,128)(2,1)}, u32[]{:S(2)}, u32[]{:S(2)}) collective-permute-start(bf16[640,1280]{1,0:T(8,128)(2,1)} %collective-permute-done.14), channel_id=1, source_target_pairs={{0,2},{2,0},{4,6},{6,4},{8,10},{10,8},{12,14},{14,12},{16,18},{18,... | collective-permute-start | bytes 4915208 | tf_op jit(solution)/shard_map/ppermute | solution.py:120
  186.9 38.7 %collective-permute-start.7 = (bf16[320,2560]{1,0:T(8,128)(2,1)}, bf16[320,2560]{1,0:T(8,128)(2,1)}, u32[]{:S(2)}, u32[]{:S(2)}) collective-permute-start(bf16[320,2560]{1,0:T(8,128)(2,1)} %collective-permute-done.5), channel_id=1, source_target_pairs={{0,2},{2,0},{4,6},{6,4},{8,10},{10,8},{12,14},{14,12},{16,18},{18,... | collective-permute-start | bytes 4915208 | tf_op jit(solution)/shard_map/ppermute | solution.py:120
  208.1 93.5 %collective-permute-start.34 = (bf16[640,1280]{1,0:T(8,128)(2,1)}, bf16[640,1280]{1,0:T(8,128)(2,1)}, u32[]{:S(2)}, u32[]{:S(2)}) collective-permute-start(bf16[640,1280]{1,0:T(8,128)(2,1)} %bitcast.47), channel_id=1, source_target_pairs={{0,2},{2,0},{4,6},{6,4},{8,10},{10,8},{12,14},{14,12},{16,18},{18,... | collective-permute-start | bytes 4915208 | tf_op jit(solution)/shard_map/ppermute | solution.py:120
  210.8 81.3 %collective-permute-start.41 = (bf16[640,1280]{1,0:T(8,128)(2,1)}, bf16[640,1280]{1,0:T(8,128)(2,1)}, u32[]{:S(2)}, u32[]{:S(2)}) collective-permute-start(bf16[640,1280]{1,0:T(8,128)(2,1)} %collective-permute-done.40), channel_id=1, source_target_pairs={{0,2},{2,0},{4,6},{6,4},{8,10},{10,8},{12,14},{14,12},{16,18},{18,... | collective-permute-start | bytes 4915208 | tf_op jit(solution)/shard_map/ppermute | solution.py:120
  214.1 95.2 %collective-permute-start.22 = (bf16[320,2560]{1,0:T(8,128)(2,1)}, bf16[320,2560]{1,0:T(8,128)(2,1)}, u32[]{:S(2)}, u32[]{:S(2)}) collective-permute-start(bf16[320,2560]{1,0:T(8,128)(2,1)} %collective-permute-done.20), channel_id=1, source_target_pairs={{0,2},{2,0},{4,6},{6,4},{8,10},{10,8},{12,14},{14,12},{16,18},{18,... | collective-permute-start | bytes 4915208 | tf_op jit(solution)/shard_map/ppermute | solution.py:120
  324.6 37.9 %collective-permute-start.86 = (bf16[2,320,1280]{2,1,0:T(8,128)(2,1)S(1)}, bf16[2,320,1280]{2,1,0:T(8,128)(2,1)S(1)}, u32[]{:S(2)}, u32[]{:S(2)}) collective-permute-start(bf16[2,320,1280]{2,1,0:T(8,128)(2,1)S(1)} %pad_maximum_fusion.25), channel_id=1, source_target_pairs={{0,4},{2,6},{4,0},{6,2},{8,12},{10,14},{12,8},{14,10},{16,20},{18,... | collective-permute-start | bytes 4915208 | tf_op jit(solution)/shard_map/ppermute | solution.py:123
  329.6 46.7 %collective-permute-start.79 = (bf16[640,1280]{1,0:T(8,128)(2,1)S(1)}, bf16[640,1280]{1,0:T(8,128)(2,1)S(1)}, u32[]{:S(2)}, u32[]{:S(2)}) collective-permute-start(bf16[640,1280]{1,0:T(8,128)(2,1)S(1)} %add_convert_fusion), channel_id=1, source_target_pairs={{0,1},{1,0},{2,3},{3,2},{4,5},{5,4},{6,7},{7,6},{8,9},{9,8},{10,11... | collective-permute-start | bytes 4915208 | tf_op jit(solution)/shard_map/ppermute | solution.py:117
  483.2 38.3 %collective-permute-start.42 = (bf16[640,1280]{1,0:T(8,128)(2,1)S(1)}, bf16[640,1280]{1,0:T(8,128)(2,1)S(1)}, u32[]{:S(2)}, u32[]{:S(2)}) collective-permute-start(bf16[640,1280]{1,0:T(8,128)(2,1)S(1)} %bitcast.643), channel_id=1, source_target_pairs={{0,1},{1,0},{2,3},{3,2},{4,5},{5,4},{6,7},{7,6},{8,9},{9,8},{10,11... | collective-permute-start | bytes 4915208 | tf_op jit(solution)/shard_map/ppermute | solution.py:117
  486.6 37.3 %collective-permute-start.27 = (bf16[320,2560]{1,0:T(8,128)(2,1)S(1)}, bf16[320,2560]{1,0:T(8,128)(2,1)S(1)}, u32[]{:S(2)}, u32[]{:S(2)}) collective-permute-start(bf16[320,2560]{1,0:T(8,128)(2,1)S(1)} %pad_maximum_fusion.20), channel_id=1, source_target_pairs={{0,4},{2,6},{4,0},{6,2},{8,12},{10,14},{12,8},{14,10},{16,20},{18,... | collective-permute-start | bytes 4915208 | tf_op jit(solution)/shard_map/ppermute | solution.py:123
  488.2 38.6 %collective-permute-start.28 = (bf16[320,2560]{1,0:T(8,128)(2,1)S(1)}, bf16[320,2560]{1,0:T(8,128)(2,1)S(1)}, u32[]{:S(2)}, u32[]{:S(2)}) collective-permute-start(bf16[320,2560]{1,0:T(8,128)(2,1)S(1)} %pad_maximum_fusion.20), channel_id=1, source_target_pairs={{0,2},{2,0},{4,6},{6,4},{8,10},{10,8},{12,14},{14,12},{16,18},{18,... | collective-permute-start | bytes 4915208 | tf_op jit(solution)/shard_map/ppermute | solution.py:120
  494.8 233.1 %collective-permute-start.71 = (bf16[640,1280]{1,0:T(8,128)(2,1)}, bf16[640,1280]{1,0:T(8,128)(2,1)}, u32[]{:S(2)}, u32[]{:S(2)}) collective-permute-start(bf16[640,1280]{1,0:T(8,128)(2,1)} %convolution_convert_fusion.10), channel_id=1, source_target_pairs={{0,2},{2,0},{4,6},{6,4},{8,10},{10,8},{12,14},{14,12},{16,18},{18,... | collective-permute-start | bytes 4915208 | tf_op jit(solution)/shard_map/ppermute | solution.py:120
  676.0 114.6 %collective-permute-start.72 = (bf16[640,1280]{1,0:T(8,128)(2,1)}, bf16[640,1280]{1,0:T(8,128)(2,1)}, u32[]{:S(2)}, u32[]{:S(2)}) collective-permute-start(bf16[640,1280]{1,0:T(8,128)(2,1)} %convolution_convert_fusion.8), channel_id=1, source_target_pairs={{0,2},{2,0},{4,6},{6,4},{8,10},{10,8},{12,14},{14,12},{16,18},{18,... | collective-permute-start | bytes 4915208 | tf_op jit(solution)/shard_map/ppermute | solution.py:120
  676.6 91.2 %collective-permute-start.59 = (bf16[640,320]{0,1:T(8,128)(2,1)}, bf16[640,320]{0,1:T(8,128)(2,1)}, u32[]{:S(2)}, u32[]{:S(2)}) collective-permute-start(bf16[640,320]{0,1:T(8,128)(2,1)} %convolution_convert_fusion.20), channel_id=1, source_target_pairs={{0,2},{2,0},{4,6},{6,4},{8,10},{10,8},{12,14},{14,12},{16,18},{18,... | collective-permute-start | bytes 1228808 | tf_op jit(solution)/shard_map/ppermute | solution.py:120
  691.3 70.0 %collective-permute-start.44 = (bf16[288,1280]{1,0:T(8,128)(2,1)}, bf16[288,1280]{1,0:T(8,128)(2,1)}, u32[]{:S(2)}, u32[]{:S(2)}) collective-permute-start(bf16[288,1280]{1,0:T(8,128)(2,1)} %slice.1386), channel_id=1, source_target_pairs={{0,1},{1,0},{2,3},{3,2},{4,5},{5,4},{6,7},{7,6},{8,9},{9,8},{10,11... | collective-permute-start | bytes 2211848 | tf_op jit(solution)/shard_map/ppermute | solution.py:117
  727.8 35.2 %collective-permute-start.46 = (bf16[288,1280]{1,0:T(8,128)(2,1)}, bf16[288,1280]{1,0:T(8,128)(2,1)}, u32[]{:S(2)}, u32[]{:S(2)}) collective-permute-start(bf16[288,1280]{1,0:T(8,128)(2,1)} %slice.1396), channel_id=1, source_target_pairs={{0,1},{1,0},{2,3},{3,2},{4,5},{5,4},{6,7},{7,6},{8,9},{9,8},{10,11... | collective-permute-start | bytes 2211848 | tf_op jit(solution)/shard_map/ppermute | solution.py:117
  778.3 38.9 %collective-permute-start.60 = (bf16[2,320,1280]{2,1,0:T(8,128)(2,1)}, bf16[2,320,1280]{2,1,0:T(8,128)(2,1)S(1)}, u32[]{:S(2)}, u32[]{:S(2)}) collective-permute-start(bf16[2,320,1280]{2,1,0:T(8,128)(2,1)} %copy.186), channel_id=1, source_target_pairs={{0,4},{2,6},{4,0},{6,2},{8,12},{10,14},{12,8},{14,10},{16,20},{18,... | collective-permute-start | bytes 4915208 | tf_op jit(solution)/shard_map/ppermute | solution.py:123
  782.5 72.3 %collective-permute-start.65 = (bf16[640,2560]{1,0:T(8,128)(2,1)}, bf16[640,2560]{1,0:T(8,128)(2,1)}, u32[]{:S(2)}, u32[]{:S(2)}) collective-permute-start(bf16[640,2560]{1,0:T(8,128)(2,1)} %convolution_convert_fusion.2), channel_id=1, source_target_pairs={{0,2},{2,0},{4,6},{6,4},{8,10},{10,8},{12,14},{14,12},{16,18},{18,... | collective-permute-start | bytes 9830408 | tf_op jit(solution)/shard_map/ppermute | solution.py:120
  786.0 52.2 %collective-permute-start.51 = (bf16[640,1280]{0,1:T(8,128)(2,1)}, bf16[640,1280]{0,1:T(8,128)(2,1)}, u32[]{:S(2)}, u32[]{:S(2)}) collective-permute-start(bf16[640,1280]{0,1:T(8,128)(2,1)} %add_convert_fusion.2), channel_id=1, source_target_pairs={{0,1},{1,0},{2,3},{3,2},{4,5},{5,4},{6,7},{7,6},{8,9},{9,8},{10,11... | collective-permute-start | bytes 4915208 | tf_op jit(solution)/shard_map/ppermute | solution.py:117
  793.3 59.1 %collective-permute-start.73 = (bf16[2,320,1280]{2,1,0:T(8,128)(2,1)}, bf16[2,320,1280]{2,1,0:T(8,128)(2,1)}, u32[]{:S(2)}, u32[]{:S(2)}) collective-permute-start(bf16[2,320,1280]{2,1,0:T(8,128)(2,1)} %pad_maximum_fusion.24), channel_id=1, source_target_pairs={{0,4},{2,6},{4,0},{6,2},{8,12},{10,14},{12,8},{14,10},{16,20},{18,... | collective-permute-start | bytes 4915208 | tf_op jit(solution)/shard_map/ppermute | solution.py:123
  858.2 69.1 %collective-permute-start.66 = (bf16[640,1280]{1,0:T(8,128)(2,1)}, bf16[640,1280]{1,0:T(8,128)(2,1)}, u32[]{:S(2)}, u32[]{:S(2)}) collective-permute-start(bf16[640,1280]{1,0:T(8,128)(2,1)} %add_convert_fusion.1), channel_id=1, source_target_pairs={{0,1},{1,0},{2,3},{3,2},{4,5},{5,4},{6,7},{7,6},{8,9},{9,8},{10,11... | collective-permute-start | bytes 4915208 | tf_op jit(solution)/shard_map/ppermute | solution.py:117
  917.5 36.8 %collective-permute-start.76 = (bf16[2,80,1280]{2,1,0:T(8,128)(2,1)}, bf16[2,80,1280]{2,1,0:T(8,128)(2,1)}, u32[]{:S(2)}, u32[]{:S(2)}) collective-permute-start(bf16[2,80,1280]{2,1,0:T(8,128)(2,1)} %pad_maximum_fusion.61), channel_id=1, source_target_pairs={{0,8},{2,10},{4,12},{6,14},{8,16},{10,18},{12,20},{14,22},{16,24},... | collective-permute-start | bytes 1228808 | tf_op jit(solution)/shard_map/ppermute | solution.py:129
  (263 other events, 3045.4 us)

commit v2 on v1

v2 whole, which is shorter than its diff:
```python
import jax
import jax.numpy as jnp
from jax import lax
from jax.experimental import pallas as pl
from jax.experimental.pallas import tpu as pltpu
from jax.sharding import PartitionSpec as P

HD = 80
SLOTS = 4
LEN = 576


NEGATIVE = -1e30
EPS_NORM = 1e-06
EPS_ADAM = 1e-06
WEIGHT_DECAY = 0.01
LEARN_RATE = 0.5
GELU_SLOPE = 1.702
F32 = jnp.float32
LOW = jnp.bfloat16


def norm_parts(values):
    center = values - jnp.mean(values, -1, keepdims=True)
    inverse = lax.rsqrt(jnp.mean(center * center, -1, keepdims=True) + EPS_NORM)
    return (center * inverse, inverse)


def norm_back(out_grad, normed, inverse, gain):
    scaled = out_grad * gain
    return inverse * (
        scaled
        - jnp.mean(scaled, -1, keepdims=True)
        - normed * jnp.mean(scaled * normed, -1, keepdims=True)
    )


def rotary_tables(rows_at, cols_at):
    quarter = HD // 4
    frequency = 10000.0 ** (-jnp.arange(quarter, dtype=F32) / quarter)
    halves = jnp.concatenate(
        [
            rows_at.astype(F32)[:, None] * frequency,
            cols_at.astype(F32)[:, None] * frequency,
        ],
        -1,
    )
    angles = jnp.concatenate([halves, halves], -1)
    return (jnp.cos(angles), jnp.sin(angles))


def dot(left, right):
    return lax.dot_general(left, right, (((1,), (0,)), ((), ())), preferred_element_type=F32)


def dot_t(left, right):
    return lax.dot_general(left, right, (((1,), (1,)), ((), ())), preferred_element_type=F32)


def outer(left, right):
    return lax.dot_general(left, right, (((0,), (0,)), ((), ())), preferred_element_type=F32)


def lamb_parts(master, moments, gradient):
    first = 0.5 * moments[0] + 0.5 * gradient
    second = 0.5 * moments[1] + 0.5 * gradient * gradient
    update = first / (jnp.sqrt(second) + EPS_ADAM) + WEIGHT_DECAY * master
    return (first, second, update)


VMEM_LIMIT = 56 * 1024 * 1024


class Order:
    def __init__(self):
        self.last = None


ORDER = Order()


def call(kernel, grid, in_specs, out_specs, out_shape, scratch=(), flops=0, moved=0, after=()):
    if ORDER.last is not None:
        after = [*after, ORDER.last]
    count, extra = len(in_specs), len(after)

    def ordered(*refs):
        kernel(*refs[:count], *refs[count + extra :])

    run = pl.pallas_call(
        ordered,
        grid=grid,
        in_specs=list(in_specs) + [pl.BlockSpec(memory_space=pl.ANY)] * extra,
        out_specs=out_specs,
        out_shape=out_shape,
        scratch_shapes=list(scratch),
        compiler_params=pltpu.CompilerParams(
            dimension_semantics=("arbitrary",) * len(grid), vmem_limit_bytes=VMEM_LIMIT
        ),
        cost_estimate=pl.CostEstimate(flops=flops, bytes_accessed=moved, transcendentals=0),
    )

    def start(*operands):
        result = run(*operands, *after)
        ORDER.last = result[0] if isinstance(result, (list, tuple)) else result
        return result

    return start


def whole(shape):
    return pl.BlockSpec(shape, lambda *_: (0,) * len(shape))


def lookup(table):
    def column(j):
        found = table[0]
        for k in range(1, len(table)):
            found = jnp.where(j == k, table[k], found)
        return found

    return column


class Parts:
    def __init__(self, sets, block):
        self.sets, self.block = sets, block
        self.steps = sum(s[2] for s in sets)
        self.width = sum(piece.shape[0] for piece, _ in sets[0][0])
        self.arrays, self.specs = [], []
        base = 0
        for pieces, _, count in sets:
            for piece, first in pieces:
                self.arrays.append(piece)
                self.specs.append(
                    pl.BlockSpec(
                        (piece.shape[0], block),
                        lambda j, first=first, base=base, count=count: (
                            0,
                            first + jnp.clip(j - base, 0, count - 1),
                        ),
                    )
                )
            base += count

    def each(self, refs, work):
        j = pl.program_id(0)
        base, at = 0, 0
        for pieces, cuts, count in self.sets:
            mine = refs[at : at + len(pieces)]

            @pl.when((j >= base) & (j < base + count))
            def _(mine=mine, cuts=cuts):
                if cuts is None:
                    values = [r[...] for r in mine]
                else:
                    values = [mine[p][r : r + n, :] for p, r, n in cuts]
                work(values[0] if len(values) == 1 else jnp.concatenate(values, 0))

            base += count
            at += len(pieces)

    @property
    def volume(self):
        return self.steps * self.block * self.width


ROWS = 96


def row_loop(rows, work):
    def step(k, carry):
        work(pl.ds(pl.multiple_of(k * ROWS, ROWS), ROWS))
        return carry

    lax.fori_loop(0, rows // ROWS, step, 0)


def times_weight(left, parts, table, ins, in_specs, outs, out_specs, finish, after=()):
    count = len(parts.arrays)

    def kernel(*refs):
        left_ref, w_refs, rest = refs[0], refs[1 : 1 + count], refs[1 + count :]

        def work(w):
            y = jnp.dot(left_ref[...], w, preferred_element_type=F32)
            finish(y, rest[: len(ins)], rest[len(ins) :])

        parts.each(w_refs, work)

    return call(
        kernel,
        (parts.steps,),
        [whole(left.shape)] + parts.specs + in_specs,
        out_specs,
        outs,
        flops=2 * left.shape[0] * parts.volume,
        moved=2 * parts.volume + 6 * left.shape[0] * parts.steps * parts.block,
        after=after,
    )(left, *parts.arrays, *ins)


def times_turned(left, parts, table, ins, in_specs, outs, out_specs, finish, after=()):
    count = len(parts.arrays)
    rows, width = left.shape[0], parts.width
    column = lookup(table)

    def kernel(*refs):
        left_ref, w_refs, rest = refs[0], refs[1 : 1 + count], refs[1 + count :]
        acc = rest[-1]
        rest = rest[:-1]

        def work(w):
            y = lax.dot_general(
                left_ref[...], w, (((1,), (1,)), ((), ())), preferred_element_type=F32
            )

            @pl.when(pl.program_id(0) == 0)
            def _():
                acc[...] = y

            @pl.when(pl.program_id(0) > 0)
            def _():
                acc[...] += y

        parts.each(w_refs, work)

        @pl.when(pl.program_id(0) == parts.steps - 1)
        def _():
            finish(acc, rest[: len(ins)], rest[len(ins) :])

    return call(
        kernel,
        (parts.steps,),
        [pl.BlockSpec((rows, parts.block), lambda j: (0, column(j)))] + parts.specs + in_specs,
        out_specs,
        outs,
        scratch=[pltpu.VMEM((rows, width), F32)],
        flops=2 * rows * parts.volume,
        moved=2 * parts.volume + 2 * left.size + 8 * rows * width,
        after=after,
    )(left, *parts.arrays, *ins)


def qkv_forward(first_in, parts, bias, table, after=()):
    column = lookup(table)
    block = parts.block

    def finish(y, ins, outs):
        outs[0][...] = y + ins[0][...]

    total_columns = parts.steps * block
    return times_weight(
        first_in,
        parts,
        table,
        [bias],
        [pl.BlockSpec((1, block), lambda j: (0, column(j)))],
        [jax.ShapeDtypeStruct((first_in.shape[0], total_columns), F32)],
        [pl.BlockSpec((first_in.shape[0], block), lambda j: (0, column(j)))],
        finish,
        after,
    )[0]


def proj_forward(attended, parts, row_low, vec, after=()):
    rows, width = row_low.shape

    def finish(acc, ins, outs):
        row_ref, vec_ref = ins
        hidden_ref, second_ref = outs

        def work(cut):
            hidden = row_ref[cut, :].astype(F32) + (acc[cut, :] + vec_ref[2:3, :])
            hidden_ref[cut, :] = hidden
            normed, _ = norm_parts(hidden)
            second_ref[cut, :] = (normed * vec_ref[3:4, :] + vec_ref[4:5, :]).astype(LOW)

        row_loop(rows, work)

    return times_turned(
        attended,
        parts,
        list(range(parts.steps)),
        [row_low, vec],
        [whole(row_low.shape), whole(vec.shape)],
        [jax.ShapeDtypeStruct((rows, width), F32), jax.ShapeDtypeStruct((rows, width), LOW)],
        [whole((rows, width))] * 2,
        finish,
        after,
    )


def up_forward(second_in, parts, bias, after=()):
    rows, block = second_in.shape[0], parts.block
    total_columns = parts.steps * block

    def finish(y, ins, outs):
        outs[0][...] = y + ins[0][...]

        def work(cut):
            u = outs[0][cut, :]
            outs[1][cut, :] = (u * jax.nn.sigmoid(GELU_SLOPE * u)).astype(LOW)

        row_loop(rows, work)

    spec = pl.BlockSpec((rows, block), lambda j: (0, j))
    return times_weight(
        second_in,
        parts,
        None,
        [bias],
        [pl.BlockSpec((1, block), lambda j: (0, j))],
        [
            jax.ShapeDtypeStruct((rows, total_columns), F32),
            jax.ShapeDtypeStruct((rows, total_columns), LOW),
        ],
        [spec, spec],
        finish,
        after,
    )


def down_forward(activated, parts, hidden1, vec, after=()):
    rows, width = hidden1.shape

    def finish(acc, ins, outs):
        def work(cut):
            outs[0][cut, :] = (ins[0][cut, :] + (acc[cut, :] + ins[1][5:6, :])).astype(LOW)

        row_loop(rows, work)

    return times_turned(
        activated,
        parts,
        list(range(parts.steps)),
        [hidden1, vec],
        [whole(hidden1.shape), whole(vec.shape)],
        [jax.ShapeDtypeStruct((rows, width), LOW)],
        [whole((rows, width))],
        finish,
        after,
    )[0]


def down_backward(down_grad, parts, upward, after=()):
    rows, block = down_grad.shape[0], parts.block
    total_columns = parts.steps * block

    def finish(y, ins, outs):
        total_ref = outs[1]
        total_ref[...] = jnp.zeros_like(total_ref)
        scratch = outs[2]
        scratch[...] = y

        def work(cut):
            u = ins[0][cut, :]
            sigma = jax.nn.sigmoid(GELU_SLOPE * u)
            g = (scratch[cut, :] * (sigma + GELU_SLOPE * u * sigma * (1.0 - sigma))).astype(LOW)
            outs[0][cut, :] = g
            total_ref[...] += jnp.sum(g.astype(F32), 0, keepdims=True)

        row_loop(rows, work)

    count = len(parts.arrays)

    def kernel(*refs):
        left_ref, w_refs, rest = refs[0], refs[1 : 1 + count], refs[1 + count :]

        def work(w):
            y = jnp.dot(left_ref[...], w, preferred_element_type=F32)
            finish(y, rest[:1], rest[1:])

        parts.each(w_refs, work)

    spec = pl.BlockSpec((rows, block), lambda j: (0, j))
    return call(
        kernel,
        (parts.steps,),
        [whole(down_grad.shape)] + parts.specs + [spec],
        [spec, pl.BlockSpec((1, block), lambda j: (0, j))],
        [
            jax.ShapeDtypeStruct((rows, total_columns), LOW),
            jax.ShapeDtypeStruct((1, total_columns), F32),
        ],
        scratch=[pltpu.VMEM((rows, block), F32)],
        flops=2 * rows * parts.volume,
        moved=2 * parts.volume + 6 * rows * total_columns,
        after=after,
    )(down_grad, *parts.arrays, upward)


def up_backward(up_grad, parts, hidden1, cot_low, token_weight, vec, after=()):
    rows, width = hidden1.shape

    def finish(acc, ins, outs):
        hidden_ref, cot_ref, weight_ref, vec_ref = ins
        grad_ref, branch_ref, sums_ref = outs
        sums_ref[...] = jnp.zeros_like(sums_ref)

        def work(cut):
            e = acc[cut, :]
            normed, inverse = norm_parts(hidden_ref[cut, :])
            grad_y = cot_ref[cut, :].astype(F32) * weight_ref[cut, :]
            grad = grad_y + norm_back(e, normed, inverse, vec_ref[3:4, :])
            branch = grad.astype(LOW)
            grad_ref[cut, :] = grad
            branch_ref[cut, :] = branch
            sums_ref[0:1, :] += jnp.sum(e * normed, 0, keepdims=True)
            sums_ref[1:2, :] += jnp.sum(e, 0, keepdims=True)
            sums_ref[2:3, :] += jnp.sum(branch.astype(F32), 0, keepdims=True)
            sums_ref[3:4, :] += jnp.sum(grad_y.astype(LOW).astype(F32), 0, keepdims=True)

        row_loop(rows, work)

    return times_turned(
        up_grad,
        parts,
        list(range(parts.steps)),
        [hidden1, cot_low, token_weight, vec],
        [whole(hidden1.shape), whole(cot_low.shape), whole(token_weight.shape), whole(vec.shape)],
        [
            jax.ShapeDtypeStruct((rows, width), F32),
            jax.ShapeDtypeStruct((rows, width), LOW),
            jax.ShapeDtypeStruct((8, width), F32),
        ],
        [whole((rows, width)), whole((rows, width)), whole((8, width))],
        finish,
        after,
    )


def proj_backward(branch_grad, parts, after=()):
    rows, block = branch_grad.shape[0], parts.block

    def finish(y, ins, outs):
        outs[0][...] = y.astype(LOW)

    return times_weight(
        branch_grad,
        parts,
        None,
        [],
        [],
        [jax.ShapeDtypeStruct((rows, parts.steps * block), LOW)],
        [pl.BlockSpec((rows, block), lambda j: (0, j))],
        finish,
        after,
    )[0]


def qkv_backward(mixed_grad, parts, table, row_low, hidden1_grad, vec, after=()):
    rows, width = row_low.shape

    def finish(acc, ins, outs):
        row_ref, grad_ref, vec_ref = ins
        sums_ref = outs[1]
        sums_ref[...] = jnp.zeros_like(sums_ref)

        def work(cut):
            e = acc[cut, :]
            normed, inverse = norm_parts(row_ref[cut, :].astype(F32))
            grad = grad_ref[cut, :] + norm_back(e, normed, inverse, vec_ref[0:1, :])
            outs[0][cut, :] = grad.astype(LOW)
            sums_ref[0:1, :] += jnp.sum(e * normed, 0, keepdims=True)
            sums_ref[1:2, :] += jnp.sum(e, 0, keepdims=True)

        row_loop(rows, work)

    return times_turned(
        mixed_grad,
        parts,
        table,
        [row_low, hidden1_grad, vec],
        [whole(row_low.shape), whole(hidden1_grad.shape), whole(vec.shape)],
        [jax.ShapeDtypeStruct((rows, width), LOW), jax.ShapeDtypeStruct((8, width), F32)],
        [whole((rows, width)), whole((8, width))],
        finish,
        after,
    )


def grad_kernel(pairs, block, kind, half, came, after=()):
    rows, width = pairs[0][0].shape
    middle = width // 2
    low = middle // 2
    steps = len(kind)
    near = steps // 2
    count = len(pairs)

    def kernel(*refs):
        lefts, rights = refs[:count], refs[count : 2 * count]
        rest = refs[2 * count :]
        turned = rest[-count:]
        j = pl.program_id(0)

        @pl.when(j == 0)
        def _():
            for k in range(count):
                turned[k][...] = lefts[k][:, half * middle : (half + 1) * middle].T

        for k in range(count):
            hits = [s for s in range(steps) if kind[s][0] == k]
            hit = j == hits[0]
            for s in hits[1:]:
                hit = hit | (j == s)

            @pl.when(hit)
            def _(k=k):
                right = rights[k][...]
                if came is None:
                    rest[0][...] = jnp.dot(
                        turned[k][...], right, preferred_element_type=F32
                    ).astype(LOW)
                    return
                came_ref, own0, own1, other0, far_a, far_b = rest[:6]
                y0 = jnp.dot(turned[k][:low, :], right, preferred_element_type=F32)
                y0 = (y0 + came_ref[:low, :].astype(F32)).astype(LOW)
                y1 = jnp.dot(turned[k][low:, :], right, preferred_element_type=F32)
                y1 = (y1 + came_ref[low:, :].astype(F32)).astype(LOW)

                @pl.when(j < near)
                def _():
                    own0[...] = y0
                    own1[...] = y1

                @pl.when(j >= near)
                def _():
                    other0[...] = y0

                @pl.when((j >= near) & (j < near + near // 2))
                def _():
                    far_a[...] = y1

                @pl.when(j >= near + near // 2)
                def _():
                    far_b[...] = y1

    right_specs = []
    for k in range(count):
        table, last = [], 0
        for s in range(steps):
            if kind[s][0] == k:
                last = kind[s][1]
            table.append(last)
        column = lookup(table)
        right_specs.append(pl.BlockSpec((rows, block), lambda j, column=column: (0, column(j))))

    def clipped(base, number, height):
        spec = pl.BlockSpec((height, block), lambda j: (0, jnp.clip(j - base, 0, number - 1)))
        return spec, jax.ShapeDtypeStruct((height, number * block), LOW)

    if came is None:
        outs = [clipped(0, steps, middle)]
    else:
        outs = [
            clipped(0, near, low),
            clipped(0, near, low),
            clipped(near, near, low),
            clipped(near, near // 2, low),
            clipped(near + near // 2, near // 2, low),
        ]
    extra = [] if came is None else [came]
    return call(
        kernel,
        (steps,),
        [whole(left.shape) for left, _ in pairs]
        + right_specs
        + [pl.BlockSpec((middle, block), lambda j: (0, j)) for _ in extra],
        [s for s, _ in outs],
        [s for _, s in outs],
        scratch=[pltpu.VMEM((middle, rows), LOW) for _ in pairs],
        flops=rows * width * steps * block,
        moved=2 * (middle + rows) * steps * block,
        after=after,
    )(*[left for left, _ in pairs], *[right for _, right in pairs], *extra)


def add_far(other0, own1, far_a, far_b):
    rows, columns = other0.shape
    block = columns // 2

    def kernel(other_ref, own_ref, a_ref, b_ref, x_ref, y_ref):
        j = pl.program_id(0)

        @pl.when(j == 0)
        def _():
            x_ref[...] = (other_ref[...].astype(F32) + a_ref[...].astype(F32)).astype(LOW)
            y_ref[...] = own_ref[...]

        @pl.when(j == 1)
        def _():
            x_ref[...] = other_ref[...]
            y_ref[...] = (own_ref[...].astype(F32) + b_ref[...].astype(F32)).astype(LOW)

    spec = pl.BlockSpec((rows, block), lambda j: (0, j))
    shape = jax.ShapeDtypeStruct((rows, columns), LOW)
    return call(
        kernel,
        (2,),
        [spec, spec, whole(far_a.shape), whole(far_b.shape)],
        [spec, spec],
        [shape, shape],
        flops=2 * rows * columns,
        moved=10 * rows * columns,
    )(other0, own1, far_a, far_b)


def stack_rows(pieces):
    rows, columns = pieces[0].shape
    count = len(pieces)
    block = columns // 2

    def kernel(*refs):
        for k in range(count):
            refs[-1][k * rows : (k + 1) * rows, :] = refs[k][...]

    return call(
        kernel,
        (2,),
        [pl.BlockSpec((rows, block), lambda j: (0, j))] * count,
        pl.BlockSpec((count * rows, block), lambda j: (0, j)),
        jax.ShapeDtypeStruct((count * rows, columns), pieces[0].dtype),
        moved=4 * count * rows * columns,
    )(*pieces)


def add_cuts(arrays, rows, columns, block_rows, block_columns, kind, after=()):
    def kernel(*refs):
        value = refs[0][...].astype(F32)
        for ref in refs[1:-1]:
            value = value + ref[...].astype(F32)
        refs[-1][...] = value.astype(kind)

    specs = [
        pl.BlockSpec(
            (block_rows, block_columns),
            lambda i, j, r=r // block_rows, c=c // block_columns: (r + i, c + j),
        )
        for _, r, c in arrays
    ]
    return call(
        kernel,
        (rows // block_rows, columns // block_columns),
        specs,
        pl.BlockSpec((block_rows, block_columns), lambda i, j: (i, j)),
        jax.ShapeDtypeStruct((rows, columns), kind),
        flops=rows * columns * len(arrays),
        moved=2 * rows * columns * (len(arrays) + 1),
        after=after,
    )(*[a for a, _, _ in arrays])


def turn_pairs(v, heads_lanes):
    middle = HD // 2
    lanes = lax.broadcasted_iota(jnp.int32, v.shape, 1)
    early = lanes % HD < middle
    width = v.shape[1]
    return jnp.where(early, -pltpu.roll(v, width - middle, 1), pltpu.roll(v, middle, 1))


def head_cut(h):
    return slice(h * HD, (h + 1) * HD)


def attention_forward(mixed, cosine, sine, key_code, query_code, groups, after=()):
    rows, columns = mixed.shape
    lanes = columns // (3 * groups)
    heads = lanes // HD
    scale = HD ** (-0.5)

    def kernel(mixed_ref, cos_ref, sin_ref, key_ref, query_ref, qkv_ref, att_ref, lse_ref, out_t):
        cos, sin = cos_ref[...], sin_ref[...]
        for part in range(2):
            cut = slice(part * lanes, (part + 1) * lanes)
            v = mixed_ref[:, cut]
            qkv_ref[:, cut] = (v * cos + turn_pairs(v, lanes) * sin).astype(LOW)
        qkv_ref[:, 2 * lanes :] = mixed_ref[:, 2 * lanes :].astype(LOW)
        query_t = qkv_ref[:, :lanes].T
        keys = qkv_ref[:, lanes : 2 * lanes]
        value_t = qkv_ref[:, 2 * lanes :].T
        allowed = key_ref[...] == query_ref[...]
        for h in range(heads):
            cut = head_cut(h)
            logits = jnp.dot(keys[:, cut], query_t[cut, :], preferred_element_type=F32)
            logits = jnp.where(allowed, logits * scale, NEGATIVE)
            top = jnp.max(logits, 0, keepdims=True)
            exponent = jnp.exp(logits - top)
            total_ = jnp.sum(exponent, 0, keepdims=True)
            prob = (exponent / total_).astype(LOW)
            out_t[cut, :] = jnp.dot(value_t[cut, :], prob, preferred_element_type=F32)
            lse_ref[0, h : h + 1, :] = top + jnp.log(total_)
        att_ref[...] = out_t[...].T.astype(LOW)

    return call(
        kernel,
        (groups,),
        [
            pl.BlockSpec((rows, 3 * lanes), lambda g: (0, g)),
            whole(cosine.shape),
            whole(sine.shape),
            whole(key_code.shape),
            whole(query_code.shape),
        ],
        [
            pl.BlockSpec((rows, 3 * lanes), lambda g: (0, g)),
            pl.BlockSpec((rows, lanes), lambda g: (0, g)),
            pl.BlockSpec((1, heads, rows), lambda g: (g, 0, 0)),
        ],
        [
            jax.ShapeDtypeStruct((rows, columns), LOW),
            jax.ShapeDtypeStruct((rows, groups * lanes), LOW),
            jax.ShapeDtypeStruct((groups, heads, rows), F32),
        ],
        scratch=[pltpu.VMEM((lanes, rows), F32)],
        flops=4 * rows * rows * lanes * groups * 3,
        moved=6 * rows * columns,
        after=after,
    )(mixed, cosine, sine, key_code, query_code)


def attention_backward(qkv, lse, attn_grad, cosine, sine, key_code, query_code, groups, after=()):
    rows, columns = qkv.shape
    lanes = columns // (3 * groups)
    heads = lanes // HD
    scale = HD ** (-0.5)

    def kernel(
        qkv_ref, lse_ref, grad_ref, cos_ref, sin_ref, key_ref, query_ref, out_ref, sum_ref, q_t, k_n, v_n
    ):
        query_t = qkv_ref[:, :lanes].T
        key_t = qkv_ref[:, lanes : 2 * lanes].T
        grad_t = grad_ref[...].T
        queries = qkv_ref[:, :lanes]
        keys = qkv_ref[:, lanes : 2 * lanes]
        values = qkv_ref[:, 2 * lanes :]
        grads = grad_ref[...]
        allowed = key_ref[...] == query_ref[...]
        for h in range(heads):
            cut = head_cut(h)
            logits = jnp.dot(keys[:, cut], query_t[cut, :], preferred_element_type=F32)
            logits = jnp.where(allowed, logits * scale, NEGATIVE)
            prob = jnp.exp(logits - lse_ref[0, h : h + 1, :])
            prob_grad = jnp.dot(values[:, cut], grad_t[cut, :], preferred_element_type=F32)
            inner = jnp.sum(prob * prob_grad, 0, keepdims=True)
            score_grad = (scale * prob * (prob_grad - inner)).astype(LOW)
            q_t[cut, :] = jnp.dot(key_t[cut, :], score_grad, preferred_element_type=F32)
            k_n[:, cut] = jnp.dot(score_grad, queries[:, cut], preferred_element_type=F32)
            v_n[:, cut] = jnp.dot(prob.astype(LOW), grads[:, cut], preferred_element_type=F32)
        cos, sin = cos_ref[...], sin_ref[...]
        for part, w in enumerate((q_t[...].T, k_n[...], v_n[...])):
            cut = slice(part * lanes, (part + 1) * lanes)
            if part < 2:
                w = w * cos - turn_pairs(w, lanes) * sin
            w = w.astype(LOW)
            out_ref[:, cut] = w
            sum_ref[:, cut] = jnp.sum(w.astype(F32), 0, keepdims=True)

    return call(
        kernel,
        (groups,),
        [
            pl.BlockSpec((rows, 3 * lanes), lambda g: (0, g)),
            pl.BlockSpec((1, heads, rows), lambda g: (g, 0, 0)),
            pl.BlockSpec((rows, lanes), lambda g: (0, g)),
            whole(cosine.shape),
            whole(sine.shape),
            whole(key_code.shape),
            whole(query_code.shape),
        ],
        [
            pl.BlockSpec((rows, 3 * lanes), lambda g: (0, g)),
            pl.BlockSpec((1, 3 * lanes), lambda g: (0, g)),
        ],
        [
            jax.ShapeDtypeStruct((rows, columns), LOW),
            jax.ShapeDtypeStruct((1, columns), F32),
        ],
        scratch=[
            pltpu.VMEM((lanes, rows), F32),
            pltpu.VMEM((rows, lanes), F32),
            pltpu.VMEM((rows, lanes), F32),
        ],
        flops=10 * rows * rows * lanes * groups * 3,
        moved=6 * rows * columns,
        after=after,
    )(qkv, lse, attn_grad, cosine, sine, key_code, query_code)
class Lanes:
    def __init__(self, dp):
        self.dp = dp
        self.ring = dp // 4

    def over_x(self, v):
        return lax.ppermute(v, "tensor", [(0, 1), (1, 0)])

    def over_core(self, v):
        return lax.ppermute(v, "dp", [(i, i ^ 1) for i in range(self.dp)])

    def over_y(self, v):
        return lax.ppermute(v, "dp", [(i, i ^ 2) for i in range(self.dp)])

    def down_z(self, v):
        return lax.ppermute(v, "dp", [(i, (i - 4) % self.dp) for i in range(self.dp)])

    def up_z(self, v):
        return lax.ppermute(v, "dp", [(i, (i + 4) % self.dp) for i in range(self.dp)])

    def order(self):
        i = lax.axis_index("dp")
        z, y, c = i // 4, (i // 2) % 2, i % 2
        blocks = []
        for dc in range(2):
            for dy in range(2):
                for dz in range(self.ring):
                    blocks.append(((z + dz) % self.ring) * 4 + (y ^ dy) * 2 + (c ^ dc))
        return jnp.stack(blocks)

    def ring_down(self, v):
        held = [v]
        for _ in range(self.ring - 1):
            held.append(self.down_z(held[-1]))
        return held

    def gather_z(self, shard):
        return stack_rows(self.ring_down(shard))

    def gather_xy(self, held):
        middle = held.shape[1] // 2
        side, across = self.over_x(held), self.over_y(held)
        far_a, far_b = self.over_y(side[:, :middle]), self.over_x(across[:, middle:])
        core = self.over_core
        own = [held, across, core(held), core(across)]
        side_core = core(side)
        other_a = [side, far_a, side_core, core(far_a)]
        other_b = [side, far_b, side_core, core(far_b)]
        return Gathered(own, other_a, other_b)

    def gather_early(self, shard):
        side, across = self.over_x(shard), self.over_y(shard)
        far = self.over_y(side)
        return jnp.concatenate(
            [jnp.concatenate([shard, side], 1), jnp.concatenate([across, far], 1)], 0
        )

    def gather_late(self, both):
        held = self.ring_down(both)
        held = held + [self.over_core(v) for v in held]
        rows = both.shape[0] // 2
        cuts = [
            (dc * self.ring + dz, dy * rows, rows)
            for dc in range(2)
            for dy in range(2)
            for dz in range(self.ring)
        ]
        return Stacked(held, cuts)

    def reduce_xy(self, kept):
        own0, own1, other0, far_a, far_b = kept
        return self.over_y(far_a), self.over_x(far_b)


class Gathered:
    def __init__(self, own, other_a, other_b):
        self.own, self.other_a, self.other_b = own, other_a, other_b

    def parts(self, block, ranges):
        half = self.own[0].shape[1] // 2 // block
        sets = []
        (first, count), (first_a, count_a), (first_b, count_b) = ranges
        if count:
            sets.append(([(v, first) for v in self.own], None, count))
        if count_a:
            sets.append(([(v, first_a) for v in self.other_a], None, count_a))
        if count_b:
            wide = [v.shape[1] // block > half for v in self.other_b]
            sets.append(
                (
                    [(v, first_b + half * w) for v, w in zip(self.other_b, wide)],
                    None,
                    count_b,
                )
            )
        return Parts(sets, block)


class Stacked:
    def __init__(self, pieces, cuts):
        self.pieces, self.cuts = pieces, cuts

    def parts(self, block):
        count = self.pieces[0].shape[1] // block
        return Parts([([(v, 0) for v in self.pieces], self.cuts, count)], block)


def butterfly(value, dp):
    if dp & (dp - 1):
        return lax.psum(value, ("dp", "tensor"))
    value = value + lax.ppermute(value, "tensor", [(0, 1), (1, 0)])
    bit = 1
    while bit < dp:
        value = value + lax.ppermute(value, "dp", [(i, i ^ bit) for i in range(dp)])
        bit *= 2
    return value


def body(
    block_input,
    out_cotangent,
    picture_ids,
    patch_positions,
    picture_lengths,
    pad_mask,
    qkv_weight,
    proj_weight,
    fc1_weight,
    fc2_weight,
    qkv_bias,
    fc1_bias,
    vectors,
    qkv_moments,
    proj_moments,
    fc1_moments,
    fc2_moments,
    qkv_bias_moments,
    fc1_bias_moments,
    vector_moments,
):
    ORDER.last = None
    dp = lax.axis_size("dp")
    relative = dp == 16
    lanes = Lanes(dp)
    slot = lax.axis_index("tensor")
    lead_dp = (lax.axis_index("dp") == 0).astype(F32)
    lead_all = lead_dp * (slot == 0).astype(F32)
    width = block_input.shape[3]
    rows_own = width // dp
    lane_columns = qkv_weight.shape[2]
    hidden = fc1_weight.shape[1]
    grad_factor = float(block_input.shape[0] * block_input.shape[1] * dp * LEN) ** (-0.5)

    shard_1 = jnp.concatenate(
        [qkv_weight.reshape(rows_own, 3 * lane_columns), proj_weight.T], 1
    ).astype(LOW)
    shard_2 = fc1_weight.astype(LOW)
    shard_3 = fc2_weight.astype(LOW).T
    if relative:
        early_3 = lanes.gather_early(shard_3)
        held_1 = lanes.gather_z(shard_1)
        held_2 = lanes.gather_z(shard_2)
        w1, w2 = lanes.gather_xy(held_1), lanes.gather_xy(held_2)
        w3 = lanes.gather_late(early_3)
        w_down = w3.parts(hidden // 2)
    else:

        def plain(shard):
            held = lax.all_gather(shard, "dp", axis=0, tiled=True)
            side = lanes.over_x(held)
            return Gathered([held], [side], [side])

        w1, w2, w3 = plain(shard_1), plain(shard_2), plain(shard_3)
        w_down = w3.parts(hidden // 2, [(0, 2), (0, 1), (0, 1)])
    w_qkv = w1.parts(lane_columns, [(0, 3), (0, 2), (0, 1)])
    w_proj = w1.parts(lane_columns, [(3, 1), (0, 0), (1, 1)])
    w_up = w2.parts(hidden // 2, [(0, 2), (0, 1), (0, 1)])

    def own_row(both):
        mine = lax.dynamic_index_in_dim(both[:, 0], slot, 0, keepdims=False)
        theirs = lax.dynamic_index_in_dim(both[:, 0], 1 - slot, 0, keepdims=False)
        return jnp.concatenate([mine, lanes.over_x(theirs)], 0)

    local_rows = block_input.shape[2]
    biases = jnp.concatenate([qkv_bias.reshape(-1), fc1_bias])
    other_biases = lanes.over_x(biases)
    cut = qkv_bias.size
    bias_qkv = jnp.concatenate([biases[:cut], other_biases[:cut]])[None]
    bias_up = jnp.concatenate([biases[cut:], other_biases[cut:]])[None]

    def pick(array, axis=0):
        return lax.dynamic_index_in_dim(array, slot, axis, keepdims=False)

    def turn(values):
        return jnp.roll(values, -slot * local_rows, axis=-1)

    ids_row = turn(pick(picture_ids[:, 0]))
    rows_at = turn(pick(patch_positions[0, :, 0]))
    cols_at = turn(pick(patch_positions[1, :, 0]))
    mask_row = turn(pick(pad_mask[:, 0]))
    length_row = pick(picture_lengths[:, 0])
    cosine, sine = rotary_tables(rows_at, cols_at)
    groups = 2
    heads = lane_columns // HD
    cosine, sine = jnp.tile(cosine, (1, heads)), jnp.tile(sine, (1, heads))
    key_code = jnp.where(mask_row == 1, ids_row, -1)[:, None]
    query_code = ids_row[None, :]
    slot_hit = (ids_row[:, None] == jnp.arange(SLOTS, dtype=jnp.int32)[None, :]).astype(F32)
    picture_size = jnp.sum(slot_hit * length_row.astype(F32)[None, :], -1)
    token_weight = (mask_row.astype(F32) * jnp.sqrt(LEN / picture_size))[:, None]

    if relative:
        order = lanes.order()
        column = (order[:, None] * rows_own + jnp.arange(rows_own)[None, :]).reshape(-1)
        shuffle = (jnp.arange(width)[:, None] == column[None, :]).astype(LOW)
        vec = lax.dot_general(
            vectors,
            shuffle.astype(F32),
            (((1,), (0,)), ((), ())),
            precision=lax.Precision.HIGHEST,
            preferred_element_type=F32,
        )
        row_low = dot(own_row(block_input), shuffle).astype(LOW)
        cot_low = dot(own_row(out_cotangent), shuffle).astype(LOW)
    else:
        vec = vectors
        row_low = own_row(block_input)
        cot_low = own_row(out_cotangent)

    def give_back(values_low):
        if relative:
            values_low = dot_t(values_low, shuffle).astype(LOW)
        mine, theirs = values_low[:local_rows], lanes.over_x(values_low[local_rows:])
        swap = slot == 0
        return jnp.stack([jnp.where(swap, mine, theirs), jnp.where(swap, theirs, mine)])[:, None]

    wide_kind = [(0, j) for j in range(4)]
    first_kind = [(0, 0), (0, 1), (0, 2), (1, 0), (0, 3), (0, 4), (0, 5), (1, 1)]

    def send_grads(pairs, block, kind):
        (sent,) = grad_kernel(pairs, block, kind, 1, None)
        return lanes.over_core(sent) if relative else sent

    def keep_grads(pairs, block, kind, came):
        return grad_kernel(pairs, block, kind, 0, came)

    def send_far(kept):
        return lanes.over_y(kept[3]), lanes.over_x(kept[4])

    def send_sides(kept, far):
        to_x, to_y = add_far(kept[2], kept[1], *far)
        return lanes.over_x(to_x), lanes.over_y(to_y)

    def ring_step(kept, sides, came, place):
        arrays = [(v, place * rows_own, 0) for v in (kept[0], *sides)]
        if came is not None:
            arrays.append((came, 0, 0))
        kind = LOW if place else F32
        total = add_cuts(arrays, rows_own, hidden, rows_own, hidden, kind)
        return lanes.up_z(total) if place else total

    def plain_grads(pairs, block, kind):
        whole_grad = jnp.concatenate(
            [
                outer(pairs[p][0], pairs[p][1][:, c * block : (c + 1) * block])
                for p, c in kind
            ],
            1,
        )
        both = whole_grad[:, :hidden] + lanes.over_x(whole_grad[:, hidden:])
        return lax.psum_scatter(both, "dp", scatter_dimension=0, tiled=True)

    normed1, _ = norm_parts(row_low.astype(F32))
    first_in = (normed1 * vec[0] + vec[1]).astype(LOW)
    down_grad = (cot_low.astype(F32) * token_weight).astype(LOW)
    mixed = qkv_forward(first_in, w_qkv, bias_qkv, list(range(6)))
    qkv, attended, lse = attention_forward(mixed, cosine, sine, key_code, query_code, groups)
    hidden1, second_in = proj_forward(attended, w_proj, row_low, vec)
    upward, activated = up_forward(second_in, w_up, bias_up)
    pair_3 = [(down_grad, activated)]
    half = hidden // 2
    if relative:
        came_3 = send_grads(pair_3, half, wide_kind)
    result = down_forward(activated, w_down, hidden1, vec)

    if relative:
        kept_3 = keep_grads(pair_3, half, wide_kind, came_3)
        far_3 = send_far(kept_3)
    up_grad, sum_up = down_backward(down_grad, w_down, upward)
    pair_2 = [(second_in, up_grad)]
    if relative:
        sides_3 = send_sides(kept_3, far_3)
        came_2 = send_grads(pair_2, half, wide_kind)
    hidden1_grad, branch_grad, sums_2 = up_backward(
        up_grad, w_up, hidden1, cot_low, token_weight, vec
    )
    if relative:
        kept_2 = keep_grads(pair_2, half, wide_kind, came_2)
        far_2 = send_far(kept_2)
    attn_grad = proj_backward(branch_grad, w_proj)
    if relative:
        ring_3 = ring_step(kept_3, sides_3, None, 3)
    mixed_grad, sum_qkv = attention_backward(
        qkv, lse, attn_grad, cosine, sine, key_code, query_code, groups
    )
    pair_1 = [(first_in, mixed_grad), (branch_grad, attended)]
    if relative:
        ring_3 = ring_step(kept_3, sides_3, ring_3, 2)
        sides_2 = send_sides(kept_2, far_2)
        came_1 = send_grads(pair_1, lane_columns, first_kind)
        ring_3 = ring_step(kept_3, sides_3, ring_3, 1)
        kept_1 = keep_grads(pair_1, lane_columns, first_kind, came_1)
        far_1 = send_far(kept_1)
    input_low, sums_1 = qkv_backward(
        mixed_grad, w_qkv, list(range(6)), row_low, hidden1_grad, vec
    )
    if relative:
        sides_1 = send_sides(kept_1, far_1)
        grad_3 = ring_step(kept_3, sides_3, ring_3, 0)
        ring_2 = ring_step(kept_2, sides_2, None, 3)
        ring_2 = ring_step(kept_2, sides_2, ring_2, 2)
        ring_2 = ring_step(kept_2, sides_2, ring_2, 1)
        grad_2 = ring_step(kept_2, sides_2, ring_2, 0)
        ring_1 = ring_step(kept_1, sides_1, None, 3)
        ring_1 = ring_step(kept_1, sides_1, ring_1, 2)
        ring_1 = ring_step(kept_1, sides_1, ring_1, 1)
        grad_1 = ring_step(kept_1, sides_1, ring_1, 0)
    else:
        grad_3 = plain_grads(pair_3, half, wide_kind)
        grad_2 = plain_grads(pair_2, half, wide_kind)
        grad_1 = plain_grads(pair_1, lane_columns, first_kind)
    block_output = give_back(result)
    input_grad = give_back(input_low)

    grad_qkv = grad_1[:, : 3 * lane_columns].reshape(rows_own, 3, lane_columns)
    grad_proj = grad_1[:, 3 * lane_columns :].T
    grad_up = grad_2
    grad_down = grad_3.T
    vector_terms = jnp.concatenate([sums_1[0:2], sums_2[2:3], sums_2[0:2], sums_2[3:4]], 0)
    if relative:
        vector_terms = lax.dot_general(
            vector_terms,
            shuffle.astype(F32),
            (((1,), (1,)), ((), ())),
            precision=lax.Precision.HIGHEST,
            preferred_element_type=F32,
        )
    qkv_columns = 3 * lane_columns
    own_small = jnp.concatenate([sum_qkv[0, :qkv_columns], sum_up[0, :hidden]])
    other_small = jnp.concatenate([sum_qkv[0, qkv_columns:], sum_up[0, hidden:]])
    first_half = slot == 0
    small = jnp.concatenate(
        [
            jnp.where(first_half, own_small, other_small),
            jnp.where(first_half, other_small, own_small),
            vector_terms.reshape(-1),
        ]
    )
    small = butterfly(small.reshape(-1, 128), dp).reshape(-1)
    size = own_small.shape[0]
    bias_sum = jnp.where(first_half, small[:size], small[size : 2 * size])
    grad_qkv_bias = bias_sum[: qkv_bias.size].reshape(qkv_bias.shape)
    grad_up_bias = bias_sum[qkv_bias.size :]
    grad_vectors = small[2 * size :].reshape(vectors.shape)

    params = (qkv_weight, proj_weight, fc1_weight, fc2_weight, qkv_bias, fc1_bias, vectors)
    moment_list = (
        qkv_moments,
        proj_moments,
        fc1_moments,
        fc2_moments,
        qkv_bias_moments,
        fc1_bias_moments,
        vector_moments,
    )
    shares = (1.0, 1.0, 1.0, 1.0, lead_dp, lead_dp, lead_all)
    summed = (grad_qkv, grad_proj, grad_up, grad_down, grad_qkv_bias, grad_up_bias, grad_vectors)
    new_moments = []
    updates = []
    terms = []
    for master, moments, gradient, factor in zip(params, moment_list, summed, shares):
        first, second, update = lamb_parts(master, moments, gradient * grad_factor)
        new_moments.append(jnp.stack([first, second]))
        updates.append(update)
        terms.append(jnp.sum(update * update) * factor)
    terms = [
        jnp.sum(master * master) * factor for master, factor in zip(params, shares)
    ] + terms
    terms = jnp.pad(jnp.stack(terms), (0, 114)).reshape(1, 128)
    terms = butterfly(terms, dp)[0]
    weight_sq, update_sq = terms[:7], terms[7:14]
    trust = jnp.sqrt(weight_sq) / jnp.sqrt(update_sq + 1e-12)
    new_params = [params[k] - LEARN_RATE * trust[k] * updates[k] for k in range(7)]
    norms = jnp.stack([jnp.sqrt(weight_sq), jnp.sqrt(update_sq)])
    return (
        block_output,
        input_grad,
        *new_params,
        *new_moments,
        *[p.astype(LOW) for p in new_params[:4]],
        norms,
        trust,
    )


def solution(mesh):
    in_specs = (
        P(None, "dp", "tensor", None),
        P(None, "dp", "tensor", None),
        P(None, "dp", None),
        P(None, None, "dp", None),
        P(None, "dp", None),
        P(None, "dp", None),
        P("dp", None, "tensor"),
        P("tensor", "dp"),
        P("dp", "tensor"),
        P("tensor", "dp"),
        P(None, "tensor"),
        P("tensor"),
        P(),
        P(None, "dp", None, "tensor"),
        P(None, "tensor", "dp"),
        P(None, "dp", "tensor"),
        P(None, "tensor", "dp"),
        P(None, None, "tensor"),
        P(None, "tensor"),
        P(),
    )
    out_specs = (
        P(None, "dp", "tensor", None),
        P(None, "dp", "tensor", None),
        P("dp", None, "tensor"),
        P("tensor", "dp"),
        P("dp", "tensor"),
        P("tensor", "dp"),
        P(None, "tensor"),
        P("tensor"),
        P(),
        P(None, "dp", None, "tensor"),
        P(None, "tensor", "dp"),
        P(None, "dp", "tensor"),
        P(None, "tensor", "dp"),
        P(None, None, "tensor"),
        P(None, "tensor"),
        P(),
        P("dp", None, "tensor"),
        P("tensor", "dp"),
        P("dp", "tensor"),
        P("tensor", "dp"),
        P(),
        P(),
    )
    return jax.shard_map(body, mesh=mesh, in_specs=in_specs, out_specs=out_specs, check_vma=False)
```

time: 1020 us -> 811 us (0.80)
  Pallas kernels: 0 us -> 284 us
  matrix products: 253 us -> 15.1 us
  other arithmetic: 173 us -> 46.7 us
  local copies, waits for them, and re-layouts: 163 us -> 60.7 us
  starting transfers between devices: 99.9 us -> 81.3 us
  waiting for transfers between devices: 312 us -> 301 us
    pallas_call x0 -> x33, Pallas kernels: none -> 284 us  [start(): result = run(*operands, *after)]
    dot_general x34 -> x0, matrix products: 125 us -> none  [the longest x28 59.2 us: outer(): lax.dot_general(left, right, (((0,), (0,)), ((), ())), preferred_element_...]
    dot_general x15 -> x2, matrix products: 63.5 us -> 4.29 us  [dot_t(): lax.dot_general(left, right, (((1,), (1,)), ((), ())), preferred_element_...]
    dot_general x16 -> x2, matrix products: 59.1 us -> 6 us  [dot(): lax.dot_general(left, right, (((1,), (0,)), ((), ())), preferred_element_...]
    convert_element_type x22 -> x2, other arithmetic: 51.6 us -> 0.12 us  [the longest x1 0.08 us: rotary_tables(): rows_at.astype(F32)[:, None] * frequency]
    another operation x39 -> x0, other arithmetic: 42 us -> none  [the longest x21 20.9 us: reduce_b(): came = self.up_z(jnp.stack([total(parts[0]), total(parts[1])]))]
    unnamed x429 -> x231, local copies, waits for them, and re-layouts: 69.5 us -> 27.9 us
    ppermute x12, waiting for transfers between devices: 74.6 us -> 43.1 us  [over_y(): return lax.ppermute(v, 'dp', [(i, i ^ 2) for i in range(self.dp)])]
  transfers between devices with their start and end apart: 101 -> 73, of which waited for: 44 -> 31; matrix products, arithmetic and copies ran while one was open for 54% -> 9% of each run, Pallas kernels for 0% -> 29%
where the time goes in v2:
time: 811 us; the launch traced here: 799 us
  waiting for transfers between devices  301 us (37%)
  Pallas kernels  284 us (35%)
  starting transfers between devices  81.3 us (10%)
  local copies, waits for them, and re-layouts  60.7 us (7%)
  other arithmetic  46.7 us (6%)
  matrix products  15.1 us (2%)
  between operations  10.6 us (1%)
    pallas_call x33, Pallas kernels, start(): result = run(*operands, *after)  284 us
    ppermute x9, waiting for transfers between devices, down_z(): lax.ppermute(v, 'dp', [(i, (i - 4) % self.dp) for i in range(self.dp)])  98.5 us
    ppermute x9, waiting for transfers between devices, up_z(): lax.ppermute(v, 'dp', [(i, (i + 4) % self.dp) for i in range(self.dp)])  57.3 us
    ppermute x16, waiting for transfers between devices, over_x(): return lax.ppermute(v, 'tensor', [(0, 1), (1, 0)])  55.3 us
    ppermute x12, waiting for transfers between devices, over_y(): return lax.ppermute(v, 'dp', [(i, i ^ 2) for i in range(self.dp)])  43.1 us
    ppermute x8, waiting for transfers between devices, butterfly(): value = value + lax.ppermute(value, 'dp', [(i, i ^ bit) for i in range(dp)])  43 us
    ppermute x9, starting transfers between devices, down_z(): lax.ppermute(v, 'dp', [(i, (i - 4) % self.dp) for i in range(self.dp)])  35.7 us
    unnamed x231, local copies, waits for them, and re-layouts  27.9 us
  transfers between devices with their start and end apart: 73, of which 31 were waited for; matrix products, arithmetic and copies ran while one was open for 9% of the time, Pallas kernels for 29%

profile of v2, /device:TPU:0, one launch (start us, length us, event | category | flops | bytes accessed | tf_op | source)
XLA Modules:
  0.0 799.5 jit_solution(3097489687585202045)
XLA Ops:
  10.8 7.2 collective-permute-done.1.refs_1_
  77.9 23.1 %collective-permute-done.27 = bf16[80,2560]{1,0:T(8,128)(2,1)} collective-permute-done((bf16[80,2560]{1,0:T(8,128)(2,1)}, bf16[80,2560]{1,0:T(8,128)(2,1)}, u32[]{:S(2)}, u32[]{:S(2)}) %collective-permute-start.27) | collective-permute-done | bytes 409632 | tf_op jit(solution)/shard_map/ppermute | solution.py:800
  105.9 26.1 %collective-permute-done.20.refs_5_.refs_9_ = bf16[320,2560]{1,0:T(8,128)(2,1)} collective-permute-done((bf16[320,2560]{1,0:T(8,128)(2,1)}, bf16[320,2560]{1,0:T(8,128)(2,1)}, u32[]{:S(2)}, u32[]{:S(2)}) %collective-permute-start.20) | collective-permute-done | bytes 1638432 | tf_op jit(solution)/shard_map/ppermute | solution.py:794
  137.8 9.9 %collective-permute-done = bf16[288,1280]{1,0:T(8,128)(2,1)S(1)} collective-permute-done((bf16[288,1280]{1,0:T(8,128)(2,1)S(1)}, bf16[288,1280]{1,0:T(8,128)(2,1)S(1)}, u32[]{:S(2)}, u32[]{:S(2)}) %collective-permute-start) | collective-permute-done | bytes 737312 | tf_op jit(solution)/shard_map/ppermute | solution.py:794
  149.2 14.3 %collective-permute-done.36 = bf16[288,1280]{1,0:T(8,128)(2,1)S(1)} collective-permute-done((bf16[288,1280]{1,0:T(8,128)(2,1)S(1)}, bf16[288,1280]{1,0:T(8,128)(2,1)S(1)}, u32[]{:S(2)}, u32[]{:S(2)}) %collective-permute-start.36) | collective-permute-done | bytes 737312 | tf_op jit(solution)/shard_map/ppermute | solution.py:794
  184.7 9.7 %collective-permute-done.21.refs_6_ = bf16[320,1280]{1,0:T(8,128)(2,1)} collective-permute-done((bf16[320,1280]{1,0:T(8,128)(2,1)S(1)}, bf16[320,1280]{1,0:T(8,128)(2,1)}, u32[]{:S(2)}, u32[]{:S(2)}) %collective-permute-start.21) | collective-permute-done | bytes 819232 | tf_op jit(solution)/shard_map/ppermute | solution.py:800
  201.8 13.9 %shard_map.365.refs_0_.refs_5_ = f32[576,3840]{1,0:T(8,128)} custom-call(bf16[576,1280]{1,0:T(8,128)(2,1)} %fusion.21.refs_0_, bf16[320,2560]{1,0:T(8,128)(2,1)} %shard_map.363.refs_4_.refs_1_, bf16[320,2560]{1,0:T(8,128)(2,1)} %collective-permute-done.4.refs_2_, bf16[320,2560]{1,0:T(8,128)(2,1)} %copy-done.5, bf16[320,2560]{1,0:T(8,128)(2,1)} %copy-done.6, ...), custom_call_target="tpu_custom_call" | custom-call | flops 5662310400 | bytes 23101440 | tf_op jit(solution)/shard_map/pallas_call | solution.py:104
  215.7 19.6 %shard_map.366 = (bf16[576,3840]{1,0:T(8,128)(2,1)}, bf16[576,1280]{1,0:T(8,128)(2,1)}, f32[2,8,576]{2,1,0:T(8,128)}) custom-call(f32[576,3840]{1,0:T(8,128)} %shard_map.365.refs_0_.refs_5_, f32[576,640]{1,0:T(8,128)} %copy.81.refs_1_.refs_3_, f32[576,640]{1,0:T(8,128)} %copy.82.refs_2_.refs_4_, s32[576,1]{1,0:T(8,128)} %broadcast_in_dim.46.refs_3_.refs_5_, ...), custom_call_target="tpu_custom_call" | custom-call | flops 5096079360 | bytes 13271040 | tf_op jit(solution)/shard_map/pallas_call | solution.py:104
  235.3 9.9 %shard_map.367 = (f32[576,1280]{1,0:T(8,128)}, bf16[576,1280]{1,0:T(8,128)(2,1)}) custom-call(bf16[576,1280]{1,0:T(8,128)(2,1)} %get-tuple-element.60.refs_0_.refs_3_, bf16[320,2560]{1,0:T(8,128)(2,1)} %shard_map.363.refs_4_.refs_1_, bf16[320,2560]{1,0:T(8,128)(2,1)} %collective-permute-done.4.refs_2_, bf16[320,2560]{1,0:T(8,128)(2,1)} %copy-done.5, ...), custom_call_target="tpu_custom_call" | custom-call | flops 1887436800 | bytes 10649600 | tf_op jit(solution)/shard_map/pallas_call | solution.py:104
  250.8 17.7 %shard_map.368 = (f32[576,5120]{1,0:T(8,128)}, bf16[576,5120]{1,0:T(8,128)(2,1)}) custom-call(bf16[576,1280]{1,0:T(8,128)(2,1)} %get-tuple-element.62.refs_0_, bf16[320,2560]{1,0:T(8,128)(2,1)} %shard_map.364.refs_14_.refs_1_, bf16[320,2560]{1,0:T(8,128)(2,1)} %collective-permute-done.17.refs_2_, bf16[320,2560]{1,0:T(8,128)(2,1)} %collective-permute-done.18.refs_3_, ...), custom_call_target="tpu_custom_call" | custom-call | flops 7549747200 | bytes 30801920 | tf_op jit(solution)/shard_map/pallas_call | solution.py:104
  268.5 9.8 %shard_map.369.refs_11_ = bf16[640,5120]{1,0:T(8,128)(2,1)} custom-call(bf16[576,1280]{1,0:T(8,128)(2,1)} %get-tuple-element.262.refs_0_, bf16[576,5120]{1,0:T(8,128)(2,1)} %get-tuple-element.64.refs_1_.refs_0_, f32[576,5120]{1,0:T(8,128)} %get-tuple-element.65.refs_2_.refs_9_), custom_call_target="tpu_custom_call" | custom-call | flops 3774873600 | bytes 12451840 | tf_op jit(solution)/shard_map/pallas_call | solution.py:104
  278.4 6.7 collective-permute-done.29.refs_2_
  289.4 34.7 %collective-permute-done.30.refs_3_ = bf16[160,5120]{1,0:T(8,128)(2,1)S(1)} collective-permute-done((bf16[160,5120]{1,0:T(8,128)(2,1)S(1)}, bf16[160,5120]{1,0:T(8,128)(2,1)S(1)}, u32[]{:S(2)}, u32[]{:S(2)}) %collective-permute-start.30) | collective-permute-done | bytes 1638432 | tf_op jit(solution)/shard_map/ppermute | solution.py:803
  328.9 33.3 %collective-permute-done.31.refs_4_ = bf16[160,5120]{1,0:T(8,128)(2,1)S(1)} collective-permute-done((bf16[160,5120]{1,0:T(8,128)(2,1)S(1)}, bf16[160,5120]{1,0:T(8,128)(2,1)S(1)}, u32[]{:S(2)}, u32[]{:S(2)}) %collective-permute-start.31) | collective-permute-done | bytes 1638432 | tf_op jit(solution)/shard_map/ppermute | solution.py:803
  365.8 15.0 %shard_map.370.refs_3_ = bf16[576,1280]{1,0:T(8,128)(2,1)} custom-call(bf16[576,5120]{1,0:T(8,128)(2,1)} %get-tuple-element.64.refs_1_.refs_0_, bf16[160,5120]{1,0:T(8,128)(2,1)} %copy-done.10, bf16[160,5120]{1,0:T(8,128)(2,1)} %copy-done.19, bf16[160,5120]{1,0:T(8,128)(2,1)} %copy-done.20, bf16[160,5120]{1,0:T(8,128)(2,1)} %copy-done.21, ...), custom_call_target="tpu_custom_call" | custom-call | flops 7549747200 | bytes 24903680 | tf_op jit(solution)/shard_map/pallas_call | solution.py:104
  380.8 12.0 %shard_map.371 = (bf16[320,2560]{1,0:T(8,128)(2,1)}, bf16[320,2560]{1,0:T(8,128)(2,1)}, bf16[320,2560]{1,0:T(8,128)(2,1)}, bf16[320,1280]{1,0:T(8,128)(2,1)}, bf16[320,1280]{1,0:T(8,128)(2,1)}) custom-call(bf16[576,1280]{1,0:T(8,128)(2,1)} %get-tuple-element.262.refs_0_, bf16[576,5120]{1,0:T(8,128)(2,1)} %get-tuple-element.64.refs_1_.refs_0_, ...), custom_call_target="tpu_custom_call" | custom-call | flops 3774873600 | bytes 12451840 | tf_op jit(solution)/shard_map/pallas_call | solution.py:104
  394.8 18.9 %shard_map.372 = (bf16[576,5120]{1,0:T(8,128)(2,1)}, f32[1,5120]{1,0:T(1,128)}) custom-call(bf16[576,1280]{1,0:T(8,128)(2,1)} %get-tuple-element.262.refs_0_, bf16[160,5120]{1,0:T(8,128)(2,1)} %copy-done.10, bf16[160,5120]{1,0:T(8,128)(2,1)} %copy-done.19, bf16[160,5120]{1,0:T(8,128)(2,1)} %copy-done.20, bf16[160,5120]{1,0:T(8,128)(2,1)} %copy-done.21, ...), custom_call_target="tpu_custom_call" | custom-call | flops 7549747200 | bytes 30801920 | tf_op jit(solution)/shard_map/pallas_call | solution.py:104
  418.7 10.0 %shard_map.374.refs_17_ = bf16[640,5120]{1,0:T(8,128)(2,1)} custom-call(bf16[576,1280]{1,0:T(8,128)(2,1)} %get-tuple-element.62.refs_0_, bf16[576,5120]{1,0:T(8,128)(2,1)} %get-tuple-element.68.refs_4_.refs_1_.refs_0_, bf16[320,2560]{1,0:T(8,128)(2,1)} %get-tuple-element.73.refs_2_), custom_call_target="tpu_custom_call" | custom-call | flops 3774873600 | bytes 12451840 | tf_op jit(solution)/shard_map/pallas_call | solution.py:104
  432.2 21.7 %shard_map.375 = (f32[576,1280]{1,0:T(8,128)}, bf16[576,1280]{1,0:T(8,128)(2,1)}, f32[8,1280]{1,0:T(8,128)}) custom-call(bf16[576,5120]{1,0:T(8,128)(2,1)} %get-tuple-element.68.refs_4_.refs_1_.refs_0_, bf16[320,2560]{1,0:T(8,128)(2,1)} %shard_map.364.refs_14_.refs_1_, bf16[320,2560]{1,0:T(8,128)(2,1)} %collective-permute-done.17.refs_2_, ...), custom_call_target="tpu_custom_call" | custom-call | flops 7549747200 | bytes 24903680 | tf_op jit(solution)/shard_map/pallas_call | solution.py:104
  453.9 12.0 %shard_map.376 = (bf16[320,2560]{1,0:T(8,128)(2,1)}, bf16[320,2560]{1,0:T(8,128)(2,1)}, bf16[320,2560]{1,0:T(8,128)(2,1)}, bf16[320,1280]{1,0:T(8,128)(2,1)}, bf16[320,1280]{1,0:T(8,128)(2,1)}) custom-call(bf16[576,1280]{1,0:T(8,128)(2,1)} %get-tuple-element.62.refs_0_, bf16[576,5120]{1,0:T(8,128)(2,1)} %get-tuple-element.68.refs_4_.refs_1_.refs_0_, ...), custom_call_target="tpu_custom_call" | custom-call | flops 3774873600 | bytes 12451840 | tf_op jit(solution)/shard_map/pallas_call | solution.py:104
  466.0 6.0 shard_map.377.refs_3_.refs_2_
  478.0 27.5 %shard_map.379 = (bf16[576,3840]{1,0:T(8,128)(2,1)}, f32[1,3840]{1,0:T(1,128)}) custom-call(bf16[576,3840]{1,0:T(8,128)(2,1)} %get-tuple-element.61.refs_11_.refs_0_, f32[2,8,576]{2,1,0:T(8,128)} %get-tuple-element.66.refs_1_, bf16[576,1280]{1,0:T(8,128)(2,1)} %shard_map.377.refs_3_.refs_2_, f32[576,640]{1,0:T(8,128)} %copy.81.refs_1_.refs_3_, ...), custom_call_target="tpu_custom_call" | custom-call | flops 12740198400 | bytes 13271040 | tf_op jit(solution)/shard_map/pallas_call | solution.py:104
  513.7 12.7 %shard_map.382.refs_4_ = bf16[640,5120]{1,0:T(8,128)(2,1)} custom-call(bf16[576,1280]{1,0:T(8,128)(2,1)} %fusion.21.refs_0_, bf16[576,1280]{1,0:T(8,128)(2,1)} %get-tuple-element.74.refs_0_.refs_1_, bf16[576,3840]{1,0:T(8,128)(2,1)} %get-tuple-element.78.refs_4_.refs_2_.refs_0_, bf16[576,1280]{1,0:T(8,128)(2,1)} %get-tuple-element.60.refs_0_.refs_3_, ...), custom_call_target="tpu_custom_call" | custom-call | flops 3774873600 | bytes 12451840 | tf_op jit(solution)/shard_map/pallas_call | solution.py:104
  534.7 11.6 %collective-permute-done.48.refs_3_ = bf16[80,2560]{1,0:T(8,128)(2,1)S(1)} collective-permute-done((bf16[80,2560]{1,0:T(8,128)(2,1)S(1)}, bf16[80,2560]{1,0:T(8,128)(2,1)S(1)}, u32[]{:S(2)}, u32[]{:S(2)}) %collective-permute-start.48) | collective-permute-done | bytes 409632 | tf_op jit(solution)/shard_map/ppermute | solution.py:806
  549.4 14.7 %shard_map.384 = (bf16[320,2560]{1,0:T(8,128)(2,1)}, bf16[320,2560]{1,0:T(8,128)(2,1)}, bf16[320,2560]{1,0:T(8,128)(2,1)}, bf16[320,1280]{1,0:T(8,128)(2,1)}, bf16[320,1280]{1,0:T(8,128)(2,1)}) custom-call(bf16[576,1280]{1,0:T(8,128)(2,1)} %fusion.21.refs_0_, bf16[576,1280]{1,0:T(8,128)(2,1)} %get-tuple-element.74.refs_0_.refs_1_, ...), custom_call_target="tpu_custom_call" | custom-call | flops 3774873600 | bytes 12451840 | tf_op jit(solution)/shard_map/pallas_call | solution.py:104
  564.1 18.2 %shard_map.385 = (bf16[576,1280]{1,0:T(8,128)(2,1)}, f32[8,1280]{1,0:T(8,128)}) custom-call(bf16[576,3840]{1,0:T(8,128)(2,1)} %get-tuple-element.78.refs_4_.refs_2_.refs_0_, bf16[320,2560]{1,0:T(8,128)(2,1)} %shard_map.363.refs_4_.refs_1_, bf16[320,2560]{1,0:T(8,128)(2,1)} %collective-permute-done.4.refs_2_, bf16[320,2560]{1,0:T(8,128)(2,1)} %copy-done.5, ...), custom_call_target="tpu_custom_call" | custom-call | flops 5662310400 | bytes 20152320 | tf_op jit(solution)/shard_map/pallas_call | solution.py:104
  598.5 34.1 %collective-permute-done.65 = f32[130,128]{1,0:T(8,128)S(1)} collective-permute-done((f32[130,128]{1,0:T(8,128)S(1)}, f32[130,128]{1,0:T(8,128)S(1)}, u32[]{:S(2)}, u32[]{:S(2)}) %collective-permute-start.65) | collective-permute-done | bytes 66592 | tf_op jit(solution)/shard_map/ppermute | solution.py:901
  644.0 5.3 collective-permute-done.50.refs_2_
  670.0 9.6 %collective-permute-done.57.refs_3_ = bf16[80,2560]{1,0:T(8,128)(2,1)S(1)} collective-permute-done((bf16[80,2560]{1,0:T(8,128)(2,1)}, bf16[80,2560]{1,0:T(8,128)(2,1)S(1)}, u32[]{:S(2)}, u32[]{:S(2)}) %collective-permute-start.57) | collective-permute-done | bytes 409632 | tf_op jit(solution)/shard_map/ppermute | solution.py:806
  682.8 10.9 %collective-permute-done.58.refs_3_ = bf16[80,2560]{1,0:T(8,128)(2,1)S(1)} collective-permute-done((bf16[80,2560]{1,0:T(8,128)(2,1)}, bf16[80,2560]{1,0:T(8,128)(2,1)S(1)}, u32[]{:S(2)}, u32[]{:S(2)}) %collective-permute-start.58) | collective-permute-done | bytes 409632 | tf_op jit(solution)/shard_map/ppermute | solution.py:806
  713.5 8.7 %collective-permute-done.60.refs_3_ = bf16[80,2560]{1,0:T(8,128)(2,1)S(1)} collective-permute-done((bf16[80,2560]{1,0:T(8,128)(2,1)}, bf16[80,2560]{1,0:T(8,128)(2,1)S(1)}, u32[]{:S(2)}, u32[]{:S(2)}) %collective-permute-start.60) | collective-permute-done | bytes 409632 | tf_op jit(solution)/shard_map/ppermute | solution.py:806
  727.7 7.5 collective-permute-done.61.refs_3_
  (504 shorter events, 296.2 us)
Async XLA Ops:
  9.3 59.1 %collective-permute-start.13 = (f32[4480]{0:T(1024)}, f32[4480]{0:T(1024)}, u32[]{:S(2)}, u32[]{:S(2)}) collective-permute-start(f32[4480]{0:T(1024)} %pad_maximum_fusion.7), channel_id=1, source_target_pairs={{0,1},{1,0},{2,3},{3,2},{4,5},{5,4},{6,7},{7,6},{8,9},{9,8},{10,11... | collective-permute-start | bytes 53768 | tf_op jit(solution)/shard_map/ppermute | solution.py:794
  31.8 45.5 %collective-permute-start.26 = (bf16[80,2560]{1,0:T(8,128)(2,1)}, bf16[80,2560]{1,0:T(8,128)(2,1)}, u32[]{:S(2)}, u32[]{:S(2)}) collective-permute-start(bf16[80,2560]{1,0:T(8,128)(2,1)} %convert_bitcast_fusion), channel_id=1, source_target_pairs={{0,1},{1,0},{2,3},{3,2},{4,5},{5,4},{6,7},{7,6},{8,9},{9,8},{10,11... | collective-permute-start | bytes 1228808 | tf_op jit(solution)/shard_map/ppermute | solution.py:794
  56.3 46.2 %collective-permute-start.4 = (bf16[320,2560]{1,0:T(8,128)(2,1)}, bf16[320,2560]{1,0:T(8,128)(2,1)}, u32[]{:S(2)}, u32[]{:S(2)}) collective-permute-start(bf16[320,2560]{1,0:T(8,128)(2,1)} %shard_map.363.refs_4_.refs_1_), channel_id=1, source_target_pairs={{0,4},{2,6},{4,0},{6,2},{8,12},{10,14},{12,8},{14,10},{16,20},{18,... | collective-permute-start | bytes 4915208 | tf_op jit(solution)/shard_map/ppermute | solution.py:800
  57.9 44.6 %collective-permute-start.7 = (bf16[320,2560]{1,0:T(8,128)(2,1)}, bf16[320,2560]{1,0:T(8,128)(2,1)S(1)}, u32[]{:S(2)}, u32[]{:S(2)}) collective-permute-start(bf16[320,2560]{1,0:T(8,128)(2,1)} %shard_map.363.refs_4_.refs_1_), channel_id=1, source_target_pairs={{0,1},{1,0},{2,3},{3,2},{4,5},{5,4},{6,7},{7,6},{8,9},{9,8},{10,11... | collective-permute-start | bytes 4915208 | tf_op jit(solution)/shard_map/ppermute | solution.py:794
  64.0 68.0 %collective-permute-start.20 = (bf16[320,2560]{1,0:T(8,128)(2,1)}, bf16[320,2560]{1,0:T(8,128)(2,1)}, u32[]{:S(2)}, u32[]{:S(2)}) collective-permute-start(bf16[320,2560]{1,0:T(8,128)(2,1)} %shard_map.364.refs_14_.refs_1_), channel_id=1, source_target_pairs={{0,1},{1,0},{2,3},{3,2},{4,5},{5,4},{6,7},{7,6},{8,9},{9,8},{10,11... | collective-permute-start | bytes 4915208 | tf_op jit(solution)/shard_map/ppermute | solution.py:794
  77.3 70.4 %collective-permute-start = (bf16[288,1280]{1,0:T(8,128)(2,1)S(1)}, bf16[288,1280]{1,0:T(8,128)(2,1)S(1)}, u32[]{:S(2)}, u32[]{:S(2)}) collective-permute-start(bf16[288,1280]{1,0:T(8,128)(2,1)S(1)} %copy-done.64), channel_id=1, source_target_pairs={{0,1},{1,0},{2,3},{3,2},{4,5},{5,4},{6,7},{7,6},{8,9},{9,8},{10,11... | collective-permute-start | bytes 2211848 | tf_op jit(solution)/shard_map/ppermute | solution.py:794
  100.9 62.6 %collective-permute-start.36 = (bf16[288,1280]{1,0:T(8,128)(2,1)S(1)}, bf16[288,1280]{1,0:T(8,128)(2,1)S(1)}, u32[]{:S(2)}, u32[]{:S(2)}) collective-permute-start(bf16[288,1280]{1,0:T(8,128)(2,1)S(1)} %get-tuple-element.210), channel_id=1, source_target_pairs={{0,1},{1,0},{2,3},{3,2},{4,5},{5,4},{6,7},{7,6},{8,9},{9,8},{10,11... | collective-permute-start | bytes 2211848 | tf_op jit(solution)/shard_map/ppermute | solution.py:794
  102.4 69.1 %collective-permute-start.5 = (bf16[320,2560]{1,0:T(8,128)(2,1)S(1)}, bf16[320,2560]{1,0:T(8,128)(2,1)S(1)}, u32[]{:S(2)}, u32[]{:S(2)}) collective-permute-start(bf16[320,2560]{1,0:T(8,128)(2,1)S(1)} %copy-done.2), channel_id=1, source_target_pairs={{0,2},{2,0},{4,6},{6,4},{8,10},{10,8},{12,14},{14,12},{16,18},{18,... | collective-permute-start | bytes 4915208 | tf_op jit(solution)/shard_map/ppermute | solution.py:797
  102.5 69.1 %collective-permute-start.17 = (bf16[320,2560]{1,0:T(8,128)(2,1)}, bf16[320,2560]{1,0:T(8,128)(2,1)}, u32[]{:S(2)}, u32[]{:S(2)}) collective-permute-start(bf16[320,2560]{1,0:T(8,128)(2,1)} %shard_map.364.refs_14_.refs_1_), channel_id=1, source_target_pairs={{0,4},{2,6},{4,0},{6,2},{8,12},{10,14},{12,8},{14,10},{16,20},{18,... | collective-permute-start | bytes 4915208 | tf_op jit(solution)/shard_map/ppermute | solution.py:800
  196.7 48.5 %collective-permute-start.18 = (bf16[320,2560]{1,0:T(8,128)(2,1)}, bf16[320,2560]{1,0:T(8,128)(2,1)}, u32[]{:S(2)}, u32[]{:S(2)}) collective-permute-start(bf16[320,2560]{1,0:T(8,128)(2,1)} %shard_map.364.refs_14_.refs_1_), channel_id=1, source_target_pairs={{0,2},{2,0},{4,6},{6,4},{8,10},{10,8},{12,14},{14,12},{16,18},{18,... | collective-permute-start | bytes 4915208 | tf_op jit(solution)/shard_map/ppermute | solution.py:797
  197.3 52.3 %collective-permute-start.19 = (bf16[320,2560]{1,0:T(8,128)(2,1)}, bf16[320,2560]{1,0:T(8,128)(2,1)}, u32[]{:S(2)}, u32[]{:S(2)}) collective-permute-start(bf16[320,2560]{1,0:T(8,128)(2,1)} %collective-permute-done.17.refs_2_), channel_id=1, source_target_pairs={{0,2},{2,0},{4,6},{6,4},{8,10},{10,8},{12,14},{14,12},{16,18},{18,... | collective-permute-start | bytes 4915208 | tf_op jit(solution)/shard_map/ppermute | solution.py:797
  198.2 51.4 %collective-permute-start.22 = (bf16[320,2560]{1,0:T(8,128)(2,1)}, bf16[320,2560]{1,0:T(8,128)(2,1)}, u32[]{:S(2)}, u32[]{:S(2)}) collective-permute-start(bf16[320,2560]{1,0:T(8,128)(2,1)} %collective-permute-done.20.refs_5_.refs_9_), channel_id=1, source_target_pairs={{0,2},{2,0},{4,6},{6,4},{8,10},{10,8},{12,14},{14,12},{16,18},{18,... | collective-permute-start | bytes 4915208 | tf_op jit(solution)/shard_map/ppermute | solution.py:797
  200.0 49.6 %collective-permute-start.23 = (bf16[320,1280]{1,0:T(8,128)(2,1)}, bf16[320,1280]{1,0:T(8,128)(2,1)S(1)}, u32[]{:S(2)}, u32[]{:S(2)}) collective-permute-start(bf16[320,1280]{1,0:T(8,128)(2,1)} %collective-permute-done.21.refs_6_), channel_id=1, source_target_pairs={{0,2},{2,0},{4,6},{6,4},{8,10},{10,8},{12,14},{14,12},{16,18},{18,... | collective-permute-start | bytes 2457608 | tf_op jit(solution)/shard_map/ppermute | solution.py:797
  200.2 49.4 %collective-permute-start.25 = (bf16[320,1280]{1,0:T(8,128)(2,1)}, bf16[320,1280]{1,0:T(8,128)(2,1)S(1)}, u32[]{:S(2)}, u32[]{:S(2)}) collective-permute-start(bf16[320,1280]{1,0:T(8,128)(2,1)} %collective-permute-done.24.refs_10_), channel_id=1, source_target_pairs={{0,2},{2,0},{4,6},{6,4},{8,10},{10,8},{12,14},{14,12},{16,18},{18,... | collective-permute-start | bytes 2457608 | tf_op jit(solution)/shard_map/ppermute | solution.py:797
  245.2 39.9 %collective-permute-start.29 = (bf16[160,5120]{1,0:T(8,128)(2,1)S(1)}, bf16[160,5120]{1,0:T(8,128)(2,1)S(1)}, u32[]{:S(2)}, u32[]{:S(2)}) collective-permute-start(bf16[160,5120]{1,0:T(8,128)(2,1)S(1)} %maximum_maximum_fusion.refs_1_), channel_id=1, source_target_pairs={{0,24},{2,26},{4,28},{6,30},{8,0},{10,2},{12,4},{14,6},{16,8},{18,... | collective-permute-start | bytes 4915208 | tf_op jit(solution)/shard_map/ppermute | solution.py:803
  278.4 102.4 %collective-permute-start.38 = (bf16[640,5120]{1,0:T(8,128)(2,1)}, bf16[640,5120]{1,0:T(8,128)(2,1)}, u32[]{:S(2)}, u32[]{:S(2)}) collective-permute-start(bf16[640,5120]{1,0:T(8,128)(2,1)} %shard_map.369.refs_11_), channel_id=1, source_target_pairs={{0,2},{2,0},{4,6},{6,4},{8,10},{10,8},{12,14},{14,12},{16,18},{18,... | collective-permute-start | bytes 19660808 | tf_op jit(solution)/shard_map/ppermute | solution.py:797
  285.1 39.0 %collective-permute-start.30 = (bf16[160,5120]{1,0:T(8,128)(2,1)S(1)}, bf16[160,5120]{1,0:T(8,128)(2,1)S(1)}, u32[]{:S(2)}, u32[]{:S(2)}) collective-permute-start(bf16[160,5120]{1,0:T(8,128)(2,1)S(1)} %collective-permute-done.29.refs_2_), channel_id=1, source_target_pairs={{0,24},{2,26},{4,28},{6,30},{8,0},{10,2},{12,4},{14,6},{16,8},{18,... | collective-permute-start | bytes 4915208 | tf_op jit(solution)/shard_map/ppermute | solution.py:803
  324.1 38.1 %collective-permute-start.31 = (bf16[160,5120]{1,0:T(8,128)(2,1)S(1)}, bf16[160,5120]{1,0:T(8,128)(2,1)S(1)}, u32[]{:S(2)}, u32[]{:S(2)}) collective-permute-start(bf16[160,5120]{1,0:T(8,128)(2,1)S(1)} %collective-permute-done.30.refs_3_), channel_id=1, source_target_pairs={{0,24},{2,26},{4,28},{6,30},{8,0},{10,2},{12,4},{14,6},{16,8},{18,... | collective-permute-start | bytes 4915208 | tf_op jit(solution)/shard_map/ppermute | solution.py:803
  328.4 33.8 %collective-permute-start.32 = (bf16[160,5120]{1,0:T(8,128)(2,1)S(1)}, bf16[160,5120]{1,0:T(8,128)(2,1)S(1)}, u32[]{:S(2)}, u32[]{:S(2)}) collective-permute-start(bf16[160,5120]{1,0:T(8,128)(2,1)S(1)} %maximum_maximum_fusion.refs_1_), channel_id=1, source_target_pairs={{0,2},{2,0},{4,6},{6,4},{8,10},{10,8},{12,14},{14,12},{16,18},{18,... | collective-permute-start | bytes 4915208 | tf_op jit(solution)/shard_map/ppermute | solution.py:797
  328.4 33.8 %collective-permute-start.33 = (bf16[160,5120]{1,0:T(8,128)(2,1)S(1)}, bf16[160,5120]{1,0:T(8,128)(2,1)S(1)}, u32[]{:S(2)}, u32[]{:S(2)}) collective-permute-start(bf16[160,5120]{1,0:T(8,128)(2,1)S(1)} %collective-permute-done.29.refs_2_), channel_id=1, source_target_pairs={{0,2},{2,0},{4,6},{6,4},{8,10},{10,8},{12,14},{14,12},{16,18},{18,... | collective-permute-start | bytes 4915208 | tf_op jit(solution)/shard_map/ppermute | solution.py:797
  328.9 33.3 %collective-permute-start.34 = (bf16[160,5120]{1,0:T(8,128)(2,1)S(1)}, bf16[160,5120]{1,0:T(8,128)(2,1)S(1)}, u32[]{:S(2)}, u32[]{:S(2)}) collective-permute-start(bf16[160,5120]{1,0:T(8,128)(2,1)S(1)} %collective-permute-done.30.refs_3_), channel_id=1, source_target_pairs={{0,2},{2,0},{4,6},{6,4},{8,10},{10,8},{12,14},{14,12},{16,18},{18,... | collective-permute-start | bytes 4915208 | tf_op jit(solution)/shard_map/ppermute | solution.py:797
  428.7 43.3 %collective-permute-start.42 = (bf16[320,2560]{1,0:T(8,128)(2,1)S(1)}, bf16[320,2560]{1,0:T(8,128)(2,1)S(1)}, u32[]{:S(2)}, u32[]{:S(2)}) collective-permute-start(bf16[320,2560]{1,0:T(8,128)(2,1)S(1)} %copy-done.43), channel_id=1, source_target_pairs={{0,1},{1,0},{2,3},{3,2},{4,5},{5,4},{6,7},{7,6},{8,9},{9,8},{10,11... | collective-permute-start | bytes 4915208 | tf_op jit(solution)/shard_map/ppermute | solution.py:794
  429.9 42.2 %collective-permute-start.43 = (bf16[320,2560]{1,0:T(8,128)(2,1)S(1)}, bf16[320,2560]{1,0:T(8,128)(2,1)S(1)}, u32[]{:S(2)}, u32[]{:S(2)}) collective-permute-start(bf16[320,2560]{1,0:T(8,128)(2,1)S(1)} %copy-done.107), channel_id=1, source_target_pairs={{0,4},{2,6},{4,0},{6,2},{8,12},{10,14},{12,8},{14,10},{16,20},{18,... | collective-permute-start | bytes 4915208 | tf_op jit(solution)/shard_map/ppermute | solution.py:800
  531.5 62.8 %collective-permute-start.37 = (bf16[288,1280]{1,0:T(8,128)(2,1)}, bf16[288,1280]{1,0:T(8,128)(2,1)}, u32[]{:S(2)}, u32[]{:S(2)}) collective-permute-start(bf16[288,1280]{1,0:T(8,128)(2,1)} %slice.232), channel_id=1, source_target_pairs={{0,1},{1,0},{2,3},{3,2},{4,5},{5,4},{6,7},{7,6},{8,9},{9,8},{10,11... | collective-permute-start | bytes 2211848 | tf_op jit(solution)/shard_map/ppermute | solution.py:794
  591.3 71.8 %collective-permute-start.54 = (bf16[320,2560]{1,0:T(8,128)(2,1)}, bf16[320,2560]{1,0:T(8,128)(2,1)S(1)}, u32[]{:S(2)}, u32[]{:S(2)}) collective-permute-start(bf16[320,2560]{1,0:T(8,128)(2,1)} %get-tuple-element.83.refs_4_), channel_id=1, source_target_pairs={{0,1},{1,0},{2,3},{3,2},{4,5},{5,4},{6,7},{7,6},{8,9},{9,8},{10,11... | collective-permute-start | bytes 4915208 | tf_op jit(solution)/shard_map/ppermute | solution.py:794
  592.2 71.0 %collective-permute-start.55 = (bf16[320,2560]{1,0:T(8,128)(2,1)}, bf16[320,2560]{1,0:T(8,128)(2,1)S(1)}, u32[]{:S(2)}, u32[]{:S(2)}) collective-permute-start(bf16[320,2560]{1,0:T(8,128)(2,1)} %get-tuple-element.92), channel_id=1, source_target_pairs={{0,4},{2,6},{4,0},{6,2},{8,12},{10,14},{12,8},{14,10},{16,20},{18,... | collective-permute-start | bytes 4915208 | tf_op jit(solution)/shard_map/ppermute | solution.py:800
  593.8 38.7 %collective-permute-start.65 = (f32[130,128]{1,0:T(8,128)S(1)}, f32[130,128]{1,0:T(8,128)S(1)}, u32[]{:S(2)}, u32[]{:S(2)}) collective-permute-start(f32[130,128]{1,0:T(8,128)S(1)} %fusion.100), channel_id=1, source_target_pairs={{0,4},{2,6},{4,0},{6,2},{8,12},{10,14},{12,8},{14,10},{16,20},{18,... | collective-permute-start | bytes 199688 | tf_op jit(solution)/shard_map/ppermute | solution.py:901
  595.8 53.6 %collective-permute-start.50 = (bf16[320,1280]{1,0:T(8,128)(2,1)S(1)}, bf16[320,1280]{1,0:T(8,128)(2,1)S(1)}, u32[]{:S(2)}, u32[]{:S(2)}) collective-permute-start(bf16[320,1280]{1,0:T(8,128)(2,1)S(1)} %copy-done.109), channel_id=1, source_target_pairs={{0,4},{2,6},{4,0},{6,2},{8,12},{10,14},{12,8},{14,10},{16,20},{18,... | collective-permute-start | bytes 2457608 | tf_op jit(solution)/shard_map/ppermute | solution.py:800
  597.4 51.9 %collective-permute-start.51 = (bf16[320,1280]{1,0:T(8,128)(2,1)S(1)}, bf16[320,1280]{1,0:T(8,128)(2,1)S(1)}, u32[]{:S(2)}, u32[]{:S(2)}) collective-permute-start(bf16[320,1280]{1,0:T(8,128)(2,1)S(1)} %copy-done.108), channel_id=1, source_target_pairs={{0,1},{1,0},{2,3},{3,2},{4,5},{5,4},{6,7},{7,6},{8,9},{9,8},{10,11... | collective-permute-start | bytes 2457608 | tf_op jit(solution)/shard_map/ppermute | solution.py:794
  654.5 55.5 %collective-permute-start.52 = (bf16[320,2560]{1,0:T(8,128)(2,1)}, bf16[320,2560]{1,0:T(8,128)(2,1)}, u32[]{:S(2)}, u32[]{:S(2)}) collective-permute-start(bf16[320,2560]{1,0:T(8,128)(2,1)} %get-tuple-element.90.refs_4_), channel_id=1, source_target_pairs={{0,1},{1,0},{2,3},{3,2},{4,5},{5,4},{6,7},{7,6},{8,9},{9,8},{10,11... | collective-permute-start | bytes 4915208 | tf_op jit(solution)/shard_map/ppermute | solution.py:794
  655.7 54.4 %collective-permute-start.53 = (bf16[320,2560]{1,0:T(8,128)(2,1)}, bf16[320,2560]{1,0:T(8,128)(2,1)}, u32[]{:S(2)}, u32[]{:S(2)}) collective-permute-start(bf16[320,2560]{1,0:T(8,128)(2,1)} %get-tuple-element.91), channel_id=1, source_target_pairs={{0,4},{2,6},{4,0},{6,2},{8,12},{10,14},{12,8},{14,10},{16,20},{18,... | collective-permute-start | bytes 4915208 | tf_op jit(solution)/shard_map/ppermute | solution.py:800
  659.7 65.6 %collective-permute-start.49 = (bf16[288,1280]{1,0:T(8,128)(2,1)}, bf16[288,1280]{1,0:T(8,128)(2,1)}, u32[]{:S(2)}, u32[]{:S(2)}) collective-permute-start(bf16[288,1280]{1,0:T(8,128)(2,1)} %slice.234), channel_id=1, source_target_pairs={{0,1},{1,0},{2,3},{3,2},{4,5},{5,4},{6,7},{7,6},{8,9},{9,8},{10,11... | collective-permute-start | bytes 2211848 | tf_op jit(solution)/shard_map/ppermute | solution.py:794
  (154 other events, 1895.3 us)

commit v3 on v2

--- a/solution.py
+++ b/solution.py
@@ -69,6 +69,7 @@
 
 
 VMEM_LIMIT = 56 * 1024 * 1024
+COST = int(8 * 1.15e9)
 
 
 class Order:
@@ -79,7 +80,9 @@
 ORDER = Order()
 
 
-def call(kernel, grid, in_specs, out_specs, out_shape, scratch=(), flops=0, moved=0, after=()):
+def call(
+    kernel, grid, in_specs, out_specs, out_shape, scratch=(), us=2.4, after=()
+):
     if ORDER.last is not None:
         after = [*after, ORDER.last]
     count, extra = len(in_specs), len(after)
@@ -97,7 +100,9 @@
         compiler_params=pltpu.CompilerParams(
             dimension_semantics=("arbitrary",) * len(grid), vmem_limit_bytes=VMEM_LIMIT
         ),
-        cost_estimate=pl.CostEstimate(flops=flops, bytes_accessed=moved, transcendentals=0),
+        cost_estimate=pl.CostEstimate(
+            flops=int(COST * us), bytes_accessed=0, transcendentals=0
+        ),
     )
 
     def start(*operands):
@@ -160,10 +165,6 @@
             base += count
             at += len(pieces)
 
-    @property
-    def volume(self):
-        return self.steps * self.block * self.width
-
 
 ROWS = 96
 
@@ -176,7 +177,7 @@
     lax.fori_loop(0, rows // ROWS, step, 0)
 
 
-def times_weight(left, parts, table, ins, in_specs, outs, out_specs, finish, after=()):
+def times_weight(left, parts, table, ins, in_specs, outs, out_specs, finish, us, after=()):
     count = len(parts.arrays)
 
     def kernel(*refs):
@@ -194,13 +195,12 @@
         [whole(left.shape)] + parts.specs + in_specs,
         out_specs,
         outs,
-        flops=2 * left.shape[0] * parts.volume,
-        moved=2 * parts.volume + 6 * left.shape[0] * parts.steps * parts.block,
+        us=us,
         after=after,
     )(left, *parts.arrays, *ins)
 
 
-def times_turned(left, parts, table, ins, in_specs, outs, out_specs, finish, after=()):
+def times_turned(left, parts, table, ins, in_specs, outs, out_specs, finish, us, after=()):
     count = len(parts.arrays)
     rows, width = left.shape[0], parts.width
     column = lookup(table)
@@ -236,8 +236,7 @@
         out_specs,
         outs,
         scratch=[pltpu.VMEM((rows, width), F32)],
-        flops=2 * rows * parts.volume,
-        moved=2 * parts.volume + 2 * left.size + 8 * rows * width,
+        us=us,
         after=after,
     )(left, *parts.arrays, *ins)
 
@@ -259,6 +258,7 @@
         [jax.ShapeDtypeStruct((first_in.shape[0], total_columns), F32)],
         [pl.BlockSpec((first_in.shape[0], block), lambda j: (0, column(j)))],
         finish,
+        14,
         after,
     )[0]
 
@@ -287,6 +287,7 @@
         [jax.ShapeDtypeStruct((rows, width), F32), jax.ShapeDtypeStruct((rows, width), LOW)],
         [whole((rows, width))] * 2,
         finish,
+        9.8,
         after,
     )
 
@@ -317,6 +318,7 @@
         ],
         [spec, spec],
         finish,
+        17.8,
         after,
     )
 
@@ -339,6 +341,7 @@
         [jax.ShapeDtypeStruct((rows, width), LOW)],
         [whole((rows, width))],
         finish,
+        15,
         after,
     )[0]
 
@@ -384,8 +387,7 @@
             jax.ShapeDtypeStruct((1, total_columns), F32),
         ],
         scratch=[pltpu.VMEM((rows, block), F32)],
-        flops=2 * rows * parts.volume,
-        moved=2 * parts.volume + 6 * rows * total_columns,
+        us=19,
         after=after,
     )(down_grad, *parts.arrays, upward)
 
@@ -426,6 +428,7 @@
         ],
         [whole((rows, width)), whole((rows, width)), whole((8, width))],
         finish,
+        21.7,
         after,
     )
 
@@ -445,6 +448,7 @@
         [jax.ShapeDtypeStruct((rows, parts.steps * block), LOW)],
         [pl.BlockSpec((rows, block), lambda j: (0, j))],
         finish,
+        6,
         after,
     )[0]
 
@@ -476,6 +480,7 @@
         [jax.ShapeDtypeStruct((rows, width), LOW), jax.ShapeDtypeStruct((8, width), F32)],
         [whole((rows, width)), whole((8, width))],
         finish,
+        18,
         after,
     )
 
@@ -486,6 +491,7 @@
     low = middle // 2
     steps = len(kind)
     near = steps // 2
+    fourth = near // 2
     count = len(pairs)
 
     def kernel(*refs):
@@ -513,7 +519,7 @@
                         turned[k][...], right, preferred_element_type=F32
                     ).astype(LOW)
                     return
-                came_ref, own0, own1, other0, far_a, far_b = rest[:6]
+                came_ref, own0, to_y, to_x, other_a, own_b = rest[:6]
                 y0 = jnp.dot(turned[k][:low, :], right, preferred_element_type=F32)
                 y0 = (y0 + came_ref[:low, :].astype(F32)).astype(LOW)
                 y1 = jnp.dot(turned[k][low:, :], right, preferred_element_type=F32)
@@ -522,19 +528,23 @@
                 @pl.when(j < near)
                 def _():
                     own0[...] = y0
-                    own1[...] = y1
-
-                @pl.when(j >= near)
+
+                @pl.when(j % near < fourth)
                 def _():
-                    other0[...] = y0
-
-                @pl.when((j >= near) & (j < near + near // 2))
+                    to_y[...] = y1
+
+                @pl.when((j >= fourth) & (j < near))
                 def _():
-                    far_a[...] = y1
-
-                @pl.when(j >= near + near // 2)
+                    own_b[...] = y1
+
+                @pl.when((j >= near) & (j < near + fourth))
                 def _():
-                    far_b[...] = y1
+                    other_a[...] = y0
+
+                @pl.when(j >= near + fourth)
+                def _():
+                    to_x[:low, :] = y0
+                    to_x[low:, :] = y1
 
     right_specs = []
     for k in range(count):
@@ -553,12 +563,15 @@
     if came is None:
         outs = [clipped(0, steps, middle)]
     else:
+        turn_spec = pl.BlockSpec(
+            (low, block), lambda j: (j // near, jnp.clip(j % near, 0, fourth - 1))
+        )
         outs = [
             clipped(0, near, low),
-            clipped(0, near, low),
-            clipped(near, near, low),
-            clipped(near, near // 2, low),
-            clipped(near + near // 2, near // 2, low),
+            (turn_spec, jax.ShapeDtypeStruct((middle, fourth * block), LOW)),
+            clipped(near + fourth, fourth, middle),
+            clipped(near, fourth, low),
+            clipped(fourth, fourth, low),
         ]
     extra = [] if came is None else [came]
     return call(
@@ -570,43 +583,113 @@
         [s for s, _ in outs],
         [s for _, s in outs],
         scratch=[pltpu.VMEM((middle, rows), LOW) for _ in pairs],
-        flops=rows * width * steps * block,
-        moved=2 * (middle + rows) * steps * block,
+        us=10 if came is None else 12,
         after=after,
     )(*[left for left, _ in pairs], *[right for _, right in pairs], *extra)
 
 
-def add_far(other0, own1, far_a, far_b):
-    rows, columns = other0.shape
+def add_second(other_a, own_b, from_y, from_x):
+    rows, columns = other_a.shape
+
+    def kernel(a_ref, b_ref, y_ref, x_ref, to_x, to_y):
+        to_x[...] = (a_ref[...].astype(F32) + y_ref[...].astype(F32)).astype(LOW)
+        to_y[...] = (b_ref[...].astype(F32) + x_ref[...].astype(F32)).astype(LOW)
+
+    shape = jax.ShapeDtypeStruct((rows, columns), LOW)
     block = columns // 2
-
-    def kernel(other_ref, own_ref, a_ref, b_ref, x_ref, y_ref):
-        j = pl.program_id(0)
-
-        @pl.when(j == 0)
-        def _():
-            x_ref[...] = (other_ref[...].astype(F32) + a_ref[...].astype(F32)).astype(LOW)
-            y_ref[...] = own_ref[...]
-
-        @pl.when(j == 1)
-        def _():
-            x_ref[...] = other_ref[...]
-            y_ref[...] = (own_ref[...].astype(F32) + b_ref[...].astype(F32)).astype(LOW)
-
     spec = pl.BlockSpec((rows, block), lambda j: (0, j))
-    shape = jax.ShapeDtypeStruct((rows, columns), LOW)
+    later = pl.BlockSpec((rows, block), lambda j: (1, j))
     return call(
         kernel,
         (2,),
-        [spec, spec, whole(far_a.shape), whole(far_b.shape)],
+        [spec, spec, later, later],
         [spec, spec],
         [shape, shape],
-        flops=2 * rows * columns,
-        moved=10 * rows * columns,
-    )(other0, own1, far_a, far_b)
-
-
-def stack_rows(pieces):
+    )(other_a, own_b, from_y, from_x)
+
+
+def add_ring(own0, from_y, from_x, second_x, second_y, came, place, rows, kind):
+    columns = own0.shape[1]
+    half = columns // 2
+
+    def kernel(*refs):
+        own, y, x, x2, y2 = refs[:5]
+        out = refs[-1]
+        a = own[:, :half].astype(F32) + y[...].astype(F32) + x2[...].astype(F32)
+        b = own[:, half:].astype(F32) + x[...].astype(F32) + y2[...].astype(F32)
+        if came is not None:
+            a = a + refs[5][:, :half].astype(F32)
+            b = b + refs[5][:, half:].astype(F32)
+        out[:, :half] = a.astype(kind)
+        out[:, half:] = b.astype(kind)
+
+    side = pl.BlockSpec((rows, half), lambda j: (place, 0))
+    extra = [] if came is None else [came]
+    return call(
+        kernel,
+        (1,),
+        [pl.BlockSpec((rows, columns), lambda j: (place, 0)), side, side, side, side]
+        + [whole(v.shape) for v in extra],
+        whole((rows, columns)),
+        jax.ShapeDtypeStruct((rows, columns), kind),
+    )(own0, from_y, from_x, second_x, second_y, *extra)
+
+
+def cut_far(side, across):
+    rows, columns = side.shape
+    half = columns // 2
+
+    def kernel(a, b, out_a, out_b):
+        out_a[...] = a[...]
+        out_b[...] = b[...]
+
+    shape = jax.ShapeDtypeStruct((rows, half), side.dtype)
+    return call(
+        kernel,
+        (1,),
+        [
+            pl.BlockSpec((rows, half), lambda j: (0, 0)),
+            pl.BlockSpec((rows, half), lambda j: (0, 1)),
+        ],
+        [whole((rows, half))] * 2,
+        [shape, shape],
+    )(side, across)
+
+
+def hold(values):
+    def kernel(in_ref, out_ref):
+        out_ref[...] = in_ref[...]
+
+    return call(
+        kernel,
+        (1,),
+        [whole(values.shape)],
+        whole(values.shape),
+        jax.ShapeDtypeStruct(values.shape, values.dtype),
+        us=1,
+    )(values)
+
+
+def stack_early(shard, side, across, far, after=()):
+    rows, columns = shard.shape
+
+    def kernel(a, b, c, d, out):
+        out[:rows, :columns] = a[...]
+        out[:rows, columns:] = b[...]
+        out[rows:, :columns] = c[...]
+        out[rows:, columns:] = d[...]
+
+    return call(
+        kernel,
+        (1,),
+        [whole(shard.shape)] * 4,
+        whole((2 * rows, 2 * columns)),
+        jax.ShapeDtypeStruct((2 * rows, 2 * columns), shard.dtype),
+        after=after,
+    )(shard, side, across, far)
+
+
+def stack_rows(pieces, after=()):
     rows, columns = pieces[0].shape
     count = len(pieces)
     block = columns // 2
@@ -621,34 +704,8 @@
         [pl.BlockSpec((rows, block), lambda j: (0, j))] * count,
         pl.BlockSpec((count * rows, block), lambda j: (0, j)),
         jax.ShapeDtypeStruct((count * rows, columns), pieces[0].dtype),
-        moved=4 * count * rows * columns,
+        after=after,
     )(*pieces)
-
-
-def add_cuts(arrays, rows, columns, block_rows, block_columns, kind, after=()):
-    def kernel(*refs):
-        value = refs[0][...].astype(F32)
-        for ref in refs[1:-1]:
-            value = value + ref[...].astype(F32)
-        refs[-1][...] = value.astype(kind)
-
-    specs = [
-        pl.BlockSpec(
-            (block_rows, block_columns),
-            lambda i, j, r=r // block_rows, c=c // block_columns: (r + i, c + j),
-        )
-        for _, r, c in arrays
-    ]
-    return call(
-        kernel,
-        (rows // block_rows, columns // block_columns),
-        specs,
-        pl.BlockSpec((block_rows, block_columns), lambda i, j: (i, j)),
-        jax.ShapeDtypeStruct((rows, columns), kind),
-        flops=rows * columns * len(arrays),
-        moved=2 * rows * columns * (len(arrays) + 1),
-        after=after,
-    )(*[a for a, _, _ in arrays])
 
 
 def turn_pairs(v, heads_lanes):
@@ -713,8 +770,7 @@
             jax.ShapeDtypeStruct((groups, heads, rows), F32),
         ],
         scratch=[pltpu.VMEM((lanes, rows), F32)],
-        flops=4 * rows * rows * lanes * groups * 3,
-        moved=6 * rows * columns,
+        us=19.6,
         after=after,
     )(mixed, cosine, sine, key_code, query_code)
 
@@ -781,8 +837,7 @@
             pltpu.VMEM((rows, lanes), F32),
             pltpu.VMEM((rows, lanes), F32),
         ],
-        flops=10 * rows * rows * lanes * groups * 3,
-        moved=6 * rows * columns,
+        us=27.3,
         after=after,
     )(qkv, lse, attn_grad, cosine, sine, key_code, query_code)
 class Lanes:
@@ -821,31 +876,27 @@
             held.append(self.down_z(held[-1]))
         return held
 
-    def gather_z(self, shard):
-        return stack_rows(self.ring_down(shard))
-
-    def gather_xy(self, held):
-        middle = held.shape[1] // 2
+    def corners(self, held):
         side, across = self.over_x(held), self.over_y(held)
-        far_a, far_b = self.over_y(side[:, :middle]), self.over_x(across[:, middle:])
+        return side, across, *self.far(side, across)
+
+    def far(self, side, across):
+        a, b = cut_far(side, across)
+        return self.over_y(a), self.over_x(b)
+
+    def gathered(self, held, corners):
+        side, across, far_a, far_b = corners
         core = self.over_core
-        own = [held, across, core(held), core(across)]
         side_core = core(side)
-        other_a = [side, far_a, side_core, core(far_a)]
-        other_b = [side, far_b, side_core, core(far_b)]
-        return Gathered(own, other_a, other_b)
-
-    def gather_early(self, shard):
-        side, across = self.over_x(shard), self.over_y(shard)
-        far = self.over_y(side)
-        return jnp.concatenate(
-            [jnp.concatenate([shard, side], 1), jnp.concatenate([across, far], 1)], 0
+        return Gathered(
+            [held, across, core(held), core(across)],
+            [side, far_a, side_core, core(far_a)],
+            [side, far_b, side_core, core(far_b)],
         )
 
-    def gather_late(self, both):
-        held = self.ring_down(both)
+    def stacked(self, held):
+        rows = held[0].shape[0] // 2
         held = held + [self.over_core(v) for v in held]
-        rows = both.shape[0] // 2
         cuts = [
             (dc * self.ring + dz, dy * rows, rows)
             for dc in range(2)
@@ -853,10 +904,6 @@
             for dz in range(self.ring)
         ]
         return Stacked(held, cuts)
-
-    def reduce_xy(self, kept):
-        own0, own1, other0, far_a, far_b = kept
-        return self.over_y(far_a), self.over_x(far_b)
 
 
 class Gathered:
@@ -944,11 +991,19 @@
     shard_2 = fc1_weight.astype(LOW)
     shard_3 = fc2_weight.astype(LOW).T
     if relative:
-        early_3 = lanes.gather_early(shard_3)
-        held_1 = lanes.gather_z(shard_1)
-        held_2 = lanes.gather_z(shard_2)
-        w1, w2 = lanes.gather_xy(held_1), lanes.gather_xy(held_2)
-        w3 = lanes.gather_late(early_3)
+        ring_1 = lanes.ring_down(shard_1)
+        side_3, across_3 = lanes.over_x(shard_3), lanes.over_y(shard_3)
+        far_3 = lanes.over_y(side_3)
+        late_3 = [stack_early(shard_3, side_3, across_3, far_3, after=[ring_1[2]])]
+        held_1 = stack_rows(ring_1)
+        corners_1 = lanes.corners(held_1)
+        w1 = lanes.gathered(held_1, corners_1)
+        for _ in range(3):
+            late_3.append(lanes.down_z(late_3[-1]))
+        ring_2 = lanes.ring_down(shard_2)
+        held_2 = stack_rows(ring_2, after=[corners_1[2], corners_1[3], late_3[1]])
+        sides_up = lanes.over_x(held_2), lanes.over_y(held_2)
+        w3 = lanes.stacked(late_3)
         w_down = w3.parts(hidden // 2)
     else:
 
@@ -958,10 +1013,10 @@
             return Gathered([held], [side], [side])
 
         w1, w2, w3 = plain(shard_1), plain(shard_2), plain(shard_3)
+        w_up = w2.parts(hidden // 2, [(0, 2), (0, 1), (0, 1)])
         w_down = w3.parts(hidden // 2, [(0, 2), (0, 1), (0, 1)])
     w_qkv = w1.parts(lane_columns, [(0, 3), (0, 2), (0, 1)])
     w_proj = w1.parts(lane_columns, [(3, 1), (0, 0), (1, 1)])
-    w_up = w2.parts(hidden // 2, [(0, 2), (0, 1), (0, 1)])
 
     def own_row(both):
         mine = lax.dynamic_index_in_dim(both[:, 0], slot, 0, keepdims=False)
@@ -1028,22 +1083,19 @@
         (sent,) = grad_kernel(pairs, block, kind, 1, None)
         return lanes.over_core(sent) if relative else sent
 
-    def keep_grads(pairs, block, kind, came):
-        return grad_kernel(pairs, block, kind, 0, came)
-
-    def send_far(kept):
-        return lanes.over_y(kept[3]), lanes.over_x(kept[4])
-
-    def send_sides(kept, far):
-        to_x, to_y = add_far(kept[2], kept[1], *far)
-        return lanes.over_x(to_x), lanes.over_y(to_y)
+    def keep_grads(pairs, block, kind, came, after=()):
+        return grad_kernel(pairs, block, kind, 0, came, after)
+
+    def send_first(kept):
+        return lanes.over_y(kept[1]), lanes.over_x(kept[2])
+
+    def send_second(kept, first):
+        to_x, to_y = add_second(kept[3], kept[4], *first)
+        return (*first, lanes.over_x(to_x), lanes.over_y(to_y))
 
     def ring_step(kept, sides, came, place):
-        arrays = [(v, place * rows_own, 0) for v in (kept[0], *sides)]
-        if came is not None:
-            arrays.append((came, 0, 0))
         kind = LOW if place else F32
-        total = add_cuts(arrays, rows_own, hidden, rows_own, hidden, kind)
+        total = add_ring(kept[0], *sides, came, place, rows_own, kind)
         return lanes.up_z(total) if place else total
 
     def plain_grads(pairs, block, kind):
@@ -1062,51 +1114,61 @@
     down_grad = (cot_low.astype(F32) * token_weight).astype(LOW)
     mixed = qkv_forward(first_in, w_qkv, bias_qkv, list(range(6)))
     qkv, attended, lse = attention_forward(mixed, cosine, sine, key_code, query_code, groups)
-    hidden1, second_in = proj_forward(attended, w_proj, row_low, vec)
+    before_proj = []
+    if relative:
+        corners_2 = (*sides_up, *lanes.far(*sides_up))
+        before_proj = [late_3[2]]
+    hidden1, second_in = proj_forward(attended, w_proj, row_low, vec, after=before_proj)
+    if relative:
+        w_up = lanes.gathered(held_2, corners_2).parts(
+            hidden // 2, [(0, 2), (0, 1), (0, 1)]
+        )
     upward, activated = up_forward(second_in, w_up, bias_up)
     pair_3 = [(down_grad, activated)]
     half = hidden // 2
     if relative:
         came_3 = send_grads(pair_3, half, wide_kind)
     result = down_forward(activated, w_down, hidden1, vec)
+    block_output = give_back(result)
 
     if relative:
         kept_3 = keep_grads(pair_3, half, wide_kind, came_3)
-        far_3 = send_far(kept_3)
+        first_3 = send_first(kept_3)
     up_grad, sum_up = down_backward(down_grad, w_down, upward)
     pair_2 = [(second_in, up_grad)]
     if relative:
-        sides_3 = send_sides(kept_3, far_3)
+        sides_3 = send_second(kept_3, first_3)
         came_2 = send_grads(pair_2, half, wide_kind)
     hidden1_grad, branch_grad, sums_2 = up_backward(
         up_grad, w_up, hidden1, cot_low, token_weight, vec
     )
     if relative:
-        kept_2 = keep_grads(pair_2, half, wide_kind, came_2)
-        far_2 = send_far(kept_2)
+        kept_2 = keep_grads(pair_2, half, wide_kind, came_2, after=[block_output])
+        first_2 = send_first(kept_2)
+        ring_3 = ring_step(kept_3, sides_3, None, 3)
     attn_grad = proj_backward(branch_grad, w_proj)
     if relative:
-        ring_3 = ring_step(kept_3, sides_3, None, 3)
+        ring_3 = ring_step(kept_3, sides_3, ring_3, 2)
     mixed_grad, sum_qkv = attention_backward(
         qkv, lse, attn_grad, cosine, sine, key_code, query_code, groups
     )
     pair_1 = [(first_in, mixed_grad), (branch_grad, attended)]
     if relative:
-        ring_3 = ring_step(kept_3, sides_3, ring_3, 2)
-        sides_2 = send_sides(kept_2, far_2)
+        sides_2 = send_second(kept_2, first_2)
+        ring_3 = ring_step(kept_3, sides_3, ring_3, 1)
         came_1 = send_grads(pair_1, lane_columns, first_kind)
-        ring_3 = ring_step(kept_3, sides_3, ring_3, 1)
+        ring_2 = ring_step(kept_2, sides_2, None, 3)
         kept_1 = keep_grads(pair_1, lane_columns, first_kind, came_1)
-        far_1 = send_far(kept_1)
+        first_1 = send_first(kept_1)
+        ring_2 = ring_step(kept_2, sides_2, ring_2, 2)
+        grad_3 = ring_step(kept_3, sides_3, ring_3, 0)
     input_low, sums_1 = qkv_backward(
         mixed_grad, w_qkv, list(range(6)), row_low, hidden1_grad, vec
     )
     if relative:
-        sides_1 = send_sides(kept_1, far_1)
-        grad_3 = ring_step(kept_3, sides_3, ring_3, 0)
-        ring_2 = ring_step(kept_2, sides_2, None, 3)
-        ring_2 = ring_step(kept_2, sides_2, ring_2, 2)
         ring_2 = ring_step(kept_2, sides_2, ring_2, 1)
+        sides_1 = send_second(kept_1, first_1)
+        sums_1 = hold(sums_1)
         grad_2 = ring_step(kept_2, sides_2, ring_2, 0)
         ring_1 = ring_step(kept_1, sides_1, None, 3)
         ring_1 = ring_step(kept_1, sides_1, ring_1, 2)
@@ -1116,7 +1178,6 @@
         grad_3 = plain_grads(pair_3, half, wide_kind)
         grad_2 = plain_grads(pair_2, half, wide_kind)
         grad_1 = plain_grads(pair_1, lane_columns, first_kind)
-    block_output = give_back(result)
     input_grad = give_back(input_low)
 
     grad_qkv = grad_1[:, : 3 * lane_columns].reshape(rows_own, 3, lane_columns)

time: 811 us -> 699 us (0.86)
  waiting for transfers between devices: 301 us -> 207 us
  local copies, waits for them, and re-layouts: 60.7 us -> 40.9 us
    ppermute x9, waiting for transfers between devices: 98.5 us -> 52.3 us  [down_z(): lax.ppermute(v, 'dp', [(i, (i - 4) % self.dp) for i in range(self.dp)])]
    ppermute x9, waiting for transfers between devices: 57.3 us -> 29.8 us  [up_z(): lax.ppermute(v, 'dp', [(i, (i + 4) % self.dp) for i in range(self.dp)])]
    ppermute x8, waiting for transfers between devices: 43 us -> 26.2 us  [butterfly(): value = value + lax.ppermute(value, 'dp', [(i, i ^ bit) for i in range(dp)])]
    ppermute x12, waiting for transfers between devices: 43.1 us -> 26.9 us  [over_y(): return lax.ppermute(v, 'dp', [(i, i ^ 2) for i in range(self.dp)])]
    unnamed x231 -> x215, local copies, waits for them, and re-layouts: 27.9 us -> 16.4 us
    ppermute x16, waiting for transfers between devices: 55.3 us -> 66 us  [over_x(): return lax.ppermute(v, 'tensor', [(0, 1), (1, 0)])]
    pallas_call x33 -> x37, Pallas kernels: 284 us -> 292 us  [start(): result = run(*operands, *after)]
  transfers between devices with their start and end apart: 73 -> 73, of which waited for: 31 -> 29; matrix products, arithmetic and copies ran while one was open for 9% -> 10% of each run, Pallas kernels for 29% -> 35%
where the time goes in v3:
time: 699 us; the launch traced here: 689 us
  Pallas kernels  292 us (42%)
  waiting for transfers between devices  207 us (30%)
  starting transfers between devices  75.2 us (11%)
  other arithmetic  42.7 us (6%)
  local copies, waits for them, and re-layouts  40.9 us (6%)
  matrix products  20.3 us (3%)
  between operations  10.6 us (2%)
    pallas_call x37, Pallas kernels, start(): result = run(*operands, *after)  292 us
    ppermute x16, waiting for transfers between devices, over_x(): return lax.ppermute(v, 'tensor', [(0, 1), (1, 0)])  66 us
    ppermute x9, waiting for transfers between devices, down_z(): lax.ppermute(v, 'dp', [(i, (i - 4) % self.dp) for i in range(self.dp)])  52.3 us
    ppermute x9, starting transfers between devices, down_z(): lax.ppermute(v, 'dp', [(i, (i - 4) % self.dp) for i in range(self.dp)])  30.6 us
    ppermute x9, waiting for transfers between devices, up_z(): lax.ppermute(v, 'dp', [(i, (i + 4) % self.dp) for i in range(self.dp)])  29.8 us
    ppermute x12, waiting for transfers between devices, over_y(): return lax.ppermute(v, 'dp', [(i, i ^ 2) for i in range(self.dp)])  26.9 us
    ppermute x8, waiting for transfers between devices, butterfly(): value = value + lax.ppermute(value, 'dp', [(i, i ^ bit) for i in range(dp)])  26.2 us
    ppermute x16, starting transfers between devices, over_x(): return lax.ppermute(v, 'tensor', [(0, 1), (1, 0)])  16.9 us
  transfers between devices with their start and end apart: 73, of which 29 were waited for; matrix products, arithmetic and copies ran while one was open for 10% of the time, Pallas kernels for 35%

profile of v3, /device:TPU:0, one launch (start us, length us, event | category | flops | bytes accessed | tf_op | source)
XLA Modules:
  0.0 689.5 jit_solution(15769572611813944220)
XLA Ops:
  14.8 8.2 %collective-permute-done.1.refs_1_ = bf16[80,2560]{1,0:T(8,128)(2,1)} collective-permute-done((bf16[80,2560]{1,0:T(8,128)(2,1)S(1)}, bf16[80,2560]{1,0:T(8,128)(2,1)}, u32[]{:S(2)}, u32[]{:S(2)}) %collective-permute-start.1) | collective-permute-done | bytes 409632 | tf_op jit(solution)/shard_map/ppermute | solution.py:858
  31.5 7.2 %collective-permute-done.2.refs_4_.refs_2_ = bf16[80,2560]{1,0:T(8,128)(2,1)S(1)} collective-permute-done((bf16[80,2560]{1,0:T(8,128)(2,1)}, bf16[80,2560]{1,0:T(8,128)(2,1)S(1)}, u32[]{:S(2)}, u32[]{:S(2)}) %collective-permute-start.2) | collective-permute-done | bytes 409632 | tf_op jit(solution)/shard_map/ppermute | solution.py:858
  71.1 17.1 %collective-permute-done.10.refs_0_.refs_5_.refs_9_ = bf16[320,2560]{1,0:T(8,128)(2,1)} collective-permute-done((bf16[320,2560]{1,0:T(8,128)(2,1)}, bf16[320,2560]{1,0:T(8,128)(2,1)}, u32[]{:S(2)}, u32[]{:S(2)}) %collective-permute-start.10) | collective-permute-done | bytes 1638432 | tf_op jit(solution)/shard_map/ppermute | solution.py:849
  99.7 17.5 %collective-permute-done.19.refs_3_ = bf16[80,2560]{1,0:T(8,128)(2,1)} collective-permute-done((bf16[80,2560]{1,0:T(8,128)(2,1)S(1)}, bf16[80,2560]{1,0:T(8,128)(2,1)}, u32[]{:S(2)}, u32[]{:S(2)}) %collective-permute-start.19) | collective-permute-done | bytes 409632 | tf_op jit(solution)/shard_map/ppermute | solution.py:858
  133.7 13.8 %shard_map.367.refs_0_.refs_5_ = f32[576,3840]{1,0:T(8,128)} custom-call(bf16[576,1280]{1,0:T(8,128)(2,1)} %fusion.21.refs_0_, bf16[320,2560]{1,0:T(8,128)(2,1)} %shard_map.364.refs_2_.refs_1_, bf16[320,2560]{1,0:T(8,128)(2,1)} %collective-permute-done.7.refs_1_.refs_2_, bf16[320,2560]{1,0:T(8,128)(2,1)} %copy-done.76, bf16[320,2560]{1,0:T(8,128)(2,1)} %copy-done.78, ...), custom_call_target="tpu_custom_call" | custom-call | flops 128799997952 | tf_op jit(solution)/shard_map/pallas_call | solution.py:109
  147.5 19.7 %shard_map.368 = (bf16[576,3840]{1,0:T(8,128)(2,1)}, bf16[576,1280]{1,0:T(8,128)(2,1)}, f32[2,8,576]{2,1,0:T(8,128)}) custom-call(f32[576,3840]{1,0:T(8,128)} %shard_map.367.refs_0_.refs_5_, f32[576,640]{1,0:T(8,128)} %copy.79.refs_1_.refs_3_, f32[576,640]{1,0:T(8,128)} %copy.80.refs_2_.refs_4_, s32[576,1]{1,0:T(8,128)} %broadcast_in_dim.46.refs_3_.refs_5_, ...), custom_call_target="tpu_custom_call" | custom-call | flops 180319993856 | tf_op jit(solution)/shard_map/pallas_call | solution.py:109
  167.2 7.4 %collective-permute-done.22.refs_0_.refs_5_.refs_9_ = bf16[320,2560]{1,0:T(8,128)(2,1)} collective-permute-done((bf16[320,2560]{1,0:T(8,128)(2,1)}, bf16[320,2560]{1,0:T(8,128)(2,1)}, u32[]{:S(2)}, u32[]{:S(2)}) %collective-permute-start.22) | collective-permute-done | bytes 1638432 | tf_op jit(solution)/shard_map/ppermute | solution.py:849
  180.3 5.0 multiply_convert_fusion
  190.2 6.8 collective-permute-done.26.refs_6_
  198.3 9.8 %shard_map.370 = (f32[576,1280]{1,0:T(8,128)}, bf16[576,1280]{1,0:T(8,128)(2,1)}) custom-call(bf16[576,1280]{1,0:T(8,128)(2,1)} %get-tuple-element.66.refs_0_.refs_3_, bf16[320,2560]{1,0:T(8,128)(2,1)} %shard_map.364.refs_2_.refs_1_, bf16[320,2560]{1,0:T(8,128)(2,1)} %collective-permute-done.7.refs_1_.refs_2_, bf16[320,2560]{1,0:T(8,128)(2,1)} %copy-done.76, ...), custom_call_target="tpu_custom_call" | custom-call | flops 90159996928 | tf_op jit(solution)/shard_map/pallas_call | solution.py:109
  208.0 15.9 %collective-permute-done.31.refs_4_ = bf16[160,5120]{1,0:T(8,128)(2,1)} collective-permute-done((bf16[160,5120]{1,0:T(8,128)(2,1)}, bf16[160,5120]{1,0:T(8,128)(2,1)}, u32[]{:S(2)}, u32[]{:S(2)}) %collective-permute-start.31) | collective-permute-done | bytes 1638432 | tf_op jit(solution)/shard_map/ppermute | solution.py:858
  226.5 17.7 %shard_map.371 = (f32[576,5120]{1,0:T(8,128)}, bf16[576,5120]{1,0:T(8,128)(2,1)}) custom-call(bf16[576,1280]{1,0:T(8,128)(2,1)} %get-tuple-element.69.refs_0_, bf16[320,2560]{1,0:T(8,128)(2,1)} %shard_map.366.refs_14_.refs_1_, bf16[320,2560]{1,0:T(8,128)(2,1)} %collective-permute-done.23.refs_1_.refs_2_, bf16[320,2560]{1,0:T(8,128)(2,1)} %collective-permute-done.24.refs_3_, ...), custom_call_target="tpu_custom_call" | custom-call | flops 163759996928 | tf_op jit(solution)/shard_map/pallas_call | solution.py:109
  244.2 9.9 %shard_map.372.refs_11_ = bf16[640,5120]{1,0:T(8,128)(2,1)} custom-call(bf16[576,1280]{1,0:T(8,128)(2,1)} %get-tuple-element.270.refs_0_, bf16[576,5120]{1,0:T(8,128)(2,1)} %get-tuple-element.72.refs_1_.refs_0_, f32[576,5120]{1,0:T(8,128)} %get-tuple-element.73.refs_2_.refs_9_), custom_call_target="tpu_custom_call" | custom-call | flops 92000002048 | tf_op jit(solution)/shard_map/pallas_call | solution.py:109
  254.3 15.0 %shard_map.373.refs_3_ = bf16[576,1280]{1,0:T(8,128)(2,1)} custom-call(bf16[576,5120]{1,0:T(8,128)(2,1)} %get-tuple-element.72.refs_1_.refs_0_, bf16[160,5120]{1,0:T(8,128)(2,1)} %shard_map.363.refs_4_.refs_1_, bf16[160,5120]{1,0:T(8,128)(2,1)} %collective-permute-done.20.refs_6_.refs_2_, bf16[160,5120]{1,0:T(8,128)(2,1)} %collective-permute-done.21.refs_11_.refs_3_, ...), custom_call_target="tpu_custom_call" | custom-call | flops 138000007168 | tf_op jit(solution)/shard_map/pallas_call | solution.py:109
  275.4 16.3 %collective-permute-done.37 = bf16[288,1280]{1,0:T(8,128)(2,1)S(1)} collective-permute-done((bf16[288,1280]{1,0:T(8,128)(2,1)S(1)}, bf16[288,1280]{1,0:T(8,128)(2,1)S(1)}, u32[]{:S(2)}, u32[]{:S(2)}) %collective-permute-start.37) | collective-permute-done | bytes 737312 | tf_op jit(solution)/shard_map/ppermute | solution.py:849
  293.0 12.2 %shard_map.374 = (bf16[320,2560]{1,0:T(8,128)(2,1)}, bf16[640,1280]{1,0:T(8,128)(2,1)}, bf16[640,1280]{1,0:T(8,128)(2,1)}, bf16[320,1280]{1,0:T(8,128)(2,1)}, bf16[320,1280]{1,0:T(8,128)(2,1)}) custom-call(bf16[576,1280]{1,0:T(8,128)(2,1)} %get-tuple-element.270.refs_0_, bf16[576,5120]{1,0:T(8,128)(2,1)} %get-tuple-element.72.refs_1_.refs_0_, ...), custom_call_target="tpu_custom_call" | custom-call | flops 110399995904 | tf_op jit(solution)/shard_map/pallas_call | solution.py:109
  307.2 18.7 %shard_map.375 = (bf16[576,5120]{1,0:T(8,128)(2,1)}, f32[1,5120]{1,0:T(1,128)}) custom-call(bf16[576,1280]{1,0:T(8,128)(2,1)} %get-tuple-element.270.refs_0_, bf16[160,5120]{1,0:T(8,128)(2,1)} %shard_map.363.refs_4_.refs_1_, bf16[160,5120]{1,0:T(8,128)(2,1)} %collective-permute-done.20.refs_6_.refs_2_, ...), custom_call_target="tpu_custom_call" | custom-call | flops 174799994880 | tf_op jit(solution)/shard_map/pallas_call | solution.py:109
  325.9 16.8 %collective-permute-done.39.refs_2_.refs_1_ = bf16[640,1280]{1,0:T(8,128)(2,1)} collective-permute-done((bf16[640,1280]{1,0:T(8,128)(2,1)}, bf16[640,1280]{1,0:T(8,128)(2,1)}, u32[]{:S(2)}, u32[]{:S(2)}) %collective-permute-start.39) | collective-permute-done | bytes 1638432 | tf_op jit(solution)/shard_map/ppermute | solution.py:855
  345.9 9.8 %shard_map.377.refs_17_ = bf16[640,5120]{1,0:T(8,128)(2,1)} custom-call(bf16[576,1280]{1,0:T(8,128)(2,1)} %get-tuple-element.69.refs_0_, bf16[576,5120]{1,0:T(8,128)(2,1)} %get-tuple-element.76.refs_4_.refs_1_.refs_0_, bf16[320,1280]{1,0:T(8,128)(2,1)} %get-tuple-element.81.refs_2_), custom_call_target="tpu_custom_call" | custom-call | flops 92000002048 | tf_op jit(solution)/shard_map/pallas_call | solution.py:109
  358.7 21.9 %shard_map.378 = (f32[576,1280]{1,0:T(8,128)}, bf16[576,1280]{1,0:T(8,128)(2,1)}, f32[8,1280]{1,0:T(8,128)}) custom-call(bf16[576,5120]{1,0:T(8,128)(2,1)} %get-tuple-element.76.refs_4_.refs_1_.refs_0_, bf16[320,2560]{1,0:T(8,128)(2,1)} %shard_map.366.refs_14_.refs_1_, bf16[320,2560]{1,0:T(8,128)(2,1)} %collective-permute-done.23.refs_1_.refs_2_, ...), custom_call_target="tpu_custom_call" | custom-call | flops 199640006656 | tf_op jit(solution)/shard_map/pallas_call | solution.py:109
  380.6 12.1 %shard_map.379 = (bf16[320,2560]{1,0:T(8,128)(2,1)}, bf16[640,1280]{1,0:T(8,128)(2,1)}, bf16[640,1280]{1,0:T(8,128)(2,1)}, bf16[320,1280]{1,0:T(8,128)(2,1)}, bf16[320,1280]{1,0:T(8,128)(2,1)}) custom-call(bf16[576,1280]{1,0:T(8,128)(2,1)} %get-tuple-element.69.refs_0_, bf16[576,5120]{1,0:T(8,128)(2,1)} %get-tuple-element.76.refs_4_.refs_1_.refs_0_, ...), custom_call_target="tpu_custom_call" | custom-call | flops 110399995904 | tf_op jit(solution)/shard_map/pallas_call | solution.py:109
  396.0 6.0 shard_map.381.refs_6_.refs_2_
  402.0 7.3 %collective-permute-done.44.refs_5_ = bf16[80,2560]{1,0:T(8,128)(2,1)S(1)} collective-permute-done((bf16[80,2560]{1,0:T(8,128)(2,1)}, bf16[80,2560]{1,0:T(8,128)(2,1)S(1)}, u32[]{:S(2)}, u32[]{:S(2)}) %collective-permute-start.44) | collective-permute-done | bytes 409632 | tf_op jit(solution)/shard_map/ppermute | solution.py:861
  412.4 27.4 %shard_map.383 = (bf16[576,3840]{1,0:T(8,128)(2,1)}, f32[1,3840]{1,0:T(1,128)}) custom-call(bf16[576,3840]{1,0:T(8,128)(2,1)} %get-tuple-element.67.refs_2_.refs_0_, f32[2,8,576]{2,1,0:T(8,128)} %get-tuple-element.74.refs_1_, bf16[576,1280]{1,0:T(8,128)(2,1)} %shard_map.381.refs_6_.refs_2_, f32[576,640]{1,0:T(8,128)} %copy.79.refs_1_.refs_3_, ...), custom_call_target="tpu_custom_call" | custom-call | flops 251160002560 | tf_op jit(solution)/shard_map/pallas_call | solution.py:109
  445.4 12.7 %shard_map.386.refs_5_ = bf16[640,5120]{1,0:T(8,128)(2,1)} custom-call(bf16[576,1280]{1,0:T(8,128)(2,1)} %fusion.21.refs_0_, bf16[576,1280]{1,0:T(8,128)(2,1)} %get-tuple-element.82.refs_0_.refs_1_, bf16[576,3840]{1,0:T(8,128)(2,1)} %get-tuple-element.86.refs_4_.refs_2_.refs_0_, bf16[576,1280]{1,0:T(8,128)(2,1)} %get-tuple-element.66.refs_0_.refs_3_, ...), custom_call_target="tpu_custom_call" | custom-call | flops 92000002048 | tf_op jit(solution)/shard_map/pallas_call | solution.py:109
  464.8 16.5 %collective-permute-done.49.refs_3_ = bf16[320,1280]{1,0:T(8,128)(2,1)S(1)} collective-permute-done((bf16[320,1280]{1,0:T(8,128)(2,1)S(1)}, bf16[320,1280]{1,0:T(8,128)(2,1)S(1)}, u32[]{:S(2)}, u32[]{:S(2)}) %collective-permute-start.49) | collective-permute-done | bytes 819232 | tf_op jit(solution)/shard_map/ppermute | solution.py:849
  485.8 14.8 %shard_map.388 = (bf16[320,2560]{1,0:T(8,128)(2,1)}, bf16[640,1280]{1,0:T(8,128)(2,1)}, bf16[640,1280]{1,0:T(8,128)(2,1)}, bf16[320,1280]{1,0:T(8,128)(2,1)}, bf16[320,1280]{1,0:T(8,128)(2,1)}) custom-call(bf16[576,1280]{1,0:T(8,128)(2,1)} %fusion.21.refs_0_, bf16[576,1280]{1,0:T(8,128)(2,1)} %get-tuple-element.82.refs_0_.refs_1_, ...), custom_call_target="tpu_custom_call" | custom-call | flops 110399995904 | tf_op jit(solution)/shard_map/pallas_call | solution.py:109
  510.0 18.4 %shard_map.391 = (bf16[576,1280]{1,0:T(8,128)(2,1)}, f32[8,1280]{1,0:T(8,128)}) custom-call(bf16[576,3840]{1,0:T(8,128)(2,1)} %get-tuple-element.86.refs_4_.refs_2_.refs_0_, bf16[320,2560]{1,0:T(8,128)(2,1)} %shard_map.364.refs_2_.refs_1_, bf16[320,2560]{1,0:T(8,128)(2,1)} %collective-permute-done.7.refs_1_.refs_2_, bf16[320,2560]{1,0:T(8,128)(2,1)} %copy-done.76, ...), custom_call_target="tpu_custom_call" | custom-call | flops 165600002048 | tf_op jit(solution)/shard_map/pallas_call | solution.py:109
  568.0 16.6 %collective-permute-done.65 = f32[130,128]{1,0:T(8,128)S(1)} collective-permute-done((f32[130,128]{1,0:T(8,128)S(1)}, f32[130,128]{1,0:T(8,128)S(1)}, u32[]{:S(2)}, u32[]{:S(2)}) %collective-permute-start.65) | collective-permute-done | bytes 66592 | tf_op jit(solution)/shard_map/ppermute | solution.py:948
  602.6 8.8 %collective-permute-done.60.refs_5_ = bf16[80,2560]{1,0:T(8,128)(2,1)S(1)} collective-permute-done((bf16[80,2560]{1,0:T(8,128)(2,1)}, bf16[80,2560]{1,0:T(8,128)(2,1)S(1)}, u32[]{:S(2)}, u32[]{:S(2)}) %collective-permute-start.60) | collective-permute-done | bytes 409632 | tf_op jit(solution)/shard_map/ppermute | solution.py:861
  628.7 9.3 %collective-permute-done.62.refs_5_ = bf16[80,2560]{1,0:T(8,128)(2,1)S(1)} collective-permute-done((bf16[80,2560]{1,0:T(8,128)(2,1)}, bf16[80,2560]{1,0:T(8,128)(2,1)S(1)}, u32[]{:S(2)}, u32[]{:S(2)}) %collective-permute-start.62) | collective-permute-done | bytes 409632 | tf_op jit(solution)/shard_map/ppermute | solution.py:861
  651.5 5.2 stack.211
  (487 shorter events, 257.1 us)
Async XLA Ops:
  7.9 59.7 %collective-permute-start = (bf16[288,1280]{1,0:T(8,128)(2,1)S(1)}, bf16[288,1280]{1,0:T(8,128)(2,1)}, u32[]{:S(2)}, u32[]{:S(2)}) collective-permute-start(bf16[288,1280]{1,0:T(8,128)(2,1)S(1)} %get-tuple-element.220), channel_id=1, source_target_pairs={{0,1},{1,0},{2,3},{3,2},{4,5},{5,4},{6,7},{7,6},{8,9},{9,8},{10,11... | collective-permute-start | bytes 2211848 | tf_op jit(solution)/shard_map/ppermute | solution.py:849
  13.9 49.4 %collective-permute-start.17 = (bf16[80,2560]{1,0:T(8,128)(2,1)}, bf16[80,2560]{1,0:T(8,128)(2,1)}, u32[]{:S(2)}, u32[]{:S(2)}) collective-permute-start(bf16[80,2560]{1,0:T(8,128)(2,1)} %convert_element_type.76.refs_0_), channel_id=1, source_target_pairs={{0,24},{2,26},{4,28},{6,30},{8,0},{10,2},{12,4},{14,6},{16,8},{18,... | collective-permute-start | bytes 1228808 | tf_op jit(solution)/shard_map/ppermute | solution.py:858
  30.0 32.8 %collective-permute-start.16 = (f32[4480]{0:T(1024)S(1)}, f32[4480]{0:T(1024)S(1)}, u32[]{:S(2)}, u32[]{:S(2)}) collective-permute-start(f32[4480]{0:T(1024)S(1)} %pad_maximum_fusion.7), channel_id=1, source_target_pairs={{0,1},{1,0},{2,3},{3,2},{4,5},{5,4},{6,7},{7,6},{8,9},{9,8},{10,11... | collective-permute-start | bytes 53768 | tf_op jit(solution)/shard_map/ppermute | solution.py:849
  53.0 35.2 %collective-permute-start.10 = (bf16[320,2560]{1,0:T(8,128)(2,1)}, bf16[320,2560]{1,0:T(8,128)(2,1)}, u32[]{:S(2)}, u32[]{:S(2)}) collective-permute-start(bf16[320,2560]{1,0:T(8,128)(2,1)} %shard_map.364.refs_2_.refs_1_), channel_id=1, source_target_pairs={{0,1},{1,0},{2,3},{3,2},{4,5},{5,4},{6,7},{7,6},{8,9},{9,8},{10,11... | collective-permute-start | bytes 4915208 | tf_op jit(solution)/shard_map/ppermute | solution.py:849
  54.5 34.9 %collective-permute-start.7 = (bf16[320,2560]{1,0:T(8,128)(2,1)}, bf16[320,2560]{1,0:T(8,128)(2,1)}, u32[]{:S(2)}, u32[]{:S(2)}) collective-permute-start(bf16[320,2560]{1,0:T(8,128)(2,1)} %shard_map.364.refs_2_.refs_1_), channel_id=1, source_target_pairs={{0,4},{2,6},{4,0},{6,2},{8,12},{10,14},{12,8},{14,10},{16,20},{18,... | collective-permute-start | bytes 4915208 | tf_op jit(solution)/shard_map/ppermute | solution.py:855
  63.3 30.3 %collective-permute-start.18 = (bf16[80,2560]{1,0:T(8,128)(2,1)}, bf16[80,2560]{1,0:T(8,128)(2,1)S(1)}, u32[]{:S(2)}, u32[]{:S(2)}) collective-permute-start(bf16[80,2560]{1,0:T(8,128)(2,1)} %collective-permute-done.17.refs_1_), channel_id=1, source_target_pairs={{0,24},{2,26},{4,28},{6,30},{8,0},{10,2},{12,4},{14,6},{16,8},{18,... | collective-permute-start | bytes 1228808 | tf_op jit(solution)/shard_map/ppermute | solution.py:858
  71.0 46.2 %collective-permute-start.20 = (bf16[160,5120]{1,0:T(8,128)(2,1)}, bf16[160,5120]{1,0:T(8,128)(2,1)}, u32[]{:S(2)}, u32[]{:S(2)}) collective-permute-start(bf16[160,5120]{1,0:T(8,128)(2,1)} %shard_map.363.refs_4_.refs_1_), channel_id=1, source_target_pairs={{0,24},{2,26},{4,28},{6,30},{8,0},{10,2},{12,4},{14,6},{16,8},{18,... | collective-permute-start | bytes 4915208 | tf_op jit(solution)/shard_map/ppermute | solution.py:858
  120.7 59.6 %collective-permute-start.36 = (bf16[288,1280]{1,0:T(8,128)(2,1)}, bf16[288,1280]{1,0:T(8,128)(2,1)}, u32[]{:S(2)}, u32[]{:S(2)}) collective-permute-start(bf16[288,1280]{1,0:T(8,128)(2,1)} %get-tuple-element.218), channel_id=1, source_target_pairs={{0,1},{1,0},{2,3},{3,2},{4,5},{5,4},{6,7},{7,6},{8,9},{9,8},{10,11... | collective-permute-start | bytes 2211848 | tf_op jit(solution)/shard_map/ppermute | solution.py:849
  125.6 59.7 %collective-permute-start.21 = (bf16[160,5120]{1,0:T(8,128)(2,1)}, bf16[160,5120]{1,0:T(8,128)(2,1)}, u32[]{:S(2)}, u32[]{:S(2)}) collective-permute-start(bf16[160,5120]{1,0:T(8,128)(2,1)} %collective-permute-done.20.refs_6_.refs_2_), channel_id=1, source_target_pairs={{0,24},{2,26},{4,28},{6,30},{8,0},{10,2},{12,4},{14,6},{16,8},{18,... | collective-permute-start | bytes 4915208 | tf_op jit(solution)/shard_map/ppermute | solution.py:858
  130.5 44.2 %collective-permute-start.22 = (bf16[320,2560]{1,0:T(8,128)(2,1)}, bf16[320,2560]{1,0:T(8,128)(2,1)}, u32[]{:S(2)}, u32[]{:S(2)}) collective-permute-start(bf16[320,2560]{1,0:T(8,128)(2,1)} %shard_map.366.refs_14_.refs_1_), channel_id=1, source_target_pairs={{0,1},{1,0},{2,3},{3,2},{4,5},{5,4},{6,7},{7,6},{8,9},{9,8},{10,11... | collective-permute-start | bytes 4915208 | tf_op jit(solution)/shard_map/ppermute | solution.py:849
  131.0 43.7 %collective-permute-start.23 = (bf16[320,2560]{1,0:T(8,128)(2,1)}, bf16[320,2560]{1,0:T(8,128)(2,1)}, u32[]{:S(2)}, u32[]{:S(2)}) collective-permute-start(bf16[320,2560]{1,0:T(8,128)(2,1)} %shard_map.366.refs_14_.refs_1_), channel_id=1, source_target_pairs={{0,4},{2,6},{4,0},{6,2},{8,12},{10,14},{12,8},{14,10},{16,20},{18,... | collective-permute-start | bytes 4915208 | tf_op jit(solution)/shard_map/ppermute | solution.py:855
  132.5 57.2 %collective-permute-start.24 = (bf16[320,2560]{1,0:T(8,128)(2,1)}, bf16[320,2560]{1,0:T(8,128)(2,1)}, u32[]{:S(2)}, u32[]{:S(2)}) collective-permute-start(bf16[320,2560]{1,0:T(8,128)(2,1)} %shard_map.366.refs_14_.refs_1_), channel_id=1, source_target_pairs={{0,2},{2,0},{4,6},{6,4},{8,10},{10,8},{12,14},{14,12},{16,18},{18,... | collective-permute-start | bytes 4915208 | tf_op jit(solution)/shard_map/ppermute | solution.py:852
  185.3 38.6 %collective-permute-start.31 = (bf16[160,5120]{1,0:T(8,128)(2,1)}, bf16[160,5120]{1,0:T(8,128)(2,1)}, u32[]{:S(2)}, u32[]{:S(2)}) collective-permute-start(bf16[160,5120]{1,0:T(8,128)(2,1)} %collective-permute-done.21.refs_11_.refs_3_), channel_id=1, source_target_pairs={{0,24},{2,26},{4,28},{6,30},{8,0},{10,2},{12,4},{14,6},{16,8},{18,... | collective-permute-start | bytes 4915208 | tf_op jit(solution)/shard_map/ppermute | solution.py:858
  189.7 34.8 %collective-permute-start.25 = (bf16[320,2560]{1,0:T(8,128)(2,1)}, bf16[320,2560]{1,0:T(8,128)(2,1)S(1)}, u32[]{:S(2)}, u32[]{:S(2)}) collective-permute-start(bf16[320,2560]{1,0:T(8,128)(2,1)} %collective-permute-done.23.refs_1_.refs_2_), channel_id=1, source_target_pairs={{0,2},{2,0},{4,6},{6,4},{8,10},{10,8},{12,14},{14,12},{16,18},{18,... | collective-permute-start | bytes 4915208 | tf_op jit(solution)/shard_map/ppermute | solution.py:852
  189.7 35.2 %collective-permute-start.27 = (bf16[320,2560]{1,0:T(8,128)(2,1)}, bf16[320,2560]{1,0:T(8,128)(2,1)S(1)}, u32[]{:S(2)}, u32[]{:S(2)}) collective-permute-start(bf16[320,2560]{1,0:T(8,128)(2,1)} %collective-permute-done.22.refs_0_.refs_5_.refs_9_), channel_id=1, source_target_pairs={{0,2},{2,0},{4,6},{6,4},{8,10},{10,8},{12,14},{14,12},{16,18},{18,... | collective-permute-start | bytes 4915208 | tf_op jit(solution)/shard_map/ppermute | solution.py:852
  223.9 30.4 %collective-permute-start.32 = (bf16[160,5120]{1,0:T(8,128)(2,1)}, bf16[160,5120]{1,0:T(8,128)(2,1)}, u32[]{:S(2)}, u32[]{:S(2)}) collective-permute-start(bf16[160,5120]{1,0:T(8,128)(2,1)} %shard_map.363.refs_4_.refs_1_), channel_id=1, source_target_pairs={{0,2},{2,0},{4,6},{6,4},{8,10},{10,8},{12,14},{14,12},{16,18},{18,... | collective-permute-start | bytes 4915208 | tf_op jit(solution)/shard_map/ppermute | solution.py:852
  223.9 30.4 %collective-permute-start.33 = (bf16[160,5120]{1,0:T(8,128)(2,1)}, bf16[160,5120]{1,0:T(8,128)(2,1)}, u32[]{:S(2)}, u32[]{:S(2)}) collective-permute-start(bf16[160,5120]{1,0:T(8,128)(2,1)} %collective-permute-done.20.refs_6_.refs_2_), channel_id=1, source_target_pairs={{0,2},{2,0},{4,6},{6,4},{8,10},{10,8},{12,14},{14,12},{16,18},{18,... | collective-permute-start | bytes 4915208 | tf_op jit(solution)/shard_map/ppermute | solution.py:852
  224.4 29.9 %collective-permute-start.34 = (bf16[160,5120]{1,0:T(8,128)(2,1)}, bf16[160,5120]{1,0:T(8,128)(2,1)}, u32[]{:S(2)}, u32[]{:S(2)}) collective-permute-start(bf16[160,5120]{1,0:T(8,128)(2,1)} %collective-permute-done.21.refs_11_.refs_3_), channel_id=1, source_target_pairs={{0,2},{2,0},{4,6},{6,4},{8,10},{10,8},{12,14},{14,12},{16,18},{18,... | collective-permute-start | bytes 4915208 | tf_op jit(solution)/shard_map/ppermute | solution.py:852
  254.0 39.0 %collective-permute-start.38 = (bf16[640,5120]{1,0:T(8,128)(2,1)}, bf16[640,5120]{1,0:T(8,128)(2,1)}, u32[]{:S(2)}, u32[]{:S(2)}) collective-permute-start(bf16[640,5120]{1,0:T(8,128)(2,1)} %shard_map.372.refs_11_), channel_id=1, source_target_pairs={{0,2},{2,0},{4,6},{6,4},{8,10},{10,8},{12,14},{14,12},{16,18},{18,... | collective-permute-start | bytes 19660808 | tf_op jit(solution)/shard_map/ppermute | solution.py:852
  305.3 37.5 %collective-permute-start.39 = (bf16[640,1280]{1,0:T(8,128)(2,1)}, bf16[640,1280]{1,0:T(8,128)(2,1)}, u32[]{:S(2)}, u32[]{:S(2)}) collective-permute-start(bf16[640,1280]{1,0:T(8,128)(2,1)} %get-tuple-element.79), channel_id=1, source_target_pairs={{0,4},{2,6},{4,0},{6,2},{8,12},{10,14},{12,8},{14,10},{16,20},{18,... | collective-permute-start | bytes 4915208 | tf_op jit(solution)/shard_map/ppermute | solution.py:855
  305.8 37.2 %collective-permute-start.40 = (bf16[640,1280]{1,0:T(8,128)(2,1)}, bf16[640,1280]{1,0:T(8,128)(2,1)}, u32[]{:S(2)}, u32[]{:S(2)}) collective-permute-start(bf16[640,1280]{1,0:T(8,128)(2,1)} %get-tuple-element.80), channel_id=1, source_target_pairs={{0,1},{1,0},{2,3},{3,2},{4,5},{5,4},{6,7},{7,6},{8,9},{9,8},{10,11... | collective-permute-start | bytes 4915208 | tf_op jit(solution)/shard_map/ppermute | solution.py:849
  355.7 37.1 %collective-permute-start.41 = (bf16[320,1280]{1,0:T(8,128)(2,1)}, bf16[320,1280]{1,0:T(8,128)(2,1)}, u32[]{:S(2)}, u32[]{:S(2)}) collective-permute-start(bf16[320,1280]{1,0:T(8,128)(2,1)} %get-tuple-element.81.refs_2_), channel_id=1, source_target_pairs={{0,1},{1,0},{2,3},{3,2},{4,5},{5,4},{6,7},{7,6},{8,9},{9,8},{10,11... | collective-permute-start | bytes 2457608 | tf_op jit(solution)/shard_map/ppermute | solution.py:849
  357.1 35.7 %collective-permute-start.42 = (bf16[320,1280]{1,0:T(8,128)(2,1)}, bf16[320,1280]{1,0:T(8,128)(2,1)}, u32[]{:S(2)}, u32[]{:S(2)}) collective-permute-start(bf16[320,1280]{1,0:T(8,128)(2,1)} %get-tuple-element.83), channel_id=1, source_target_pairs={{0,4},{2,6},{4,0},{6,2},{8,12},{10,14},{12,8},{14,10},{16,20},{18,... | collective-permute-start | bytes 2457608 | tf_op jit(solution)/shard_map/ppermute | solution.py:855
  395.0 44.9 %collective-permute-start.46 = (bf16[640,1280]{1,0:T(8,128)(2,1)}, bf16[640,1280]{1,0:T(8,128)(2,1)}, u32[]{:S(2)}, u32[]{:S(2)}) collective-permute-start(bf16[640,1280]{1,0:T(8,128)(2,1)} %get-tuple-element.89), channel_id=1, source_target_pairs={{0,4},{2,6},{4,0},{6,2},{8,12},{10,14},{12,8},{14,10},{16,20},{18,... | collective-permute-start | bytes 4915208 | tf_op jit(solution)/shard_map/ppermute | solution.py:855
  395.4 44.5 %collective-permute-start.47 = (bf16[640,1280]{1,0:T(8,128)(2,1)}, bf16[640,1280]{1,0:T(8,128)(2,1)}, u32[]{:S(2)}, u32[]{:S(2)}) collective-permute-start(bf16[640,1280]{1,0:T(8,128)(2,1)} %get-tuple-element.90), channel_id=1, source_target_pairs={{0,1},{1,0},{2,3},{3,2},{4,5},{5,4},{6,7},{7,6},{8,9},{9,8},{10,11... | collective-permute-start | bytes 4915208 | tf_op jit(solution)/shard_map/ppermute | solution.py:849
  412.4 30.6 %collective-permute-start.45 = (bf16[80,2560]{1,0:T(8,128)(2,1)}, bf16[80,2560]{1,0:T(8,128)(2,1)}, u32[]{:S(2)}, u32[]{:S(2)}) collective-permute-start(bf16[80,2560]{1,0:T(8,128)(2,1)} %shard_map.382.refs_7_), channel_id=1, source_target_pairs={{0,8},{2,10},{4,12},{6,14},{8,16},{10,18},{12,20},{14,22},{16,24},... | collective-permute-start | bytes 1228808 | tf_op jit(solution)/shard_map/ppermute | solution.py:861
  464.3 43.1 %collective-permute-start.48 = (bf16[80,2560]{1,0:T(8,128)(2,1)}, bf16[80,2560]{1,0:T(8,128)(2,1)}, u32[]{:S(2)}, u32[]{:S(2)}) collective-permute-start(bf16[80,2560]{1,0:T(8,128)(2,1)} %shard_map.385.refs_4_), channel_id=1, source_target_pairs={{0,8},{2,10},{4,12},{6,14},{8,16},{10,18},{12,20},{14,22},{16,24},... | collective-permute-start | bytes 1228808 | tf_op jit(solution)/shard_map/ppermute | solution.py:861
  503.7 33.2 %collective-permute-start.56 = (bf16[80,2560]{1,0:T(8,128)(2,1)}, bf16[80,2560]{1,0:T(8,128)(2,1)}, u32[]{:S(2)}, u32[]{:S(2)}) collective-permute-start(bf16[80,2560]{1,0:T(8,128)(2,1)} %shard_map.389.refs_6_), channel_id=1, source_target_pairs={{0,8},{2,10},{4,12},{6,14},{8,16},{10,18},{12,20},{14,22},{16,24},... | collective-permute-start | bytes 1228808 | tf_op jit(solution)/shard_map/ppermute | solution.py:861
  506.1 37.2 %collective-permute-start.54 = (bf16[640,1280]{1,0:T(8,128)(2,1)}, bf16[640,1280]{1,0:T(8,128)(2,1)}, u32[]{:S(2)}, u32[]{:S(2)}) collective-permute-start(bf16[640,1280]{1,0:T(8,128)(2,1)} %get-tuple-element.95), channel_id=1, source_target_pairs={{0,4},{2,6},{4,0},{6,2},{8,12},{10,14},{12,8},{14,10},{16,20},{18,... | collective-permute-start | bytes 4915208 | tf_op jit(solution)/shard_map/ppermute | solution.py:855
  506.6 39.1 %collective-permute-start.55 = (bf16[640,1280]{1,0:T(8,128)(2,1)}, bf16[640,1280]{1,0:T(8,128)(2,1)}, u32[]{:S(2)}, u32[]{:S(2)}) collective-permute-start(bf16[640,1280]{1,0:T(8,128)(2,1)} %get-tuple-element.96), channel_id=1, source_target_pairs={{0,1},{1,0},{2,3},{3,2},{4,5},{5,4},{6,7},{7,6},{8,9},{9,8},{10,11... | collective-permute-start | bytes 4915208 | tf_op jit(solution)/shard_map/ppermute | solution.py:849
  562.0 34.3 %collective-permute-start.57 = (bf16[320,1280]{1,0:T(8,128)(2,1)}, bf16[320,1280]{1,0:T(8,128)(2,1)S(1)}, u32[]{:S(2)}, u32[]{:S(2)}) collective-permute-start(bf16[320,1280]{1,0:T(8,128)(2,1)} %get-tuple-element.99.refs_1_), channel_id=1, source_target_pairs={{0,1},{1,0},{2,3},{3,2},{4,5},{5,4},{6,7},{7,6},{8,9},{9,8},{10,11... | collective-permute-start | bytes 2457608 | tf_op jit(solution)/shard_map/ppermute | solution.py:849
  562.6 33.8 %collective-permute-start.58 = (bf16[320,1280]{1,0:T(8,128)(2,1)}, bf16[320,1280]{1,0:T(8,128)(2,1)S(1)}, u32[]{:S(2)}, u32[]{:S(2)}) collective-permute-start(bf16[320,1280]{1,0:T(8,128)(2,1)} %get-tuple-element.100), channel_id=1, source_target_pairs={{0,4},{2,6},{4,0},{6,2},{8,12},{10,14},{12,8},{14,10},{16,20},{18,... | collective-permute-start | bytes 2457608 | tf_op jit(solution)/shard_map/ppermute | solution.py:855
  (146 other events, 1330.6 us)

commit v4 on v3

--- a/solution.py
+++ b/solution.py
@@ -166,15 +166,8 @@
             at += len(pieces)
 
 
-ROWS = 96
-
-
 def row_loop(rows, work):
-    def step(k, carry):
-        work(pl.ds(pl.multiple_of(k * ROWS, ROWS), ROWS))
-        return carry
-
-    lax.fori_loop(0, rows // ROWS, step, 0)
+    work(pl.ds(0, rows))
 
 
 def times_weight(left, parts, table, ins, in_specs, outs, out_specs, finish, us, after=()):
@@ -485,13 +478,12 @@
     )
 
 
-def grad_kernel(pairs, block, kind, half, came, after=()):
+def grad_kernel(pairs, block, kind, half, came=None, part=None, us=10, after=()):
     rows, width = pairs[0][0].shape
     middle = width // 2
     low = middle // 2
     steps = len(kind)
     near = steps // 2
-    fourth = near // 2
     count = len(pairs)
 
     def kernel(*refs):
@@ -519,7 +511,7 @@
                         turned[k][...], right, preferred_element_type=F32
                     ).astype(LOW)
                     return
-                came_ref, own0, to_y, to_x, other_a, own_b = rest[:6]
+                came_ref, out0, out1, out2 = rest[:4]
                 y0 = jnp.dot(turned[k][:low, :], right, preferred_element_type=F32)
                 y0 = (y0 + came_ref[:low, :].astype(F32)).astype(LOW)
                 y1 = jnp.dot(turned[k][low:, :], right, preferred_element_type=F32)
@@ -527,24 +519,17 @@
 
                 @pl.when(j < near)
                 def _():
-                    own0[...] = y0
-
-                @pl.when(j % near < fourth)
+                    out0[...] = y0
+                    out1[...] = y1
+
+                @pl.when(j >= near)
                 def _():
-                    to_y[...] = y1
-
-                @pl.when((j >= fourth) & (j < near))
-                def _():
-                    own_b[...] = y1
-
-                @pl.when((j >= near) & (j < near + fourth))
-                def _():
-                    other_a[...] = y0
-
-                @pl.when(j >= near + fourth)
-                def _():
-                    to_x[:low, :] = y0
-                    to_x[low:, :] = y1
+                    if part == "a":
+                        out2[...] = y0
+                        out1[...] = y1
+                    else:
+                        out2[:low, :] = y0
+                        out2[low:, :] = y1
 
     right_specs = []
     for k in range(count):
@@ -560,30 +545,30 @@
         spec = pl.BlockSpec((height, block), lambda j: (0, jnp.clip(j - base, 0, number - 1)))
         return spec, jax.ShapeDtypeStruct((height, number * block), LOW)
 
+    extra, extra_specs = [], []
     if came is None:
         outs = [clipped(0, steps, middle)]
     else:
-        turn_spec = pl.BlockSpec(
-            (low, block), lambda j: (j // near, jnp.clip(j % near, 0, fourth - 1))
-        )
-        outs = [
-            clipped(0, near, low),
-            (turn_spec, jax.ShapeDtypeStruct((middle, fourth * block), LOW)),
-            clipped(near + fourth, fourth, middle),
-            clipped(near, fourth, low),
-            clipped(fourth, fourth, low),
-        ]
-    extra = [] if came is None else [came]
+        extra = [came[0]]
+        column = lookup(came[1])
+        extra_specs = [pl.BlockSpec((middle, block), lambda j: (0, column(j)))]
+        if part == "a":
+            both = pl.BlockSpec((low, block), lambda j: (j // near, j % near))
+            outs = [
+                clipped(0, near, low),
+                (both, jax.ShapeDtypeStruct((middle, near * block), LOW)),
+                clipped(near, near, low),
+            ]
+        else:
+            outs = [clipped(0, near, low), clipped(0, near, low), clipped(near, near, middle)]
     return call(
         kernel,
         (steps,),
-        [whole(left.shape) for left, _ in pairs]
-        + right_specs
-        + [pl.BlockSpec((middle, block), lambda j: (0, j)) for _ in extra],
+        [whole(left.shape) for left, _ in pairs] + right_specs + extra_specs,
         [s for s, _ in outs],
         [s for _, s in outs],
         scratch=[pltpu.VMEM((middle, rows), LOW) for _ in pairs],
-        us=10 if came is None else 12,
+        us=us,
         after=after,
     )(*[left for left, _ in pairs], *[right for _, right in pairs], *extra)
 
@@ -608,18 +593,18 @@
     )(other_a, own_b, from_y, from_x)
 
 
-def add_ring(own0, from_y, from_x, second_x, second_y, came, place, rows, kind):
-    columns = own0.shape[1]
-    half = columns // 2
+def add_ring(own_a, own_b, from_y, from_x, second_x, second_y, came, place, rows, kind):
+    half = own_a.shape[1]
+    columns = 2 * half
 
     def kernel(*refs):
-        own, y, x, x2, y2 = refs[:5]
+        own_a, own_b, y, x, x2, y2 = refs[:6]
         out = refs[-1]
-        a = own[:, :half].astype(F32) + y[...].astype(F32) + x2[...].astype(F32)
-        b = own[:, half:].astype(F32) + x[...].astype(F32) + y2[...].astype(F32)
+        a = own_a[...].astype(F32) + y[...].astype(F32) + x2[...].astype(F32)
+        b = own_b[...].astype(F32) + x[...].astype(F32) + y2[...].astype(F32)
         if came is not None:
-            a = a + refs[5][:, :half].astype(F32)
-            b = b + refs[5][:, half:].astype(F32)
+            a = a + refs[6][:, :half].astype(F32)
+            b = b + refs[6][:, half:].astype(F32)
         out[:, :half] = a.astype(kind)
         out[:, half:] = b.astype(kind)
 
@@ -628,32 +613,176 @@
     return call(
         kernel,
         (1,),
-        [pl.BlockSpec((rows, columns), lambda j: (place, 0)), side, side, side, side]
+        [side] * 6
         + [whole(v.shape) for v in extra],
         whole((rows, columns)),
         jax.ShapeDtypeStruct((rows, columns), kind),
-    )(own0, from_y, from_x, second_x, second_y, *extra)
-
-
-def cut_far(side, across):
+    )(own_a, own_b, from_y, from_x, second_x, second_y, *extra)
+
+
+def cut_far(side, across, split):
     rows, columns = side.shape
-    half = columns // 2
 
     def kernel(a, b, out_a, out_b):
-        out_a[...] = a[...]
-        out_b[...] = b[...]
-
-    shape = jax.ShapeDtypeStruct((rows, half), side.dtype)
+        out_a[...] = a[:, :split]
+        out_b[...] = b[:, split:]
+
+    return call(
+        kernel,
+        (1,),
+        [whole(side.shape)] * 2,
+        [whole((rows, split)), whole((rows, columns - split))],
+        [
+            jax.ShapeDtypeStruct((rows, split), side.dtype),
+            jax.ShapeDtypeStruct((rows, columns - split), side.dtype),
+        ],
+    )(side, across)
+
+
+def unshuffle(values, shuffle):
+    rows, width = values.shape
+    half = rows // 2
+
+    def kernel(in_ref, s_ref, first, second):
+        y = lax.dot_general(
+            in_ref[...], s_ref[...], (((1,), (1,)), ((), ())), preferred_element_type=F32
+        ).astype(LOW)
+        first[...] = y[:half]
+        second[...] = y[half:]
+
+    shape = jax.ShapeDtypeStruct((half, width), LOW)
+    return call(
+        kernel,
+        (1,),
+        [whole(values.shape), whole(shuffle.shape)],
+        [whole((half, width))] * 2,
+        [shape, shape],
+        us=5,
+    )(values, shuffle)
+
+
+def lamb_row(index, master_sq, update_sq):
+    lane = lax.broadcasted_iota(jnp.int32, (1, 128), 1)
+    row = jnp.where(lane == index, master_sq, 0.0)
+    return row + jnp.where(lane == 7 + index, update_sq, 0.0)
+
+
+def lamb_first(master, moments, grad, column, turned, index, factor):
+    shape = master.shape
+
+    def kernel(p_ref, m_ref, g_ref, new_ref, u_ref, row_ref):
+        if len(shape) == 2:
+            g = g_ref[...]
+            g = (g.T if turned else g) * factor
+            p = p_ref[...]
+            first, second, update = lamb_parts(p, (m_ref[0], m_ref[1]), g)
+            new_ref[0] = first
+            new_ref[1] = second
+            u_ref[...] = update
+            row_ref[...] = lamb_row(index, jnp.sum(p * p), jnp.sum(update * update))
+            return
+        row = jnp.zeros((1, 128), F32)
+        for k in range(shape[1]):
+            g = g_ref[:, k * shape[2] : (k + 1) * shape[2]] * factor
+            p = p_ref[:, k, :]
+            first, second, update = lamb_parts(p, (m_ref[0, :, k, :], m_ref[1, :, k, :]), g)
+            new_ref[0, :, k, :] = first
+            new_ref[1, :, k, :] = second
+            u_ref[:, k, :] = update
+            row = row + lamb_row(index, jnp.sum(p * p), jnp.sum(update * update))
+        row_ref[...] = row
+
+    if turned:
+        columns = shape[0]
+    else:
+        columns = shape[-1] * (shape[1] if len(shape) == 3 else 1)
+    rows = shape[1] if turned else shape[0]
     return call(
         kernel,
         (1,),
         [
-            pl.BlockSpec((rows, half), lambda j: (0, 0)),
-            pl.BlockSpec((rows, half), lambda j: (0, 1)),
+            whole(shape),
+            whole(moments.shape),
+            pl.BlockSpec((rows, columns), lambda j: (0, column)),
         ],
-        [whole((rows, half))] * 2,
-        [shape, shape],
-    )(side, across)
+        [whole(moments.shape), whole(shape), whole((1, 128))],
+        [
+            jax.ShapeDtypeStruct(moments.shape, F32),
+            jax.ShapeDtypeStruct(shape, F32),
+            jax.ShapeDtypeStruct((1, 128), F32),
+        ],
+        us=4,
+    )(master, moments, grad)
+
+
+def lamb_small(masters, moments, grads, shares, factor):
+    count = len(masters)
+
+    def kernel(*refs):
+        p_refs, m_refs, g_refs = refs[:count], refs[count : 2 * count], refs[2 * count : 3 * count]
+        share_ref = refs[3 * count]
+        outs = refs[3 * count + 1 :]
+        row = jnp.zeros((1, 128), F32)
+        for k in range(count):
+            p = p_refs[k][...]
+            if len(m_refs[k].shape) == 2:
+                old = (m_refs[k][0:1, :], m_refs[k][1:2, :])
+            else:
+                old = (m_refs[k][0], m_refs[k][1])
+            first, second, update = lamb_parts(p, old, g_refs[k][...] * factor)
+            if len(m_refs[k].shape) == 2:
+                outs[k][0:1, :] = first
+                outs[k][1:2, :] = second
+            else:
+                outs[k][0] = first
+                outs[k][1] = second
+            outs[count + k][...] = update
+            row = row + lamb_row(4 + k, jnp.sum(p * p), jnp.sum(update * update))
+        outs[2 * count][...] = row * share_ref[...]
+
+    operands = [*masters, *moments, *grads, shares]
+    shapes = [v.shape for v in (*moments, *masters)] + [(1, 128)]
+    return call(
+        kernel,
+        (1,),
+        [whole(v.shape) for v in operands],
+        [whole(v) for v in shapes],
+        [jax.ShapeDtypeStruct(v, F32) for v in shapes],
+    )(*operands)
+
+
+def lamb_last(masters, updates, rows, copies):
+    count = len(masters)
+
+    def kernel(*refs):
+        p_refs, u_refs, row_ref = refs[:count], refs[count : 2 * count], refs[2 * count]
+        outs = refs[2 * count + 1 :]
+        row = row_ref[...]
+        stats = outs[count + copies]
+        stats[0:1, :] = jnp.sqrt(row)
+        for k in range(count):
+            master_sq, update_sq = row[:, k : k + 1], row[:, 7 + k : 8 + k]
+            trust = jnp.sqrt(master_sq) / jnp.sqrt(update_sq + 1e-12)
+            stats[1:2, k : k + 1] = trust
+            if len(p_refs[k].shape) == 3:
+                trust = trust[:, :, None]
+            new = p_refs[k][...] - LEARN_RATE * trust * u_refs[k][...]
+            outs[k][...] = new
+            if k < copies:
+                outs[count + k][...] = new.astype(LOW)
+
+    shapes = [jax.ShapeDtypeStruct(v.shape, F32) for v in masters]
+    shapes += [jax.ShapeDtypeStruct(v.shape, LOW) for v in masters[:copies]]
+    shapes += [jax.ShapeDtypeStruct((2, 128), F32)]
+    operands = [*masters, *updates, rows]
+    return call(
+        kernel,
+        (1,),
+        [whole(v.shape) for v in operands],
+        [whole(v.shape) for v in shapes],
+        shapes,
+        us=8,
+    )(*operands)
 
 
 def hold(values):
@@ -692,7 +821,7 @@
 def stack_rows(pieces, after=()):
     rows, columns = pieces[0].shape
     count = len(pieces)
-    block = columns // 2
+    block = columns // (columns // 640)
 
     def kernel(*refs):
         for k in range(count):
@@ -700,7 +829,7 @@
 
     return call(
         kernel,
-        (2,),
+        (columns // block,),
         [pl.BlockSpec((rows, block), lambda j: (0, j))] * count,
         pl.BlockSpec((count * rows, block), lambda j: (0, j)),
         jax.ShapeDtypeStruct((count * rows, columns), pieces[0].dtype),
@@ -876,22 +1005,18 @@
             held.append(self.down_z(held[-1]))
         return held
 
-    def corners(self, held):
-        side, across = self.over_x(held), self.over_y(held)
-        return side, across, *self.far(side, across)
-
-    def far(self, side, across):
-        a, b = cut_far(side, across)
+    def far(self, side, across, split):
+        a, b = cut_far(side, across, split)
         return self.over_y(a), self.over_x(b)
 
-    def gathered(self, held, corners):
-        side, across, far_a, far_b = corners
+    def gathered(self, held, side, across, far_a, far_b):
         core = self.over_core
         side_core = core(side)
         return Gathered(
             [held, across, core(held), core(across)],
             [side, far_a, side_core, core(far_a)],
             [side, far_b, side_core, core(far_b)],
+            far_a.shape[1],
         )
 
     def stacked(self, held):
@@ -907,26 +1032,20 @@
 
 
 class Gathered:
-    def __init__(self, own, other_a, other_b):
-        self.own, self.other_a, self.other_b = own, other_a, other_b
-
-    def parts(self, block, ranges):
-        half = self.own[0].shape[1] // 2 // block
-        sets = []
-        (first, count), (first_a, count_a), (first_b, count_b) = ranges
-        if count:
-            sets.append(([(v, first) for v in self.own], None, count))
+    def __init__(self, own, other_a, other_b, split):
+        self.own, self.other_a, self.other_b, self.split = own, other_a, other_b, split
+
+    def parts(self, block, first, count):
+        columns = self.own[0].shape[1]
+        split = self.split // block
+        sets = [([(v, first) for v in self.own], None, count)]
+        count_a = max(0, min(first + count, split) - first)
         if count_a:
-            sets.append(([(v, first_a) for v in self.other_a], None, count_a))
-        if count_b:
-            wide = [v.shape[1] // block > half for v in self.other_b]
-            sets.append(
-                (
-                    [(v, first_b + half * w) for v, w in zip(self.other_b, wide)],
-                    None,
-                    count_b,
-                )
-            )
+            sets.append(([(v, first) for v in self.other_a], None, count_a))
+        if count > count_a:
+            start = max(first, split)
+            pieces = [(v, start if v.shape[1] == columns else start - split) for v in self.other_b]
+            sets.append((pieces, None, count - count_a))
         return Parts(sets, block)
 
 
@@ -985,38 +1104,36 @@
     hidden = fc1_weight.shape[1]
     grad_factor = float(block_input.shape[0] * block_input.shape[1] * dp * LEN) ** (-0.5)
 
-    shard_1 = jnp.concatenate(
-        [qkv_weight.reshape(rows_own, 3 * lane_columns), proj_weight.T], 1
-    ).astype(LOW)
-    shard_2 = fc1_weight.astype(LOW)
+    shard_1 = qkv_weight.astype(LOW).reshape(rows_own, 3 * lane_columns)
+    shard_2 = jnp.concatenate([fc1_weight.astype(LOW), proj_weight.astype(LOW).T], 1)
     shard_3 = fc2_weight.astype(LOW).T
+    half = hidden // 2
     if relative:
         ring_1 = lanes.ring_down(shard_1)
         side_3, across_3 = lanes.over_x(shard_3), lanes.over_y(shard_3)
         far_3 = lanes.over_y(side_3)
         late_3 = [stack_early(shard_3, side_3, across_3, far_3, after=[ring_1[2]])]
         held_1 = stack_rows(ring_1)
-        corners_1 = lanes.corners(held_1)
-        w1 = lanes.gathered(held_1, corners_1)
+        sides_w1 = lanes.over_x(held_1), lanes.over_y(held_1)
+        fars_w1 = lanes.far(*sides_w1, 2 * lane_columns)
+        w1 = lanes.gathered(held_1, *sides_w1, *fars_w1)
         for _ in range(3):
             late_3.append(lanes.down_z(late_3[-1]))
         ring_2 = lanes.ring_down(shard_2)
-        held_2 = stack_rows(ring_2, after=[corners_1[2], corners_1[3], late_3[1]])
-        sides_up = lanes.over_x(held_2), lanes.over_y(held_2)
+        held_2 = stack_rows(ring_2, after=[*fars_w1, late_3[1]])
+        sides_w2 = lanes.over_x(held_2), lanes.over_y(held_2)
         w3 = lanes.stacked(late_3)
-        w_down = w3.parts(hidden // 2)
+        w_down = w3.parts(half)
     else:
 
         def plain(shard):
             held = lax.all_gather(shard, "dp", axis=0, tiled=True)
             side = lanes.over_x(held)
-            return Gathered([held], [side], [side])
+            return Gathered([held], [side], [side], half)
 
         w1, w2, w3 = plain(shard_1), plain(shard_2), plain(shard_3)
-        w_up = w2.parts(hidden // 2, [(0, 2), (0, 1), (0, 1)])
-        w_down = w3.parts(hidden // 2, [(0, 2), (0, 1), (0, 1)])
-    w_qkv = w1.parts(lane_columns, [(0, 3), (0, 2), (0, 1)])
-    w_proj = w1.parts(lane_columns, [(3, 1), (0, 0), (1, 1)])
+        w_down = w3.parts(half, 0, 2)
+    w_qkv = w1.parts(lane_columns, 0, 3)
 
     def own_row(both):
         mine = lax.dynamic_index_in_dim(both[:, 0], slot, 0, keepdims=False)
@@ -1071,31 +1188,33 @@
 
     def give_back(values_low):
         if relative:
-            values_low = dot_t(values_low, shuffle).astype(LOW)
-        mine, theirs = values_low[:local_rows], lanes.over_x(values_low[local_rows:])
+            mine, theirs = unshuffle(values_low, shuffle)
+        else:
+            mine, theirs = values_low[:local_rows], values_low[local_rows:]
+        theirs = lanes.over_x(theirs)
         swap = slot == 0
         return jnp.stack([jnp.where(swap, mine, theirs), jnp.where(swap, theirs, mine)])[:, None]
 
     wide_kind = [(0, j) for j in range(4)]
     first_kind = [(0, 0), (0, 1), (0, 2), (1, 0), (0, 3), (0, 4), (0, 5), (1, 1)]
 
-    def send_grads(pairs, block, kind):
-        (sent,) = grad_kernel(pairs, block, kind, 1, None)
-        return lanes.over_core(sent) if relative else sent
-
-    def keep_grads(pairs, block, kind, came, after=()):
-        return grad_kernel(pairs, block, kind, 0, came, after)
-
-    def send_first(kept):
-        return lanes.over_y(kept[1]), lanes.over_x(kept[2])
+    def send_grads(pairs, block, kind, us):
+        (sent,) = grad_kernel(pairs, block, kind, 1, us=us)
+        return lanes.over_core(sent)
+
+    def wide_grads(pairs, came):
+        a = grad_kernel(pairs, half, [(0, 0), (0, 2)], 0, (came, [0, 2]), "a", 7)
+        from_y = lanes.over_y(a[1])
+        b = grad_kernel(pairs, half, [(0, 1), (0, 3)], 0, (came, [1, 3]), "b", 7)
+        return (a[0], b[0]), (a[2], b[1]), (from_y, lanes.over_x(b[2]))
 
     def send_second(kept, first):
-        to_x, to_y = add_second(kept[3], kept[4], *first)
+        to_x, to_y = add_second(*kept, *first)
         return (*first, lanes.over_x(to_x), lanes.over_y(to_y))
 
-    def ring_step(kept, sides, came, place):
+    def ring_step(own, sides, came, place):
         kind = LOW if place else F32
-        total = add_ring(kept[0], *sides, came, place, rows_own, kind)
+        total = add_ring(*own, *sides, came, place, rows_own, kind)
         return lanes.up_z(total) if place else total
 
     def plain_grads(pairs, block, kind):
@@ -1116,74 +1235,78 @@
     qkv, attended, lse = attention_forward(mixed, cosine, sine, key_code, query_code, groups)
     before_proj = []
     if relative:
-        corners_2 = (*sides_up, *lanes.far(*sides_up))
+        fars_w2 = lanes.far(*sides_w2, half)
+        w2 = lanes.gathered(held_2, *sides_w2, *fars_w2)
         before_proj = [late_3[2]]
+    w_proj = w2.parts(lane_columns, hidden // lane_columns, 1)
+    w_up = w2.parts(half, 0, 2)
     hidden1, second_in = proj_forward(attended, w_proj, row_low, vec, after=before_proj)
-    if relative:
-        w_up = lanes.gathered(held_2, corners_2).parts(
-            hidden // 2, [(0, 2), (0, 1), (0, 1)]
-        )
     upward, activated = up_forward(second_in, w_up, bias_up)
     pair_3 = [(down_grad, activated)]
-    half = hidden // 2
     if relative:
-        came_3 = send_grads(pair_3, half, wide_kind)
+        came_3 = send_grads(pair_3, half, wide_kind, 10)
     result = down_forward(activated, w_down, hidden1, vec)
-    block_output = give_back(result)
 
     if relative:
-        kept_3 = keep_grads(pair_3, half, wide_kind, came_3)
-        first_3 = send_first(kept_3)
+        own_3, later_3, first_3 = wide_grads(pair_3, came_3)
     up_grad, sum_up = down_backward(down_grad, w_down, upward)
     pair_2 = [(second_in, up_grad)]
     if relative:
-        sides_3 = send_second(kept_3, first_3)
-        came_2 = send_grads(pair_2, half, wide_kind)
+        came_2 = send_grads(pair_2, half, wide_kind, 10)
+        sides_3 = send_second(later_3, first_3)
+    block_output = give_back(result)
     hidden1_grad, branch_grad, sums_2 = up_backward(
         up_grad, w_up, hidden1, cot_low, token_weight, vec
     )
     if relative:
-        kept_2 = keep_grads(pair_2, half, wide_kind, came_2, after=[block_output])
-        first_2 = send_first(kept_2)
-        ring_3 = ring_step(kept_3, sides_3, None, 3)
+        ring_3 = ring_step(own_3, sides_3, None, 3)
+        own_2, later_2, first_2 = wide_grads(pair_2, came_2)
     attn_grad = proj_backward(branch_grad, w_proj)
     if relative:
-        ring_3 = ring_step(kept_3, sides_3, ring_3, 2)
+        ring_3 = ring_step(own_3, sides_3, ring_3, 2)
     mixed_grad, sum_qkv = attention_backward(
         qkv, lse, attn_grad, cosine, sine, key_code, query_code, groups
     )
-    pair_1 = [(first_in, mixed_grad), (branch_grad, attended)]
+    pair_q, pair_p = (first_in, mixed_grad), (branch_grad, attended)
+    factor = grad_factor
     if relative:
-        sides_2 = send_second(kept_2, first_2)
-        ring_3 = ring_step(kept_3, sides_3, ring_3, 1)
-        came_1 = send_grads(pair_1, lane_columns, first_kind)
-        ring_2 = ring_step(kept_2, sides_2, None, 3)
-        kept_1 = keep_grads(pair_1, lane_columns, first_kind, came_1)
-        first_1 = send_first(kept_1)
-        ring_2 = ring_step(kept_2, sides_2, ring_2, 2)
-        grad_3 = ring_step(kept_3, sides_3, ring_3, 0)
+        kind_a = [(0, 0), (0, 1), (0, 3), (0, 4)]
+        kind_b = [(0, 2), (1, 0), (0, 5), (1, 1)]
+        sides_2 = send_second(later_2, first_2)
+        ring_3 = ring_step(own_3, sides_3, ring_3, 1)
+        came_a = send_grads([pair_q], lane_columns, kind_a, 7)
+        came_b = send_grads([pair_q, pair_p], lane_columns, kind_b, 7)
+        part_a = grad_kernel([pair_q], lane_columns, kind_a, 0, (came_a, [0, 1, 2, 3]), "a", 8)
+        first_y = lanes.over_y(part_a[1])
+        ring_2 = ring_step(own_2, sides_2, None, 3)
+        part_b = grad_kernel(
+            [pair_q, pair_p], lane_columns, kind_b, 0, (came_b, [0, 1, 2, 3]), "b", 8
+        )
+        own_1, later_1 = (part_a[0], part_b[0]), (part_a[2], part_b[1])
+        first_1 = first_y, lanes.over_x(part_b[2])
+        grad_3 = ring_step(own_3, sides_3, ring_3, 0)
+        lamb_3 = lamb_first(fc2_weight, fc2_moments, grad_3, 0, True, 3, factor)
+        ring_2 = ring_step(own_2, sides_2, ring_2, 2)
     input_low, sums_1 = qkv_backward(
         mixed_grad, w_qkv, list(range(6)), row_low, hidden1_grad, vec
     )
     if relative:
-        ring_2 = ring_step(kept_2, sides_2, ring_2, 1)
-        sides_1 = send_second(kept_1, first_1)
+        ring_2 = ring_step(own_2, sides_2, ring_2, 1)
+        sides_1 = send_second(later_1, first_1)
+        input_grad = give_back(input_low)
+        grad_2 = ring_step(own_2, sides_2, ring_2, 0)
+        lamb_2 = lamb_first(fc1_weight, fc1_moments, grad_2, 0, False, 2, factor)
         sums_1 = hold(sums_1)
-        grad_2 = ring_step(kept_2, sides_2, ring_2, 0)
-        ring_1 = ring_step(kept_1, sides_1, None, 3)
-        ring_1 = ring_step(kept_1, sides_1, ring_1, 2)
-        ring_1 = ring_step(kept_1, sides_1, ring_1, 1)
-        grad_1 = ring_step(kept_1, sides_1, ring_1, 0)
+        ring_1 = ring_step(own_1, sides_1, None, 3)
+        ring_1 = ring_step(own_1, sides_1, ring_1, 2)
+        ring_1 = ring_step(own_1, sides_1, ring_1, 1)
     else:
-        grad_3 = plain_grads(pair_3, half, wide_kind)
+        input_grad = give_back(input_low)
+        grad_3 = plain_grads(pair_3, half, wide_kind).T
+        lamb_3 = lamb_first(fc2_weight, fc2_moments, grad_3, 0, False, 3, factor)
         grad_2 = plain_grads(pair_2, half, wide_kind)
-        grad_1 = plain_grads(pair_1, lane_columns, first_kind)
-    input_grad = give_back(input_low)
-
-    grad_qkv = grad_1[:, : 3 * lane_columns].reshape(rows_own, 3, lane_columns)
-    grad_proj = grad_1[:, 3 * lane_columns :].T
-    grad_up = grad_2
-    grad_down = grad_3.T
+        lamb_2 = lamb_first(fc1_weight, fc1_moments, grad_2, 0, False, 2, factor)
+
     vector_terms = jnp.concatenate([sums_1[0:2], sums_2[2:3], sums_2[0:2], sums_2[3:4]], 0)
     if relative:
         vector_terms = lax.dot_general(
@@ -1207,47 +1330,55 @@
     small = butterfly(small.reshape(-1, 128), dp).reshape(-1)
     size = own_small.shape[0]
     bias_sum = jnp.where(first_half, small[:size], small[size : 2 * size])
-    grad_qkv_bias = bias_sum[: qkv_bias.size].reshape(qkv_bias.shape)
-    grad_up_bias = bias_sum[qkv_bias.size :]
-    grad_vectors = small[2 * size :].reshape(vectors.shape)
-
-    params = (qkv_weight, proj_weight, fc1_weight, fc2_weight, qkv_bias, fc1_bias, vectors)
-    moment_list = (
-        qkv_moments,
-        proj_moments,
-        fc1_moments,
-        fc2_moments,
-        qkv_bias_moments,
-        fc1_bias_moments,
-        vector_moments,
-    )
-    shares = (1.0, 1.0, 1.0, 1.0, lead_dp, lead_dp, lead_all)
-    summed = (grad_qkv, grad_proj, grad_up, grad_down, grad_qkv_bias, grad_up_bias, grad_vectors)
-    new_moments = []
-    updates = []
-    terms = []
-    for master, moments, gradient, factor in zip(params, moment_list, summed, shares):
-        first, second, update = lamb_parts(master, moments, gradient * grad_factor)
-        new_moments.append(jnp.stack([first, second]))
-        updates.append(update)
-        terms.append(jnp.sum(update * update) * factor)
-    terms = [
-        jnp.sum(master * master) * factor for master, factor in zip(params, shares)
-    ] + terms
-    terms = jnp.pad(jnp.stack(terms), (0, 114)).reshape(1, 128)
-    terms = butterfly(terms, dp)[0]
-    weight_sq, update_sq = terms[:7], terms[7:14]
-    trust = jnp.sqrt(weight_sq) / jnp.sqrt(update_sq + 1e-12)
-    new_params = [params[k] - LEARN_RATE * trust[k] * updates[k] for k in range(7)]
-    norms = jnp.stack([jnp.sqrt(weight_sq), jnp.sqrt(update_sq)])
+    small_grads = [
+        bias_sum[:qkv_columns].reshape(qkv_bias.shape),
+        bias_sum[None, qkv_columns:],
+        small[2 * size :].reshape(vectors.shape),
+    ]
+    small_masters = [qkv_bias, fc1_bias[None], vectors]
+    lane = jnp.arange(128)
+    is_bias = (lane == 4) | (lane == 5) | (lane == 11) | (lane == 12)
+    shares = jnp.where(is_bias, lead_dp, lead_all)[None]
+    *small_lamb, small_row = lamb_small(
+        small_masters,
+        [qkv_bias_moments, fc1_bias_moments, vector_moments],
+        small_grads,
+        shares,
+        factor,
+    )
+
+    if relative:
+        grad_1 = ring_step(own_1, sides_1, ring_1, 0)
+        lamb_p = lamb_first(proj_weight, proj_moments, grad_1, 3, True, 1, factor)
+    else:
+        grad_1 = plain_grads([pair_q, pair_p], lane_columns, first_kind)
+        lamb_p = lamb_first(
+            proj_weight, proj_moments, grad_1[:, qkv_columns:].T, 0, False, 1, factor
+        )
+    lamb_q = lamb_first(qkv_weight, qkv_moments, grad_1, 0, False, 0, factor)
+    rows = lamb_q[2] + lamb_p[2] + lamb_2[2] + lamb_3[2] + small_row
+    rows = butterfly(rows, dp)
+    last = lamb_last(
+        [qkv_weight, proj_weight, fc1_weight, fc2_weight, *small_masters],
+        [lamb_q[1], lamb_p[1], lamb_2[1], lamb_3[1], *small_lamb[3:]],
+        rows,
+        4,
+    )
+    new_params, copies, stats = last[:7], last[7:11], last[11]
     return (
         block_output,
         input_grad,
-        *new_params,
-        *new_moments,
-        *[p.astype(LOW) for p in new_params[:4]],
-        norms,
-        trust,
+        *new_params[:5],
+        new_params[5][0],
+        new_params[6],
+        lamb_q[0],
+        lamb_p[0],
+        lamb_2[0],
+        lamb_3[0],
+        *small_lamb[:3],
+        *copies,
+        jnp.concatenate([stats[0:1, :7], stats[0:1, 7:14]], 0),
+        stats[1, :7],
     )
 
 

time: 699 us -> 686 us (0.981)
  Pallas kernels: 292 us -> 335 us
  other arithmetic: 42.7 us -> 17.9 us
  waiting for transfers between devices: 207 us -> 183 us
  local copies, waits for them, and re-layouts: 40.9 us -> 58.8 us
  between operations: 10.6 us -> 1.87 us
  matrix products: 20.3 us -> 11.9 us
    pallas_call x37 -> x49, Pallas kernels: 292 us -> 335 us  [start(): result = run(*operands, *after)]
    unnamed x215 -> x203, local copies, waits for them, and re-layouts: 16.4 us -> 42.4 us
    ppermute x8, waiting for transfers between devices: 26.2 us -> 10 us  [butterfly(): value = value + lax.ppermute(value, 'dp', [(i, i ^ bit) for i in range(dp)])]
    another operation x11 -> x0, other arithmetic: 14.6 us -> none  [the longest x10 14 us: body(): new_moments.append(jnp.stack([first, second]))]
    ppermute x16, waiting for transfers between devices: 66 us -> 76.1 us  [over_x(): return lax.ppermute(v, 'tensor', [(0, 1), (1, 0)])]
    ppermute x9, waiting for transfers between devices: 52.3 us -> 44.2 us  [down_z(): lax.ppermute(v, 'dp', [(i, (i - 4) % self.dp) for i in range(self.dp)])]
    reduce_sum x5 -> x0, other arithmetic: 7.87 us -> none  [the longest x4 7.03 us: body(): terms.append(jnp.sum(update * update) * factor)]
    dot_general x2 -> x0, matrix products: 7.19 us -> none  [dot_t(): lax.dot_general(left, right, (((1,), (1,)), ((), ())), preferred_element_...]
  transfers between devices with their start and end apart: 73 -> 74, of which waited for: 29 -> 24; matrix products, arithmetic and copies ran while one was open for 10% -> 9% of each run, Pallas kernels for 35% -> 46%
where the time goes in v4:
time: 686 us; the launch traced here: 677 us
  Pallas kernels  335 us (49%)
  waiting for transfers between devices  183 us (27%)
  starting transfers between devices  68.5 us (10%)
  local copies, waits for them, and re-layouts  58.8 us (9%)
  other arithmetic  17.9 us (3%)
  matrix products  11.9 us (2%)
    pallas_call x49, Pallas kernels, start(): result = run(*operands, *after)  335 us
    ppermute x16, waiting for transfers between devices, over_x(): return lax.ppermute(v, 'tensor', [(0, 1), (1, 0)])  76.1 us
    ppermute x9, waiting for transfers between devices, down_z(): lax.ppermute(v, 'dp', [(i, (i - 4) % self.dp) for i in range(self.dp)])  44.2 us
    unnamed x203, local copies, waits for them, and re-layouts  42.4 us
    ppermute x9, starting transfers between devices, down_z(): lax.ppermute(v, 'dp', [(i, (i - 4) % self.dp) for i in range(self.dp)])  26.3 us
    ppermute x12, waiting for transfers between devices, over_y(): return lax.ppermute(v, 'dp', [(i, i ^ 2) for i in range(self.dp)])  23.7 us
    ppermute x9, waiting for transfers between devices, up_z(): lax.ppermute(v, 'dp', [(i, (i + 4) % self.dp) for i in range(self.dp)])  22.7 us
    ppermute x16, starting transfers between devices, over_x(): return lax.ppermute(v, 'tensor', [(0, 1), (1, 0)])  18 us
  transfers between devices with their start and end apart: 74, of which 24 were waited for; matrix products, arithmetic and copies ran while one was open for 9% of the time, Pallas kernels for 46%

profile of v4, /device:TPU:0, one launch (start us, length us, event | category | flops | bytes accessed | tf_op | source)
XLA Modules:
  0.0 676.8 jit_solution(14789752148826810457)
XLA Ops:
  26.0 9.6 %collective-permute-done.2.refs_4_.refs_2_ = bf16[80,1920]{1,0:T(8,128)(2,1)S(1)} collective-permute-done((bf16[80,1920]{1,0:T(8,128)(2,1)S(1)}, bf16[80,1920]{1,0:T(8,128)(2,1)S(1)}, u32[]{:S(2)}, u32[]{:S(2)}) %collective-permute-start.2) | collective-permute-done | bytes 307232 | tf_op jit(solution)/shard_map/ppermute | solution.py:987
  66.7 8.3 %collective-permute-done.10.refs_0_.refs_5_.refs_9_ = bf16[320,1920]{1,0:T(8,128)(2,1)} collective-permute-done((bf16[320,1920]{1,0:T(8,128)(2,1)}, bf16[320,1920]{1,0:T(8,128)(2,1)}, u32[]{:S(2)}, u32[]{:S(2)}) %collective-permute-start.10) | collective-permute-done | bytes 1228832 | tf_op jit(solution)/shard_map/ppermute | solution.py:978
  86.7 30.5 %collective-permute-done.19.refs_3_ = bf16[80,3200]{1,0:T(8,128)(2,1)S(1)} collective-permute-done((bf16[80,3200]{1,0:T(8,128)(2,1)S(1)}, bf16[80,3200]{1,0:T(8,128)(2,1)S(1)}, u32[]{:S(2)}, u32[]{:S(2)}) %collective-permute-start.19) | collective-permute-done | bytes 512032 | tf_op jit(solution)/shard_map/ppermute | solution.py:987
  131.8 13.8 %shard_map.367.refs_0_.refs_5_ = f32[576,3840]{1,0:T(8,128)} custom-call(bf16[576,1280]{1,0:T(8,128)(2,1)} %fusion.16.refs_0_, bf16[320,1920]{1,0:T(8,128)(2,1)} %shard_map.364.refs_2_.refs_1_, bf16[320,1920]{1,0:T(8,128)(2,1)} %collective-permute-done.7.refs_1_.refs_2_, bf16[320,1920]{1,0:T(8,128)(2,1)} %copy-done.63, bf16[320,1920]{1,0:T(8,128)(2,1)} %copy-done.65, ...), custom_call_target="tpu_custom_call" | custom-call | flops 128799997952 | tf_op jit(solution)/shard_map/pallas_call | solution.py:109
  145.6 19.6 %shard_map.368 = (bf16[576,3840]{1,0:T(8,128)(2,1)}, bf16[576,1280]{1,0:T(8,128)(2,1)}, f32[2,8,576]{2,1,0:T(8,128)}) custom-call(f32[576,3840]{1,0:T(8,128)} %shard_map.367.refs_0_.refs_5_, f32[576,640]{1,0:T(8,128)} %copy.100.refs_1_.refs_3_, f32[576,640]{1,0:T(8,128)} %copy.101.refs_2_.refs_4_, s32[576,1]{1,0:T(8,128)} %broadcast_in_dim.65.refs_3_.refs_5_, ...), custom_call_target="tpu_custom_call" | custom-call | flops 180319993856 | tf_op jit(solution)/shard_map/pallas_call | solution.py:109
  165.2 9.5 %collective-permute-done.21.refs_1_.refs_2_ = bf16[320,3200]{1,0:T(8,128)(2,1)} collective-permute-done((bf16[320,3200]{1,0:T(8,128)(2,1)}, bf16[320,3200]{1,0:T(8,128)(2,1)}, u32[]{:S(2)}, u32[]{:S(2)}) %collective-permute-start.21) | collective-permute-done | bytes 2048032 | tf_op jit(solution)/shard_map/ppermute | solution.py:984
  182.3 41.2 %collective-permute-done.36 = bf16[288,1280]{1,0:T(8,128)(2,1)S(1)} collective-permute-done((bf16[288,1280]{1,0:T(8,128)(2,1)S(1)}, bf16[288,1280]{1,0:T(8,128)(2,1)S(1)}, u32[]{:S(2)}, u32[]{:S(2)}) %collective-permute-start.36) | collective-permute-done | bytes 737312 | tf_op jit(solution)/shard_map/ppermute | solution.py:978
  238.8 10.2 %collective-permute-done.29.refs_6_ = bf16[320,1280]{1,0:T(8,128)(2,1)} collective-permute-done((bf16[320,1280]{1,0:T(8,128)(2,1)}, bf16[320,1280]{1,0:T(8,128)(2,1)}, u32[]{:S(2)}, u32[]{:S(2)}) %collective-permute-start.29) | collective-permute-done | bytes 819232 | tf_op jit(solution)/shard_map/ppermute | solution.py:984
  250.1 9.0 %shard_map.370 = (f32[576,1280]{1,0:T(8,128)}, bf16[576,1280]{1,0:T(8,128)(2,1)}) custom-call(bf16[576,1280]{1,0:T(8,128)(2,1)} %get-tuple-element.104.refs_0_.refs_3_, bf16[320,3200]{1,0:T(8,128)(2,1)} %shard_map.366.refs_14_.refs_1_, bf16[320,3200]{1,0:T(8,128)(2,1)} %collective-permute-done.21.refs_1_.refs_2_, bf16[320,3200]{1,0:T(8,128)(2,1)} %copy-done.61, ...), custom_call_target="tpu_custom_call" | custom-call | flops 90159996928 | tf_op jit(solution)/shard_map/pallas_call | solution.py:109
  259.9 15.5 %shard_map.371 = (f32[576,5120]{1,0:T(8,128)}, bf16[576,5120]{1,0:T(8,128)(2,1)}) custom-call(bf16[576,1280]{1,0:T(8,128)(2,1)} %get-tuple-element.108.refs_0_, bf16[320,3200]{1,0:T(8,128)(2,1)} %shard_map.366.refs_14_.refs_1_, bf16[320,3200]{1,0:T(8,128)(2,1)} %collective-permute-done.21.refs_1_.refs_2_, bf16[320,3200]{1,0:T(8,128)(2,1)} %copy-done.61, ...), custom_call_target="tpu_custom_call" | custom-call | flops 163759996928 | tf_op jit(solution)/shard_map/pallas_call | solution.py:109
  275.5 10.0 %shard_map.372.refs_11_ = bf16[640,5120]{1,0:T(8,128)(2,1)} custom-call(bf16[576,1280]{1,0:T(8,128)(2,1)} %get-tuple-element.276.refs_0_, bf16[576,5120]{1,0:T(8,128)(2,1)} %get-tuple-element.110.refs_1_.refs_0_, f32[576,5120]{1,0:T(8,128)} %get-tuple-element.111.refs_2_.refs_9_), custom_call_target="tpu_custom_call" | custom-call | flops 92000002048 | tf_op jit(solution)/shard_map/pallas_call | solution.py:109
  285.6 14.8 %shard_map.373.refs_3_.refs_0_ = bf16[576,1280]{1,0:T(8,128)(2,1)} custom-call(bf16[576,5120]{1,0:T(8,128)(2,1)} %get-tuple-element.110.refs_1_.refs_0_, bf16[160,5120]{1,0:T(8,128)(2,1)} %shard_map.363.refs_4_.refs_1_, bf16[160,5120]{1,0:T(8,128)(2,1)} %collective-permute-done.20.refs_6_.refs_2_, ...), custom_call_target="tpu_custom_call" | custom-call | flops 138000007168 | tf_op jit(solution)/shard_map/pallas_call | solution.py:109
  303.1 7.3 %shard_map.374 = (bf16[320,1280]{1,0:T(8,128)(2,1)}, bf16[640,1280]{1,0:T(8,128)(2,1)}, bf16[320,1280]{1,0:T(8,128)(2,1)}) custom-call(bf16[576,1280]{1,0:T(8,128)(2,1)} %get-tuple-element.276.refs_0_, bf16[576,5120]{1,0:T(8,128)(2,1)} %get-tuple-element.110.refs_1_.refs_0_, bf16[640,5120]{1,0:T(8,128)(2,1)} %copy-done.57, ...), custom_call_target="tpu_custom_call" | custom-call | flops 64399998976 | tf_op jit(solution)/shard_map/pallas_call | solution.py:109
  310.4 7.5 %shard_map.375 = (bf16[320,1280]{1,0:T(8,128)(2,1)}, bf16[320,1280]{1,0:T(8,128)(2,1)}, bf16[640,1280]{1,0:T(8,128)(2,1)}) custom-call(bf16[576,1280]{1,0:T(8,128)(2,1)} %get-tuple-element.276.refs_0_, bf16[576,5120]{1,0:T(8,128)(2,1)} %get-tuple-element.110.refs_1_.refs_0_, bf16[640,5120]{1,0:T(8,128)(2,1)} %copy-done.57, ...), custom_call_target="tpu_custom_call" | custom-call | flops 64399998976 | tf_op jit(solution)/shard_map/pallas_call | solution.py:109
  319.1 16.4 %shard_map.376 = (bf16[576,5120]{1,0:T(8,128)(2,1)}, f32[1,5120]{1,0:T(1,128)}) custom-call(bf16[576,1280]{1,0:T(8,128)(2,1)} %get-tuple-element.276.refs_0_, bf16[160,5120]{1,0:T(8,128)(2,1)} %shard_map.363.refs_4_.refs_1_, bf16[160,5120]{1,0:T(8,128)(2,1)} %collective-permute-done.20.refs_6_.refs_2_, ...), custom_call_target="tpu_custom_call" | custom-call | flops 174799994880 | tf_op jit(solution)/shard_map/pallas_call | solution.py:109
  335.5 9.8 %shard_map.377.refs_4_ = bf16[640,5120]{1,0:T(8,128)(2,1)} custom-call(bf16[576,1280]{1,0:T(8,128)(2,1)} %get-tuple-element.108.refs_0_, bf16[576,5120]{1,0:T(8,128)(2,1)} %get-tuple-element.118.refs_1_.refs_2_.refs_0_, bf16[576,5120]{1,0:T(8,128)(2,1)} %get-tuple-element.118.refs_1_.refs_2_.refs_0_), custom_call_target="tpu_custom_call" | custom-call | flops 92000002048 | tf_op jit(solution)/shard_map/pallas_call | solution.py:109
  346.0 10.5 %collective-permute-done.39.refs_3_ = bf16[640,1280]{1,0:T(8,128)(2,1)} collective-permute-done((bf16[640,1280]{1,0:T(8,128)(2,1)}, bf16[640,1280]{1,0:T(8,128)(2,1)}, u32[]{:S(2)}, u32[]{:S(2)}) %collective-permute-start.39) | collective-permute-done | bytes 1638432 | tf_op jit(solution)/shard_map/ppermute | solution.py:978
  367.2 20.7 %shard_map.380 = (f32[576,1280]{1,0:T(8,128)}, bf16[576,1280]{1,0:T(8,128)(2,1)}, f32[8,1280]{1,0:T(8,128)}) custom-call(bf16[576,5120]{1,0:T(8,128)(2,1)} %get-tuple-element.118.refs_1_.refs_2_.refs_0_, bf16[320,3200]{1,0:T(8,128)(2,1)} %shard_map.366.refs_14_.refs_1_, bf16[320,3200]{1,0:T(8,128)(2,1)} %collective-permute-done.21.refs_1_.refs_2_, ...), custom_call_target="tpu_custom_call" | custom-call | flops 199640006656 | tf_op jit(solution)/shard_map/pallas_call | solution.py:109
  393.0 7.3 %shard_map.382 = (bf16[320,1280]{1,0:T(8,128)(2,1)}, bf16[640,1280]{1,0:T(8,128)(2,1)}, bf16[320,1280]{1,0:T(8,128)(2,1)}) custom-call(bf16[576,1280]{1,0:T(8,128)(2,1)} %get-tuple-element.108.refs_0_, bf16[576,5120]{1,0:T(8,128)(2,1)} %get-tuple-element.118.refs_1_.refs_2_.refs_0_, bf16[640,5120]{1,0:T(8,128)(2,1)} %collective-permute-done.41.refs_2_, ...), custom_call_target="tpu_custom_call" | custom-call | flops 64399998976 | tf_op jit(solution)/shard_map/pallas_call | solution.py:109
  400.3 7.6 %shard_map.383 = (bf16[320,1280]{1,0:T(8,128)(2,1)}, bf16[320,1280]{1,0:T(8,128)(2,1)}, bf16[640,1280]{1,0:T(8,128)(2,1)}) custom-call(bf16[576,1280]{1,0:T(8,128)(2,1)} %get-tuple-element.108.refs_0_, bf16[576,5120]{1,0:T(8,128)(2,1)} %get-tuple-element.118.refs_1_.refs_2_.refs_0_, bf16[640,5120]{1,0:T(8,128)(2,1)} %collective-permute-done.41.refs_2_, ...), custom_call_target="tpu_custom_call" | custom-call | flops 64399998976 | tf_op jit(solution)/shard_map/pallas_call | solution.py:109
  409.9 6.0 shard_map.384.refs_7_.refs_2_
  418.3 27.4 %shard_map.386 = (bf16[576,3840]{1,0:T(8,128)(2,1)}, f32[1,3840]{1,0:T(1,128)}) custom-call(bf16[576,3840]{1,0:T(8,128)(2,1)} %get-tuple-element.105.refs_2_.refs_0_, f32[2,8,576]{2,1,0:T(8,128)} %get-tuple-element.122.refs_1_, bf16[576,1280]{1,0:T(8,128)(2,1)} %shard_map.384.refs_7_.refs_2_, f32[576,640]{1,0:T(8,128)} %copy.100.refs_1_.refs_3_, ...), custom_call_target="tpu_custom_call" | custom-call | flops 251160002560 | tf_op jit(solution)/shard_map/pallas_call | solution.py:109
  454.4 7.0 %shard_map.389.refs_4_ = bf16[640,2560]{1,0:T(8,128)(2,1)} custom-call(bf16[576,1280]{1,0:T(8,128)(2,1)} %fusion.16.refs_0_, bf16[576,3840]{1,0:T(8,128)(2,1)} %get-tuple-element.128.refs_4_.refs_1_.refs_2_.refs_0_, bf16[80,2560]{1,0:T(8,128)(2,1)} %shard_map.388.refs_2_), custom_call_target="tpu_custom_call" | custom-call | flops 64399998976 | tf_op jit(solution)/shard_map/pallas_call | solution.py:109
  463.8 7.9 %shard_map.390.refs_3_ = bf16[640,2560]{1,0:T(8,128)(2,1)} custom-call(bf16[576,1280]{1,0:T(8,128)(2,1)} %fusion.16.refs_0_, bf16[576,1280]{1,0:T(8,128)(2,1)} %get-tuple-element.123.refs_0_.refs_1_, bf16[576,3840]{1,0:T(8,128)(2,1)} %get-tuple-element.128.refs_4_.refs_1_.refs_2_.refs_0_, bf16[576,1280]{1,0:T(8,128)(2,1)} %get-tuple-element.104.refs_0_.refs_3_, ...), custom_call_target="tpu_custom_call" | custom-call | flops 64399998976 | tf_op jit(solution)/shard_map/pallas_call | solution.py:109
  473.7 7.9 %shard_map.391 = (bf16[320,1280]{1,0:T(8,128)(2,1)}, bf16[640,1280]{1,0:T(8,128)(2,1)}, bf16[320,1280]{1,0:T(8,128)(2,1)}) custom-call(bf16[576,1280]{1,0:T(8,128)(2,1)} %fusion.16.refs_0_, bf16[576,3840]{1,0:T(8,128)(2,1)} %get-tuple-element.128.refs_4_.refs_1_.refs_2_.refs_0_, bf16[640,2560]{1,0:T(8,128)(2,1)} %copy-done.59, ...), custom_call_target="tpu_custom_call" | custom-call | flops 73600000000 | tf_op jit(solution)/shard_map/pallas_call | solution.py:109
  491.9 8.9 %shard_map.393 = (bf16[320,1280]{1,0:T(8,128)(2,1)}, bf16[320,1280]{1,0:T(8,128)(2,1)}, bf16[640,1280]{1,0:T(8,128)(2,1)}) custom-call(bf16[576,1280]{1,0:T(8,128)(2,1)} %fusion.16.refs_0_, bf16[576,1280]{1,0:T(8,128)(2,1)} %get-tuple-element.123.refs_0_.refs_1_, bf16[576,3840]{1,0:T(8,128)(2,1)} %get-tuple-element.128.refs_4_.refs_1_.refs_2_.refs_0_, ...), custom_call_target="tpu_custom_call" | custom-call | flops 73600000000 | tf_op jit(solution)/shard_map/pallas_call | solution.py:109
  513.2 17.9 %shard_map.397 = (bf16[576,1280]{1,0:T(8,128)(2,1)}, f32[8,1280]{1,0:T(8,128)}) custom-call(bf16[576,3840]{1,0:T(8,128)(2,1)} %get-tuple-element.128.refs_4_.refs_1_.refs_2_.refs_0_, bf16[320,1920]{1,0:T(8,128)(2,1)} %shard_map.364.refs_2_.refs_1_, bf16[320,1920]{1,0:T(8,128)(2,1)} %collective-permute-done.7.refs_1_.refs_2_, bf16[320,1920]{1,0:T(8,128)(2,1)} %copy-done.63, ...), custom_call_target="tpu_custom_call" | custom-call | flops 165600002048 | tf_op jit(solution)/shard_map/pallas_call | solution.py:109
  541.6 5.6 shard_map.400
  597.8 12.0 %collective-permute-done.62.refs_6_ = bf16[80,2560]{1,0:T(8,128)(2,1)S(1)} collective-permute-done((bf16[80,2560]{1,0:T(8,128)(2,1)}, bf16[80,2560]{1,0:T(8,128)(2,1)S(1)}, u32[]{:S(2)}, u32[]{:S(2)}) %collective-permute-start.62) | collective-permute-done | bytes 409632 | tf_op jit(solution)/shard_map/ppermute | solution.py:990
  614.6 10.7 %collective-permute-done.63.refs_6_ = bf16[80,2560]{1,0:T(8,128)(2,1)S(1)} collective-permute-done((bf16[80,2560]{1,0:T(8,128)(2,1)}, bf16[80,2560]{1,0:T(8,128)(2,1)S(1)}, u32[]{:S(2)}, u32[]{:S(2)}) %collective-permute-start.63) | collective-permute-done | bytes 409632 | tf_op jit(solution)/shard_map/ppermute | solution.py:990
  646.0 9.1 %collective-permute-done.57 = bf16[288,1280]{1,0:T(8,128)(2,1)} collective-permute-done((bf16[288,1280]{1,0:T(8,128)(2,1)}, bf16[288,1280]{1,0:T(8,128)(2,1)}, u32[]{:S(2)}, u32[]{:S(2)}) %collective-permute-start.57) | collective-permute-done | bytes 737312 | tf_op jit(solution)/shard_map/ppermute | solution.py:978
  661.6 5.6 shard_map.411
  (449 shorter events, 269.9 us)
Async XLA Ops:
  7.9 55.3 %collective-permute-start = (bf16[288,1280]{1,0:T(8,128)(2,1)S(1)}, bf16[288,1280]{1,0:T(8,128)(2,1)}, u32[]{:S(2)}, u32[]{:S(2)}) collective-permute-start(bf16[288,1280]{1,0:T(8,128)(2,1)S(1)} %get-tuple-element.262), channel_id=1, source_target_pairs={{0,1},{1,0},{2,3},{3,2},{4,5},{5,4},{6,7},{7,6},{8,9},{9,8},{10,11... | collective-permute-start | bytes 2211848 | tf_op jit(solution)/shard_map/ppermute | solution.py:978
  13.2 45.7 %collective-permute-start.17 = (bf16[80,3200]{1,0:T(8,128)(2,1)}, bf16[80,3200]{1,0:T(8,128)(2,1)}, u32[]{:S(2)}, u32[]{:S(2)}) collective-permute-start(bf16[80,3200]{1,0:T(8,128)(2,1)} %pad_maximum_fusion.refs_0_), channel_id=1, source_target_pairs={{0,24},{2,26},{4,28},{6,30},{8,0},{10,2},{12,4},{14,6},{16,8},{18,... | collective-permute-start | bytes 1536008 | tf_op jit(solution)/shard_map/ppermute | solution.py:987
  24.4 33.9 %collective-permute-start.16 = (f32[4480]{0:T(1024)S(1)}, f32[4480]{0:T(1024)S(1)}, u32[]{:S(2)}, u32[]{:S(2)}) collective-permute-start(f32[4480]{0:T(1024)S(1)} %pad_maximum_fusion.2), channel_id=1, source_target_pairs={{0,1},{1,0},{2,3},{3,2},{4,5},{5,4},{6,7},{7,6},{8,9},{9,8},{10,11... | collective-permute-start | bytes 53768 | tf_op jit(solution)/shard_map/ppermute | solution.py:978
  66.6 50.6 %collective-permute-start.20 = (bf16[160,5120]{1,0:T(8,128)(2,1)}, bf16[160,5120]{1,0:T(8,128)(2,1)}, u32[]{:S(2)}, u32[]{:S(2)}) collective-permute-start(bf16[160,5120]{1,0:T(8,128)(2,1)} %shard_map.363.refs_4_.refs_1_), channel_id=1, source_target_pairs={{0,24},{2,26},{4,28},{6,30},{8,0},{10,2},{12,4},{14,6},{16,8},{18,... | collective-permute-start | bytes 4915208 | tf_op jit(solution)/shard_map/ppermute | solution.py:987
  79.0 38.8 %collective-permute-start.11 = (bf16[320,1280]{1,0:T(8,128)(2,1)}, bf16[320,1280]{1,0:T(8,128)(2,1)S(1)}, u32[]{:S(2)}, u32[]{:S(2)}) collective-permute-start(bf16[320,1280]{1,0:T(8,128)(2,1)} %get-tuple-element.102.refs_7_), channel_id=1, source_target_pairs={{0,4},{2,6},{4,0},{6,2},{8,12},{10,14},{12,8},{14,10},{16,20},{18,... | collective-permute-start | bytes 2457608 | tf_op jit(solution)/shard_map/ppermute | solution.py:984
  80.1 37.1 %collective-permute-start.19 = (bf16[80,3200]{1,0:T(8,128)(2,1)S(1)}, bf16[80,3200]{1,0:T(8,128)(2,1)S(1)}, u32[]{:S(2)}, u32[]{:S(2)}) collective-permute-start(bf16[80,3200]{1,0:T(8,128)(2,1)S(1)} %collective-permute-done.18.refs_2_), channel_id=1, source_target_pairs={{0,24},{2,26},{4,28},{6,30},{8,0},{10,2},{12,4},{14,6},{16,8},{18,... | collective-permute-start | bytes 1536008 | tf_op jit(solution)/shard_map/ppermute | solution.py:987
  84.4 33.3 %collective-permute-start.14 = (bf16[320,640]{1,0:T(8,128)(2,1)}, bf16[320,640]{1,0:T(8,128)(2,1)S(1)}, u32[]{:S(2)}, u32[]{:S(2)}) collective-permute-start(bf16[320,640]{1,0:T(8,128)(2,1)} %get-tuple-element.103), channel_id=1, source_target_pairs={{0,1},{1,0},{2,3},{3,2},{4,5},{5,4},{6,7},{7,6},{8,9},{9,8},{10,11... | collective-permute-start | bytes 1228808 | tf_op jit(solution)/shard_map/ppermute | solution.py:978
  86.7 36.6 %collective-permute-start.8 = (bf16[320,1920]{1,0:T(8,128)(2,1)S(1)}, bf16[320,1920]{1,0:T(8,128)(2,1)S(1)}, u32[]{:S(2)}, u32[]{:S(2)}) collective-permute-start(bf16[320,1920]{1,0:T(8,128)(2,1)S(1)} %copy-done.62), channel_id=1, source_target_pairs={{0,2},{2,0},{4,6},{6,4},{8,10},{10,8},{12,14},{14,12},{16,18},{18,... | collective-permute-start | bytes 3686408 | tf_op jit(solution)/shard_map/ppermute | solution.py:981
  123.3 58.7 %collective-permute-start.28 = (bf16[160,5120]{1,0:T(8,128)(2,1)}, bf16[160,5120]{1,0:T(8,128)(2,1)}, u32[]{:S(2)}, u32[]{:S(2)}) collective-permute-start(bf16[160,5120]{1,0:T(8,128)(2,1)} %collective-permute-done.20.refs_6_.refs_2_), channel_id=1, source_target_pairs={{0,24},{2,26},{4,28},{6,30},{8,0},{10,2},{12,4},{14,6},{16,8},{18,... | collective-permute-start | bytes 4915208 | tf_op jit(solution)/shard_map/ppermute | solution.py:987
  127.9 46.9 %collective-permute-start.21 = (bf16[320,3200]{1,0:T(8,128)(2,1)}, bf16[320,3200]{1,0:T(8,128)(2,1)}, u32[]{:S(2)}, u32[]{:S(2)}) collective-permute-start(bf16[320,3200]{1,0:T(8,128)(2,1)} %shard_map.366.refs_14_.refs_1_), channel_id=1, source_target_pairs={{0,4},{2,6},{4,0},{6,2},{8,12},{10,14},{12,8},{14,10},{16,20},{18,... | collective-permute-start | bytes 6144008 | tf_op jit(solution)/shard_map/ppermute | solution.py:984
  129.4 46.6 %collective-permute-start.24 = (bf16[320,3200]{1,0:T(8,128)(2,1)}, bf16[320,3200]{1,0:T(8,128)(2,1)}, u32[]{:S(2)}, u32[]{:S(2)}) collective-permute-start(bf16[320,3200]{1,0:T(8,128)(2,1)} %shard_map.366.refs_14_.refs_1_), channel_id=1, source_target_pairs={{0,1},{1,0},{2,3},{3,2},{4,5},{5,4},{6,7},{7,6},{8,9},{9,8},{10,11... | collective-permute-start | bytes 6144008 | tf_op jit(solution)/shard_map/ppermute | solution.py:978
  179.7 43.9 %collective-permute-start.25 = (bf16[320,1920]{1,0:T(8,128)(2,1)}, bf16[320,1920]{1,0:T(8,128)(2,1)}, u32[]{:S(2)}, u32[]{:S(2)}) collective-permute-start(bf16[320,1920]{1,0:T(8,128)(2,1)} %get-tuple-element.106), channel_id=1, source_target_pairs={{0,1},{1,0},{2,3},{3,2},{4,5},{5,4},{6,7},{7,6},{8,9},{9,8},{10,11... | collective-permute-start | bytes 3686408 | tf_op jit(solution)/shard_map/ppermute | solution.py:978
  180.2 47.3 %collective-permute-start.22 = (bf16[320,3200]{1,0:T(8,128)(2,1)S(1)}, bf16[320,3200]{1,0:T(8,128)(2,1)S(1)}, u32[]{:S(2)}, u32[]{:S(2)}) collective-permute-start(bf16[320,3200]{1,0:T(8,128)(2,1)S(1)} %copy-done.60), channel_id=1, source_target_pairs={{0,2},{2,0},{4,6},{6,4},{8,10},{10,8},{12,14},{14,12},{16,18},{18,... | collective-permute-start | bytes 6144008 | tf_op jit(solution)/shard_map/ppermute | solution.py:981
  180.4 43.2 %collective-permute-start.36 = (bf16[288,1280]{1,0:T(8,128)(2,1)S(1)}, bf16[288,1280]{1,0:T(8,128)(2,1)S(1)}, u32[]{:S(2)}, u32[]{:S(2)}) collective-permute-start(bf16[288,1280]{1,0:T(8,128)(2,1)S(1)} %get-tuple-element.260), channel_id=1, source_target_pairs={{0,1},{1,0},{2,3},{3,2},{4,5},{5,4},{6,7},{7,6},{8,9},{9,8},{10,11... | collective-permute-start | bytes 2211848 | tf_op jit(solution)/shard_map/ppermute | solution.py:978
  181.9 56.9 %collective-permute-start.31 = (bf16[160,5120]{1,0:T(8,128)(2,1)}, bf16[160,5120]{1,0:T(8,128)(2,1)}, u32[]{:S(2)}, u32[]{:S(2)}) collective-permute-start(bf16[160,5120]{1,0:T(8,128)(2,1)} %collective-permute-done.28.refs_11_.refs_3_), channel_id=1, source_target_pairs={{0,24},{2,26},{4,28},{6,30},{8,0},{10,2},{12,4},{14,6},{16,8},{18,... | collective-permute-start | bytes 4915208 | tf_op jit(solution)/shard_map/ppermute | solution.py:987
  182.3 66.7 %collective-permute-start.23 = (bf16[320,3200]{1,0:T(8,128)(2,1)}, bf16[320,3200]{1,0:T(8,128)(2,1)}, u32[]{:S(2)}, u32[]{:S(2)}) collective-permute-start(bf16[320,3200]{1,0:T(8,128)(2,1)} %collective-permute-done.21.refs_1_.refs_2_), channel_id=1, source_target_pairs={{0,2},{2,0},{4,6},{6,4},{8,10},{10,8},{12,14},{14,12},{16,18},{18,... | collective-permute-start | bytes 6144008 | tf_op jit(solution)/shard_map/ppermute | solution.py:981
  238.8 46.8 %collective-permute-start.32 = (bf16[160,5120]{1,0:T(8,128)(2,1)}, bf16[160,5120]{1,0:T(8,128)(2,1)}, u32[]{:S(2)}, u32[]{:S(2)}) collective-permute-start(bf16[160,5120]{1,0:T(8,128)(2,1)} %shard_map.363.refs_4_.refs_1_), channel_id=1, source_target_pairs={{0,2},{2,0},{4,6},{6,4},{8,10},{10,8},{12,14},{14,12},{16,18},{18,... | collective-permute-start | bytes 4915208 | tf_op jit(solution)/shard_map/ppermute | solution.py:981
  249.0 36.6 %collective-permute-start.33 = (bf16[160,5120]{1,0:T(8,128)(2,1)}, bf16[160,5120]{1,0:T(8,128)(2,1)}, u32[]{:S(2)}, u32[]{:S(2)}) collective-permute-start(bf16[160,5120]{1,0:T(8,128)(2,1)} %collective-permute-done.20.refs_6_.refs_2_), channel_id=1, source_target_pairs={{0,2},{2,0},{4,6},{6,4},{8,10},{10,8},{12,14},{14,12},{16,18},{18,... | collective-permute-start | bytes 4915208 | tf_op jit(solution)/shard_map/ppermute | solution.py:981
  249.0 36.6 %collective-permute-start.34 = (bf16[160,5120]{1,0:T(8,128)(2,1)}, bf16[160,5120]{1,0:T(8,128)(2,1)}, u32[]{:S(2)}, u32[]{:S(2)}) collective-permute-start(bf16[160,5120]{1,0:T(8,128)(2,1)} %collective-permute-done.28.refs_11_.refs_3_), channel_id=1, source_target_pairs={{0,2},{2,0},{4,6},{6,4},{8,10},{10,8},{12,14},{14,12},{16,18},{18,... | collective-permute-start | bytes 4915208 | tf_op jit(solution)/shard_map/ppermute | solution.py:981
  249.5 36.1 %collective-permute-start.35 = (bf16[160,5120]{1,0:T(8,128)(2,1)}, bf16[160,5120]{1,0:T(8,128)(2,1)}, u32[]{:S(2)}, u32[]{:S(2)}) collective-permute-start(bf16[160,5120]{1,0:T(8,128)(2,1)} %collective-permute-done.31.refs_4_), channel_id=1, source_target_pairs={{0,2},{2,0},{4,6},{6,4},{8,10},{10,8},{12,14},{14,12},{16,18},{18,... | collective-permute-start | bytes 4915208 | tf_op jit(solution)/shard_map/ppermute | solution.py:981
  317.9 38.5 %collective-permute-start.39 = (bf16[640,1280]{1,0:T(8,128)(2,1)}, bf16[640,1280]{1,0:T(8,128)(2,1)}, u32[]{:S(2)}, u32[]{:S(2)}) collective-permute-start(bf16[640,1280]{1,0:T(8,128)(2,1)} %get-tuple-element.116), channel_id=1, source_target_pairs={{0,1},{1,0},{2,3},{3,2},{4,5},{5,4},{6,7},{7,6},{8,9},{9,8},{10,11... | collective-permute-start | bytes 4915208 | tf_op jit(solution)/shard_map/ppermute | solution.py:978
  318.5 38.2 %collective-permute-start.38 = (bf16[640,1280]{1,0:T(8,128)(2,1)}, bf16[640,1280]{1,0:T(8,128)(2,1)}, u32[]{:S(2)}, u32[]{:S(2)}) collective-permute-start(bf16[640,1280]{1,0:T(8,128)(2,1)} %get-tuple-element.115), channel_id=1, source_target_pairs={{0,4},{2,6},{4,0},{6,2},{8,12},{10,14},{12,8},{14,10},{16,20},{18,... | collective-permute-start | bytes 4915208 | tf_op jit(solution)/shard_map/ppermute | solution.py:984
  345.3 47.7 %collective-permute-start.41 = (bf16[640,5120]{1,0:T(8,128)(2,1)}, bf16[640,5120]{1,0:T(8,128)(2,1)}, u32[]{:S(2)}, u32[]{:S(2)}) collective-permute-start(bf16[640,5120]{1,0:T(8,128)(2,1)} %shard_map.377.refs_4_), channel_id=1, source_target_pairs={{0,2},{2,0},{4,6},{6,4},{8,10},{10,8},{12,14},{14,12},{16,18},{18,... | collective-permute-start | bytes 19660808 | tf_op jit(solution)/shard_map/ppermute | solution.py:981
  359.6 31.2 %collective-permute-start.42 = (bf16[320,1280]{1,0:T(8,128)(2,1)}, bf16[320,1280]{1,0:T(8,128)(2,1)}, u32[]{:S(2)}, u32[]{:S(2)}) collective-permute-start(bf16[320,1280]{1,0:T(8,128)(2,1)} %get-tuple-element.119.refs_2_), channel_id=1, source_target_pairs={{0,1},{1,0},{2,3},{3,2},{4,5},{5,4},{6,7},{7,6},{8,9},{9,8},{10,11... | collective-permute-start | bytes 2457608 | tf_op jit(solution)/shard_map/ppermute | solution.py:978
  407.9 39.3 %collective-permute-start.46 = (bf16[640,1280]{1,0:T(8,128)(2,1)}, bf16[640,1280]{1,0:T(8,128)(2,1)}, u32[]{:S(2)}, u32[]{:S(2)}) collective-permute-start(bf16[640,1280]{1,0:T(8,128)(2,1)} %get-tuple-element.130), channel_id=1, source_target_pairs={{0,1},{1,0},{2,3},{3,2},{4,5},{5,4},{6,7},{7,6},{8,9},{9,8},{10,11... | collective-permute-start | bytes 4915208 | tf_op jit(solution)/shard_map/ppermute | solution.py:978
  408.4 38.7 %collective-permute-start.45 = (bf16[640,1280]{1,0:T(8,128)(2,1)}, bf16[640,1280]{1,0:T(8,128)(2,1)}, u32[]{:S(2)}, u32[]{:S(2)}) collective-permute-start(bf16[640,1280]{1,0:T(8,128)(2,1)} %get-tuple-element.129), channel_id=1, source_target_pairs={{0,4},{2,6},{4,0},{6,2},{8,12},{10,14},{12,8},{14,10},{16,20},{18,... | collective-permute-start | bytes 4915208 | tf_op jit(solution)/shard_map/ppermute | solution.py:984
  418.3 33.7 %collective-permute-start.49 = (bf16[80,2560]{1,0:T(8,128)(2,1)}, bf16[80,2560]{1,0:T(8,128)(2,1)}, u32[]{:S(2)}, u32[]{:S(2)}) collective-permute-start(bf16[80,2560]{1,0:T(8,128)(2,1)} %shard_map.385.refs_7_), channel_id=1, source_target_pairs={{0,8},{2,10},{4,12},{6,14},{8,16},{10,18},{12,20},{14,22},{16,24},... | collective-permute-start | bytes 1228808 | tf_op jit(solution)/shard_map/ppermute | solution.py:990
  450.4 31.2 %collective-permute-start.47 = (bf16[320,1280]{1,0:T(8,128)(2,1)}, bf16[320,1280]{1,0:T(8,128)(2,1)}, u32[]{:S(2)}, u32[]{:S(2)}) collective-permute-start(bf16[320,1280]{1,0:T(8,128)(2,1)} %get-tuple-element.133.refs_7_), channel_id=1, source_target_pairs={{0,1},{1,0},{2,3},{3,2},{4,5},{5,4},{6,7},{7,6},{8,9},{9,8},{10,11... | collective-permute-start | bytes 2457608 | tf_op jit(solution)/shard_map/ppermute | solution.py:978
  461.5 40.5 %collective-permute-start.52 = (bf16[80,2560]{1,0:T(8,128)(2,1)}, bf16[80,2560]{1,0:T(8,128)(2,1)}, u32[]{:S(2)}, u32[]{:S(2)}) collective-permute-start(bf16[80,2560]{1,0:T(8,128)(2,1)} %shard_map.388.refs_2_), channel_id=1, source_target_pairs={{0,8},{2,10},{4,12},{6,14},{8,16},{10,18},{12,20},{14,22},{16,24},... | collective-permute-start | bytes 1228808 | tf_op jit(solution)/shard_map/ppermute | solution.py:990
  500.8 37.5 %collective-permute-start.55 = (bf16[640,1280]{1,0:T(8,128)(2,1)}, bf16[640,1280]{1,0:T(8,128)(2,1)}, u32[]{:S(2)}, u32[]{:S(2)}) collective-permute-start(bf16[640,1280]{1,0:T(8,128)(2,1)} %get-tuple-element.142), channel_id=1, source_target_pairs={{0,1},{1,0},{2,3},{3,2},{4,5},{5,4},{6,7},{7,6},{8,9},{9,8},{10,11... | collective-permute-start | bytes 4915208 | tf_op jit(solution)/shard_map/ppermute | solution.py:978
  501.4 37.2 %collective-permute-start.54 = (bf16[640,1280]{1,0:T(8,128)(2,1)}, bf16[640,1280]{1,0:T(8,128)(2,1)}, u32[]{:S(2)}, u32[]{:S(2)}) collective-permute-start(bf16[640,1280]{1,0:T(8,128)(2,1)} %get-tuple-element.141), channel_id=1, source_target_pairs={{0,4},{2,6},{4,0},{6,2},{8,12},{10,14},{12,8},{14,10},{16,20},{18,... | collective-permute-start | bytes 4915208 | tf_op jit(solution)/shard_map/ppermute | solution.py:984
  588.1 52.7 %collective-permute-start.40 = (bf16[288,1280]{1,0:T(8,128)(2,1)}, bf16[288,1280]{1,0:T(8,128)(2,1)}, u32[]{:S(2)}, u32[]{:S(2)}) collective-permute-start(bf16[288,1280]{1,0:T(8,128)(2,1)} %get-tuple-element.121), channel_id=1, source_target_pairs={{0,1},{1,0},{2,3},{3,2},{4,5},{5,4},{6,7},{7,6},{8,9},{9,8},{10,11... | collective-permute-start | bytes 2211848 | tf_op jit(solution)/shard_map/ppermute | solution.py:978
  (133 other events, 1361.2 us)

commit v5 on v4

--- a/solution.py
+++ b/solution.py
@@ -620,23 +620,93 @@
     )(own_a, own_b, from_y, from_x, second_x, second_y, *extra)
 
 
-def cut_far(side, across, split):
+def cut_far(side, across, near, after=()):
     rows, columns = side.shape
+    far, at = [], 0
+    for start, stop in near:
+        if start > at:
+            far.append((at, start))
+        at = stop
+    if at < columns:
+        far.append((at, columns))
 
     def kernel(a, b, out_a, out_b):
-        out_a[...] = a[:, :split]
-        out_b[...] = b[:, split:]
-
+        for source, out, ranges in ((a, out_a, near), (b, out_b, far)):
+            at = 0
+            for start, stop in ranges:
+                out[:, at : at + stop - start] = source[:, start:stop]
+                at += stop - start
+
+    widths = [sum(stop - start for start, stop in ranges) for ranges in (near, far)]
     return call(
         kernel,
         (1,),
         [whole(side.shape)] * 2,
-        [whole((rows, split)), whole((rows, columns - split))],
-        [
-            jax.ShapeDtypeStruct((rows, split), side.dtype),
-            jax.ShapeDtypeStruct((rows, columns - split), side.dtype),
-        ],
+        [whole((rows, w)) for w in widths],
+        [jax.ShapeDtypeStruct((rows, w), side.dtype) for w in widths],
+        after=after,
     )(side, across)
+
+
+def pack_columns(values, after=()):
+    rows = values[0].shape[0]
+    columns = sum(v.shape[1] for v in values)
+
+    def kernel(*refs):
+        at = 0
+        for ref in refs[:-1]:
+            n = ref.shape[1]
+            refs[-1][:, at : at + n] = ref[...].astype(LOW)
+            at += n
+
+    return call(
+        kernel,
+        (1,),
+        [whole(v.shape) for v in values],
+        whole((rows, columns)),
+        jax.ShapeDtypeStruct((rows, columns), LOW),
+        after=after,
+    )(*values)
+
+
+def hold(*values, after=()):
+    def kernel(*refs):
+        total = refs[0][...]
+        for ref in refs[1:-1]:
+            total = total + ref[...]
+        refs[-1][...] = total
+
+    shape = values[0].shape
+    return call(
+        kernel,
+        (1,),
+        [whole(shape)] * len(values),
+        whole(shape),
+        jax.ShapeDtypeStruct(shape, values[0].dtype),
+        us=1,
+        after=after,
+    )(*values)
+
+
+def place_halves(mine, theirs, slot, after=()):
+    shape = (2, 1, *mine.shape)
+
+    def kernel(slot_ref, mine_ref, their_ref, out_ref):
+        for k in range(2):
+
+            @pl.when(slot_ref[0] == k)
+            def _(k=k):
+                out_ref[k, 0] = mine_ref[...]
+                out_ref[1 - k, 0] = their_ref[...]
+
+    return call(
+        kernel,
+        (1,),
+        [pl.BlockSpec(memory_space=pltpu.SMEM), whole(mine.shape), whole(theirs.shape)],
+        whole(shape),
+        jax.ShapeDtypeStruct(shape, mine.dtype),
+        after=after,
+    )(slot.reshape(1), mine, theirs)
 
 
 def unshuffle(values, shuffle):
@@ -667,52 +737,41 @@
     return row + jnp.where(lane == 7 + index, update_sq, 0.0)
 
 
-def lamb_first(master, moments, grad, column, turned, index, factor):
-    shape = master.shape
-
-    def kernel(p_ref, m_ref, g_ref, new_ref, u_ref, row_ref):
-        if len(shape) == 2:
-            g = g_ref[...]
-            g = (g.T if turned else g) * factor
-            p = p_ref[...]
-            first, second, update = lamb_parts(p, (m_ref[0], m_ref[1]), g)
-            new_ref[0] = first
-            new_ref[1] = second
-            u_ref[...] = update
-            row_ref[...] = lamb_row(index, jnp.sum(p * p), jnp.sum(update * update))
-            return
+def lamb_first(items, grad, factor, rows=()):
+    count = len(items)
+
+    def kernel(*refs):
+        p_refs, m_refs = refs[:count], refs[count : 2 * count]
+        g_ref = refs[2 * count]
+        row_refs = refs[2 * count + 1 : 2 * count + 1 + len(rows)]
+        outs = refs[2 * count + 1 + len(rows) :]
         row = jnp.zeros((1, 128), F32)
-        for k in range(shape[1]):
-            g = g_ref[:, k * shape[2] : (k + 1) * shape[2]] * factor
-            p = p_ref[:, k, :]
-            first, second, update = lamb_parts(p, (m_ref[0, :, k, :], m_ref[1, :, k, :]), g)
-            new_ref[0, :, k, :] = first
-            new_ref[1, :, k, :] = second
-            u_ref[:, k, :] = update
-            row = row + lamb_row(index, jnp.sum(p * p), jnp.sum(update * update))
-        row_ref[...] = row
-
-    if turned:
-        columns = shape[0]
-    else:
-        columns = shape[-1] * (shape[1] if len(shape) == 3 else 1)
-    rows = shape[1] if turned else shape[0]
+        for ref in row_refs:
+            row = row + ref[...]
+        for n, (place, master, _, at) in enumerate(items):
+            width = master.shape[-1]
+            for k in range(1 if master.ndim == 2 else master.shape[0]):
+                cut = () if master.ndim == 2 else (k,)
+                g = g_ref[:, at + k * width : at + (k + 1) * width] * factor
+                p = p_refs[n][(*cut, ...)]
+                old = (m_refs[n][(0, *cut, ...)], m_refs[n][(1, *cut, ...)])
+                first, second, update = lamb_parts(p, old, g)
+                outs[n][(0, *cut, ...)] = first
+                outs[n][(1, *cut, ...)] = second
+                outs[count + n][(*cut, ...)] = update
+                row = row + lamb_row(place, jnp.sum(p * p), jnp.sum(update * update))
+        outs[2 * count][...] = row
+
+    operands = [*[i[1] for i in items], *[i[2] for i in items], grad, *rows]
+    shapes = [i[2].shape for i in items] + [i[1].shape for i in items] + [(1, 128)]
     return call(
         kernel,
         (1,),
-        [
-            whole(shape),
-            whole(moments.shape),
-            pl.BlockSpec((rows, columns), lambda j: (0, column)),
-        ],
-        [whole(moments.shape), whole(shape), whole((1, 128))],
-        [
-            jax.ShapeDtypeStruct(moments.shape, F32),
-            jax.ShapeDtypeStruct(shape, F32),
-            jax.ShapeDtypeStruct((1, 128), F32),
-        ],
+        [whole(v.shape) for v in operands],
+        [whole(v) for v in shapes],
+        [jax.ShapeDtypeStruct(v, F32) for v in shapes],
         us=4,
-    )(master, moments, grad)
+    )(*operands)
 
 
 def lamb_small(masters, moments, grads, shares, factor):
@@ -728,14 +787,14 @@
             if len(m_refs[k].shape) == 2:
                 old = (m_refs[k][0:1, :], m_refs[k][1:2, :])
             else:
-                old = (m_refs[k][0], m_refs[k][1])
+                old = (m_refs[k][:, 0, :], m_refs[k][:, 1, :])
             first, second, update = lamb_parts(p, old, g_refs[k][...] * factor)
             if len(m_refs[k].shape) == 2:
                 outs[k][0:1, :] = first
                 outs[k][1:2, :] = second
             else:
-                outs[k][0] = first
-                outs[k][1] = second
+                outs[k][:, 0, :] = first
+                outs[k][:, 1, :] = second
             outs[count + k][...] = update
             row = row + lamb_row(4 + k, jnp.sum(p * p), jnp.sum(update * update))
         outs[2 * count][...] = row * share_ref[...]
@@ -751,30 +810,30 @@
     )(*operands)
 
 
-def lamb_last(masters, updates, rows, copies):
+def lamb_last(masters, updates, row, copies):
     count = len(masters)
 
     def kernel(*refs):
         p_refs, u_refs, row_ref = refs[:count], refs[count : 2 * count], refs[2 * count]
         outs = refs[2 * count + 1 :]
-        row = row_ref[...]
-        stats = outs[count + copies]
-        stats[0:1, :] = jnp.sqrt(row)
+        norms, trust_ref = outs[count + copies :]
+        master_sq, update_sq = row_ref[:, :count], row_ref[:, count : 2 * count]
+        trust = jnp.sqrt(master_sq) / jnp.sqrt(update_sq + 1e-12)
+        norms[0:1, :] = jnp.sqrt(master_sq)
+        norms[1:2, :] = jnp.sqrt(update_sq)
+        trust_ref[...] = trust
         for k in range(count):
-            master_sq, update_sq = row[:, k : k + 1], row[:, 7 + k : 8 + k]
-            trust = jnp.sqrt(master_sq) / jnp.sqrt(update_sq + 1e-12)
-            stats[1:2, k : k + 1] = trust
-            if len(p_refs[k].shape) == 3:
-                trust = trust[:, :, None]
-            new = p_refs[k][...] - LEARN_RATE * trust * u_refs[k][...]
-            outs[k][...] = new
-            if k < copies:
-                outs[count + k][...] = new.astype(LOW)
+            for c in range(1 if len(p_refs[k].shape) == 2 else p_refs[k].shape[0]):
+                cut = (...,) if len(p_refs[k].shape) == 2 else (c, ...)
+                new = p_refs[k][cut] - LEARN_RATE * trust[:, k : k + 1] * u_refs[k][cut]
+                outs[k][cut] = new
+                if k < copies:
+                    outs[count + k][cut] = new.astype(LOW)
 
     shapes = [jax.ShapeDtypeStruct(v.shape, F32) for v in masters]
     shapes += [jax.ShapeDtypeStruct(v.shape, LOW) for v in masters[:copies]]
-    shapes += [jax.ShapeDtypeStruct((2, 128), F32)]
-    operands = [*masters, *updates, rows]
+    shapes += [jax.ShapeDtypeStruct((2, count), F32), jax.ShapeDtypeStruct((1, count), F32)]
+    operands = [*masters, *updates, row]
     return call(
         kernel,
         (1,),
@@ -783,20 +842,6 @@
         shapes,
         us=8,
     )(*operands)
-
-
-def hold(values):
-    def kernel(in_ref, out_ref):
-        out_ref[...] = in_ref[...]
-
-    return call(
-        kernel,
-        (1,),
-        [whole(values.shape)],
-        whole(values.shape),
-        jax.ShapeDtypeStruct(values.shape, values.dtype),
-        us=1,
-    )(values)
 
 
 def stack_early(shard, side, across, far, after=()):
@@ -989,6 +1034,9 @@
     def up_z(self, v):
         return lax.ppermute(v, "dp", [(i, (i + 4) % self.dp) for i in range(self.dp)])
 
+    def exchange(self, v, bit):
+        return lax.ppermute(v, "dp", [(i, i ^ bit) for i in range(self.dp)])
+
     def order(self):
         i = lax.axis_index("dp")
         z, y, c = i // 4, (i // 2) % 2, i % 2
@@ -1005,47 +1053,54 @@
             held.append(self.down_z(held[-1]))
         return held
 
-    def far(self, side, across, split):
-        a, b = cut_far(side, across, split)
+    def far(self, side, across, near, after=()):
+        a, b = cut_far(side, across, near, after)
         return self.over_y(a), self.over_x(b)
 
-    def gathered(self, held, side, across, far_a, far_b):
-        core = self.over_core
-        side_core = core(side)
-        return Gathered(
-            [held, across, core(held), core(across)],
-            [side, far_a, side_core, core(far_a)],
-            [side, far_b, side_core, core(far_b)],
-            far_a.shape[1],
-        )
-
-    def stacked(self, held):
-        rows = held[0].shape[0] // 2
-        held = held + [self.over_core(v) for v in held]
+    def both_cores(self, values):
+        return [(v, self.over_core(v)) for v in values]
+
+    def stacked(self, pairs):
+        rows = pairs[0][0].shape[0] // 2
         cuts = [
             (dc * self.ring + dz, dy * rows, rows)
             for dc in range(2)
             for dy in range(2)
             for dz in range(self.ring)
         ]
-        return Stacked(held, cuts)
+        return Stacked([p[0] for p in pairs] + [p[1] for p in pairs], cuts)
 
 
 class Gathered:
-    def __init__(self, own, other_a, other_b, split):
-        self.own, self.other_a, self.other_b, self.split = own, other_a, other_b, split
+    def __init__(self, own, other, far=None, near=()):
+        self.own, self.other, self.far, self.near = own, other, far, near
+
+    def pieces(self, column):
+        if self.far is None:
+            return [(v, column) for v in self.other]
+        side, side_core = self.other
+        place, spent, before = 1, column, 0
+        for start, stop in self.near:
+            if start <= column < stop:
+                place, spent = 0, before + column - start
+            before += stop - start
+            if place and stop <= column:
+                spent -= stop - start
+        a, a_core = self.far[place]
+        return [(side, column), (a, spent), (side_core, column), (a_core, spent)]
 
     def parts(self, block, first, count):
-        columns = self.own[0].shape[1]
-        split = self.split // block
         sets = [([(v, first) for v in self.own], None, count)]
-        count_a = max(0, min(first + count, split) - first)
-        if count_a:
-            sets.append(([(v, first) for v in self.other_a], None, count_a))
-        if count > count_a:
-            start = max(first, split)
-            pieces = [(v, start if v.shape[1] == columns else start - split) for v in self.other_b]
-            sets.append((pieces, None, count - count_a))
+        last = None
+        for b in range(first, first + count):
+            here = [(v, c // block) for v, c in self.pieces(b * block)]
+            if last is not None and all(
+                v is w and c == d + sets[-1][2] for (v, c), (w, d) in zip(here, last)
+            ):
+                sets[-1] = (last, None, sets[-1][2] + 1)
+            else:
+                last = here
+                sets.append((here, None, 1))
         return Parts(sets, block)
 
 
@@ -1104,43 +1159,62 @@
     hidden = fc1_weight.shape[1]
     grad_factor = float(block_input.shape[0] * block_input.shape[1] * dp * LEN) ** (-0.5)
 
-    shard_1 = qkv_weight.astype(LOW).reshape(rows_own, 3 * lane_columns)
-    shard_2 = jnp.concatenate([fc1_weight.astype(LOW), proj_weight.astype(LOW).T], 1)
-    shard_3 = fc2_weight.astype(LOW).T
+    def row_view(v):
+        return jnp.swapaxes(v, -1, -2)
+
+    qkv_view, qkv_moments_view = jnp.swapaxes(qkv_weight, 0, 1), jnp.swapaxes(qkv_moments, 1, 2)
+    proj_view, proj_moments_view = row_view(proj_weight), row_view(proj_moments)
+    fc2_view, fc2_moments_view = row_view(fc2_weight), row_view(fc2_moments)
+
+    local_rows = block_input.shape[2]
+
+    def half_of(both, place):
+        return lax.dynamic_index_in_dim(both[:, 0], place, 0, keepdims=False)
+
+    input_came = lanes.over_x(half_of(block_input, 1 - slot))
+    cot_came = lanes.over_x(half_of(out_cotangent, 1 - slot))
+
+    shard_1 = jnp.concatenate([qkv_view[k].astype(LOW) for k in range(3)], 1)
+    shard_3 = fc2_view.astype(LOW)
     half = hidden // 2
     if relative:
         ring_1 = lanes.ring_down(shard_1)
         side_3, across_3 = lanes.over_x(shard_3), lanes.over_y(shard_3)
         far_3 = lanes.over_y(side_3)
-        late_3 = [stack_early(shard_3, side_3, across_3, far_3, after=[ring_1[2]])]
-        held_1 = stack_rows(ring_1)
-        sides_w1 = lanes.over_x(held_1), lanes.over_y(held_1)
-        fars_w1 = lanes.far(*sides_w1, 2 * lane_columns)
-        w1 = lanes.gathered(held_1, *sides_w1, *fars_w1)
-        for _ in range(3):
-            late_3.append(lanes.down_z(late_3[-1]))
+        shard_2 = pack_columns([fc1_weight, proj_view], after=[ring_1[2]])
+        held_1 = stack_rows(ring_1, after=[input_came, cot_came, side_3, across_3, far_3])
         ring_2 = lanes.ring_down(shard_2)
-        held_2 = stack_rows(ring_2, after=[*fars_w1, late_3[1]])
-        sides_w2 = lanes.over_x(held_2), lanes.over_y(held_2)
-        w3 = lanes.stacked(late_3)
-        w_down = w3.parts(half)
+        core_held_1 = lanes.over_core(held_1)
+        sides_1 = lanes.over_x(held_1), lanes.over_y(held_1)
+        near_1 = [(0, 2 * lane_columns)]
+        fars_1 = lanes.far(*sides_1, near_1, after=[core_held_1])
+        late_3 = [stack_early(shard_3, side_3, across_3, far_3, after=[ring_2[3]])]
+        late_came = lanes.down_z(late_3[0])
+        core_late = lanes.over_core(late_3[0])
+        cores_1 = lanes.both_cores(sides_1)
+        held_2 = stack_rows(ring_2, after=[*fars_1, cores_1[0][1], cores_1[1][1]])
+        sides_2 = lanes.over_x(held_2), lanes.over_y(held_2)
+        core_held_2 = lanes.over_core(held_2)
+        w1 = Gathered(
+            [held_1, sides_1[1], core_held_1, cores_1[1][1]],
+            cores_1[0],
+            lanes.both_cores(fars_1),
+            near_1,
+        )
     else:
 
         def plain(shard):
             held = lax.all_gather(shard, "dp", axis=0, tiled=True)
-            side = lanes.over_x(held)
-            return Gathered([held], [side], [side], half)
-
+            return Gathered([held], [lanes.over_x(held)])
+
+        shard_2 = jnp.concatenate([fc1_weight.astype(LOW), proj_view.astype(LOW)], 1)
         w1, w2, w3 = plain(shard_1), plain(shard_2), plain(shard_3)
         w_down = w3.parts(half, 0, 2)
     w_qkv = w1.parts(lane_columns, 0, 3)
 
-    def own_row(both):
-        mine = lax.dynamic_index_in_dim(both[:, 0], slot, 0, keepdims=False)
-        theirs = lax.dynamic_index_in_dim(both[:, 0], 1 - slot, 0, keepdims=False)
-        return jnp.concatenate([mine, lanes.over_x(theirs)], 0)
-
-    local_rows = block_input.shape[2]
+    def own_row(both, came):
+        return jnp.concatenate([half_of(both, slot), came], 0)
+
     biases = jnp.concatenate([qkv_bias.reshape(-1), fc1_bias])
     other_biases = lanes.over_x(biases)
     cut = qkv_bias.size
@@ -1179,21 +1253,19 @@
             precision=lax.Precision.HIGHEST,
             preferred_element_type=F32,
         )
-        row_low = dot(own_row(block_input), shuffle).astype(LOW)
-        cot_low = dot(own_row(out_cotangent), shuffle).astype(LOW)
+        row_low = dot(own_row(block_input, input_came), shuffle).astype(LOW)
+        cot_low = dot(own_row(out_cotangent, cot_came), shuffle).astype(LOW)
     else:
         vec = vectors
-        row_low = own_row(block_input)
-        cot_low = own_row(out_cotangent)
+        row_low = own_row(block_input, input_came)
+        cot_low = own_row(out_cotangent, cot_came)
 
     def give_back(values_low):
         if relative:
             mine, theirs = unshuffle(values_low, shuffle)
         else:
             mine, theirs = values_low[:local_rows], values_low[local_rows:]
-        theirs = lanes.over_x(theirs)
-        swap = slot == 0
-        return jnp.stack([jnp.where(swap, mine, theirs), jnp.where(swap, theirs, mine)])[:, None]
+        return mine, lanes.over_x(theirs)
 
     wide_kind = [(0, j) for j in range(4)]
     first_kind = [(0, 0), (0, 1), (0, 2), (1, 0), (0, 3), (0, 4), (0, 5), (1, 1)]
@@ -1228,33 +1300,72 @@
         both = whole_grad[:, :hidden] + lanes.over_x(whole_grad[:, hidden:])
         return lax.psum_scatter(both, "dp", scatter_dimension=0, tiled=True)
 
+    qkv_columns = 3 * lane_columns
+
+    def small_sums(sums_1, sums_2, sum_qkv, sum_up):
+        terms = jnp.concatenate([sums_1[0:2], sums_2[2:3], sums_2[0:2], sums_2[3:4]], 0)
+        if relative:
+            terms = lax.dot_general(
+                terms,
+                shuffle.astype(F32),
+                (((1,), (1,)), ((), ())),
+                precision=lax.Precision.HIGHEST,
+                preferred_element_type=F32,
+            )
+        own = jnp.concatenate([sum_qkv[0, :qkv_columns], sum_up[0, :hidden]])
+        other = jnp.concatenate([sum_qkv[0, qkv_columns:], sum_up[0, hidden:]])
+        first_half = slot == 0
+        return jnp.concatenate(
+            [
+                jnp.where(first_half, own, other),
+                jnp.where(first_half, other, own),
+                terms.reshape(-1),
+            ]
+        ).reshape(-1, 128)
+
     normed1, _ = norm_parts(row_low.astype(F32))
     first_in = (normed1 * vec[0] + vec[1]).astype(LOW)
     down_grad = (cot_low.astype(F32) * token_weight).astype(LOW)
     mixed = qkv_forward(first_in, w_qkv, bias_qkv, list(range(6)))
-    qkv, attended, lse = attention_forward(mixed, cosine, sine, key_code, query_code, groups)
-    before_proj = []
+    before_attention = [core_held_2, core_late, cot_came] if relative else []
+    qkv, attended, lse = attention_forward(
+        mixed, cosine, sine, key_code, query_code, groups, after=before_attention
+    )
     if relative:
-        fars_w2 = lanes.far(*sides_w2, half)
-        w2 = lanes.gathered(held_2, *sides_w2, *fars_w2)
-        before_proj = [late_3[2]]
+        late_3.append(hold(late_came))
+        late_3.append(lanes.down_z(late_3[1]))
+        late_came = lanes.down_z(late_3[2])
+        late_cores = [(late_3[0], core_late), *lanes.both_cores(late_3[1:])]
+        before_far = [late_cores[1][1]]
+        near_2 = [(0, half), (hidden, hidden + lane_columns)]
+        fars_2 = lanes.far(*sides_2, near_2, after=before_far)
+        hold(query_code, after=fars_2)
+        cores_2 = lanes.both_cores(sides_2)
+        w2 = Gathered(
+            [held_2, sides_2[1], core_held_2, cores_2[1][1]],
+            cores_2[0],
+            lanes.both_cores(fars_2),
+            near_2,
+        )
     w_proj = w2.parts(lane_columns, hidden // lane_columns, 1)
     w_up = w2.parts(half, 0, 2)
-    hidden1, second_in = proj_forward(attended, w_proj, row_low, vec, after=before_proj)
+    hidden1, second_in = proj_forward(attended, w_proj, row_low, vec)
     upward, activated = up_forward(second_in, w_up, bias_up)
     pair_3 = [(down_grad, activated)]
     if relative:
-        came_3 = send_grads(pair_3, half, wide_kind, 10)
+        late_cores += lanes.both_cores([hold(late_came)])
+        w_down = lanes.stacked(late_cores).parts(half)
+        came_3 = send_grads(pair_3, half, wide_kind, 60)
     result = down_forward(activated, w_down, hidden1, vec)
 
     if relative:
         own_3, later_3, first_3 = wide_grads(pair_3, came_3)
     up_grad, sum_up = down_backward(down_grad, w_down, upward)
     pair_2 = [(second_in, up_grad)]
+    output_halves = give_back(result)
     if relative:
         came_2 = send_grads(pair_2, half, wide_kind, 10)
         sides_3 = send_second(later_3, first_3)
-    block_output = give_back(result)
     hidden1_grad, branch_grad, sums_2 = up_backward(
         up_grad, w_up, hidden1, cot_low, token_weight, vec
     )
@@ -1264,6 +1375,7 @@
     attn_grad = proj_backward(branch_grad, w_proj)
     if relative:
         ring_3 = ring_step(own_3, sides_3, ring_3, 2)
+    block_output = place_halves(*output_halves, slot)
     mixed_grad, sum_qkv = attention_backward(
         qkv, lse, attn_grad, cosine, sine, key_code, query_code, groups
     )
@@ -1285,50 +1397,43 @@
         own_1, later_1 = (part_a[0], part_b[0]), (part_a[2], part_b[1])
         first_1 = first_y, lanes.over_x(part_b[2])
         grad_3 = ring_step(own_3, sides_3, ring_3, 0)
-        lamb_3 = lamb_first(fc2_weight, fc2_moments, grad_3, 0, True, 3, factor)
+        lamb_3 = lamb_first([(3, fc2_view, fc2_moments_view, 0)], grad_3, factor)
         ring_2 = ring_step(own_2, sides_2, ring_2, 2)
     input_low, sums_1 = qkv_backward(
         mixed_grad, w_qkv, list(range(6)), row_low, hidden1_grad, vec
     )
+    input_halves = give_back(input_low)
+    small = small_sums(sums_1, sums_2, sum_qkv, sum_up)
     if relative:
+        small = hold(small)
+        came = lanes.over_x(small)
         ring_2 = ring_step(own_2, sides_2, ring_2, 1)
+        small = hold(small, came)
+        came = lanes.over_core(small)
         sides_1 = send_second(later_1, first_1)
-        input_grad = give_back(input_low)
+        small = hold(small, came)
+        came = lanes.over_y(small)
         grad_2 = ring_step(own_2, sides_2, ring_2, 0)
-        lamb_2 = lamb_first(fc1_weight, fc1_moments, grad_2, 0, False, 2, factor)
-        sums_1 = hold(sums_1)
+        small = hold(small, came)
+        came = lanes.exchange(small, 4)
+    else:
+        grad_3 = plain_grads(pair_3, half, wide_kind)
+        lamb_3 = lamb_first([(3, fc2_view, fc2_moments_view, 0)], grad_3, factor)
+        grad_2 = plain_grads(pair_2, half, wide_kind)
+    lamb_2 = lamb_first([(2, fc1_weight, fc1_moments, 0)], grad_2, factor)
+    if relative:
+        small = hold(small, came)
+        came = lanes.exchange(small, 8)
         ring_1 = ring_step(own_1, sides_1, None, 3)
+        small = hold(small, came)
         ring_1 = ring_step(own_1, sides_1, ring_1, 2)
         ring_1 = ring_step(own_1, sides_1, ring_1, 1)
-    else:
-        input_grad = give_back(input_low)
-        grad_3 = plain_grads(pair_3, half, wide_kind).T
-        lamb_3 = lamb_first(fc2_weight, fc2_moments, grad_3, 0, False, 3, factor)
-        grad_2 = plain_grads(pair_2, half, wide_kind)
-        lamb_2 = lamb_first(fc1_weight, fc1_moments, grad_2, 0, False, 2, factor)
-
-    vector_terms = jnp.concatenate([sums_1[0:2], sums_2[2:3], sums_2[0:2], sums_2[3:4]], 0)
-    if relative:
-        vector_terms = lax.dot_general(
-            vector_terms,
-            shuffle.astype(F32),
-            (((1,), (1,)), ((), ())),
-            precision=lax.Precision.HIGHEST,
-            preferred_element_type=F32,
-        )
-    qkv_columns = 3 * lane_columns
-    own_small = jnp.concatenate([sum_qkv[0, :qkv_columns], sum_up[0, :hidden]])
-    other_small = jnp.concatenate([sum_qkv[0, qkv_columns:], sum_up[0, hidden:]])
+
+    if not relative:
+        small = butterfly(small, dp)
+    small = small.reshape(-1)
     first_half = slot == 0
-    small = jnp.concatenate(
-        [
-            jnp.where(first_half, own_small, other_small),
-            jnp.where(first_half, other_small, own_small),
-            vector_terms.reshape(-1),
-        ]
-    )
-    small = butterfly(small.reshape(-1, 128), dp).reshape(-1)
-    size = own_small.shape[0]
+    size = qkv_columns + hidden
     bias_sum = jnp.where(first_half, small[:size], small[size : 2 * size])
     small_grads = [
         bias_sum[:qkv_columns].reshape(qkv_bias.shape),
@@ -1341,44 +1446,57 @@
     shares = jnp.where(is_bias, lead_dp, lead_all)[None]
     *small_lamb, small_row = lamb_small(
         small_masters,
-        [qkv_bias_moments, fc1_bias_moments, vector_moments],
+        [
+            jnp.swapaxes(qkv_bias_moments, 0, 1),
+            fc1_bias_moments,
+            jnp.swapaxes(vector_moments, 0, 1),
+        ],
         small_grads,
         shares,
         factor,
     )
 
     if relative:
+        input_grad = place_halves(*input_halves, slot)
         grad_1 = ring_step(own_1, sides_1, ring_1, 0)
-        lamb_p = lamb_first(proj_weight, proj_moments, grad_1, 3, True, 1, factor)
     else:
+        input_grad = place_halves(*input_halves, slot)
         grad_1 = plain_grads([pair_q, pair_p], lane_columns, first_kind)
-        lamb_p = lamb_first(
-            proj_weight, proj_moments, grad_1[:, qkv_columns:].T, 0, False, 1, factor
-        )
-    lamb_q = lamb_first(qkv_weight, qkv_moments, grad_1, 0, False, 0, factor)
-    rows = lamb_q[2] + lamb_p[2] + lamb_2[2] + lamb_3[2] + small_row
-    rows = butterfly(rows, dp)
+    q_moments, p_moments, q_update, p_update, row = lamb_first(
+        [(0, qkv_view, qkv_moments_view, 0), (1, proj_view, proj_moments_view, qkv_columns)],
+        grad_1,
+        factor,
+        [lamb_2[2], lamb_3[2], small_row],
+    )
+    row = butterfly(row, dp)
     last = lamb_last(
-        [qkv_weight, proj_weight, fc1_weight, fc2_weight, *small_masters],
-        [lamb_q[1], lamb_p[1], lamb_2[1], lamb_3[1], *small_lamb[3:]],
-        rows,
+        [qkv_view, proj_view, fc1_weight, fc2_view, *small_masters],
+        [q_update, p_update, lamb_2[1], lamb_3[1], *small_lamb[3:]],
+        row,
         4,
     )
-    new_params, copies, stats = last[:7], last[7:11], last[11]
+    new_params, copies, norms, trust = last[:7], last[7:11], last[11], last[12]
+    new_weights, copies = [
+        [jnp.swapaxes(v[0], 0, 1), row_view(v[1]), v[2], row_view(v[3])]
+        for v in (new_params, copies)
+    ]
     return (
         block_output,
         input_grad,
-        *new_params[:5],
+        *new_weights,
+        new_params[4],
         new_params[5][0],
         new_params[6],
-        lamb_q[0],
-        lamb_p[0],
+        jnp.swapaxes(q_moments, 1, 2),
+        row_view(p_moments),
         lamb_2[0],
-        lamb_3[0],
-        *small_lamb[:3],
+        row_view(lamb_3[0]),
+        jnp.swapaxes(small_lamb[0], 0, 1),
+        small_lamb[1],
+        jnp.swapaxes(small_lamb[2], 0, 1),
         *copies,
-        jnp.concatenate([stats[0:1, :7], stats[0:1, 7:14]], 0),
-        stats[1, :7],
+        norms,
+        trust[0],
     )
 
 

time: 686 us -> 638 us (0.930)
  waiting for transfers between devices: 183 us -> 115 us
  starting transfers between devices: 68.5 us -> 91.8 us
  Pallas kernels: 335 us -> 350 us
  local copies, waits for them, and re-layouts: 58.8 us -> 44.5 us
    ppermute x16 -> x17, waiting for transfers between devices: 76.1 us -> 30.8 us  [over_x(): return lax.ppermute(v, 'tensor', [(0, 1), (1, 0)])]
    ppermute x9, waiting for transfers between devices: 44.2 us -> 20.4 us  [down_z(): lax.ppermute(v, 'dp', [(i, (i - 4) % self.dp) for i in range(self.dp)])]
    unnamed x203 -> x140, local copies, waits for them, and re-layouts: 42.4 us -> 26.9 us
    pallas_call x49 -> x59, Pallas kernels: 335 us -> 350 us  [start(): result = run(*operands, *after)]
    ppermute x9, starting transfers between devices: 26.3 us -> 36.6 us  [down_z(): lax.ppermute(v, 'dp', [(i, (i - 4) % self.dp) for i in range(self.dp)])]
    ppermute x12 -> x13, waiting for transfers between devices: 23.7 us -> 29.6 us  [over_y(): return lax.ppermute(v, 'dp', [(i, i ^ 2) for i in range(self.dp)])]
    ppermute x12 -> x13, starting transfers between devices: 11.1 us -> 14.9 us  [over_y(): return lax.ppermute(v, 'dp', [(i, i ^ 2) for i in range(self.dp)])]
    ppermute x16 -> x17, starting transfers between devices: 18 us -> 20.1 us  [over_x(): return lax.ppermute(v, 'tensor', [(0, 1), (1, 0)])]
  transfers between devices with their start and end apart: 74 -> 74, of which waited for: 24 -> 25; matrix products, arithmetic and copies ran while one was open for 9% -> 6% of each run, Pallas kernels for 46% -> 51%
where the time goes in v5:
time: 638 us; the launch traced here: 629 us
  Pallas kernels  350 us (55%)
  waiting for transfers between devices  115 us (18%)
  starting transfers between devices  91.8 us (14%)
  local copies, waits for them, and re-layouts  44.5 us (7%)
  other arithmetic  14.4 us (2%)
  matrix products  12 us (2%)
    pallas_call x59, Pallas kernels, start(): result = run(*operands, *after)  350 us
    ppermute x9, starting transfers between devices, down_z(): lax.ppermute(v, 'dp', [(i, (i - 4) % self.dp) for i in range(self.dp)])  36.6 us
    ppermute x17, waiting for transfers between devices, over_x(): return lax.ppermute(v, 'tensor', [(0, 1), (1, 0)])  30.8 us
    ppermute x13, waiting for transfers between devices, over_y(): return lax.ppermute(v, 'dp', [(i, i ^ 2) for i in range(self.dp)])  29.6 us
    unnamed x140, local copies, waits for them, and re-layouts  26.9 us
    ppermute x9, waiting for transfers between devices, down_z(): lax.ppermute(v, 'dp', [(i, (i - 4) % self.dp) for i in range(self.dp)])  20.4 us
    ppermute x17, starting transfers between devices, over_x(): return lax.ppermute(v, 'tensor', [(0, 1), (1, 0)])  20.1 us
    ppermute x9, waiting for transfers between devices, up_z(): lax.ppermute(v, 'dp', [(i, (i + 4) % self.dp) for i in range(self.dp)])  19.4 us
  transfers between devices with their start and end apart: 74, of which 25 were waited for; matrix products, arithmetic and copies ran while one was open for 6% of the time, Pallas kernels for 51%

profile of v5, /device:TPU:0, one launch (start us, length us, event | category | flops | bytes accessed | tf_op | source)
XLA Modules:
  0.0 628.6 jit_solution(14637849990323030935)
XLA Ops:
  41.0 8.5 %collective-permute-done.refs_4_ = bf16[288,1280]{1,0:T(8,128)(2,1)S(1)} collective-permute-done((bf16[288,1280]{1,0:T(8,128)(2,1)}, bf16[288,1280]{1,0:T(8,128)(2,1)S(1)}, u32[]{:S(2)}, u32[]{:S(2)}) %collective-permute-start) | collective-permute-done | bytes 737312 | tf_op jit(solution)/shard_map/ppermute | solution.py:1023
  71.6 9.9 %collective-permute-done.19.refs_2_ = bf16[80,3200]{1,0:T(8,128)(2,1)S(1)} collective-permute-done((bf16[80,3200]{1,0:T(8,128)(2,1)S(1)}, bf16[80,3200]{1,0:T(8,128)(2,1)S(1)}, u32[]{:S(2)}, u32[]{:S(2)}) %collective-permute-start.19) | collective-permute-done | bytes 512032 | tf_op jit(solution)/shard_map/ppermute | solution.py:1032
  120.8 13.7 %shard_map.368.refs_0_.refs_8_ = f32[576,3840]{1,0:T(8,128)} custom-call(bf16[576,1280]{1,0:T(8,128)(2,1)} %fusion.16.refs_0_, bf16[320,1920]{1,0:T(8,128)(2,1)} %shard_map.364.refs_3_.refs_1_, bf16[320,1920]{1,0:T(8,128)(2,1)} %copy-done.36, bf16[320,1920]{1,0:T(8,128)(2,1)} %copy-done.37, bf16[320,1920]{1,0:T(8,128)(2,1)} %copy-done.38, ...), custom_call_target="tpu_custom_call" | custom-call | flops 128799997952 | tf_op jit(solution)/shard_map/pallas_call | solution.py:109
  135.8 19.7 %shard_map.369 = (bf16[576,3840]{1,0:T(8,128)(2,1)}, bf16[576,1280]{1,0:T(8,128)(2,1)}, f32[2,8,576]{2,1,0:T(8,128)}) custom-call(f32[576,3840]{1,0:T(8,128)} %shard_map.368.refs_0_.refs_8_, f32[576,640]{1,0:T(8,128)} %copy.49.refs_1_.refs_3_, f32[576,640]{1,0:T(8,128)} %copy.50.refs_2_.refs_4_, s32[576,1]{1,0:T(8,128)} %broadcast_in_dim.57.refs_3_.refs_5_, ...), custom_call_target="tpu_custom_call" | custom-call | flops 180319993856 | tf_op jit(solution)/shard_map/pallas_call | solution.py:109
  179.2 22.0 %collective-permute-done.28.refs_1_.refs_6_ = bf16[320,1920]{1,0:T(8,128)(2,1)} collective-permute-done((bf16[320,1920]{1,0:T(8,128)(2,1)}, bf16[320,1920]{1,0:T(8,128)(2,1)}, u32[]{:S(2)}, u32[]{:S(2)}) %collective-permute-start.28) | collective-permute-done | bytes 1228832 | tf_op jit(solution)/shard_map/ppermute | solution.py:1029
  201.2 5.0 multiply_convert_fusion
  213.6 9.0 %shard_map.373 = (f32[576,1280]{1,0:T(8,128)}, bf16[576,1280]{1,0:T(8,128)(2,1)}) custom-call(bf16[576,1280]{1,0:T(8,128)(2,1)} %get-tuple-element.104.refs_0_.refs_3_, bf16[320,3200]{1,0:T(8,128)(2,1)} %shard_map.367.refs_14_.refs_1_, bf16[320,3200]{1,0:T(8,128)(2,1)} %collective-permute-done.23.refs_1_.refs_2_, bf16[320,3200]{1,0:T(8,128)(2,1)} %copy-done.32, ...), custom_call_target="tpu_custom_call" | custom-call | flops 90159996928 | tf_op jit(solution)/shard_map/pallas_call | solution.py:109
  223.6 15.4 %shard_map.374 = (f32[576,5120]{1,0:T(8,128)}, bf16[576,5120]{1,0:T(8,128)(2,1)}) custom-call(bf16[576,1280]{1,0:T(8,128)(2,1)} %get-tuple-element.108.refs_0_, bf16[320,3200]{1,0:T(8,128)(2,1)} %shard_map.367.refs_14_.refs_1_, bf16[320,3200]{1,0:T(8,128)(2,1)} %collective-permute-done.23.refs_1_.refs_2_, bf16[320,3200]{1,0:T(8,128)(2,1)} %copy-done.32, ...), custom_call_target="tpu_custom_call" | custom-call | flops 163759996928 | tf_op jit(solution)/shard_map/pallas_call | solution.py:109
  239.0 7.5 %collective-permute-done.34.refs_0_ = bf16[160,5120]{1,0:T(8,128)(2,1)} collective-permute-done((bf16[160,5120]{1,0:T(8,128)(2,1)}, bf16[160,5120]{1,0:T(8,128)(2,1)}, u32[]{:S(2)}, u32[]{:S(2)}) %collective-permute-start.34) | collective-permute-done | bytes 1638432 | tf_op jit(solution)/shard_map/ppermute | solution.py:1032
  249.3 9.8 %shard_map.376.refs_11_ = bf16[640,5120]{1,0:T(8,128)(2,1)} custom-call(bf16[576,1280]{1,0:T(8,128)(2,1)} %get-tuple-element.208.refs_0_, bf16[576,5120]{1,0:T(8,128)(2,1)} %get-tuple-element.110.refs_1_.refs_0_, bf16[160,5120]{1,0:T(8,128)(2,1)} %shard_map.375.refs_2_.refs_4_), custom_call_target="tpu_custom_call" | custom-call | flops 552000028672 | tf_op jit(solution)/shard_map/pallas_call | solution.py:109
  259.6 14.8 %shard_map.377.refs_3_.refs_0_ = bf16[576,1280]{1,0:T(8,128)(2,1)} custom-call(bf16[576,5120]{1,0:T(8,128)(2,1)} %get-tuple-element.110.refs_1_.refs_0_, bf16[160,5120]{1,0:T(8,128)(2,1)} %shard_map.366.refs_8_.refs_1_, bf16[160,5120]{1,0:T(8,128)(2,1)} %shard_map.370.refs_3_.refs_2_, bf16[160,5120]{1,0:T(8,128)(2,1)} %collective-permute-done.33.refs_3_, ...), custom_call_target="tpu_custom_call" | custom-call | flops 138000007168 | tf_op jit(solution)/shard_map/pallas_call | solution.py:109
  277.1 7.5 %shard_map.378 = (bf16[320,1280]{1,0:T(8,128)(2,1)}, bf16[640,1280]{1,0:T(8,128)(2,1)}, bf16[320,1280]{1,0:T(8,128)(2,1)}) custom-call(bf16[576,1280]{1,0:T(8,128)(2,1)} %get-tuple-element.208.refs_0_, bf16[576,5120]{1,0:T(8,128)(2,1)} %get-tuple-element.110.refs_1_.refs_0_, bf16[640,5120]{1,0:T(8,128)(2,1)} %copy-done.29, ...), custom_call_target="tpu_custom_call" | custom-call | flops 64399998976 | tf_op jit(solution)/shard_map/pallas_call | solution.py:109
  284.5 7.6 %shard_map.379 = (bf16[320,1280]{1,0:T(8,128)(2,1)}, bf16[320,1280]{1,0:T(8,128)(2,1)}, bf16[640,1280]{1,0:T(8,128)(2,1)}) custom-call(bf16[576,1280]{1,0:T(8,128)(2,1)} %get-tuple-element.208.refs_0_, bf16[576,5120]{1,0:T(8,128)(2,1)} %get-tuple-element.110.refs_1_.refs_0_, bf16[640,5120]{1,0:T(8,128)(2,1)} %copy-done.29, ...), custom_call_target="tpu_custom_call" | custom-call | flops 64399998976 | tf_op jit(solution)/shard_map/pallas_call | solution.py:109
  293.6 16.4 %shard_map.380 = (bf16[576,5120]{1,0:T(8,128)(2,1)}, f32[1,5120]{1,0:T(1,128)}) custom-call(bf16[576,1280]{1,0:T(8,128)(2,1)} %get-tuple-element.208.refs_0_, bf16[160,5120]{1,0:T(8,128)(2,1)} %shard_map.366.refs_8_.refs_1_, bf16[160,5120]{1,0:T(8,128)(2,1)} %shard_map.370.refs_3_.refs_2_, bf16[160,5120]{1,0:T(8,128)(2,1)} %collective-permute-done.33.refs_3_, ...), custom_call_target="tpu_custom_call" | custom-call | flops 174799994880 | tf_op jit(solution)/shard_map/pallas_call | solution.py:109
  310.0 5.6 shard_map.381
  315.6 9.8 %shard_map.382.refs_4_ = bf16[640,5120]{1,0:T(8,128)(2,1)} custom-call(bf16[576,1280]{1,0:T(8,128)(2,1)} %get-tuple-element.108.refs_0_, bf16[576,5120]{1,0:T(8,128)(2,1)} %get-tuple-element.114.refs_2_.refs_1_.refs_0_, bf16[288,1280]{1,0:T(8,128)(2,1)} %get-tuple-element.115.refs_2_.refs_1_), custom_call_target="tpu_custom_call" | custom-call | flops 92000002048 | tf_op jit(solution)/shard_map/pallas_call | solution.py:109
  335.3 20.7 %shard_map.384 = (f32[576,1280]{1,0:T(8,128)}, bf16[576,1280]{1,0:T(8,128)(2,1)}, f32[8,1280]{1,0:T(8,128)}) custom-call(bf16[576,5120]{1,0:T(8,128)(2,1)} %get-tuple-element.114.refs_2_.refs_1_.refs_0_, bf16[320,3200]{1,0:T(8,128)(2,1)} %shard_map.367.refs_14_.refs_1_, bf16[320,3200]{1,0:T(8,128)(2,1)} %collective-permute-done.23.refs_1_.refs_2_, ...), custom_call_target="tpu_custom_call" | custom-call | flops 199640006656 | tf_op jit(solution)/shard_map/pallas_call | solution.py:109
  358.9 4.7 collective-permute-done.41.refs_4_
  365.8 7.3 %shard_map.386 = (bf16[320,1280]{1,0:T(8,128)(2,1)}, bf16[640,1280]{1,0:T(8,128)(2,1)}, bf16[320,1280]{1,0:T(8,128)(2,1)}) custom-call(bf16[576,1280]{1,0:T(8,128)(2,1)} %get-tuple-element.108.refs_0_, bf16[576,5120]{1,0:T(8,128)(2,1)} %get-tuple-element.114.refs_2_.refs_1_.refs_0_, bf16[640,5120]{1,0:T(8,128)(2,1)} %collective-permute-done.44.refs_2_, ...), custom_call_target="tpu_custom_call" | custom-call | flops 64399998976 | tf_op jit(solution)/shard_map/pallas_call | solution.py:109
  373.1 7.6 %shard_map.387 = (bf16[320,1280]{1,0:T(8,128)(2,1)}, bf16[320,1280]{1,0:T(8,128)(2,1)}, bf16[640,1280]{1,0:T(8,128)(2,1)}) custom-call(bf16[576,1280]{1,0:T(8,128)(2,1)} %get-tuple-element.108.refs_0_, bf16[576,5120]{1,0:T(8,128)(2,1)} %get-tuple-element.114.refs_2_.refs_1_.refs_0_, bf16[640,5120]{1,0:T(8,128)(2,1)} %collective-permute-done.44.refs_2_, ...), custom_call_target="tpu_custom_call" | custom-call | flops 64399998976 | tf_op jit(solution)/shard_map/pallas_call | solution.py:109
  382.2 6.0 shard_map.388.refs_7_.refs_2_
  395.0 27.3 %shard_map.391 = (bf16[576,3840]{1,0:T(8,128)(2,1)}, f32[1,3840]{1,0:T(1,128)}) custom-call(bf16[576,3840]{1,0:T(8,128)(2,1)} %get-tuple-element.105.refs_1_.refs_0_, f32[2,8,576]{2,1,0:T(8,128)} %get-tuple-element.127.refs_1_, bf16[576,1280]{1,0:T(8,128)(2,1)} %shard_map.388.refs_7_.refs_2_, f32[576,640]{1,0:T(8,128)} %copy.49.refs_1_.refs_3_, ...), custom_call_target="tpu_custom_call" | custom-call | flops 251160002560 | tf_op jit(solution)/shard_map/pallas_call | solution.py:109
  430.4 7.1 %shard_map.394.refs_4_ = bf16[640,2560]{1,0:T(8,128)(2,1)} custom-call(bf16[576,1280]{1,0:T(8,128)(2,1)} %fusion.16.refs_0_, bf16[576,3840]{1,0:T(8,128)(2,1)} %get-tuple-element.128.refs_4_.refs_1_.refs_2_.refs_0_, bf16[80,2560]{1,0:T(8,128)(2,1)} %shard_map.393.refs_2_), custom_call_target="tpu_custom_call" | custom-call | flops 64399998976 | tf_op jit(solution)/shard_map/pallas_call | solution.py:109
  442.5 7.9 %shard_map.395.refs_3_ = bf16[640,2560]{1,0:T(8,128)(2,1)} custom-call(bf16[576,1280]{1,0:T(8,128)(2,1)} %fusion.16.refs_0_, bf16[576,1280]{1,0:T(8,128)(2,1)} %get-tuple-element.124.refs_0_.refs_1_, bf16[576,3840]{1,0:T(8,128)(2,1)} %get-tuple-element.128.refs_4_.refs_1_.refs_2_.refs_0_, bf16[576,1280]{1,0:T(8,128)(2,1)} %get-tuple-element.104.refs_0_.refs_3_, ...), custom_call_target="tpu_custom_call" | custom-call | flops 64399998976 | tf_op jit(solution)/shard_map/pallas_call | solution.py:109
  452.4 7.9 %shard_map.396 = (bf16[320,1280]{1,0:T(8,128)(2,1)}, bf16[640,1280]{1,0:T(8,128)(2,1)}, bf16[320,1280]{1,0:T(8,128)(2,1)}) custom-call(bf16[576,1280]{1,0:T(8,128)(2,1)} %fusion.16.refs_0_, bf16[576,3840]{1,0:T(8,128)(2,1)} %get-tuple-element.128.refs_4_.refs_1_.refs_2_.refs_0_, bf16[640,2560]{1,0:T(8,128)(2,1)} %copy-done.31, ...), custom_call_target="tpu_custom_call" | custom-call | flops 73600000000 | tf_op jit(solution)/shard_map/pallas_call | solution.py:109
  466.5 9.0 %shard_map.398 = (bf16[320,1280]{1,0:T(8,128)(2,1)}, bf16[320,1280]{1,0:T(8,128)(2,1)}, bf16[640,1280]{1,0:T(8,128)(2,1)}) custom-call(bf16[576,1280]{1,0:T(8,128)(2,1)} %fusion.16.refs_0_, bf16[576,1280]{1,0:T(8,128)(2,1)} %get-tuple-element.124.refs_0_.refs_1_, bf16[576,3840]{1,0:T(8,128)(2,1)} %get-tuple-element.128.refs_4_.refs_1_.refs_2_.refs_0_, ...), custom_call_target="tpu_custom_call" | custom-call | flops 73600000000 | tf_op jit(solution)/shard_map/pallas_call | solution.py:109
  487.7 18.2 %shard_map.402 = (bf16[576,1280]{1,0:T(8,128)(2,1)}, f32[8,1280]{1,0:T(8,128)}) custom-call(bf16[576,3840]{1,0:T(8,128)(2,1)} %get-tuple-element.128.refs_4_.refs_1_.refs_2_.refs_0_, bf16[320,1920]{1,0:T(8,128)(2,1)} %shard_map.364.refs_3_.refs_1_, bf16[320,1920]{1,0:T(8,128)(2,1)} %copy-done.36, bf16[320,1920]{1,0:T(8,128)(2,1)} %copy-done.37, ...), custom_call_target="tpu_custom_call" | custom-call | flops 165600002048 | tf_op jit(solution)/shard_map/pallas_call | solution.py:109
  509.8 5.5 shard_map.403
  564.2 5.8 collective-permute-done.66.refs_6_
  576.0 8.2 %collective-permute-done.67.refs_6_ = bf16[80,2560]{1,0:T(8,128)(2,1)S(1)} collective-permute-done((bf16[80,2560]{1,0:T(8,128)(2,1)}, bf16[80,2560]{1,0:T(8,128)(2,1)S(1)}, u32[]{:S(2)}, u32[]{:S(2)}) %collective-permute-start.67) | collective-permute-done | bytes 409632 | tf_op jit(solution)/shard_map/ppermute | solution.py:1035
  592.3 5.4 collective-permute-done.68.refs_6_
  622.4 4.6 shard_map.421
  (382 shorter events, 291.9 us)
Async XLA Ops:
  2.6 31.2 %collective-permute-start.5 = (bf16[80,2560]{1,0:T(8,128)(2,1)}, bf16[80,2560]{1,0:T(8,128)(2,1)}, u32[]{:S(2)}, u32[]{:S(2)}) collective-permute-start(bf16[80,2560]{1,0:T(8,128)(2,1)} %bitcast_convert_fusion.refs_0_), channel_id=1, source_target_pairs={{0,1},{1,0},{2,3},{3,2},{4,5},{5,4},{6,7},{7,6},{8,9},{9,8},{10,11... | collective-permute-start | bytes 1228808 | tf_op jit(solution)/shard_map/ppermute | solution.py:1023
  5.5 49.7 %collective-permute-start.6 = (bf16[80,2560]{1,0:T(8,128)(2,1)}, bf16[80,2560]{1,0:T(8,128)(2,1)}, u32[]{:S(2)}, u32[]{:S(2)}) collective-permute-start(bf16[80,2560]{1,0:T(8,128)(2,1)} %bitcast_convert_fusion.refs_0_), channel_id=1, source_target_pairs={{0,4},{2,6},{4,0},{6,2},{8,12},{10,14},{12,8},{14,10},{16,20},{18,... | collective-permute-start | bytes 1228808 | tf_op jit(solution)/shard_map/ppermute | solution.py:1029
  9.3 45.9 %collective-permute-start.4 = (bf16[288,1280]{1,0:T(8,128)(2,1)S(1)}, bf16[288,1280]{1,0:T(8,128)(2,1)}, u32[]{:S(2)}, u32[]{:S(2)}) collective-permute-start(bf16[288,1280]{1,0:T(8,128)(2,1)S(1)} %get-tuple-element.190), channel_id=1, source_target_pairs={{0,1},{1,0},{2,3},{3,2},{4,5},{5,4},{6,7},{7,6},{8,9},{9,8},{10,11... | collective-permute-start | bytes 2211848 | tf_op jit(solution)/shard_map/ppermute | solution.py:1023
  37.4 28.3 %collective-permute-start.18 = (bf16[80,3200]{1,0:T(8,128)(2,1)}, bf16[80,3200]{1,0:T(8,128)(2,1)S(1)}, u32[]{:S(2)}, u32[]{:S(2)}) collective-permute-start(bf16[80,3200]{1,0:T(8,128)(2,1)} %shard_map.363.refs_9_.refs_0_), channel_id=1, source_target_pairs={{0,24},{2,26},{4,28},{6,30},{8,0},{10,2},{12,4},{14,6},{16,8},{18,... | collective-permute-start | bytes 1536008 | tf_op jit(solution)/shard_map/ppermute | solution.py:1032
  62.1 26.4 %collective-permute-start.11 = (bf16[320,1920]{1,0:T(8,128)(2,1)}, bf16[320,1920]{1,0:T(8,128)(2,1)S(1)}, u32[]{:S(2)}, u32[]{:S(2)}) collective-permute-start(bf16[320,1920]{1,0:T(8,128)(2,1)} %shard_map.364.refs_3_.refs_1_), channel_id=1, source_target_pairs={{0,1},{1,0},{2,3},{3,2},{4,5},{5,4},{6,7},{7,6},{8,9},{9,8},{10,11... | collective-permute-start | bytes 3686408 | tf_op jit(solution)/shard_map/ppermute | solution.py:1023
  63.6 26.1 %collective-permute-start.8 = (bf16[320,1920]{1,0:T(8,128)(2,1)}, bf16[320,1920]{1,0:T(8,128)(2,1)S(1)}, u32[]{:S(2)}, u32[]{:S(2)}) collective-permute-start(bf16[320,1920]{1,0:T(8,128)(2,1)} %shard_map.364.refs_3_.refs_1_), channel_id=1, source_target_pairs={{0,4},{2,6},{4,0},{6,2},{8,12},{10,14},{12,8},{14,10},{16,20},{18,... | collective-permute-start | bytes 3686408 | tf_op jit(solution)/shard_map/ppermute | solution.py:1029
  100.8 33.8 %collective-permute-start.22 = (bf16[160,5120]{1,0:T(8,128)(2,1)}, bf16[160,5120]{1,0:T(8,128)(2,1)}, u32[]{:S(2)}, u32[]{:S(2)}) collective-permute-start(bf16[160,5120]{1,0:T(8,128)(2,1)} %shard_map.366.refs_8_.refs_1_), channel_id=1, source_target_pairs={{0,2},{2,0},{4,6},{6,4},{8,10},{10,8},{12,14},{14,12},{16,18},{18,... | collective-permute-start | bytes 4915208 | tf_op jit(solution)/shard_map/ppermute | solution.py:1026
  104.3 51.2 %collective-permute-start.26 = (bf16[160,5120]{1,0:T(8,128)(2,1)}, bf16[160,5120]{1,0:T(8,128)(2,1)}, u32[]{:S(2)}, u32[]{:S(2)}) collective-permute-start(bf16[160,5120]{1,0:T(8,128)(2,1)} %shard_map.366.refs_8_.refs_1_), channel_id=1, source_target_pairs={{0,24},{2,26},{4,28},{6,30},{8,0},{10,2},{12,4},{14,6},{16,8},{18,... | collective-permute-start | bytes 4915208 | tf_op jit(solution)/shard_map/ppermute | solution.py:1032
  118.3 47.1 %collective-permute-start.23 = (bf16[320,3200]{1,0:T(8,128)(2,1)}, bf16[320,3200]{1,0:T(8,128)(2,1)}, u32[]{:S(2)}, u32[]{:S(2)}) collective-permute-start(bf16[320,3200]{1,0:T(8,128)(2,1)} %shard_map.367.refs_14_.refs_1_), channel_id=1, source_target_pairs={{0,4},{2,6},{4,0},{6,2},{8,12},{10,14},{12,8},{14,10},{16,20},{18,... | collective-permute-start | bytes 6144008 | tf_op jit(solution)/shard_map/ppermute | solution.py:1029
  119.8 46.8 %collective-permute-start.25 = (bf16[320,3200]{1,0:T(8,128)(2,1)}, bf16[320,3200]{1,0:T(8,128)(2,1)}, u32[]{:S(2)}, u32[]{:S(2)}) collective-permute-start(bf16[320,3200]{1,0:T(8,128)(2,1)} %shard_map.367.refs_14_.refs_1_), channel_id=1, source_target_pairs={{0,1},{1,0},{2,3},{3,2},{4,5},{5,4},{6,7},{7,6},{8,9},{9,8},{10,11... | collective-permute-start | bytes 6144008 | tf_op jit(solution)/shard_map/ppermute | solution.py:1023
  158.2 47.9 %collective-permute-start.33 = (bf16[160,5120]{1,0:T(8,128)(2,1)}, bf16[160,5120]{1,0:T(8,128)(2,1)}, u32[]{:S(2)}, u32[]{:S(2)}) collective-permute-start(bf16[160,5120]{1,0:T(8,128)(2,1)} %shard_map.370.refs_3_.refs_2_), channel_id=1, source_target_pairs={{0,24},{2,26},{4,28},{6,30},{8,0},{10,2},{12,4},{14,6},{16,8},{18,... | collective-permute-start | bytes 4915208 | tf_op jit(solution)/shard_map/ppermute | solution.py:1032
  165.3 46.6 %collective-permute-start.24 = (bf16[320,3200]{1,0:T(8,128)(2,1)}, bf16[320,3200]{1,0:T(8,128)(2,1)S(1)}, u32[]{:S(2)}, u32[]{:S(2)}) collective-permute-start(bf16[320,3200]{1,0:T(8,128)(2,1)} %collective-permute-done.23.refs_1_.refs_2_), channel_id=1, source_target_pairs={{0,2},{2,0},{4,6},{6,4},{8,10},{10,8},{12,14},{14,12},{16,18},{18,... | collective-permute-start | bytes 6144008 | tf_op jit(solution)/shard_map/ppermute | solution.py:1026
  166.6 45.7 %collective-permute-start.29 = (bf16[320,3200]{1,0:T(8,128)(2,1)}, bf16[320,3200]{1,0:T(8,128)(2,1)}, u32[]{:S(2)}, u32[]{:S(2)}) collective-permute-start(bf16[320,3200]{1,0:T(8,128)(2,1)} %collective-permute-done.25.refs_0_.refs_5_.refs_9_), channel_id=1, source_target_pairs={{0,2},{2,0},{4,6},{6,4},{8,10},{10,8},{12,14},{14,12},{16,18},{18,... | collective-permute-start | bytes 6144008 | tf_op jit(solution)/shard_map/ppermute | solution.py:1026
  171.4 29.8 %collective-permute-start.28 = (bf16[320,1920]{1,0:T(8,128)(2,1)}, bf16[320,1920]{1,0:T(8,128)(2,1)}, u32[]{:S(2)}, u32[]{:S(2)}) collective-permute-start(bf16[320,1920]{1,0:T(8,128)(2,1)} %get-tuple-element.106.refs_3_), channel_id=1, source_target_pairs={{0,4},{2,6},{4,0},{6,2},{8,12},{10,14},{12,8},{14,10},{16,20},{18,... | collective-permute-start | bytes 3686408 | tf_op jit(solution)/shard_map/ppermute | solution.py:1029
  176.0 34.5 %collective-permute-start.31 = (bf16[320,1280]{1,0:T(8,128)(2,1)}, bf16[320,1280]{1,0:T(8,128)(2,1)}, u32[]{:S(2)}, u32[]{:S(2)}) collective-permute-start(bf16[320,1280]{1,0:T(8,128)(2,1)} %get-tuple-element.107), channel_id=1, source_target_pairs={{0,1},{1,0},{2,3},{3,2},{4,5},{5,4},{6,7},{7,6},{8,9},{9,8},{10,11... | collective-permute-start | bytes 2457608 | tf_op jit(solution)/shard_map/ppermute | solution.py:1023
  206.1 40.4 %collective-permute-start.34 = (bf16[160,5120]{1,0:T(8,128)(2,1)}, bf16[160,5120]{1,0:T(8,128)(2,1)}, u32[]{:S(2)}, u32[]{:S(2)}) collective-permute-start(bf16[160,5120]{1,0:T(8,128)(2,1)} %collective-permute-done.33.refs_3_), channel_id=1, source_target_pairs={{0,24},{2,26},{4,28},{6,30},{8,0},{10,2},{12,4},{14,6},{16,8},{18,... | collective-permute-start | bytes 4915208 | tf_op jit(solution)/shard_map/ppermute | solution.py:1032
  210.5 49.1 %collective-permute-start.35 = (bf16[160,5120]{1,0:T(8,128)(2,1)}, bf16[160,5120]{1,0:T(8,128)(2,1)}, u32[]{:S(2)}, u32[]{:S(2)}) collective-permute-start(bf16[160,5120]{1,0:T(8,128)(2,1)} %collective-permute-done.33.refs_3_), channel_id=1, source_target_pairs={{0,2},{2,0},{4,6},{6,4},{8,10},{10,8},{12,14},{14,12},{16,18},{18,... | collective-permute-start | bytes 4915208 | tf_op jit(solution)/shard_map/ppermute | solution.py:1026
  292.2 39.0 %collective-permute-start.40 = (bf16[640,1280]{1,0:T(8,128)(2,1)}, bf16[640,1280]{1,0:T(8,128)(2,1)}, u32[]{:S(2)}, u32[]{:S(2)}) collective-permute-start(bf16[640,1280]{1,0:T(8,128)(2,1)} %get-tuple-element.118), channel_id=1, source_target_pairs={{0,1},{1,0},{2,3},{3,2},{4,5},{5,4},{6,7},{7,6},{8,9},{9,8},{10,11... | collective-permute-start | bytes 4915208 | tf_op jit(solution)/shard_map/ppermute | solution.py:1023
  293.1 38.0 %collective-permute-start.39 = (bf16[640,1280]{1,0:T(8,128)(2,1)}, bf16[640,1280]{1,0:T(8,128)(2,1)}, u32[]{:S(2)}, u32[]{:S(2)}) collective-permute-start(bf16[640,1280]{1,0:T(8,128)(2,1)} %get-tuple-element.117), channel_id=1, source_target_pairs={{0,4},{2,6},{4,0},{6,2},{8,12},{10,14},{12,8},{14,10},{16,20},{18,... | collective-permute-start | bytes 4915208 | tf_op jit(solution)/shard_map/ppermute | solution.py:1029
  325.4 40.4 %collective-permute-start.44 = (bf16[640,5120]{1,0:T(8,128)(2,1)}, bf16[640,5120]{1,0:T(8,128)(2,1)}, u32[]{:S(2)}, u32[]{:S(2)}) collective-permute-start(bf16[640,5120]{1,0:T(8,128)(2,1)} %shard_map.382.refs_4_), channel_id=1, source_target_pairs={{0,2},{2,0},{4,6},{6,4},{8,10},{10,8},{12,14},{14,12},{16,18},{18,... | collective-permute-start | bytes 19660808 | tf_op jit(solution)/shard_map/ppermute | solution.py:1026
  325.4 67.1 %collective-permute-start.38 = (bf16[288,1280]{1,0:T(8,128)(2,1)}, bf16[288,1280]{1,0:T(8,128)(2,1)}, u32[]{:S(2)}, u32[]{:S(2)}) collective-permute-start(bf16[288,1280]{1,0:T(8,128)(2,1)} %get-tuple-element.116), channel_id=1, source_target_pairs={{0,1},{1,0},{2,3},{3,2},{4,5},{5,4},{6,7},{7,6},{8,9},{9,8},{10,11... | collective-permute-start | bytes 2211848 | tf_op jit(solution)/shard_map/ppermute | solution.py:1023
  334.0 29.5 %collective-permute-start.41 = (bf16[320,1280]{1,0:T(8,128)(2,1)}, bf16[320,1280]{1,0:T(8,128)(2,1)}, u32[]{:S(2)}, u32[]{:S(2)}) collective-permute-start(bf16[320,1280]{1,0:T(8,128)(2,1)} %get-tuple-element.121.refs_17_), channel_id=1, source_target_pairs={{0,1},{1,0},{2,3},{3,2},{4,5},{5,4},{6,7},{7,6},{8,9},{9,8},{10,11... | collective-permute-start | bytes 2457608 | tf_op jit(solution)/shard_map/ppermute | solution.py:1023
  335.0 28.6 %collective-permute-start.42 = (bf16[320,1280]{1,0:T(8,128)(2,1)}, bf16[320,1280]{1,0:T(8,128)(2,1)}, u32[]{:S(2)}, u32[]{:S(2)}) collective-permute-start(bf16[320,1280]{1,0:T(8,128)(2,1)} %get-tuple-element.122), channel_id=1, source_target_pairs={{0,4},{2,6},{4,0},{6,2},{8,12},{10,14},{12,8},{14,10},{16,20},{18,... | collective-permute-start | bytes 2457608 | tf_op jit(solution)/shard_map/ppermute | solution.py:1029
  380.7 43.0 %collective-permute-start.46 = (bf16[640,1280]{1,0:T(8,128)(2,1)}, bf16[640,1280]{1,0:T(8,128)(2,1)}, u32[]{:S(2)}, u32[]{:S(2)}) collective-permute-start(bf16[640,1280]{1,0:T(8,128)(2,1)} %get-tuple-element.130), channel_id=1, source_target_pairs={{0,1},{1,0},{2,3},{3,2},{4,5},{5,4},{6,7},{7,6},{8,9},{9,8},{10,11... | collective-permute-start | bytes 4915208 | tf_op jit(solution)/shard_map/ppermute | solution.py:1023
  381.7 42.0 %collective-permute-start.45 = (bf16[640,1280]{1,0:T(8,128)(2,1)}, bf16[640,1280]{1,0:T(8,128)(2,1)}, u32[]{:S(2)}, u32[]{:S(2)}) collective-permute-start(bf16[640,1280]{1,0:T(8,128)(2,1)} %get-tuple-element.129), channel_id=1, source_target_pairs={{0,4},{2,6},{4,0},{6,2},{8,12},{10,14},{12,8},{14,10},{16,20},{18,... | collective-permute-start | bytes 4915208 | tf_op jit(solution)/shard_map/ppermute | solution.py:1029
  390.6 37.3 %collective-permute-start.49 = (bf16[80,2560]{1,0:T(8,128)(2,1)}, bf16[80,2560]{1,0:T(8,128)(2,1)}, u32[]{:S(2)}, u32[]{:S(2)}) collective-permute-start(bf16[80,2560]{1,0:T(8,128)(2,1)} %shard_map.389.refs_3_), channel_id=1, source_target_pairs={{0,8},{2,10},{4,12},{6,14},{8,16},{10,18},{12,20},{14,22},{16,24},... | collective-permute-start | bytes 1228808 | tf_op jit(solution)/shard_map/ppermute | solution.py:1035
  426.8 33.5 %collective-permute-start.47 = (bf16[320,1280]{1,0:T(8,128)(2,1)}, bf16[320,1280]{1,0:T(8,128)(2,1)}, u32[]{:S(2)}, u32[]{:S(2)}) collective-permute-start(bf16[320,1280]{1,0:T(8,128)(2,1)} %get-tuple-element.133.refs_7_), channel_id=1, source_target_pairs={{0,1},{1,0},{2,3},{3,2},{4,5},{5,4},{6,7},{7,6},{8,9},{9,8},{10,11... | collective-permute-start | bytes 2457608 | tf_op jit(solution)/shard_map/ppermute | solution.py:1023
  437.4 40.7 %collective-permute-start.52 = (bf16[80,2560]{1,0:T(8,128)(2,1)}, bf16[80,2560]{1,0:T(8,128)(2,1)}, u32[]{:S(2)}, u32[]{:S(2)}) collective-permute-start(bf16[80,2560]{1,0:T(8,128)(2,1)} %shard_map.393.refs_2_), channel_id=1, source_target_pairs={{0,8},{2,10},{4,12},{6,14},{8,16},{10,18},{12,20},{14,22},{16,24},... | collective-permute-start | bytes 1228808 | tf_op jit(solution)/shard_map/ppermute | solution.py:1035
  475.6 50.0 %collective-permute-start.59 = (bf16[640,1280]{1,0:T(8,128)(2,1)}, bf16[640,1280]{1,0:T(8,128)(2,1)}, u32[]{:S(2)}, u32[]{:S(2)}) collective-permute-start(bf16[640,1280]{1,0:T(8,128)(2,1)} %get-tuple-element.148), channel_id=1, source_target_pairs={{0,1},{1,0},{2,3},{3,2},{4,5},{5,4},{6,7},{7,6},{8,9},{9,8},{10,11... | collective-permute-start | bytes 4915208 | tf_op jit(solution)/shard_map/ppermute | solution.py:1023
  476.6 49.0 %collective-permute-start.58 = (bf16[640,1280]{1,0:T(8,128)(2,1)}, bf16[640,1280]{1,0:T(8,128)(2,1)}, u32[]{:S(2)}, u32[]{:S(2)}) collective-permute-start(bf16[640,1280]{1,0:T(8,128)(2,1)} %get-tuple-element.147), channel_id=1, source_target_pairs={{0,4},{2,6},{4,0},{6,2},{8,12},{10,14},{12,8},{14,10},{16,20},{18,... | collective-permute-start | bytes 4915208 | tf_op jit(solution)/shard_map/ppermute | solution.py:1029
  487.7 31.8 %collective-permute-start.56 = (bf16[80,2560]{1,0:T(8,128)(2,1)}, bf16[80,2560]{1,0:T(8,128)(2,1)}, u32[]{:S(2)}, u32[]{:S(2)}) collective-permute-start(bf16[80,2560]{1,0:T(8,128)(2,1)} %shard_map.401.refs_16_), channel_id=1, source_target_pairs={{0,8},{2,10},{4,12},{6,14},{8,16},{10,18},{12,20},{14,22},{16,24},... | collective-permute-start | bytes 1228808 | tf_op jit(solution)/shard_map/ppermute | solution.py:1035
  518.5 71.2 %collective-permute-start.54 = (bf16[288,1280]{1,0:T(8,128)(2,1)}, bf16[288,1280]{1,0:T(8,128)(2,1)}, u32[]{:S(2)}, u32[]{:S(2)}) collective-permute-start(bf16[288,1280]{1,0:T(8,128)(2,1)} %get-tuple-element.140), channel_id=1, source_target_pairs={{0,1},{1,0},{2,3},{3,2},{4,5},{5,4},{6,7},{7,6},{8,9},{9,8},{10,11... | collective-permute-start | bytes 2211848 | tf_op jit(solution)/shard_map/ppermute | solution.py:1023
  (111 other events, 960.8 us)

commit v6 on v5

--- a/solution.py
+++ b/solution.py
@@ -1,3 +1,5 @@
+import math
+
 import jax
 import jax.numpy as jnp
 from jax import lax
@@ -68,7 +70,8 @@
     return (first, second, update)
 
 
-VMEM_LIMIT = 56 * 1024 * 1024
+VMEM_MOST = 56 * 1024 * 1024
+VMEM_SPARE = 14 * 1024 * 1024
 COST = int(8 * 1.15e9)
 
 
@@ -86,27 +89,42 @@
     if ORDER.last is not None:
         after = [*after, ORDER.last]
     count, extra = len(in_specs), len(after)
+    shapes = out_shape if isinstance(out_shape, (list, tuple)) else [out_shape]
+    outs = out_specs if isinstance(out_specs, (list, tuple)) else [out_specs]
+    out_bytes = sum(
+        2 * math.prod(o.block_shape) * v.dtype.itemsize for o, v in zip(outs, shapes)
+    )
+    scratch_bytes = sum(math.prod(v.shape) * v.dtype.itemsize for v in scratch)
+
+    def room(operands):
+        in_bytes = sum(
+            2 * math.prod(i.block_shape) * v.dtype.itemsize
+            for i, v in zip(in_specs, operands)
+            if i.block_shape is not None
+        )
+        return min(VMEM_MOST, in_bytes + out_bytes + scratch_bytes + VMEM_SPARE)
 
     def ordered(*refs):
         kernel(*refs[:count], *refs[count + extra :])
 
-    run = pl.pallas_call(
-        ordered,
-        grid=grid,
-        in_specs=list(in_specs) + [pl.BlockSpec(memory_space=pl.ANY)] * extra,
-        out_specs=out_specs,
-        out_shape=out_shape,
-        scratch_shapes=list(scratch),
-        compiler_params=pltpu.CompilerParams(
-            dimension_semantics=("arbitrary",) * len(grid), vmem_limit_bytes=VMEM_LIMIT
-        ),
-        cost_estimate=pl.CostEstimate(
-            flops=int(COST * us), bytes_accessed=0, transcendentals=0
-        ),
-    )
+    def run(*operands):
+        return pl.pallas_call(
+            ordered,
+            grid=grid,
+            in_specs=list(in_specs) + [pl.BlockSpec(memory_space=pl.ANY)] * extra,
+            out_specs=out_specs,
+            out_shape=out_shape,
+            scratch_shapes=list(scratch),
+            compiler_params=pltpu.CompilerParams(
+                dimension_semantics=("arbitrary",) * len(grid), vmem_limit_bytes=room(operands)
+            ),
+            cost_estimate=pl.CostEstimate(
+                flops=int(COST * us), bytes_accessed=0, transcendentals=0
+            ),
+        )(*operands, *after)
 
     def start(*operands):
-        result = run(*operands, *after)
+        result = run(*operands)
         ORDER.last = result[0] if isinstance(result, (list, tuple)) else result
         return result
 
@@ -380,7 +398,7 @@
             jax.ShapeDtypeStruct((1, total_columns), F32),
         ],
         scratch=[pltpu.VMEM((rows, block), F32)],
-        us=19,
+        us=0.1,
         after=after,
     )(down_grad, *parts.arrays, upward)
 
@@ -421,7 +439,7 @@
         ],
         [whole((rows, width)), whole((rows, width)), whole((8, width))],
         finish,
-        21.7,
+        0.1,
         after,
     )
 
@@ -441,7 +459,7 @@
         [jax.ShapeDtypeStruct((rows, parts.steps * block), LOW)],
         [pl.BlockSpec((rows, block), lambda j: (0, j))],
         finish,
-        6,
+        250,
         after,
     )[0]
 
@@ -489,13 +507,7 @@
     def kernel(*refs):
         lefts, rights = refs[:count], refs[count : 2 * count]
         rest = refs[2 * count :]
-        turned = rest[-count:]
         j = pl.program_id(0)
-
-        @pl.when(j == 0)
-        def _():
-            for k in range(count):
-                turned[k][...] = lefts[k][:, half * middle : (half + 1) * middle].T
 
         for k in range(count):
             hits = [s for s in range(steps) if kind[s][0] == k]
@@ -507,14 +519,13 @@
             def _(k=k):
                 right = rights[k][...]
                 if came is None:
-                    rest[0][...] = jnp.dot(
-                        turned[k][...], right, preferred_element_type=F32
-                    ).astype(LOW)
+                    rest[0][...] = outer(lefts[k][...], right).astype(LOW)
                     return
                 came_ref, out0, out1, out2 = rest[:4]
-                y0 = jnp.dot(turned[k][:low, :], right, preferred_element_type=F32)
+                y = outer(lefts[k][...], right)
+                y0 = y[:low]
                 y0 = (y0 + came_ref[:low, :].astype(F32)).astype(LOW)
-                y1 = jnp.dot(turned[k][low:, :], right, preferred_element_type=F32)
+                y1 = y[low:]
                 y1 = (y1 + came_ref[low:, :].astype(F32)).astype(LOW)
 
                 @pl.when(j < near)
@@ -564,10 +575,11 @@
     return call(
         kernel,
         (steps,),
-        [whole(left.shape) for left, _ in pairs] + right_specs + extra_specs,
+        [pl.BlockSpec((rows, middle), lambda j: (0, half)) for _ in pairs]
+        + right_specs
+        + extra_specs,
         [s for s, _ in outs],
         [s for _, s in outs],
-        scratch=[pltpu.VMEM((middle, rows), LOW) for _ in pairs],
         us=us,
         after=after,
     )(*[left for left, _ in pairs], *[right for _, right in pairs], *extra)
@@ -688,6 +700,63 @@
     )(*values)
 
 
+def enter_input(mine, came, shuffle, vec):
+    half, width = mine.shape
+    rows = 2 * half
+
+    def kernel(mine_ref, came_ref, s_ref, vec_ref, row_ref, first_ref):
+        row_ref[:half, :] = jnp.dot(
+            mine_ref[...], s_ref[...], preferred_element_type=F32
+        ).astype(LOW)
+        row_ref[half:, :] = jnp.dot(
+            came_ref[0], s_ref[...], preferred_element_type=F32
+        ).astype(LOW)
+        normed, _ = norm_parts(row_ref[...].astype(F32))
+        first_ref[...] = (normed * vec_ref[0:1, :] + vec_ref[1:2, :]).astype(LOW)
+
+    shape = jax.ShapeDtypeStruct((rows, width), LOW)
+    return call(
+        kernel,
+        (1,),
+        [
+            whole(mine.shape),
+            pl.BlockSpec((1, half, width), lambda j: (0, 0, 0)),
+            whole(shuffle.shape),
+            whole(vec.shape),
+        ],
+        [whole((rows, width))] * 2,
+        [shape, shape],
+        us=7,
+    )(mine, came, shuffle, vec)
+
+
+def enter_cotangent(mine, came, shuffle, token_weight):
+    half, width = mine.shape
+    rows = 2 * half
+
+    def kernel(mine_ref, came_ref, s_ref, weight_ref, row_ref, grad_ref):
+        for k, part in enumerate((mine_ref[...], came_ref[0])):
+            cut = slice(k * half, (k + 1) * half)
+            y = jnp.dot(part, s_ref[...], preferred_element_type=F32)
+            row_ref[cut, :] = y.astype(LOW)
+            grad_ref[cut, :] = (y * weight_ref[cut, :]).astype(LOW)
+
+    shape = jax.ShapeDtypeStruct((rows, width), LOW)
+    return call(
+        kernel,
+        (1,),
+        [
+            whole(mine.shape),
+            pl.BlockSpec((1, half, width), lambda j: (1, 0, 0)),
+            whole(shuffle.shape),
+            whole(token_weight.shape),
+        ],
+        [whole((rows, width))] * 2,
+        [shape, shape],
+        us=7,
+    )(mine, came, shuffle, token_weight)
+
+
 def place_halves(mine, theirs, slot, after=()):
     shape = (2, 1, *mine.shape)
 
@@ -727,7 +796,7 @@
         [whole(values.shape), whole(shuffle.shape)],
         [whole((half, width))] * 2,
         [shape, shape],
-        us=5,
+        us=0.1,
     )(values, shuffle)
 
 
@@ -1159,6 +1228,8 @@
     hidden = fc1_weight.shape[1]
     grad_factor = float(block_input.shape[0] * block_input.shape[1] * dp * LEN) ** (-0.5)
 
+    biases = jnp.concatenate([qkv_bias.reshape(-1), fc1_bias]).reshape(-1, 128)
+
     def row_view(v):
         return jnp.swapaxes(v, -1, -2)
 
@@ -1171,8 +1242,10 @@
     def half_of(both, place):
         return lax.dynamic_index_in_dim(both[:, 0], place, 0, keepdims=False)
 
-    input_came = lanes.over_x(half_of(block_input, 1 - slot))
-    cot_came = lanes.over_x(half_of(out_cotangent, 1 - slot))
+    both_came = lanes.over_x(
+        jnp.stack([half_of(block_input, 1 - slot), half_of(out_cotangent, 1 - slot)])
+    )
+    input_mine, cot_mine = half_of(block_input, slot), half_of(out_cotangent, slot)
 
     shard_1 = jnp.concatenate([qkv_view[k].astype(LOW) for k in range(3)], 1)
     shard_3 = fc2_view.astype(LOW)
@@ -1181,11 +1254,57 @@
         ring_1 = lanes.ring_down(shard_1)
         side_3, across_3 = lanes.over_x(shard_3), lanes.over_y(shard_3)
         far_3 = lanes.over_y(side_3)
-        shard_2 = pack_columns([fc1_weight, proj_view], after=[ring_1[2]])
-        held_1 = stack_rows(ring_1, after=[input_came, cot_came, side_3, across_3, far_3])
-        ring_2 = lanes.ring_down(shard_2)
+        shard_2 = pack_columns([fc1_weight, proj_view])
+        ring_2 = [shard_2, lanes.down_z(shard_2)]
+        held_1 = stack_rows(ring_1, after=[side_3, across_3, far_3, both_came])
+        ring_2[1] = hold(ring_2[1])
+        for _ in range(2):
+            ring_2.append(lanes.down_z(ring_2[-1]))
+    else:
+
+        def plain(shard):
+            held = lax.all_gather(shard, "dp", axis=0, tiled=True)
+            return Gathered([held], [lanes.over_x(held)])
+
+        shard_2 = jnp.concatenate([fc1_weight.astype(LOW), proj_view.astype(LOW)], 1)
+        w1, w2, w3 = plain(shard_1), plain(shard_2), plain(shard_3)
+        w_down = w3.parts(half, 0, 2)
+    def pick(array, axis=0):
+        return lax.dynamic_index_in_dim(array, slot, axis, keepdims=False)
+
+    def turn(values):
+        return jnp.roll(values, -slot * local_rows, axis=-1)
+
+    ids_row = turn(pick(picture_ids[:, 0]))
+    rows_at = turn(pick(patch_positions[0, :, 0]))
+    cols_at = turn(pick(patch_positions[1, :, 0]))
+    mask_row = turn(pick(pad_mask[:, 0]))
+    length_row = pick(picture_lengths[:, 0])
+    cosine, sine = rotary_tables(rows_at, cols_at)
+    groups = 2
+    heads = lane_columns // HD
+    cosine, sine = jnp.tile(cosine, (1, heads)), jnp.tile(sine, (1, heads))
+    key_code = jnp.where(mask_row == 1, ids_row, -1)[:, None]
+    query_code = ids_row[None, :]
+    slot_hit = (ids_row[:, None] == jnp.arange(SLOTS, dtype=jnp.int32)[None, :]).astype(F32)
+    picture_size = jnp.sum(slot_hit * length_row.astype(F32)[None, :], -1)
+    token_weight = (mask_row.astype(F32) * jnp.sqrt(LEN / picture_size))[:, None]
+
+    if relative:
+        order = lanes.order()
+        column = (order[:, None] * rows_own + jnp.arange(rows_own)[None, :]).reshape(-1)
+        shuffle = (jnp.arange(width)[:, None] == column[None, :]).astype(LOW)
+        vec = lax.dot_general(
+            vectors,
+            shuffle.astype(F32),
+            (((1,), (0,)), ((), ())),
+            precision=lax.Precision.HIGHEST,
+            preferred_element_type=F32,
+        )
         core_held_1 = lanes.over_core(held_1)
         sides_1 = lanes.over_x(held_1), lanes.over_y(held_1)
+        row_low, first_in = enter_input(input_mine, both_came, shuffle, vec)
+        biases = hold(biases)
         near_1 = [(0, 2 * lane_columns)]
         fars_1 = lanes.far(*sides_1, near_1, after=[core_held_1])
         late_3 = [stack_early(shard_3, side_3, across_3, far_3, after=[ring_2[3]])]
@@ -1202,63 +1321,18 @@
             near_1,
         )
     else:
-
-        def plain(shard):
-            held = lax.all_gather(shard, "dp", axis=0, tiled=True)
-            return Gathered([held], [lanes.over_x(held)])
-
-        shard_2 = jnp.concatenate([fc1_weight.astype(LOW), proj_view.astype(LOW)], 1)
-        w1, w2, w3 = plain(shard_1), plain(shard_2), plain(shard_3)
-        w_down = w3.parts(half, 0, 2)
+        vec = vectors
+        row_low = jnp.concatenate([input_mine, both_came[0]], 0)
+        cot_low = jnp.concatenate([cot_mine, both_came[1]], 0)
+        normed1, _ = norm_parts(row_low.astype(F32))
+        first_in = (normed1 * vec[0] + vec[1]).astype(LOW)
+        down_grad = (cot_low.astype(F32) * token_weight).astype(LOW)
     w_qkv = w1.parts(lane_columns, 0, 3)
-
-    def own_row(both, came):
-        return jnp.concatenate([half_of(both, slot), came], 0)
-
-    biases = jnp.concatenate([qkv_bias.reshape(-1), fc1_bias])
-    other_biases = lanes.over_x(biases)
+    other_biases = lanes.over_x(biases).reshape(-1)
+    biases = biases.reshape(-1)
     cut = qkv_bias.size
     bias_qkv = jnp.concatenate([biases[:cut], other_biases[:cut]])[None]
     bias_up = jnp.concatenate([biases[cut:], other_biases[cut:]])[None]
-
-    def pick(array, axis=0):
-        return lax.dynamic_index_in_dim(array, slot, axis, keepdims=False)
-
-    def turn(values):
-        return jnp.roll(values, -slot * local_rows, axis=-1)
-
-    ids_row = turn(pick(picture_ids[:, 0]))
-    rows_at = turn(pick(patch_positions[0, :, 0]))
-    cols_at = turn(pick(patch_positions[1, :, 0]))
-    mask_row = turn(pick(pad_mask[:, 0]))
-    length_row = pick(picture_lengths[:, 0])
-    cosine, sine = rotary_tables(rows_at, cols_at)
-    groups = 2
-    heads = lane_columns // HD
-    cosine, sine = jnp.tile(cosine, (1, heads)), jnp.tile(sine, (1, heads))
-    key_code = jnp.where(mask_row == 1, ids_row, -1)[:, None]
-    query_code = ids_row[None, :]
-    slot_hit = (ids_row[:, None] == jnp.arange(SLOTS, dtype=jnp.int32)[None, :]).astype(F32)
-    picture_size = jnp.sum(slot_hit * length_row.astype(F32)[None, :], -1)
-    token_weight = (mask_row.astype(F32) * jnp.sqrt(LEN / picture_size))[:, None]
-
-    if relative:
-        order = lanes.order()
-        column = (order[:, None] * rows_own + jnp.arange(rows_own)[None, :]).reshape(-1)
-        shuffle = (jnp.arange(width)[:, None] == column[None, :]).astype(LOW)
-        vec = lax.dot_general(
-            vectors,
-            shuffle.astype(F32),
-            (((1,), (0,)), ((), ())),
-            precision=lax.Precision.HIGHEST,
-            preferred_element_type=F32,
-        )
-        row_low = dot(own_row(block_input, input_came), shuffle).astype(LOW)
-        cot_low = dot(own_row(out_cotangent, cot_came), shuffle).astype(LOW)
-    else:
-        vec = vectors
-        row_low = own_row(block_input, input_came)
-        cot_low = own_row(out_cotangent, cot_came)
 
     def give_back(values_low):
         if relative:
@@ -1323,22 +1397,21 @@
             ]
         ).reshape(-1, 128)
 
-    normed1, _ = norm_parts(row_low.astype(F32))
-    first_in = (normed1 * vec[0] + vec[1]).astype(LOW)
-    down_grad = (cot_low.astype(F32) * token_weight).astype(LOW)
     mixed = qkv_forward(first_in, w_qkv, bias_qkv, list(range(6)))
-    before_attention = [core_held_2, core_late, cot_came] if relative else []
+    if relative:
+        late_3.append(hold(late_came))
+    before_attention = [core_held_2, core_late] if relative else []
     qkv, attended, lse = attention_forward(
         mixed, cosine, sine, key_code, query_code, groups, after=before_attention
     )
     if relative:
-        late_3.append(hold(late_came))
         late_3.append(lanes.down_z(late_3[1]))
         late_came = lanes.down_z(late_3[2])
         late_cores = [(late_3[0], core_late), *lanes.both_cores(late_3[1:])]
         before_far = [late_cores[1][1]]
         near_2 = [(0, half), (hidden, hidden + lane_columns)]
         fars_2 = lanes.far(*sides_2, near_2, after=before_far)
+        cot_low, down_grad = enter_cotangent(cot_mine, both_came, shuffle, token_weight)
         hold(query_code, after=fars_2)
         cores_2 = lanes.both_cores(sides_2)
         w2 = Gathered(
@@ -1353,9 +1426,9 @@
     upward, activated = up_forward(second_in, w_up, bias_up)
     pair_3 = [(down_grad, activated)]
     if relative:
+        came_3 = send_grads(pair_3, half, wide_kind, 60)
         late_cores += lanes.both_cores([hold(late_came)])
         w_down = lanes.stacked(late_cores).parts(half)
-        came_3 = send_grads(pair_3, half, wide_kind, 60)
     result = down_forward(activated, w_down, hidden1, vec)
 
     if relative:
@@ -1364,17 +1437,16 @@
     pair_2 = [(second_in, up_grad)]
     output_halves = give_back(result)
     if relative:
-        came_2 = send_grads(pair_2, half, wide_kind, 10)
-        sides_3 = send_second(later_3, first_3)
+        came_2 = send_grads(pair_2, half, wide_kind, 0.1)
     hidden1_grad, branch_grad, sums_2 = up_backward(
         up_grad, w_up, hidden1, cot_low, token_weight, vec
     )
     if relative:
-        ring_3 = ring_step(own_3, sides_3, None, 3)
-        own_2, later_2, first_2 = wide_grads(pair_2, came_2)
+        sides_3 = send_second(later_3, first_3)
     attn_grad = proj_backward(branch_grad, w_proj)
     if relative:
-        ring_3 = ring_step(own_3, sides_3, ring_3, 2)
+        own_2, later_2, first_2 = wide_grads(pair_2, came_2)
+        ring_3 = ring_step(own_3, sides_3, None, 3)
     block_output = place_halves(*output_halves, slot)
     mixed_grad, sum_qkv = attention_backward(
         qkv, lse, attn_grad, cosine, sine, key_code, query_code, groups
@@ -1385,11 +1457,12 @@
         kind_a = [(0, 0), (0, 1), (0, 3), (0, 4)]
         kind_b = [(0, 2), (1, 0), (0, 5), (1, 1)]
         sides_2 = send_second(later_2, first_2)
-        ring_3 = ring_step(own_3, sides_3, ring_3, 1)
-        came_a = send_grads([pair_q], lane_columns, kind_a, 7)
-        came_b = send_grads([pair_q, pair_p], lane_columns, kind_b, 7)
+        ring_3 = ring_step(own_3, sides_3, ring_3, 2)
+        came_a = send_grads([pair_q], lane_columns, kind_a, 1)
+        came_b = send_grads([pair_q, pair_p], lane_columns, kind_b, 1)
         part_a = grad_kernel([pair_q], lane_columns, kind_a, 0, (came_a, [0, 1, 2, 3]), "a", 8)
         first_y = lanes.over_y(part_a[1])
+        ring_3 = ring_step(own_3, sides_3, ring_3, 1)
         ring_2 = ring_step(own_2, sides_2, None, 3)
         part_b = grad_kernel(
             [pair_q, pair_p], lane_columns, kind_b, 0, (came_b, [0, 1, 2, 3]), "b", 8
@@ -1398,25 +1471,21 @@
         first_1 = first_y, lanes.over_x(part_b[2])
         grad_3 = ring_step(own_3, sides_3, ring_3, 0)
         lamb_3 = lamb_first([(3, fc2_view, fc2_moments_view, 0)], grad_3, factor)
-        ring_2 = ring_step(own_2, sides_2, ring_2, 2)
     input_low, sums_1 = qkv_backward(
         mixed_grad, w_qkv, list(range(6)), row_low, hidden1_grad, vec
     )
-    input_halves = give_back(input_low)
-    small = small_sums(sums_1, sums_2, sum_qkv, sum_up)
     if relative:
-        small = hold(small)
-        came = lanes.over_x(small)
+        ring_2 = ring_step(own_2, sides_2, ring_2, 2)
+        sides_1 = send_second(later_1, first_1)
         ring_2 = ring_step(own_2, sides_2, ring_2, 1)
-        small = hold(small, came)
+        small = hold(small_sums(sums_1, sums_2, sum_qkv, sum_up))
         came = lanes.over_core(small)
-        sides_1 = send_second(later_1, first_1)
-        small = hold(small, came)
-        came = lanes.over_y(small)
         grad_2 = ring_step(own_2, sides_2, ring_2, 0)
         small = hold(small, came)
         came = lanes.exchange(small, 4)
     else:
+        input_halves = give_back(input_low)
+        small = small_sums(sums_1, sums_2, sum_qkv, sum_up)
         grad_3 = plain_grads(pair_3, half, wide_kind)
         lamb_3 = lamb_first([(3, fc2_view, fc2_moments_view, 0)], grad_3, factor)
         grad_2 = plain_grads(pair_2, half, wide_kind)
@@ -1425,9 +1494,14 @@
         small = hold(small, came)
         came = lanes.exchange(small, 8)
         ring_1 = ring_step(own_1, sides_1, None, 3)
+        input_halves = give_back(input_low)
         small = hold(small, came)
+        came = lanes.over_y(small)
         ring_1 = ring_step(own_1, sides_1, ring_1, 2)
+        small = hold(small, came)
+        came = lanes.over_x(small)
         ring_1 = ring_step(own_1, sides_1, ring_1, 1)
+        small = hold(small, came)
 
     if not relative:
         small = butterfly(small, dp)

time: 638 us -> 571 us (0.89)
  Pallas kernels: 350 us -> 278 us
  local copies, waits for them, and re-layouts: 44.5 us -> 58.9 us
  waiting for transfers between devices: 115 us -> 129 us
  starting transfers between devices: 91.8 us -> 78.7 us
  matrix products: 12 us -> 4.79 us
    pallas_call x59 -> x63, Pallas kernels: 350 us -> 278 us  [run(): pl.pallas_call(ordered, grid=grid, in_specs=list(in_specs) + [pl.BlockSpe...]
    unnamed x140 -> x352, local copies, waits for them, and re-layouts: 26.9 us -> 44.4 us
    ppermute x9, waiting for transfers between devices: 19.4 us -> 34.9 us  [up_z(): lax.ppermute(v, 'dp', [(i, (i + 4) % self.dp) for i in range(self.dp)])]
    ppermute x9, waiting for transfers between devices: 20.4 us -> 32.1 us  [down_z(): lax.ppermute(v, 'dp', [(i, (i - 4) % self.dp) for i in range(self.dp)])]
    ppermute x17 -> x16, waiting for transfers between devices: 30.8 us -> 20.7 us  [over_x(): return lax.ppermute(v, 'tensor', [(0, 1), (1, 0)])]
    ppermute x13, waiting for transfers between devices: 29.6 us -> 22 us  [over_y(): return lax.ppermute(v, 'dp', [(i, i ^ 2) for i in range(self.dp)])]
    dot_general x2 -> x0, matrix products: 7.21 us -> none  [dot(): lax.dot_general(left, right, (((1,), (0,)), ((), ())), preferred_element_...]
    ppermute x17 -> x16, starting transfers between devices: 20.1 us -> 19.9 us  [over_x(): return lax.ppermute(v, 'tensor', [(0, 1), (1, 0)])]
  transfers between devices with their start and end apart: 74 -> 73, of which waited for: 25 -> 28; matrix products, arithmetic and copies ran while one was open for 6% -> 5% of each run, Pallas kernels for 51% -> 45%
where the time goes in v6:
time: 571 us; the launch traced here: 562 us
  Pallas kernels  278 us (49%)
  waiting for transfers between devices  129 us (23%)
  starting transfers between devices  78.7 us (14%)
  local copies, waits for them, and re-layouts  58.9 us (10%)
  other arithmetic  9.5 us (2%)
    pallas_call x63, Pallas kernels, run(): pl.pallas_call(ordered, grid=grid, in_specs=list(in_specs) + [pl.BlockSpe...  278 us
    unnamed x352, local copies, waits for them, and re-layouts  44.4 us
    ppermute x9, waiting for transfers between devices, up_z(): lax.ppermute(v, 'dp', [(i, (i + 4) % self.dp) for i in range(self.dp)])  34.9 us
    ppermute x9, starting transfers between devices, down_z(): lax.ppermute(v, 'dp', [(i, (i - 4) % self.dp) for i in range(self.dp)])  32.2 us
    ppermute x9, waiting for transfers between devices, down_z(): lax.ppermute(v, 'dp', [(i, (i - 4) % self.dp) for i in range(self.dp)])  32.1 us
    ppermute x13, waiting for transfers between devices, over_y(): return lax.ppermute(v, 'dp', [(i, i ^ 2) for i in range(self.dp)])  22 us
    ppermute x16, waiting for transfers between devices, over_x(): return lax.ppermute(v, 'tensor', [(0, 1), (1, 0)])  20.7 us
    ppermute x16, starting transfers between devices, over_x(): return lax.ppermute(v, 'tensor', [(0, 1), (1, 0)])  19.9 us
  transfers between devices with their start and end apart: 73, of which 28 were waited for; matrix products, arithmetic and copies ran while one was open for 5% of the time, Pallas kernels for 45%

profile of v6, /device:TPU:0, one launch (start us, length us, event | category | flops | bytes accessed | tf_op | source)
XLA Modules:
  0.0 561.6 jit_solution(15520617270556633686)
XLA Ops:
  19.8 4.8 collective-permute-done.2.refs_1_
  64.5 13.7 %collective-permute-done.17 = f32[35,128]{1,0:T(8,128)S(1)} collective-permute-done((f32[35,128]{1,0:T(8,128)S(1)}, f32[35,128]{1,0:T(8,128)S(1)}, u32[]{:S(2)}, u32[]{:S(2)}) %collective-permute-start.17) | collective-permute-done | bytes 17952 | tf_op jit(solution)/shard_map/ppermute | solution.py:1092
  85.8 4.6 collective-permute-done.19.refs_4_.refs_3_
  92.9 4.7 collective-permute-start.22
  106.1 9.9 %shard_map.371.refs_1_.refs_0_ = f32[576,3840]{1,0:T(8,128)S(1)} custom-call(bf16[576,1280]{1,0:T(8,128)(2,1)S(1)} %get-tuple-element.106.refs_0_, bf16[320,1920]{1,0:T(8,128)(2,1)S(1)} %shard_map.364.refs_1_, bf16[320,1920]{1,0:T(8,128)(2,1)S(1)} %collective-permute-done.8.refs_1_.refs_2_, bf16[320,1920]{1,0:T(8,128)(2,1)S(1)} %collective-permute-done.9.refs_2_.refs_3_, ...), custom_call_target="tpu_custom_call" | custom-call | flops 128799997952 | tf_op jit(solution)/shard_map/pallas_call | solution.py:111
  116.1 12.4 %collective-permute-done.22.refs_0_ = bf16[160,5120]{1,0:T(8,128)(2,1)} collective-permute-done((bf16[160,5120]{1,0:T(8,128)(2,1)}, bf16[160,5120]{1,0:T(8,128)(2,1)}, u32[]{:S(2)}, u32[]{:S(2)}) %collective-permute-start.22) | collective-permute-done | bytes 1638432 | tf_op jit(solution)/shard_map/ppermute | solution.py:1101
  135.6 18.7 %shard_map.373 = (bf16[576,3840]{1,0:T(8,128)(2,1)S(1)}, bf16[576,1280]{1,0:T(8,128)(2,1)S(1)}, f32[2,8,576]{2,1,0:T(8,128)S(1)}) custom-call(f32[576,3840]{1,0:T(8,128)} %copy-done.109, f32[576,640]{1,0:T(8,128)S(1)} %copy-done.15, f32[576,640]{1,0:T(8,128)S(1)} %copy-done.17, s32[576,1]{1,0:T(8,128)S(1)} %broadcast_in_dim.54.refs_3_.refs_5_, ...), custom_call_target="tpu_custom_call" | custom-call | flops 180319993856 | tf_op jit(solution)/shard_map/pallas_call | solution.py:111
  161.9 9.6 %collective-permute-done.32.refs_3_ = bf16[160,5120]{1,0:T(8,128)(2,1)} collective-permute-done((bf16[160,5120]{1,0:T(8,128)(2,1)}, bf16[160,5120]{1,0:T(8,128)(2,1)}, u32[]{:S(2)}, u32[]{:S(2)}) %collective-permute-start.32) | collective-permute-done | bytes 1638432 | tf_op jit(solution)/shard_map/ppermute | solution.py:1101
  175.8 12.2 %collective-permute-done.27.refs_1_.refs_6_ = bf16[320,1920]{1,0:T(8,128)(2,1)S(1)} collective-permute-done((bf16[320,1920]{1,0:T(8,128)(2,1)S(1)}, bf16[320,1920]{1,0:T(8,128)(2,1)S(1)}, u32[]{:S(2)}, u32[]{:S(2)}) %collective-permute-start.27) | collective-permute-done | bytes 1228832 | tf_op jit(solution)/shard_map/ppermute | solution.py:1098
  194.4 7.5 %shard_map.377 = (f32[576,1280]{1,0:T(8,128)}, bf16[576,1280]{1,0:T(8,128)(2,1)S(1)}) custom-call(bf16[576,1280]{1,0:T(8,128)(2,1)S(1)} %get-tuple-element.110.refs_0_.refs_3_, bf16[320,3200]{1,0:T(8,128)(2,1)} %shard_map.370.refs_14_.refs_1_, bf16[320,3200]{1,0:T(8,128)(2,1)} %collective-permute-done.23.refs_1_.refs_2_, ...), custom_call_target="tpu_custom_call" | custom-call | flops 90159996928 | tf_op jit(solution)/shard_map/pallas_call | solution.py:111
  206.7 14.1 %shard_map.378 = (f32[576,5120]{1,0:T(8,128)}, bf16[576,5120]{1,0:T(8,128)(2,1)}) custom-call(bf16[576,1280]{1,0:T(8,128)(2,1)S(1)} %get-tuple-element.115.refs_0_, bf16[320,3200]{1,0:T(8,128)(2,1)} %shard_map.370.refs_14_.refs_1_, bf16[320,3200]{1,0:T(8,128)(2,1)} %collective-permute-done.23.refs_1_.refs_2_, bf16[320,3200]{1,0:T(8,128)(2,1)} %copy-done.10, ...), custom_call_target="tpu_custom_call" | custom-call | flops 163759996928 | tf_op jit(solution)/shard_map/pallas_call | solution.py:111
  227.8 7.8 %shard_map.379.refs_1_ = bf16[640,5120]{1,0:T(8,128)(2,1)} custom-call(bf16[576,1280]{1,0:T(8,128)(2,1)S(1)} %get-tuple-element.118.refs_0_, bf16[576,5120]{1,0:T(8,128)(2,1)S(1)} %copy-done.145, f32[576,5120]{1,0:T(8,128)S(1)} %copy-done.6), custom_call_target="tpu_custom_call" | custom-call | flops 552000028672 | tf_op jit(solution)/shard_map/pallas_call | solution.py:111
  237.9 4.6 collective-permute-done.35.refs_8_
  242.5 12.3 %shard_map.381.refs_3_.refs_0_ = bf16[576,1280]{1,0:T(8,128)(2,1)S(1)} custom-call(bf16[576,5120]{1,0:T(8,128)(2,1)} %get-tuple-element.117.refs_1_.refs_0_, bf16[160,5120]{1,0:T(8,128)(2,1)} %shard_map.369.refs_8_.refs_1_, bf16[160,5120]{1,0:T(8,128)(2,1)} %shard_map.372.refs_7_.refs_2_, bf16[160,5120]{1,0:T(8,128)(2,1)} %collective-permute-done.32.refs_3_, ...), custom_call_target="tpu_custom_call" | custom-call | flops 138000007168 | tf_op jit(solution)/shard_map/pallas_call | solution.py:111
  254.8 6.1 %shard_map.382 = (bf16[320,1280]{1,0:T(8,128)(2,1)S(1)}, bf16[640,1280]{1,0:T(8,128)(2,1)}, bf16[320,1280]{1,0:T(8,128)(2,1)S(1)}) custom-call(bf16[576,1280]{1,0:T(8,128)(2,1)S(1)} %get-tuple-element.118.refs_0_, bf16[576,5120]{1,0:T(8,128)(2,1)S(1)} %copy-done.146, bf16[640,5120]{1,0:T(8,128)(2,1)} %collective-permute-done.36.refs_2_, ...), custom_call_target="tpu_custom_call" | custom-call | flops 64399998976 | tf_op jit(solution)/shard_map/pallas_call | solution.py:111
  261.0 6.2 %shard_map.383 = (bf16[320,1280]{1,0:T(8,128)(2,1)S(1)}, bf16[320,1280]{1,0:T(8,128)(2,1)S(1)}, bf16[640,1280]{1,0:T(8,128)(2,1)}) custom-call(bf16[576,1280]{1,0:T(8,128)(2,1)S(1)} %get-tuple-element.118.refs_0_, bf16[576,5120]{1,0:T(8,128)(2,1)S(1)} %copy-done.146, bf16[640,5120]{1,0:T(8,128)(2,1)} %collective-permute-done.36.refs_2_, ...), custom_call_target="tpu_custom_call" | custom-call | flops 64399998976 | tf_op jit(solution)/shard_map/pallas_call | solution.py:111
  269.3 15.1 %shard_map.384 = (bf16[576,5120]{1,0:T(8,128)(2,1)}, f32[1,5120]{1,0:T(1,128)S(1)}) custom-call(bf16[576,1280]{1,0:T(8,128)(2,1)S(1)} %get-tuple-element.118.refs_0_, bf16[160,5120]{1,0:T(8,128)(2,1)} %shard_map.369.refs_8_.refs_1_, bf16[160,5120]{1,0:T(8,128)(2,1)} %shard_map.372.refs_7_.refs_2_, bf16[160,5120]{1,0:T(8,128)(2,1)} %collective-permute-done.32.refs_3_, ...), custom_call_target="tpu_custom_call" | custom-call | flops 920000000 | tf_op jit(solution)/shard_map/pallas_call | solution.py:111
  290.1 7.8 %shard_map.386.refs_17_ = bf16[640,5120]{1,0:T(8,128)(2,1)} custom-call(bf16[576,1280]{1,0:T(8,128)(2,1)S(1)} %copy-done.20, bf16[576,5120]{1,0:T(8,128)(2,1)S(1)} %copy-done.1, bf16[288,1280]{1,0:T(8,128)(2,1)S(1)} %get-tuple-element.123.refs_2_.refs_1_), custom_call_target="tpu_custom_call" | custom-call | flops 920000000 | tf_op jit(solution)/shard_map/pallas_call | solution.py:111
  298.4 20.7 %shard_map.387 = (f32[576,1280]{1,0:T(8,128)}, bf16[576,1280]{1,0:T(8,128)(2,1)}, f32[8,1280]{1,0:T(8,128)}) custom-call(bf16[576,5120]{1,0:T(8,128)(2,1)} %get-tuple-element.122.refs_2_.refs_1_.refs_0_, bf16[320,3200]{1,0:T(8,128)(2,1)} %shard_map.370.refs_14_.refs_1_, bf16[320,3200]{1,0:T(8,128)(2,1)} %collective-permute-done.23.refs_1_.refs_2_, ...), custom_call_target="tpu_custom_call" | custom-call | flops 920000000 | tf_op jit(solution)/shard_map/pallas_call | solution.py:111
  331.5 5.8 %shard_map.390 = (bf16[320,1280]{1,0:T(8,128)(2,1)S(1)}, bf16[640,1280]{1,0:T(8,128)(2,1)}, bf16[320,1280]{1,0:T(8,128)(2,1)S(1)}) custom-call(bf16[576,1280]{1,0:T(8,128)(2,1)S(1)} %copy-done.21, bf16[576,5120]{1,0:T(8,128)(2,1)S(1)} %copy-done.2, bf16[640,5120]{1,0:T(8,128)(2,1)} %collective-permute-done.42.refs_2_, ...), custom_call_target="tpu_custom_call" | custom-call | flops 64399998976 | tf_op jit(solution)/shard_map/pallas_call | solution.py:111
  337.3 6.4 %shard_map.391 = (bf16[320,1280]{1,0:T(8,128)(2,1)S(1)}, bf16[320,1280]{1,0:T(8,128)(2,1)S(1)}, bf16[640,1280]{1,0:T(8,128)(2,1)}) custom-call(bf16[576,1280]{1,0:T(8,128)(2,1)S(1)} %copy-done.21, bf16[576,5120]{1,0:T(8,128)(2,1)S(1)} %copy-done.2, bf16[640,5120]{1,0:T(8,128)(2,1)} %collective-permute-done.42.refs_2_, ...), custom_call_target="tpu_custom_call" | custom-call | flops 64399998976 | tf_op jit(solution)/shard_map/pallas_call | solution.py:111
  352.3 24.6 %shard_map.394 = (bf16[576,3840]{1,0:T(8,128)(2,1)S(1)}, f32[1,3840]{1,0:T(1,128)S(1)}) custom-call(bf16[576,3840]{1,0:T(8,128)(2,1)S(1)} %bitcast.97, f32[2,8,576]{2,1,0:T(8,128)S(1)} %get-tuple-element.135.refs_1_, bf16[576,1280]{1,0:T(8,128)(2,1)S(1)} %shard_map.389.refs_3_.refs_2_, f32[576,640]{1,0:T(8,128)S(1)} %copy-done.16, ...), custom_call_target="tpu_custom_call" | custom-call | flops 251160002560 | tf_op jit(solution)/shard_map/pallas_call | solution.py:111
  386.4 5.1 shard_map.397.refs_4_
  401.9 4.5 shard_map.398.refs_3_
  406.6 6.6 %shard_map.399 = (bf16[320,1280]{1,0:T(8,128)(2,1)S(1)}, bf16[640,1280]{1,0:T(8,128)(2,1)}, bf16[320,1280]{1,0:T(8,128)(2,1)S(1)}) custom-call(bf16[576,1280]{1,0:T(8,128)(2,1)S(1)} %copy-done.116, bf16[576,3840]{1,0:T(8,128)(2,1)S(1)} %copy-done.112, bf16[640,2560]{1,0:T(8,128)(2,1)} %collective-permute-done.47.refs_2_, ...), custom_call_target="tpu_custom_call" | custom-call | flops 73600000000 | tf_op jit(solution)/shard_map/pallas_call | solution.py:111
  419.8 6.1 %shard_map.402 = (bf16[320,1280]{1,0:T(8,128)(2,1)S(1)}, bf16[320,1280]{1,0:T(8,128)(2,1)S(1)}, bf16[640,1280]{1,0:T(8,128)(2,1)}) custom-call(bf16[576,1280]{1,0:T(8,128)(2,1)S(1)} %copy-done.116, bf16[576,1280]{1,0:T(8,128)(2,1)S(1)} %copy-done.64, bf16[576,3840]{1,0:T(8,128)(2,1)S(1)} %copy-done.112, bf16[576,1280]{1,0:T(8,128)(2,1)S(1)} %copy-done.119, ...), custom_call_target="tpu_custom_call" | custom-call | flops 73600000000 | tf_op jit(solution)/shard_map/pallas_call | solution.py:111
  438.6 15.2 %shard_map.405 = (bf16[576,1280]{1,0:T(8,128)(2,1)S(1)}, f32[8,1280]{1,0:T(8,128)S(1)}) custom-call(bf16[576,3840]{1,0:T(8,128)(2,1)} %copy-done.110, bf16[320,1920]{1,0:T(8,128)(2,1)S(1)} %copy-done.67, bf16[320,1920]{1,0:T(8,128)(2,1)S(1)} %copy-done.71, bf16[320,1920]{1,0:T(8,128)(2,1)S(1)} %copy-done.73, bf16[320,1920]{1,0:T(8,128)(2,1)S(1)} %copy-done.75, ...), custom_call_target="tpu_custom_call" | custom-call | flops 165600002048 | tf_op jit(solution)/shard_map/pallas_call | solution.py:111
  475.6 7.8 %collective-permute-done.59.refs_6_ = bf16[80,2560]{1,0:T(8,128)(2,1)S(1)} collective-permute-done((bf16[80,2560]{1,0:T(8,128)(2,1)S(1)}, bf16[80,2560]{1,0:T(8,128)(2,1)S(1)}, u32[]{:S(2)}, u32[]{:S(2)}) %collective-permute-start.59) | collective-permute-done | bytes 409632 | tf_op jit(solution)/shard_map/ppermute | solution.py:1104
  501.7 7.9 %collective-permute-done.64.refs_6_ = bf16[80,2560]{1,0:T(8,128)(2,1)S(1)} collective-permute-done((bf16[80,2560]{1,0:T(8,128)(2,1)S(1)}, bf16[80,2560]{1,0:T(8,128)(2,1)S(1)}, u32[]{:S(2)}, u32[]{:S(2)}) %collective-permute-start.64) | collective-permute-done | bytes 409632 | tf_op jit(solution)/shard_map/ppermute | solution.py:1104
  512.5 10.3 %collective-permute-done.66.refs_6_ = bf16[80,2560]{1,0:T(8,128)(2,1)S(1)} collective-permute-done((bf16[80,2560]{1,0:T(8,128)(2,1)S(1)}, bf16[80,2560]{1,0:T(8,128)(2,1)S(1)}, u32[]{:S(2)}, u32[]{:S(2)}) %collective-permute-start.66) | collective-permute-done | bytes 409632 | tf_op jit(solution)/shard_map/ppermute | solution.py:1104
  529.6 6.7 %collective-permute-done.67.refs_6_ = bf16[80,2560]{1,0:T(8,128)(2,1)} collective-permute-done((bf16[80,2560]{1,0:T(8,128)(2,1)}, bf16[80,2560]{1,0:T(8,128)(2,1)}, u32[]{:S(2)}, u32[]{:S(2)}) %collective-permute-start.67) | collective-permute-done | bytes 409632 | tf_op jit(solution)/shard_map/ppermute | solution.py:1104
  552.9 4.4 collective-permute-done.72
  (593 shorter events, 254.5 us)
Async XLA Ops:
  2.6 38.0 %collective-permute-start.5 = (bf16[80,2560]{1,0:T(8,128)(2,1)}, bf16[80,2560]{1,0:T(8,128)(2,1)}, u32[]{:S(2)}, u32[]{:S(2)}) collective-permute-start(bf16[80,2560]{1,0:T(8,128)(2,1)} %bitcast_convert_fusion.refs_0_), channel_id=1, source_target_pairs={{0,1},{1,0},{2,3},{3,2},{4,5},{5,4},{6,7},{7,6},{8,9},{9,8},{10,11... | collective-permute-start | bytes 1228808 | tf_op jit(solution)/shard_map/ppermute | solution.py:1092
  5.5 40.7 %collective-permute-start.6 = (bf16[80,2560]{1,0:T(8,128)(2,1)}, bf16[80,2560]{1,0:T(8,128)(2,1)}, u32[]{:S(2)}, u32[]{:S(2)}) collective-permute-start(bf16[80,2560]{1,0:T(8,128)(2,1)} %bitcast_convert_fusion.refs_0_), channel_id=1, source_target_pairs={{0,4},{2,6},{4,0},{6,2},{8,12},{10,14},{12,8},{14,10},{16,20},{18,... | collective-permute-start | bytes 1228808 | tf_op jit(solution)/shard_map/ppermute | solution.py:1098
  11.6 37.9 %collective-permute-start = (bf16[2,288,1280]{2,1,0:T(8,128)(2,1)}, bf16[2,288,1280]{2,1,0:T(8,128)(2,1)}, u32[]{:S(2)}, u32[]{:S(2)}) collective-permute-start(bf16[2,288,1280]{2,1,0:T(8,128)(2,1)} %pad_maximum_fusion), channel_id=1, source_target_pairs={{0,1},{1,0},{2,3},{3,2},{4,5},{5,4},{6,7},{7,6},{8,9},{9,8},{10,11... | collective-permute-start | bytes 4423688 | tf_op jit(solution)/shard_map/ppermute | solution.py:1092
  17.4 36.8 %collective-permute-start.1 = (bf16[80,3200]{1,0:T(8,128)(2,1)}, bf16[80,3200]{1,0:T(8,128)(2,1)}, u32[]{:S(2)}, u32[]{:S(2)}) collective-permute-start(bf16[80,3200]{1,0:T(8,128)(2,1)} %shard_map.363.refs_8_.refs_0_), channel_id=1, source_target_pairs={{0,24},{2,26},{4,28},{6,30},{8,0},{10,2},{12,4},{14,6},{16,8},{18,... | collective-permute-start | bytes 1536008 | tf_op jit(solution)/shard_map/ppermute | solution.py:1101
  51.6 31.5 %collective-permute-start.11 = (bf16[320,1920]{1,0:T(8,128)(2,1)S(1)}, bf16[320,1920]{1,0:T(8,128)(2,1)S(1)}, u32[]{:S(2)}, u32[]{:S(2)}) collective-permute-start(bf16[320,1920]{1,0:T(8,128)(2,1)S(1)} %shard_map.364.refs_1_), channel_id=1, source_target_pairs={{0,1},{1,0},{2,3},{3,2},{4,5},{5,4},{6,7},{7,6},{8,9},{9,8},{10,11... | collective-permute-start | bytes 3686408 | tf_op jit(solution)/shard_map/ppermute | solution.py:1092
  53.2 29.9 %collective-permute-start.8 = (bf16[320,1920]{1,0:T(8,128)(2,1)S(1)}, bf16[320,1920]{1,0:T(8,128)(2,1)S(1)}, u32[]{:S(2)}, u32[]{:S(2)}) collective-permute-start(bf16[320,1920]{1,0:T(8,128)(2,1)S(1)} %shard_map.364.refs_1_), channel_id=1, source_target_pairs={{0,4},{2,6},{4,0},{6,2},{8,12},{10,14},{12,8},{14,10},{16,20},{18,... | collective-permute-start | bytes 3686408 | tf_op jit(solution)/shard_map/ppermute | solution.py:1098
  54.2 28.9 %collective-permute-start.9 = (bf16[320,1920]{1,0:T(8,128)(2,1)S(1)}, bf16[320,1920]{1,0:T(8,128)(2,1)S(1)}, u32[]{:S(2)}, u32[]{:S(2)}) collective-permute-start(bf16[320,1920]{1,0:T(8,128)(2,1)S(1)} %shard_map.364.refs_1_), channel_id=1, source_target_pairs={{0,2},{2,0},{4,6},{6,4},{8,10},{10,8},{12,14},{14,12},{16,18},{18,... | collective-permute-start | bytes 3686408 | tf_op jit(solution)/shard_map/ppermute | solution.py:1095
  55.3 23.6 %collective-permute-start.18 = (bf16[80,3200]{1,0:T(8,128)(2,1)S(1)}, bf16[80,3200]{1,0:T(8,128)(2,1)S(1)}, u32[]{:S(2)}, u32[]{:S(2)}) collective-permute-start(bf16[80,3200]{1,0:T(8,128)(2,1)S(1)} %shard_map.365.refs_4_.refs_1_), channel_id=1, source_target_pairs={{0,24},{2,26},{4,28},{6,30},{8,0},{10,2},{12,4},{14,6},{16,8},{18,... | collective-permute-start | bytes 1536008 | tf_op jit(solution)/shard_map/ppermute | solution.py:1101
  92.9 35.6 %collective-permute-start.22 = (bf16[160,5120]{1,0:T(8,128)(2,1)}, bf16[160,5120]{1,0:T(8,128)(2,1)}, u32[]{:S(2)}, u32[]{:S(2)}) collective-permute-start(bf16[160,5120]{1,0:T(8,128)(2,1)} %shard_map.369.refs_8_.refs_1_), channel_id=1, source_target_pairs={{0,24},{2,26},{4,28},{6,30},{8,0},{10,2},{12,4},{14,6},{16,8},{18,... | collective-permute-start | bytes 4915208 | tf_op jit(solution)/shard_map/ppermute | solution.py:1101
  97.7 33.5 %collective-permute-start.21 = (bf16[160,5120]{1,0:T(8,128)(2,1)}, bf16[160,5120]{1,0:T(8,128)(2,1)}, u32[]{:S(2)}, u32[]{:S(2)}) collective-permute-start(bf16[160,5120]{1,0:T(8,128)(2,1)} %shard_map.369.refs_8_.refs_1_), channel_id=1, source_target_pairs={{0,2},{2,0},{4,6},{6,4},{8,10},{10,8},{12,14},{14,12},{16,18},{18,... | collective-permute-start | bytes 4915208 | tf_op jit(solution)/shard_map/ppermute | solution.py:1095
  103.9 31.6 %collective-permute-start.20 = (bf16[320,3200]{1,0:T(8,128)(2,1)}, bf16[320,3200]{1,0:T(8,128)(2,1)S(1)}, u32[]{:S(2)}, u32[]{:S(2)}) collective-permute-start(bf16[320,3200]{1,0:T(8,128)(2,1)} %shard_map.370.refs_14_.refs_1_), channel_id=1, source_target_pairs={{0,2},{2,0},{4,6},{6,4},{8,10},{10,8},{12,14},{14,12},{16,18},{18,... | collective-permute-start | bytes 6144008 | tf_op jit(solution)/shard_map/ppermute | solution.py:1095
  104.0 50.3 %collective-permute-start.23 = (bf16[320,3200]{1,0:T(8,128)(2,1)}, bf16[320,3200]{1,0:T(8,128)(2,1)}, u32[]{:S(2)}, u32[]{:S(2)}) collective-permute-start(bf16[320,3200]{1,0:T(8,128)(2,1)} %shard_map.370.refs_14_.refs_1_), channel_id=1, source_target_pairs={{0,4},{2,6},{4,0},{6,2},{8,12},{10,14},{12,8},{14,10},{16,20},{18,... | collective-permute-start | bytes 6144008 | tf_op jit(solution)/shard_map/ppermute | solution.py:1098
  104.5 49.8 %collective-permute-start.25 = (bf16[320,3200]{1,0:T(8,128)(2,1)}, bf16[320,3200]{1,0:T(8,128)(2,1)}, u32[]{:S(2)}, u32[]{:S(2)}) collective-permute-start(bf16[320,3200]{1,0:T(8,128)(2,1)} %shard_map.370.refs_14_.refs_1_), channel_id=1, source_target_pairs={{0,1},{1,0},{2,3},{3,2},{4,5},{5,4},{6,7},{7,6},{8,9},{9,8},{10,11... | collective-permute-start | bytes 6144008 | tf_op jit(solution)/shard_map/ppermute | solution.py:1092
  131.2 40.3 %collective-permute-start.32 = (bf16[160,5120]{1,0:T(8,128)(2,1)}, bf16[160,5120]{1,0:T(8,128)(2,1)}, u32[]{:S(2)}, u32[]{:S(2)}) collective-permute-start(bf16[160,5120]{1,0:T(8,128)(2,1)} %shard_map.372.refs_7_.refs_2_), channel_id=1, source_target_pairs={{0,24},{2,26},{4,28},{6,30},{8,0},{10,2},{12,4},{14,6},{16,8},{18,... | collective-permute-start | bytes 4915208 | tf_op jit(solution)/shard_map/ppermute | solution.py:1101
  158.9 29.2 %collective-permute-start.27 = (bf16[320,1920]{1,0:T(8,128)(2,1)S(1)}, bf16[320,1920]{1,0:T(8,128)(2,1)S(1)}, u32[]{:S(2)}, u32[]{:S(2)}) collective-permute-start(bf16[320,1920]{1,0:T(8,128)(2,1)S(1)} %get-tuple-element.112.refs_4_), channel_id=1, source_target_pairs={{0,4},{2,6},{4,0},{6,2},{8,12},{10,14},{12,8},{14,10},{16,20},{18,... | collective-permute-start | bytes 3686408 | tf_op jit(solution)/shard_map/ppermute | solution.py:1098
  159.8 31.9 %collective-permute-start.30 = (bf16[320,1280]{1,0:T(8,128)(2,1)S(1)}, bf16[320,1280]{1,0:T(8,128)(2,1)S(1)}, u32[]{:S(2)}, u32[]{:S(2)}) collective-permute-start(bf16[320,1280]{1,0:T(8,128)(2,1)S(1)} %get-tuple-element.113), channel_id=1, source_target_pairs={{0,1},{1,0},{2,3},{3,2},{4,5},{5,4},{6,7},{7,6},{8,9},{9,8},{10,11... | collective-permute-start | bytes 2457608 | tf_op jit(solution)/shard_map/ppermute | solution.py:1092
  161.4 31.5 %collective-permute-start.24 = (bf16[320,3200]{1,0:T(8,128)(2,1)}, bf16[320,3200]{1,0:T(8,128)(2,1)S(1)}, u32[]{:S(2)}, u32[]{:S(2)}) collective-permute-start(bf16[320,3200]{1,0:T(8,128)(2,1)} %collective-permute-done.23.refs_1_.refs_2_), channel_id=1, source_target_pairs={{0,2},{2,0},{4,6},{6,4},{8,10},{10,8},{12,14},{14,12},{16,18},{18,... | collective-permute-start | bytes 6144008 | tf_op jit(solution)/shard_map/ppermute | solution.py:1095
  161.4 31.7 %collective-permute-start.28 = (bf16[320,3200]{1,0:T(8,128)(2,1)}, bf16[320,3200]{1,0:T(8,128)(2,1)S(1)}, u32[]{:S(2)}, u32[]{:S(2)}) collective-permute-start(bf16[320,3200]{1,0:T(8,128)(2,1)} %collective-permute-done.25.refs_0_.refs_5_.refs_9_), channel_id=1, source_target_pairs={{0,2},{2,0},{4,6},{6,4},{8,10},{10,8},{12,14},{14,12},{16,18},{18,... | collective-permute-start | bytes 6144008 | tf_op jit(solution)/shard_map/ppermute | solution.py:1095
  171.5 64.0 %collective-permute-start.33 = (bf16[160,5120]{1,0:T(8,128)(2,1)}, bf16[160,5120]{1,0:T(8,128)(2,1)}, u32[]{:S(2)}, u32[]{:S(2)}) collective-permute-start(bf16[160,5120]{1,0:T(8,128)(2,1)} %collective-permute-done.32.refs_3_), channel_id=1, source_target_pairs={{0,24},{2,26},{4,28},{6,30},{8,0},{10,2},{12,4},{14,6},{16,8},{18,... | collective-permute-start | bytes 4915208 | tf_op jit(solution)/shard_map/ppermute | solution.py:1101
  191.7 46.1 %collective-permute-start.34 = (bf16[160,5120]{1,0:T(8,128)(2,1)}, bf16[160,5120]{1,0:T(8,128)(2,1)}, u32[]{:S(2)}, u32[]{:S(2)}) collective-permute-start(bf16[160,5120]{1,0:T(8,128)(2,1)} %collective-permute-done.32.refs_3_), channel_id=1, source_target_pairs={{0,2},{2,0},{4,6},{6,4},{8,10},{10,8},{12,14},{14,12},{16,18},{18,... | collective-permute-start | bytes 4915208 | tf_op jit(solution)/shard_map/ppermute | solution.py:1095
  267.2 52.0 %collective-permute-start.39 = (bf16[640,1280]{1,0:T(8,128)(2,1)}, bf16[640,1280]{1,0:T(8,128)(2,1)S(1)}, u32[]{:S(2)}, u32[]{:S(2)}) collective-permute-start(bf16[640,1280]{1,0:T(8,128)(2,1)} %get-tuple-element.126), channel_id=1, source_target_pairs={{0,1},{1,0},{2,3},{3,2},{4,5},{5,4},{6,7},{7,6},{8,9},{9,8},{10,11... | collective-permute-start | bytes 4915208 | tf_op jit(solution)/shard_map/ppermute | solution.py:1092
  268.7 50.5 %collective-permute-start.38 = (bf16[640,1280]{1,0:T(8,128)(2,1)}, bf16[640,1280]{1,0:T(8,128)(2,1)}, u32[]{:S(2)}, u32[]{:S(2)}) collective-permute-start(bf16[640,1280]{1,0:T(8,128)(2,1)} %get-tuple-element.125), channel_id=1, source_target_pairs={{0,4},{2,6},{4,0},{6,2},{8,12},{10,14},{12,8},{14,10},{16,20},{18,... | collective-permute-start | bytes 4915208 | tf_op jit(solution)/shard_map/ppermute | solution.py:1098
  297.9 33.6 %collective-permute-start.42 = (bf16[640,5120]{1,0:T(8,128)(2,1)}, bf16[640,5120]{1,0:T(8,128)(2,1)}, u32[]{:S(2)}, u32[]{:S(2)}) collective-permute-start(bf16[640,5120]{1,0:T(8,128)(2,1)} %shard_map.386.refs_17_), channel_id=1, source_target_pairs={{0,2},{2,0},{4,6},{6,4},{8,10},{10,8},{12,14},{14,12},{16,18},{18,... | collective-permute-start | bytes 19660808 | tf_op jit(solution)/shard_map/ppermute | solution.py:1095
  297.9 50.4 %collective-permute-start.37 = (bf16[288,1280]{1,0:T(8,128)(2,1)}, bf16[288,1280]{1,0:T(8,128)(2,1)}, u32[]{:S(2)}, u32[]{:S(2)}) collective-permute-start(bf16[288,1280]{1,0:T(8,128)(2,1)} %get-tuple-element.124), channel_id=1, source_target_pairs={{0,1},{1,0},{2,3},{3,2},{4,5},{5,4},{6,7},{7,6},{8,9},{9,8},{10,11... | collective-permute-start | bytes 2211848 | tf_op jit(solution)/shard_map/ppermute | solution.py:1092
  343.7 37.6 %collective-permute-start.45 = (bf16[640,1280]{1,0:T(8,128)(2,1)}, bf16[640,1280]{1,0:T(8,128)(2,1)}, u32[]{:S(2)}, u32[]{:S(2)}) collective-permute-start(bf16[640,1280]{1,0:T(8,128)(2,1)} %get-tuple-element.140), channel_id=1, source_target_pairs={{0,1},{1,0},{2,3},{3,2},{4,5},{5,4},{6,7},{7,6},{8,9},{9,8},{10,11... | collective-permute-start | bytes 4915208 | tf_op jit(solution)/shard_map/ppermute | solution.py:1092
  344.3 37.9 %collective-permute-start.44 = (bf16[640,1280]{1,0:T(8,128)(2,1)}, bf16[640,1280]{1,0:T(8,128)(2,1)}, u32[]{:S(2)}, u32[]{:S(2)}) collective-permute-start(bf16[640,1280]{1,0:T(8,128)(2,1)} %get-tuple-element.139), channel_id=1, source_target_pairs={{0,4},{2,6},{4,0},{6,2},{8,12},{10,14},{12,8},{14,10},{16,20},{18,... | collective-permute-start | bytes 4915208 | tf_op jit(solution)/shard_map/ppermute | solution.py:1098
  348.3 35.8 %collective-permute-start.43 = (bf16[80,2560]{1,0:T(8,128)(2,1)}, bf16[80,2560]{1,0:T(8,128)(2,1)}, u32[]{:S(2)}, u32[]{:S(2)}) collective-permute-start(bf16[80,2560]{1,0:T(8,128)(2,1)} %shard_map.392.refs_3_), channel_id=1, source_target_pairs={{0,8},{2,10},{4,12},{6,14},{8,16},{10,18},{12,20},{14,22},{16,24},... | collective-permute-start | bytes 1228808 | tf_op jit(solution)/shard_map/ppermute | solution.py:1104
  418.8 35.1 %collective-permute-start.54 = (bf16[80,2560]{1,0:T(8,128)(2,1)}, bf16[80,2560]{1,0:T(8,128)(2,1)}, u32[]{:S(2)}, u32[]{:S(2)}) collective-permute-start(bf16[80,2560]{1,0:T(8,128)(2,1)} %shard_map.401.refs_5_), channel_id=1, source_target_pairs={{0,8},{2,10},{4,12},{6,14},{8,16},{10,18},{12,20},{14,22},{16,24},... | collective-permute-start | bytes 1228808 | tf_op jit(solution)/shard_map/ppermute | solution.py:1104
  425.8 37.9 %collective-permute-start.53 = (bf16[640,1280]{1,0:T(8,128)(2,1)}, bf16[640,1280]{1,0:T(8,128)(2,1)}, u32[]{:S(2)}, u32[]{:S(2)}) collective-permute-start(bf16[640,1280]{1,0:T(8,128)(2,1)} %get-tuple-element.148), channel_id=1, source_target_pairs={{0,1},{1,0},{2,3},{3,2},{4,5},{5,4},{6,7},{7,6},{8,9},{9,8},{10,11... | collective-permute-start | bytes 4915208 | tf_op jit(solution)/shard_map/ppermute | solution.py:1092
  427.3 37.6 %collective-permute-start.52 = (bf16[640,1280]{1,0:T(8,128)(2,1)}, bf16[640,1280]{1,0:T(8,128)(2,1)}, u32[]{:S(2)}, u32[]{:S(2)}) collective-permute-start(bf16[640,1280]{1,0:T(8,128)(2,1)} %get-tuple-element.147), channel_id=1, source_target_pairs={{0,4},{2,6},{4,0},{6,2},{8,12},{10,14},{12,8},{14,10},{16,20},{18,... | collective-permute-start | bytes 4915208 | tf_op jit(solution)/shard_map/ppermute | solution.py:1098
  469.1 23.2 %collective-permute-start.55 = (bf16[320,1280]{1,0:T(8,128)(2,1)S(1)}, bf16[320,1280]{1,0:T(8,128)(2,1)S(1)}, u32[]{:S(2)}, u32[]{:S(2)}) collective-permute-start(bf16[320,1280]{1,0:T(8,128)(2,1)S(1)} %get-tuple-element.151.refs_7_), channel_id=1, source_target_pairs={{0,1},{1,0},{2,3},{3,2},{4,5},{5,4},{6,7},{7,6},{8,9},{9,8},{10,11... | collective-permute-start | bytes 2457608 | tf_op jit(solution)/shard_map/ppermute | solution.py:1092
  500.5 25.9 %collective-permute-start.61 = (bf16[288,1280]{1,0:T(8,128)(2,1)S(1)}, bf16[288,1280]{1,0:T(8,128)(2,1)}, u32[]{:S(2)}, u32[]{:S(2)}) collective-permute-start(bf16[288,1280]{1,0:T(8,128)(2,1)S(1)} %get-tuple-element.159), channel_id=1, source_target_pairs={{0,1},{1,0},{2,3},{3,2},{4,5},{5,4},{6,7},{7,6},{8,9},{9,8},{10,11... | collective-permute-start | bytes 2211848 | tf_op jit(solution)/shard_map/ppermute | solution.py:1092
  (216 other events, 2169.4 us)

commit v7 on v6

--- a/solution.py
+++ b/solution.py
@@ -71,7 +71,7 @@
 
 
 VMEM_MOST = 56 * 1024 * 1024
-VMEM_SPARE = 14 * 1024 * 1024
+VMEM_SPARE = 6 * 1024 * 1024
 COST = int(8 * 1.15e9)
 
 

time: 571 us -> 562 us (0.984)
  Pallas kernels: 278 us -> 271 us
    pallas_call x63, Pallas kernels: 278 us -> 271 us  [run(): pl.pallas_call(ordered, grid=grid, in_specs=list(in_specs) + [pl.BlockSpe...]
    unnamed x352 -> x362, local copies, waits for them, and re-layouts: 44.4 us -> 43.6 us
where the time goes in v7:
time: 562 us; the launch traced here: 553 us
  Pallas kernels  271 us (48%)
  waiting for transfers between devices  127 us (23%)
  starting transfers between devices  78.8 us (14%)
  local copies, waits for them, and re-layouts  59.4 us (11%)
  other arithmetic  9.51 us (2%)
    pallas_call x63, Pallas kernels, run(): pl.pallas_call(ordered, grid=grid, in_specs=list(in_specs) + [pl.BlockSpe...  271 us
    unnamed x362, local copies, waits for them, and re-layouts  43.6 us
    ppermute x9, waiting for transfers between devices, down_z(): lax.ppermute(v, 'dp', [(i, (i - 4) % self.dp) for i in range(self.dp)])  34.5 us
    ppermute x9, starting transfers between devices, down_z(): lax.ppermute(v, 'dp', [(i, (i - 4) % self.dp) for i in range(self.dp)])  33 us
    ppermute x9, waiting for transfers between devices, up_z(): lax.ppermute(v, 'dp', [(i, (i + 4) % self.dp) for i in range(self.dp)])  31.7 us
    ppermute x16, waiting for transfers between devices, over_x(): return lax.ppermute(v, 'tensor', [(0, 1), (1, 0)])  21.5 us
    ppermute x13, waiting for transfers between devices, over_y(): return lax.ppermute(v, 'dp', [(i, i ^ 2) for i in range(self.dp)])  20.5 us
    ppermute x16, starting transfers between devices, over_x(): return lax.ppermute(v, 'tensor', [(0, 1), (1, 0)])  19.7 us
  transfers between devices with their start and end apart: 73, of which 28 were waited for; matrix products, arithmetic and copies ran while one was open for 5% of the time, Pallas kernels for 45%

profile of v7, /device:TPU:0, one launch (start us, length us, event | category | flops | bytes accessed | tf_op | source)
XLA Modules:
  0.0 552.9 jit_solution(2443865832622536260)
XLA Ops:
  21.1 4.8 collective-permute-done.2.refs_1_
  65.8 13.7 %collective-permute-done.17 = f32[35,128]{1,0:T(8,128)S(1)} collective-permute-done((f32[35,128]{1,0:T(8,128)S(1)}, f32[35,128]{1,0:T(8,128)S(1)}, u32[]{:S(2)}, u32[]{:S(2)}) %collective-permute-start.17) | collective-permute-done | bytes 17952 | tf_op jit(solution)/shard_map/ppermute | solution.py:1092
  87.1 4.6 collective-permute-done.19.refs_4_.refs_3_
  94.3 4.7 collective-permute-start.22
  107.4 9.9 %shard_map.371.refs_1_.refs_0_ = f32[576,3840]{1,0:T(8,128)S(1)} custom-call(bf16[576,1280]{1,0:T(8,128)(2,1)S(1)} %get-tuple-element.106.refs_0_, bf16[320,1920]{1,0:T(8,128)(2,1)S(1)} %shard_map.364.refs_1_, bf16[320,1920]{1,0:T(8,128)(2,1)S(1)} %collective-permute-done.8.refs_1_.refs_2_, bf16[320,1920]{1,0:T(8,128)(2,1)S(1)} %collective-permute-done.9.refs_2_.refs_3_, ...), custom_call_target="tpu_custom_call" | custom-call | flops 128799997952 | tf_op jit(solution)/shard_map/pallas_call | solution.py:111
  117.4 12.4 %collective-permute-done.22.refs_0_ = bf16[160,5120]{1,0:T(8,128)(2,1)} collective-permute-done((bf16[160,5120]{1,0:T(8,128)(2,1)}, bf16[160,5120]{1,0:T(8,128)(2,1)}, u32[]{:S(2)}, u32[]{:S(2)}) %collective-permute-start.22) | collective-permute-done | bytes 1638432 | tf_op jit(solution)/shard_map/ppermute | solution.py:1101
  136.8 16.5 %shard_map.373 = (bf16[576,3840]{1,0:T(8,128)(2,1)S(1)}, bf16[576,1280]{1,0:T(8,128)(2,1)S(1)}, f32[2,8,576]{2,1,0:T(8,128)S(1)}) custom-call(f32[576,3840]{1,0:T(8,128)S(1)} %shard_map.371.refs_1_.refs_0_, f32[576,640]{1,0:T(8,128)S(1)} %copy-done.12, f32[576,640]{1,0:T(8,128)S(1)} %copy-done.14, s32[576,1]{1,0:T(8,128)S(1)} %broadcast_in_dim.54.refs_3_.refs_5_, ...), custom_call_target="tpu_custom_call" | custom-call | flops 180319993856 | tf_op jit(solution)/shard_map/pallas_call | solution.py:111
  160.9 12.0 %collective-permute-done.32.refs_3_ = bf16[160,5120]{1,0:T(8,128)(2,1)} collective-permute-done((bf16[160,5120]{1,0:T(8,128)(2,1)}, bf16[160,5120]{1,0:T(8,128)(2,1)}, u32[]{:S(2)}, u32[]{:S(2)}) %collective-permute-start.32) | collective-permute-done | bytes 1638432 | tf_op jit(solution)/shard_map/ppermute | solution.py:1101
  177.1 10.0 %collective-permute-done.27.refs_1_.refs_6_ = bf16[320,1920]{1,0:T(8,128)(2,1)S(1)} collective-permute-done((bf16[320,1920]{1,0:T(8,128)(2,1)S(1)}, bf16[320,1920]{1,0:T(8,128)(2,1)S(1)}, u32[]{:S(2)}, u32[]{:S(2)}) %collective-permute-start.27) | collective-permute-done | bytes 1228832 | tf_op jit(solution)/shard_map/ppermute | solution.py:1098
  193.5 6.5 %shard_map.377 = (f32[576,1280]{1,0:T(8,128)S(1)}, bf16[576,1280]{1,0:T(8,128)(2,1)S(1)}) custom-call(bf16[576,1280]{1,0:T(8,128)(2,1)S(1)} %get-tuple-element.110.refs_0_.refs_3_, bf16[320,3200]{1,0:T(8,128)(2,1)} %shard_map.370.refs_14_.refs_1_, bf16[320,3200]{1,0:T(8,128)(2,1)} %collective-permute-done.23.refs_1_.refs_2_, ...), custom_call_target="tpu_custom_call" | custom-call | flops 90159996928 | tf_op jit(solution)/shard_map/pallas_call | solution.py:111
  201.6 13.8 %shard_map.378 = (f32[576,5120]{1,0:T(8,128)}, bf16[576,5120]{1,0:T(8,128)(2,1)}) custom-call(bf16[576,1280]{1,0:T(8,128)(2,1)S(1)} %get-tuple-element.115.refs_0_, bf16[320,3200]{1,0:T(8,128)(2,1)} %shard_map.370.refs_14_.refs_1_, bf16[320,3200]{1,0:T(8,128)(2,1)} %collective-permute-done.23.refs_1_.refs_2_, ...), custom_call_target="tpu_custom_call" | custom-call | flops 163759996928 | tf_op jit(solution)/shard_map/pallas_call | solution.py:111
  222.4 7.0 %shard_map.379.refs_1_ = bf16[640,5120]{1,0:T(8,128)(2,1)S(1)} custom-call(bf16[576,1280]{1,0:T(8,128)(2,1)S(1)} %get-tuple-element.118.refs_0_, bf16[576,5120]{1,0:T(8,128)(2,1)S(1)} %copy-done.152, f32[576,5120]{1,0:T(8,128)S(1)} %copy-done.2), custom_call_target="tpu_custom_call" | custom-call | flops 552000028672 | tf_op jit(solution)/shard_map/pallas_call | solution.py:111
  231.7 4.5 collective-permute-done.35.refs_8_
  236.2 12.4 %shard_map.381.refs_3_.refs_0_ = bf16[576,1280]{1,0:T(8,128)(2,1)S(1)} custom-call(bf16[576,5120]{1,0:T(8,128)(2,1)S(1)} %copy-done.153, bf16[160,5120]{1,0:T(8,128)(2,1)} %shard_map.369.refs_8_.refs_1_, bf16[160,5120]{1,0:T(8,128)(2,1)} %shard_map.372.refs_7_.refs_2_, bf16[160,5120]{1,0:T(8,128)(2,1)} %collective-permute-done.32.refs_3_, ...), custom_call_target="tpu_custom_call" | custom-call | flops 138000007168 | tf_op jit(solution)/shard_map/pallas_call | solution.py:111
  248.6 5.7 %shard_map.382 = (bf16[320,1280]{1,0:T(8,128)(2,1)S(1)}, bf16[640,1280]{1,0:T(8,128)(2,1)}, bf16[320,1280]{1,0:T(8,128)(2,1)S(1)}) custom-call(bf16[576,1280]{1,0:T(8,128)(2,1)S(1)} %copy-done.21, bf16[576,5120]{1,0:T(8,128)(2,1)S(1)} %copy-done.153, bf16[640,5120]{1,0:T(8,128)(2,1)} %collective-permute-done.36.refs_2_, ...), custom_call_target="tpu_custom_call" | custom-call | flops 64399998976 | tf_op jit(solution)/shard_map/pallas_call | solution.py:111
  255.3 6.2 %shard_map.383 = (bf16[320,1280]{1,0:T(8,128)(2,1)S(1)}, bf16[320,1280]{1,0:T(8,128)(2,1)S(1)}, bf16[640,1280]{1,0:T(8,128)(2,1)}) custom-call(bf16[576,1280]{1,0:T(8,128)(2,1)S(1)} %copy-done.21, bf16[576,5120]{1,0:T(8,128)(2,1)S(1)} %copy-done.153, bf16[640,5120]{1,0:T(8,128)(2,1)} %collective-permute-done.36.refs_2_, ...), custom_call_target="tpu_custom_call" | custom-call | flops 64399998976 | tf_op jit(solution)/shard_map/pallas_call | solution.py:111
  263.6 13.7 %shard_map.384 = (bf16[576,5120]{1,0:T(8,128)(2,1)S(1)}, f32[1,5120]{1,0:T(1,128)S(1)}) custom-call(bf16[576,1280]{1,0:T(8,128)(2,1)S(1)} %copy-done.21, bf16[160,5120]{1,0:T(8,128)(2,1)} %shard_map.369.refs_8_.refs_1_, bf16[160,5120]{1,0:T(8,128)(2,1)} %shard_map.372.refs_7_.refs_2_, bf16[160,5120]{1,0:T(8,128)(2,1)} %collective-permute-done.32.refs_3_, ...), custom_call_target="tpu_custom_call" | custom-call | flops 920000000 | tf_op jit(solution)/shard_map/pallas_call | solution.py:111
  280.4 7.8 %shard_map.386.refs_17_ = bf16[640,5120]{1,0:T(8,128)(2,1)} custom-call(bf16[576,1280]{1,0:T(8,128)(2,1)S(1)} %get-tuple-element.115.refs_0_, bf16[576,5120]{1,0:T(8,128)(2,1)S(1)} %get-tuple-element.122.refs_2_.refs_1_.refs_0_, bf16[288,1280]{1,0:T(8,128)(2,1)S(1)} %get-tuple-element.123.refs_2_.refs_1_), custom_call_target="tpu_custom_call" | custom-call | flops 920000000 | tf_op jit(solution)/shard_map/pallas_call | solution.py:111
  288.7 19.4 %shard_map.387 = (f32[576,1280]{1,0:T(8,128)}, bf16[576,1280]{1,0:T(8,128)(2,1)S(1)}, f32[8,1280]{1,0:T(8,128)S(1)}) custom-call(bf16[576,5120]{1,0:T(8,128)(2,1)} %copy-done, bf16[320,3200]{1,0:T(8,128)(2,1)} %shard_map.370.refs_14_.refs_1_, bf16[320,3200]{1,0:T(8,128)(2,1)} %collective-permute-done.23.refs_1_.refs_2_, bf16[320,3200]{1,0:T(8,128)(2,1)} %copy-done.7, ...), custom_call_target="tpu_custom_call" | custom-call | flops 920000000 | tf_op jit(solution)/shard_map/pallas_call | solution.py:111
  322.7 5.8 %shard_map.390 = (bf16[320,1280]{1,0:T(8,128)(2,1)S(1)}, bf16[640,1280]{1,0:T(8,128)(2,1)}, bf16[320,1280]{1,0:T(8,128)(2,1)S(1)}) custom-call(bf16[576,1280]{1,0:T(8,128)(2,1)S(1)} %copy-done.17, bf16[576,5120]{1,0:T(8,128)(2,1)S(1)} %copy-done.1, bf16[640,5120]{1,0:T(8,128)(2,1)} %collective-permute-done.42.refs_2_, ...), custom_call_target="tpu_custom_call" | custom-call | flops 64399998976 | tf_op jit(solution)/shard_map/pallas_call | solution.py:111
  328.5 6.4 %shard_map.391 = (bf16[320,1280]{1,0:T(8,128)(2,1)S(1)}, bf16[320,1280]{1,0:T(8,128)(2,1)S(1)}, bf16[640,1280]{1,0:T(8,128)(2,1)}) custom-call(bf16[576,1280]{1,0:T(8,128)(2,1)S(1)} %copy-done.17, bf16[576,5120]{1,0:T(8,128)(2,1)S(1)} %copy-done.1, bf16[640,5120]{1,0:T(8,128)(2,1)} %collective-permute-done.42.refs_2_, ...), custom_call_target="tpu_custom_call" | custom-call | flops 64399998976 | tf_op jit(solution)/shard_map/pallas_call | solution.py:111
  343.6 24.6 %shard_map.394 = (bf16[576,3840]{1,0:T(8,128)(2,1)S(1)}, f32[1,3840]{1,0:T(1,128)S(1)}) custom-call(bf16[576,3840]{1,0:T(8,128)(2,1)S(1)} %bitcast.97, f32[2,8,576]{2,1,0:T(8,128)S(1)} %get-tuple-element.135.refs_1_, bf16[576,1280]{1,0:T(8,128)(2,1)S(1)} %shard_map.389.refs_3_.refs_2_, f32[576,640]{1,0:T(8,128)S(1)} %copy-done.13, ...), custom_call_target="tpu_custom_call" | custom-call | flops 251160002560 | tf_op jit(solution)/shard_map/pallas_call | solution.py:111
  377.1 5.1 shard_map.397.refs_4_
  392.6 4.5 shard_map.398.refs_3_
  397.3 6.7 %shard_map.399 = (bf16[320,1280]{1,0:T(8,128)(2,1)S(1)}, bf16[640,1280]{1,0:T(8,128)(2,1)}, bf16[320,1280]{1,0:T(8,128)(2,1)S(1)}) custom-call(bf16[576,1280]{1,0:T(8,128)(2,1)S(1)} %copy-done.118, bf16[576,3840]{1,0:T(8,128)(2,1)S(1)} %copy-done.114, bf16[640,2560]{1,0:T(8,128)(2,1)} %collective-permute-done.47.refs_2_, ...), custom_call_target="tpu_custom_call" | custom-call | flops 73600000000 | tf_op jit(solution)/shard_map/pallas_call | solution.py:111
  411.7 6.1 %shard_map.402 = (bf16[320,1280]{1,0:T(8,128)(2,1)S(1)}, bf16[320,1280]{1,0:T(8,128)(2,1)S(1)}, bf16[640,1280]{1,0:T(8,128)(2,1)}) custom-call(bf16[576,1280]{1,0:T(8,128)(2,1)S(1)} %copy-done.118, bf16[576,1280]{1,0:T(8,128)(2,1)S(1)} %copy-done.58, bf16[576,3840]{1,0:T(8,128)(2,1)S(1)} %copy-done.114, bf16[576,1280]{1,0:T(8,128)(2,1)S(1)} %copy-done.121, ...), custom_call_target="tpu_custom_call" | custom-call | flops 73600000000 | tf_op jit(solution)/shard_map/pallas_call | solution.py:111
  431.0 13.6 %shard_map.405 = (bf16[576,1280]{1,0:T(8,128)(2,1)S(1)}, f32[8,1280]{1,0:T(8,128)S(1)}) custom-call(bf16[576,3840]{1,0:T(8,128)(2,1)S(1)} %copy-done.114, bf16[320,1920]{1,0:T(8,128)(2,1)S(1)} %copy-done.61, bf16[320,1920]{1,0:T(8,128)(2,1)S(1)} %copy-done.65, bf16[320,1920]{1,0:T(8,128)(2,1)S(1)} %copy-done.67, bf16[320,1920]{1,0:T(8,128)(2,1)S(1)} %copy-done.69, ...), custom_call_target="tpu_custom_call" | custom-call | flops 165600002048 | tf_op jit(solution)/shard_map/pallas_call | solution.py:111
  467.8 6.9 %collective-permute-done.59.refs_6_ = bf16[80,2560]{1,0:T(8,128)(2,1)S(1)} collective-permute-done((bf16[80,2560]{1,0:T(8,128)(2,1)S(1)}, bf16[80,2560]{1,0:T(8,128)(2,1)S(1)}, u32[]{:S(2)}, u32[]{:S(2)}) %collective-permute-start.59) | collective-permute-done | bytes 409632 | tf_op jit(solution)/shard_map/ppermute | solution.py:1104
  494.8 6.5 %collective-permute-done.64.refs_6_ = bf16[80,2560]{1,0:T(8,128)(2,1)S(1)} collective-permute-done((bf16[80,2560]{1,0:T(8,128)(2,1)S(1)}, bf16[80,2560]{1,0:T(8,128)(2,1)S(1)}, u32[]{:S(2)}, u32[]{:S(2)}) %collective-permute-start.64) | collective-permute-done | bytes 409632 | tf_op jit(solution)/shard_map/ppermute | solution.py:1104
  503.9 10.5 %collective-permute-done.66.refs_6_ = bf16[80,2560]{1,0:T(8,128)(2,1)S(1)} collective-permute-done((bf16[80,2560]{1,0:T(8,128)(2,1)S(1)}, bf16[80,2560]{1,0:T(8,128)(2,1)S(1)}, u32[]{:S(2)}, u32[]{:S(2)}) %collective-permute-start.66) | collective-permute-done | bytes 409632 | tf_op jit(solution)/shard_map/ppermute | solution.py:1104
  521.7 6.1 %collective-permute-done.67.refs_6_ = bf16[80,2560]{1,0:T(8,128)(2,1)S(1)} collective-permute-done((bf16[80,2560]{1,0:T(8,128)(2,1)}, bf16[80,2560]{1,0:T(8,128)(2,1)S(1)}, u32[]{:S(2)}, u32[]{:S(2)}) %collective-permute-start.67) | collective-permute-done | bytes 409632 | tf_op jit(solution)/shard_map/ppermute | solution.py:1104
  544.2 4.4 collective-permute-done.72
  (603 shorter events, 257.2 us)
Async XLA Ops:
  2.6 39.3 %collective-permute-start.5 = (bf16[80,2560]{1,0:T(8,128)(2,1)}, bf16[80,2560]{1,0:T(8,128)(2,1)}, u32[]{:S(2)}, u32[]{:S(2)}) collective-permute-start(bf16[80,2560]{1,0:T(8,128)(2,1)} %bitcast_convert_fusion.refs_0_), channel_id=1, source_target_pairs={{0,1},{1,0},{2,3},{3,2},{4,5},{5,4},{6,7},{7,6},{8,9},{9,8},{10,11... | collective-permute-start | bytes 1228808 | tf_op jit(solution)/shard_map/ppermute | solution.py:1092
  5.5 42.0 %collective-permute-start.6 = (bf16[80,2560]{1,0:T(8,128)(2,1)}, bf16[80,2560]{1,0:T(8,128)(2,1)}, u32[]{:S(2)}, u32[]{:S(2)}) collective-permute-start(bf16[80,2560]{1,0:T(8,128)(2,1)} %bitcast_convert_fusion.refs_0_), channel_id=1, source_target_pairs={{0,4},{2,6},{4,0},{6,2},{8,12},{10,14},{12,8},{14,10},{16,20},{18,... | collective-permute-start | bytes 1228808 | tf_op jit(solution)/shard_map/ppermute | solution.py:1098
  12.9 37.9 %collective-permute-start = (bf16[2,288,1280]{2,1,0:T(8,128)(2,1)}, bf16[2,288,1280]{2,1,0:T(8,128)(2,1)}, u32[]{:S(2)}, u32[]{:S(2)}) collective-permute-start(bf16[2,288,1280]{2,1,0:T(8,128)(2,1)} %pad_maximum_fusion), channel_id=1, source_target_pairs={{0,1},{1,0},{2,3},{3,2},{4,5},{5,4},{6,7},{7,6},{8,9},{9,8},{10,11... | collective-permute-start | bytes 4423688 | tf_op jit(solution)/shard_map/ppermute | solution.py:1092
  18.7 36.4 %collective-permute-start.1 = (bf16[80,3200]{1,0:T(8,128)(2,1)}, bf16[80,3200]{1,0:T(8,128)(2,1)}, u32[]{:S(2)}, u32[]{:S(2)}) collective-permute-start(bf16[80,3200]{1,0:T(8,128)(2,1)} %shard_map.363.refs_8_.refs_0_), channel_id=1, source_target_pairs={{0,24},{2,26},{4,28},{6,30},{8,0},{10,2},{12,4},{14,6},{16,8},{18,... | collective-permute-start | bytes 1536008 | tf_op jit(solution)/shard_map/ppermute | solution.py:1101
  53.0 31.5 %collective-permute-start.11 = (bf16[320,1920]{1,0:T(8,128)(2,1)S(1)}, bf16[320,1920]{1,0:T(8,128)(2,1)S(1)}, u32[]{:S(2)}, u32[]{:S(2)}) collective-permute-start(bf16[320,1920]{1,0:T(8,128)(2,1)S(1)} %shard_map.364.refs_1_), channel_id=1, source_target_pairs={{0,1},{1,0},{2,3},{3,2},{4,5},{5,4},{6,7},{7,6},{8,9},{9,8},{10,11... | collective-permute-start | bytes 3686408 | tf_op jit(solution)/shard_map/ppermute | solution.py:1092
  54.5 29.9 %collective-permute-start.8 = (bf16[320,1920]{1,0:T(8,128)(2,1)S(1)}, bf16[320,1920]{1,0:T(8,128)(2,1)S(1)}, u32[]{:S(2)}, u32[]{:S(2)}) collective-permute-start(bf16[320,1920]{1,0:T(8,128)(2,1)S(1)} %shard_map.364.refs_1_), channel_id=1, source_target_pairs={{0,4},{2,6},{4,0},{6,2},{8,12},{10,14},{12,8},{14,10},{16,20},{18,... | collective-permute-start | bytes 3686408 | tf_op jit(solution)/shard_map/ppermute | solution.py:1098
  55.1 29.3 %collective-permute-start.9 = (bf16[320,1920]{1,0:T(8,128)(2,1)S(1)}, bf16[320,1920]{1,0:T(8,128)(2,1)S(1)}, u32[]{:S(2)}, u32[]{:S(2)}) collective-permute-start(bf16[320,1920]{1,0:T(8,128)(2,1)S(1)} %shard_map.364.refs_1_), channel_id=1, source_target_pairs={{0,2},{2,0},{4,6},{6,4},{8,10},{10,8},{12,14},{14,12},{16,18},{18,... | collective-permute-start | bytes 3686408 | tf_op jit(solution)/shard_map/ppermute | solution.py:1095
  56.2 24.0 %collective-permute-start.18 = (bf16[80,3200]{1,0:T(8,128)(2,1)S(1)}, bf16[80,3200]{1,0:T(8,128)(2,1)S(1)}, u32[]{:S(2)}, u32[]{:S(2)}) collective-permute-start(bf16[80,3200]{1,0:T(8,128)(2,1)S(1)} %shard_map.365.refs_4_.refs_1_), channel_id=1, source_target_pairs={{0,24},{2,26},{4,28},{6,30},{8,0},{10,2},{12,4},{14,6},{16,8},{18,... | collective-permute-start | bytes 1536008 | tf_op jit(solution)/shard_map/ppermute | solution.py:1101
  94.3 35.6 %collective-permute-start.22 = (bf16[160,5120]{1,0:T(8,128)(2,1)}, bf16[160,5120]{1,0:T(8,128)(2,1)}, u32[]{:S(2)}, u32[]{:S(2)}) collective-permute-start(bf16[160,5120]{1,0:T(8,128)(2,1)} %shard_map.369.refs_8_.refs_1_), channel_id=1, source_target_pairs={{0,24},{2,26},{4,28},{6,30},{8,0},{10,2},{12,4},{14,6},{16,8},{18,... | collective-permute-start | bytes 4915208 | tf_op jit(solution)/shard_map/ppermute | solution.py:1101
  99.0 33.5 %collective-permute-start.21 = (bf16[160,5120]{1,0:T(8,128)(2,1)}, bf16[160,5120]{1,0:T(8,128)(2,1)}, u32[]{:S(2)}, u32[]{:S(2)}) collective-permute-start(bf16[160,5120]{1,0:T(8,128)(2,1)} %shard_map.369.refs_8_.refs_1_), channel_id=1, source_target_pairs={{0,2},{2,0},{4,6},{6,4},{8,10},{10,8},{12,14},{14,12},{16,18},{18,... | collective-permute-start | bytes 4915208 | tf_op jit(solution)/shard_map/ppermute | solution.py:1095
  105.3 31.5 %collective-permute-start.20 = (bf16[320,3200]{1,0:T(8,128)(2,1)}, bf16[320,3200]{1,0:T(8,128)(2,1)S(1)}, u32[]{:S(2)}, u32[]{:S(2)}) collective-permute-start(bf16[320,3200]{1,0:T(8,128)(2,1)} %shard_map.370.refs_14_.refs_1_), channel_id=1, source_target_pairs={{0,2},{2,0},{4,6},{6,4},{8,10},{10,8},{12,14},{14,12},{16,18},{18,... | collective-permute-start | bytes 6144008 | tf_op jit(solution)/shard_map/ppermute | solution.py:1095
  105.4 48.0 %collective-permute-start.23 = (bf16[320,3200]{1,0:T(8,128)(2,1)}, bf16[320,3200]{1,0:T(8,128)(2,1)}, u32[]{:S(2)}, u32[]{:S(2)}) collective-permute-start(bf16[320,3200]{1,0:T(8,128)(2,1)} %shard_map.370.refs_14_.refs_1_), channel_id=1, source_target_pairs={{0,4},{2,6},{4,0},{6,2},{8,12},{10,14},{12,8},{14,10},{16,20},{18,... | collective-permute-start | bytes 6144008 | tf_op jit(solution)/shard_map/ppermute | solution.py:1098
  105.9 47.5 %collective-permute-start.25 = (bf16[320,3200]{1,0:T(8,128)(2,1)}, bf16[320,3200]{1,0:T(8,128)(2,1)}, u32[]{:S(2)}, u32[]{:S(2)}) collective-permute-start(bf16[320,3200]{1,0:T(8,128)(2,1)} %shard_map.370.refs_14_.refs_1_), channel_id=1, source_target_pairs={{0,1},{1,0},{2,3},{3,2},{4,5},{5,4},{6,7},{7,6},{8,9},{9,8},{10,11... | collective-permute-start | bytes 6144008 | tf_op jit(solution)/shard_map/ppermute | solution.py:1092
  132.5 40.3 %collective-permute-start.32 = (bf16[160,5120]{1,0:T(8,128)(2,1)}, bf16[160,5120]{1,0:T(8,128)(2,1)}, u32[]{:S(2)}, u32[]{:S(2)}) collective-permute-start(bf16[160,5120]{1,0:T(8,128)(2,1)} %shard_map.372.refs_7_.refs_2_), channel_id=1, source_target_pairs={{0,24},{2,26},{4,28},{6,30},{8,0},{10,2},{12,4},{14,6},{16,8},{18,... | collective-permute-start | bytes 4915208 | tf_op jit(solution)/shard_map/ppermute | solution.py:1101
  157.9 29.2 %collective-permute-start.27 = (bf16[320,1920]{1,0:T(8,128)(2,1)S(1)}, bf16[320,1920]{1,0:T(8,128)(2,1)S(1)}, u32[]{:S(2)}, u32[]{:S(2)}) collective-permute-start(bf16[320,1920]{1,0:T(8,128)(2,1)S(1)} %get-tuple-element.112.refs_4_), channel_id=1, source_target_pairs={{0,4},{2,6},{4,0},{6,2},{8,12},{10,14},{12,8},{14,10},{16,20},{18,... | collective-permute-start | bytes 3686408 | tf_op jit(solution)/shard_map/ppermute | solution.py:1098
  158.8 32.0 %collective-permute-start.30 = (bf16[320,1280]{1,0:T(8,128)(2,1)S(1)}, bf16[320,1280]{1,0:T(8,128)(2,1)S(1)}, u32[]{:S(2)}, u32[]{:S(2)}) collective-permute-start(bf16[320,1280]{1,0:T(8,128)(2,1)S(1)} %get-tuple-element.113), channel_id=1, source_target_pairs={{0,1},{1,0},{2,3},{3,2},{4,5},{5,4},{6,7},{7,6},{8,9},{9,8},{10,11... | collective-permute-start | bytes 2457608 | tf_op jit(solution)/shard_map/ppermute | solution.py:1092
  160.4 31.5 %collective-permute-start.24 = (bf16[320,3200]{1,0:T(8,128)(2,1)}, bf16[320,3200]{1,0:T(8,128)(2,1)S(1)}, u32[]{:S(2)}, u32[]{:S(2)}) collective-permute-start(bf16[320,3200]{1,0:T(8,128)(2,1)} %collective-permute-done.23.refs_1_.refs_2_), channel_id=1, source_target_pairs={{0,2},{2,0},{4,6},{6,4},{8,10},{10,8},{12,14},{14,12},{16,18},{18,... | collective-permute-start | bytes 6144008 | tf_op jit(solution)/shard_map/ppermute | solution.py:1095
  160.4 31.6 %collective-permute-start.28 = (bf16[320,3200]{1,0:T(8,128)(2,1)}, bf16[320,3200]{1,0:T(8,128)(2,1)S(1)}, u32[]{:S(2)}, u32[]{:S(2)}) collective-permute-start(bf16[320,3200]{1,0:T(8,128)(2,1)} %collective-permute-done.25.refs_0_.refs_5_.refs_9_), channel_id=1, source_target_pairs={{0,2},{2,0},{4,6},{6,4},{8,10},{10,8},{12,14},{14,12},{16,18},{18,... | collective-permute-start | bytes 6144008 | tf_op jit(solution)/shard_map/ppermute | solution.py:1095
  172.9 56.5 %collective-permute-start.33 = (bf16[160,5120]{1,0:T(8,128)(2,1)}, bf16[160,5120]{1,0:T(8,128)(2,1)}, u32[]{:S(2)}, u32[]{:S(2)}) collective-permute-start(bf16[160,5120]{1,0:T(8,128)(2,1)} %collective-permute-done.32.refs_3_), channel_id=1, source_target_pairs={{0,24},{2,26},{4,28},{6,30},{8,0},{10,2},{12,4},{14,6},{16,8},{18,... | collective-permute-start | bytes 4915208 | tf_op jit(solution)/shard_map/ppermute | solution.py:1101
  190.8 40.9 %collective-permute-start.34 = (bf16[160,5120]{1,0:T(8,128)(2,1)}, bf16[160,5120]{1,0:T(8,128)(2,1)}, u32[]{:S(2)}, u32[]{:S(2)}) collective-permute-start(bf16[160,5120]{1,0:T(8,128)(2,1)} %collective-permute-done.32.refs_3_), channel_id=1, source_target_pairs={{0,2},{2,0},{4,6},{6,4},{8,10},{10,8},{12,14},{14,12},{16,18},{18,... | collective-permute-start | bytes 4915208 | tf_op jit(solution)/shard_map/ppermute | solution.py:1095
  261.5 46.6 %collective-permute-start.39 = (bf16[640,1280]{1,0:T(8,128)(2,1)}, bf16[640,1280]{1,0:T(8,128)(2,1)}, u32[]{:S(2)}, u32[]{:S(2)}) collective-permute-start(bf16[640,1280]{1,0:T(8,128)(2,1)} %get-tuple-element.126), channel_id=1, source_target_pairs={{0,1},{1,0},{2,3},{3,2},{4,5},{5,4},{6,7},{7,6},{8,9},{9,8},{10,11... | collective-permute-start | bytes 4915208 | tf_op jit(solution)/shard_map/ppermute | solution.py:1092
  263.1 45.1 %collective-permute-start.38 = (bf16[640,1280]{1,0:T(8,128)(2,1)}, bf16[640,1280]{1,0:T(8,128)(2,1)}, u32[]{:S(2)}, u32[]{:S(2)}) collective-permute-start(bf16[640,1280]{1,0:T(8,128)(2,1)} %get-tuple-element.125), channel_id=1, source_target_pairs={{0,4},{2,6},{4,0},{6,2},{8,12},{10,14},{12,8},{14,10},{16,20},{18,... | collective-permute-start | bytes 4915208 | tf_op jit(solution)/shard_map/ppermute | solution.py:1098
  288.2 34.5 %collective-permute-start.42 = (bf16[640,5120]{1,0:T(8,128)(2,1)}, bf16[640,5120]{1,0:T(8,128)(2,1)}, u32[]{:S(2)}, u32[]{:S(2)}) collective-permute-start(bf16[640,5120]{1,0:T(8,128)(2,1)} %shard_map.386.refs_17_), channel_id=1, source_target_pairs={{0,2},{2,0},{4,6},{6,4},{8,10},{10,8},{12,14},{14,12},{16,18},{18,... | collective-permute-start | bytes 19660808 | tf_op jit(solution)/shard_map/ppermute | solution.py:1095
  288.2 51.5 %collective-permute-start.37 = (bf16[288,1280]{1,0:T(8,128)(2,1)}, bf16[288,1280]{1,0:T(8,128)(2,1)}, u32[]{:S(2)}, u32[]{:S(2)}) collective-permute-start(bf16[288,1280]{1,0:T(8,128)(2,1)} %get-tuple-element.124), channel_id=1, source_target_pairs={{0,1},{1,0},{2,3},{3,2},{4,5},{5,4},{6,7},{7,6},{8,9},{9,8},{10,11... | collective-permute-start | bytes 2211848 | tf_op jit(solution)/shard_map/ppermute | solution.py:1092
  334.9 37.7 %collective-permute-start.45 = (bf16[640,1280]{1,0:T(8,128)(2,1)}, bf16[640,1280]{1,0:T(8,128)(2,1)}, u32[]{:S(2)}, u32[]{:S(2)}) collective-permute-start(bf16[640,1280]{1,0:T(8,128)(2,1)} %get-tuple-element.140), channel_id=1, source_target_pairs={{0,1},{1,0},{2,3},{3,2},{4,5},{5,4},{6,7},{7,6},{8,9},{9,8},{10,11... | collective-permute-start | bytes 4915208 | tf_op jit(solution)/shard_map/ppermute | solution.py:1092
  335.4 37.4 %collective-permute-start.44 = (bf16[640,1280]{1,0:T(8,128)(2,1)}, bf16[640,1280]{1,0:T(8,128)(2,1)}, u32[]{:S(2)}, u32[]{:S(2)}) collective-permute-start(bf16[640,1280]{1,0:T(8,128)(2,1)} %get-tuple-element.139), channel_id=1, source_target_pairs={{0,4},{2,6},{4,0},{6,2},{8,12},{10,14},{12,8},{14,10},{16,20},{18,... | collective-permute-start | bytes 4915208 | tf_op jit(solution)/shard_map/ppermute | solution.py:1098
  339.6 35.1 %collective-permute-start.43 = (bf16[80,2560]{1,0:T(8,128)(2,1)}, bf16[80,2560]{1,0:T(8,128)(2,1)}, u32[]{:S(2)}, u32[]{:S(2)}) collective-permute-start(bf16[80,2560]{1,0:T(8,128)(2,1)} %shard_map.392.refs_3_), channel_id=1, source_target_pairs={{0,8},{2,10},{4,12},{6,14},{8,16},{10,18},{12,20},{14,22},{16,24},... | collective-permute-start | bytes 1228808 | tf_op jit(solution)/shard_map/ppermute | solution.py:1104
  384.2 23.1 %collective-permute-start.50 = (bf16[320,1280]{1,0:T(8,128)(2,1)}, bf16[320,1280]{1,0:T(8,128)(2,1)S(1)}, u32[]{:S(2)}, u32[]{:S(2)}) collective-permute-start(bf16[320,1280]{1,0:T(8,128)(2,1)} %copy-done.90), channel_id=1, source_target_pairs={{0,1},{1,0},{2,3},{3,2},{4,5},{5,4},{6,7},{7,6},{8,9},{9,8},{10,11... | collective-permute-start | bytes 2457608 | tf_op jit(solution)/shard_map/ppermute | solution.py:1092
  410.0 34.7 %collective-permute-start.54 = (bf16[80,2560]{1,0:T(8,128)(2,1)}, bf16[80,2560]{1,0:T(8,128)(2,1)}, u32[]{:S(2)}, u32[]{:S(2)}) collective-permute-start(bf16[80,2560]{1,0:T(8,128)(2,1)} %shard_map.401.refs_5_), channel_id=1, source_target_pairs={{0,8},{2,10},{4,12},{6,14},{8,16},{10,18},{12,20},{14,22},{16,24},... | collective-permute-start | bytes 1228808 | tf_op jit(solution)/shard_map/ppermute | solution.py:1104
  417.8 37.8 %collective-permute-start.53 = (bf16[640,1280]{1,0:T(8,128)(2,1)}, bf16[640,1280]{1,0:T(8,128)(2,1)}, u32[]{:S(2)}, u32[]{:S(2)}) collective-permute-start(bf16[640,1280]{1,0:T(8,128)(2,1)} %get-tuple-element.148), channel_id=1, source_target_pairs={{0,1},{1,0},{2,3},{3,2},{4,5},{5,4},{6,7},{7,6},{8,9},{9,8},{10,11... | collective-permute-start | bytes 4915208 | tf_op jit(solution)/shard_map/ppermute | solution.py:1092
  419.3 37.5 %collective-permute-start.52 = (bf16[640,1280]{1,0:T(8,128)(2,1)}, bf16[640,1280]{1,0:T(8,128)(2,1)}, u32[]{:S(2)}, u32[]{:S(2)}) collective-permute-start(bf16[640,1280]{1,0:T(8,128)(2,1)} %get-tuple-element.147), channel_id=1, source_target_pairs={{0,4},{2,6},{4,0},{6,2},{8,12},{10,14},{12,8},{14,10},{16,20},{18,... | collective-permute-start | bytes 4915208 | tf_op jit(solution)/shard_map/ppermute | solution.py:1098
  494.3 23.8 %collective-permute-start.61 = (bf16[288,1280]{1,0:T(8,128)(2,1)}, bf16[288,1280]{1,0:T(8,128)(2,1)}, u32[]{:S(2)}, u32[]{:S(2)}) collective-permute-start(bf16[288,1280]{1,0:T(8,128)(2,1)} %get-tuple-element.159), channel_id=1, source_target_pairs={{0,1},{1,0},{2,3},{3,2},{4,5},{5,4},{6,7},{7,6},{8,9},{9,8},{10,11... | collective-permute-start | bytes 2211848 | tf_op jit(solution)/shard_map/ppermute | solution.py:1092
  (221 other events, 2032.8 us)

commit v8 on v7

--- a/solution.py
+++ b/solution.py
@@ -681,7 +681,7 @@
     )(*values)
 
 
-def hold(*values, after=()):
+def hold(*values, us=1, after=()):
     def kernel(*refs):
         total = refs[0][...]
         for ref in refs[1:-1]:
@@ -695,7 +695,7 @@
         [whole(shape)] * len(values),
         whole(shape),
         jax.ShapeDtypeStruct(shape, values[0].dtype),
-        us=1,
+        us=us,
         after=after,
     )(*values)
 
@@ -987,7 +987,7 @@
             top = jnp.max(logits, 0, keepdims=True)
             exponent = jnp.exp(logits - top)
             total_ = jnp.sum(exponent, 0, keepdims=True)
-            prob = (exponent / total_).astype(LOW)
+            prob = (exponent * (1.0 / total_)).astype(LOW)
             out_t[cut, :] = jnp.dot(value_t[cut, :], prob, preferred_element_type=F32)
             lse_ref[0, h : h + 1, :] = top + jnp.log(total_)
         att_ref[...] = out_t[...].T.astype(LOW)
@@ -1304,6 +1304,7 @@
         core_held_1 = lanes.over_core(held_1)
         sides_1 = lanes.over_x(held_1), lanes.over_y(held_1)
         row_low, first_in = enter_input(input_mine, both_came, shuffle, vec)
+        cot_low, down_grad = enter_cotangent(cot_mine, both_came, shuffle, token_weight)
         biases = hold(biases)
         near_1 = [(0, 2 * lane_columns)]
         fars_1 = lanes.far(*sides_1, near_1, after=[core_held_1])
@@ -1411,8 +1412,7 @@
         before_far = [late_cores[1][1]]
         near_2 = [(0, half), (hidden, hidden + lane_columns)]
         fars_2 = lanes.far(*sides_2, near_2, after=before_far)
-        cot_low, down_grad = enter_cotangent(cot_mine, both_came, shuffle, token_weight)
-        hold(query_code, after=fars_2)
+        hold(query_code, us=8, after=fars_2)
         cores_2 = lanes.both_cores(sides_2)
         w2 = Gathered(
             [held_2, sides_2[1], core_held_2, cores_2[1][1]],

time: 562 us -> 560 us (level)
    unnamed x362 -> x342, local copies, waits for them, and re-layouts: 43.6 us -> 40.3 us
  transfers between devices with their start and end apart: 73 -> 73, of which waited for: 28 -> 30; matrix products, arithmetic and copies ran while one was open for 5% -> 5% of each run, Pallas kernels for 45% -> 45%
where the time goes in v8:
time: 560 us; the launch traced here: 550 us
  Pallas kernels  275 us (49%)
  waiting for transfers between devices  123 us (22%)
  starting transfers between devices  80.3 us (14%)
  local copies, waits for them, and re-layouts  56.2 us (10%)
  other arithmetic  8 us (1%)
    pallas_call x63, Pallas kernels, run(): pl.pallas_call(ordered, grid=grid, in_specs=list(in_specs) + [pl.BlockSpe...  275 us
    unnamed x342, local copies, waits for them, and re-layouts  40.3 us
    ppermute x9, starting transfers between devices, down_z(): lax.ppermute(v, 'dp', [(i, (i - 4) % self.dp) for i in range(self.dp)])  34.5 us
    ppermute x9, waiting for transfers between devices, down_z(): lax.ppermute(v, 'dp', [(i, (i - 4) % self.dp) for i in range(self.dp)])  32.7 us
    ppermute x9, waiting for transfers between devices, up_z(): lax.ppermute(v, 'dp', [(i, (i + 4) % self.dp) for i in range(self.dp)])  31.7 us
    ppermute x16, waiting for transfers between devices, over_x(): return lax.ppermute(v, 'tensor', [(0, 1), (1, 0)])  20.3 us
    ppermute x16, starting transfers between devices, over_x(): return lax.ppermute(v, 'tensor', [(0, 1), (1, 0)])  19.4 us
    ppermute x13, waiting for transfers between devices, over_y(): return lax.ppermute(v, 'dp', [(i, i ^ 2) for i in range(self.dp)])  18.1 us
  transfers between devices with their start and end apart: 73, of which 30 were waited for; matrix products, arithmetic and copies ran while one was open for 5% of the time, Pallas kernels for 45%

profile of v8, /device:TPU:0, one launch (start us, length us, event | category | flops | bytes accessed | tf_op | source)
XLA Modules:
  0.0 550.3 jit_solution(884885471897995190)
XLA Ops:
  70.6 10.0 %collective-permute-done.17 = f32[35,128]{1,0:T(8,128)S(1)} collective-permute-done((f32[35,128]{1,0:T(8,128)S(1)}, f32[35,128]{1,0:T(8,128)S(1)}, u32[]{:S(2)}, u32[]{:S(2)}) %collective-permute-start.17) | collective-permute-done | bytes 17952 | tf_op jit(solution)/shard_map/ppermute | solution.py:1092
  95.0 4.7 collective-permute-start.22
  109.6 10.8 %shard_map.372.refs_1_.refs_0_ = f32[576,3840]{1,0:T(8,128)S(1)} custom-call(bf16[576,1280]{1,0:T(8,128)(2,1)S(1)} %get-tuple-element.106.refs_0_, bf16[320,1920]{1,0:T(8,128)(2,1)} %shard_map.364.refs_1_, bf16[320,1920]{1,0:T(8,128)(2,1)} %collective-permute-done.8.refs_1_.refs_2_, bf16[320,1920]{1,0:T(8,128)(2,1)} %collective-permute-done.9.refs_2_.refs_3_, ...), custom_call_target="tpu_custom_call" | custom-call | flops 128799997952 | tf_op jit(solution)/shard_map/pallas_call | solution.py:111
  120.5 10.2 %collective-permute-done.22.refs_0_ = bf16[160,5120]{1,0:T(8,128)(2,1)} collective-permute-done((bf16[160,5120]{1,0:T(8,128)(2,1)}, bf16[160,5120]{1,0:T(8,128)(2,1)}, u32[]{:S(2)}, u32[]{:S(2)}) %collective-permute-start.22) | collective-permute-done | bytes 1638432 | tf_op jit(solution)/shard_map/ppermute | solution.py:1101
  133.4 4.3 collective-permute-start.32
  137.7 16.6 %shard_map.374 = (bf16[576,3840]{1,0:T(8,128)(2,1)S(1)}, bf16[576,1280]{1,0:T(8,128)(2,1)S(1)}, f32[2,8,576]{2,1,0:T(8,128)S(1)}) custom-call(f32[576,3840]{1,0:T(8,128)S(1)} %shard_map.372.refs_1_.refs_0_, f32[576,640]{1,0:T(8,128)S(1)} %copy-done.12, f32[576,640]{1,0:T(8,128)S(1)} %copy-done.14, s32[576,1]{1,0:T(8,128)S(1)} %broadcast_in_dim.55.refs_3_.refs_5_, ...), custom_call_target="tpu_custom_call" | custom-call | flops 180319993856 | tf_op jit(solution)/shard_map/pallas_call | solution.py:111
  162.0 11.7 %collective-permute-done.32.refs_3_ = bf16[160,5120]{1,0:T(8,128)(2,1)} collective-permute-done((bf16[160,5120]{1,0:T(8,128)(2,1)}, bf16[160,5120]{1,0:T(8,128)(2,1)}, u32[]{:S(2)}, u32[]{:S(2)}) %collective-permute-start.32) | collective-permute-done | bytes 1638432 | tf_op jit(solution)/shard_map/ppermute | solution.py:1101
  173.7 4.4 collective-permute-start.33
  180.0 8.6 %collective-permute-done.27.refs_1_.refs_6_ = bf16[320,1920]{1,0:T(8,128)(2,1)S(1)} collective-permute-done((bf16[320,1920]{1,0:T(8,128)(2,1)S(1)}, bf16[320,1920]{1,0:T(8,128)(2,1)S(1)}, u32[]{:S(2)}, u32[]{:S(2)}) %collective-permute-start.27) | collective-permute-done | bytes 1228832 | tf_op jit(solution)/shard_map/ppermute | solution.py:1098
  191.5 6.1 %shard_map.377 = (f32[576,1280]{1,0:T(8,128)S(1)}, bf16[576,1280]{1,0:T(8,128)(2,1)S(1)}) custom-call(bf16[576,1280]{1,0:T(8,128)(2,1)S(1)} %copy-done.114, bf16[320,3200]{1,0:T(8,128)(2,1)} %shard_map.371.refs_14_.refs_1_, bf16[320,3200]{1,0:T(8,128)(2,1)} %collective-permute-done.23.refs_1_.refs_2_, ...), custom_call_target="tpu_custom_call" | custom-call | flops 90159996928 | tf_op jit(solution)/shard_map/pallas_call | solution.py:111
  199.3 13.8 %shard_map.378 = (f32[576,5120]{1,0:T(8,128)}, bf16[576,5120]{1,0:T(8,128)(2,1)}) custom-call(bf16[576,1280]{1,0:T(8,128)(2,1)S(1)} %get-tuple-element.115.refs_0_, bf16[320,3200]{1,0:T(8,128)(2,1)} %shard_map.371.refs_14_.refs_1_, bf16[320,3200]{1,0:T(8,128)(2,1)} %collective-permute-done.23.refs_1_.refs_2_, ...), custom_call_target="tpu_custom_call" | custom-call | flops 163759996928 | tf_op jit(solution)/shard_map/pallas_call | solution.py:111
  213.1 4.3 copy-done.2
  220.1 7.0 %shard_map.379.refs_1_ = bf16[640,5120]{1,0:T(8,128)(2,1)S(1)} custom-call(bf16[576,1280]{1,0:T(8,128)(2,1)S(1)} %get-tuple-element.118.refs_0_, bf16[576,5120]{1,0:T(8,128)(2,1)S(1)} %copy-done.144, f32[576,5120]{1,0:T(8,128)S(1)} %copy-done.2), custom_call_target="tpu_custom_call" | custom-call | flops 552000028672 | tf_op jit(solution)/shard_map/pallas_call | solution.py:111
  233.4 12.4 %shard_map.381.refs_3_.refs_0_ = bf16[576,1280]{1,0:T(8,128)(2,1)S(1)} custom-call(bf16[576,5120]{1,0:T(8,128)(2,1)S(1)} %copy-done.145, bf16[160,5120]{1,0:T(8,128)(2,1)} %shard_map.370.refs_8_.refs_1_, bf16[160,5120]{1,0:T(8,128)(2,1)} %shard_map.373.refs_7_.refs_2_, bf16[160,5120]{1,0:T(8,128)(2,1)} %collective-permute-done.32.refs_3_, ...), custom_call_target="tpu_custom_call" | custom-call | flops 138000007168 | tf_op jit(solution)/shard_map/pallas_call | solution.py:111
  245.8 5.8 %shard_map.382 = (bf16[320,1280]{1,0:T(8,128)(2,1)S(1)}, bf16[640,1280]{1,0:T(8,128)(2,1)}, bf16[320,1280]{1,0:T(8,128)(2,1)S(1)}) custom-call(bf16[576,1280]{1,0:T(8,128)(2,1)S(1)} %copy-done.17, bf16[576,5120]{1,0:T(8,128)(2,1)S(1)} %copy-done.145, bf16[640,5120]{1,0:T(8,128)(2,1)} %collective-permute-done.36.refs_2_, ...), custom_call_target="tpu_custom_call" | custom-call | flops 64399998976 | tf_op jit(solution)/shard_map/pallas_call | solution.py:111
  252.5 6.2 %shard_map.383 = (bf16[320,1280]{1,0:T(8,128)(2,1)S(1)}, bf16[320,1280]{1,0:T(8,128)(2,1)S(1)}, bf16[640,1280]{1,0:T(8,128)(2,1)}) custom-call(bf16[576,1280]{1,0:T(8,128)(2,1)S(1)} %copy-done.17, bf16[576,5120]{1,0:T(8,128)(2,1)S(1)} %copy-done.145, bf16[640,5120]{1,0:T(8,128)(2,1)} %collective-permute-done.36.refs_2_, ...), custom_call_target="tpu_custom_call" | custom-call | flops 64399998976 | tf_op jit(solution)/shard_map/pallas_call | solution.py:111
  260.8 13.7 %shard_map.384 = (bf16[576,5120]{1,0:T(8,128)(2,1)S(1)}, f32[1,5120]{1,0:T(1,128)S(1)}) custom-call(bf16[576,1280]{1,0:T(8,128)(2,1)S(1)} %copy-done.17, bf16[160,5120]{1,0:T(8,128)(2,1)} %shard_map.370.refs_8_.refs_1_, bf16[160,5120]{1,0:T(8,128)(2,1)} %shard_map.373.refs_7_.refs_2_, bf16[160,5120]{1,0:T(8,128)(2,1)} %collective-permute-done.32.refs_3_, ...), custom_call_target="tpu_custom_call" | custom-call | flops 920000000 | tf_op jit(solution)/shard_map/pallas_call | solution.py:111
  277.6 7.8 %shard_map.386.refs_17_ = bf16[640,5120]{1,0:T(8,128)(2,1)} custom-call(bf16[576,1280]{1,0:T(8,128)(2,1)S(1)} %get-tuple-element.115.refs_0_, bf16[576,5120]{1,0:T(8,128)(2,1)S(1)} %get-tuple-element.122.refs_2_.refs_1_.refs_0_, bf16[288,1280]{1,0:T(8,128)(2,1)S(1)} %get-tuple-element.123.refs_2_.refs_1_), custom_call_target="tpu_custom_call" | custom-call | flops 920000000 | tf_op jit(solution)/shard_map/pallas_call | solution.py:111
  285.9 19.4 %shard_map.387 = (f32[576,1280]{1,0:T(8,128)}, bf16[576,1280]{1,0:T(8,128)(2,1)S(1)}, f32[8,1280]{1,0:T(8,128)S(1)}) custom-call(bf16[576,5120]{1,0:T(8,128)(2,1)} %copy-done, bf16[320,3200]{1,0:T(8,128)(2,1)} %shard_map.371.refs_14_.refs_1_, bf16[320,3200]{1,0:T(8,128)(2,1)} %collective-permute-done.23.refs_1_.refs_2_, bf16[320,3200]{1,0:T(8,128)(2,1)} %copy-done.7, ...), custom_call_target="tpu_custom_call" | custom-call | flops 920000000 | tf_op jit(solution)/shard_map/pallas_call | solution.py:111
  319.9 5.8 %shard_map.390 = (bf16[320,1280]{1,0:T(8,128)(2,1)S(1)}, bf16[640,1280]{1,0:T(8,128)(2,1)}, bf16[320,1280]{1,0:T(8,128)(2,1)S(1)}) custom-call(bf16[576,1280]{1,0:T(8,128)(2,1)S(1)} %copy-done.19, bf16[576,5120]{1,0:T(8,128)(2,1)S(1)} %copy-done.1, bf16[640,5120]{1,0:T(8,128)(2,1)} %collective-permute-done.42.refs_2_, ...), custom_call_target="tpu_custom_call" | custom-call | flops 64399998976 | tf_op jit(solution)/shard_map/pallas_call | solution.py:111
  325.7 6.4 %shard_map.391 = (bf16[320,1280]{1,0:T(8,128)(2,1)S(1)}, bf16[320,1280]{1,0:T(8,128)(2,1)S(1)}, bf16[640,1280]{1,0:T(8,128)(2,1)}) custom-call(bf16[576,1280]{1,0:T(8,128)(2,1)S(1)} %copy-done.19, bf16[576,5120]{1,0:T(8,128)(2,1)S(1)} %copy-done.1, bf16[640,5120]{1,0:T(8,128)(2,1)} %collective-permute-done.42.refs_2_, ...), custom_call_target="tpu_custom_call" | custom-call | flops 64399998976 | tf_op jit(solution)/shard_map/pallas_call | solution.py:111
  340.9 24.6 %shard_map.394 = (bf16[576,3840]{1,0:T(8,128)(2,1)S(1)}, f32[1,3840]{1,0:T(1,128)S(1)}) custom-call(bf16[576,3840]{1,0:T(8,128)(2,1)S(1)} %bitcast.97, f32[2,8,576]{2,1,0:T(8,128)S(1)} %get-tuple-element.135.refs_1_, bf16[576,1280]{1,0:T(8,128)(2,1)S(1)} %shard_map.389.refs_3_.refs_2_, f32[576,640]{1,0:T(8,128)S(1)} %copy-done.13, ...), custom_call_target="tpu_custom_call" | custom-call | flops 251160002560 | tf_op jit(solution)/shard_map/pallas_call | solution.py:111
  374.4 5.1 shard_map.397.refs_4_
  389.9 4.5 shard_map.398.refs_3_
  394.5 6.7 %shard_map.399 = (bf16[320,1280]{1,0:T(8,128)(2,1)S(1)}, bf16[640,1280]{1,0:T(8,128)(2,1)}, bf16[320,1280]{1,0:T(8,128)(2,1)S(1)}) custom-call(bf16[576,1280]{1,0:T(8,128)(2,1)S(1)} %copy-done.112, bf16[576,3840]{1,0:T(8,128)(2,1)S(1)} %copy-done.108, bf16[640,2560]{1,0:T(8,128)(2,1)} %collective-permute-done.47.refs_2_, ...), custom_call_target="tpu_custom_call" | custom-call | flops 73600000000 | tf_op jit(solution)/shard_map/pallas_call | solution.py:111
  409.0 6.1 %shard_map.402 = (bf16[320,1280]{1,0:T(8,128)(2,1)S(1)}, bf16[320,1280]{1,0:T(8,128)(2,1)S(1)}, bf16[640,1280]{1,0:T(8,128)(2,1)}) custom-call(bf16[576,1280]{1,0:T(8,128)(2,1)S(1)} %copy-done.112, bf16[576,1280]{1,0:T(8,128)(2,1)S(1)} %copy-done.60, bf16[576,3840]{1,0:T(8,128)(2,1)S(1)} %copy-done.108, bf16[576,1280]{1,0:T(8,128)(2,1)S(1)} %copy-done.116, ...), custom_call_target="tpu_custom_call" | custom-call | flops 73600000000 | tf_op jit(solution)/shard_map/pallas_call | solution.py:111
  426.8 14.6 %shard_map.405 = (bf16[576,1280]{1,0:T(8,128)(2,1)S(1)}, f32[8,1280]{1,0:T(8,128)S(1)}) custom-call(bf16[576,3840]{1,0:T(8,128)(2,1)S(1)} %copy-done.108, bf16[320,1920]{1,0:T(8,128)(2,1)} %shard_map.364.refs_1_, bf16[320,1920]{1,0:T(8,128)(2,1)} %collective-permute-done.8.refs_1_.refs_2_, bf16[320,1920]{1,0:T(8,128)(2,1)} %collective-permute-done.9.refs_2_.refs_3_, ...), custom_call_target="tpu_custom_call" | custom-call | flops 165600002048 | tf_op jit(solution)/shard_map/pallas_call | solution.py:111
  465.0 6.9 %collective-permute-done.59.refs_6_ = bf16[80,2560]{1,0:T(8,128)(2,1)S(1)} collective-permute-done((bf16[80,2560]{1,0:T(8,128)(2,1)S(1)}, bf16[80,2560]{1,0:T(8,128)(2,1)S(1)}, u32[]{:S(2)}, u32[]{:S(2)}) %collective-permute-start.59) | collective-permute-done | bytes 409632 | tf_op jit(solution)/shard_map/ppermute | solution.py:1104
  492.1 6.5 %collective-permute-done.64.refs_6_ = bf16[80,2560]{1,0:T(8,128)(2,1)S(1)} collective-permute-done((bf16[80,2560]{1,0:T(8,128)(2,1)S(1)}, bf16[80,2560]{1,0:T(8,128)(2,1)S(1)}, u32[]{:S(2)}, u32[]{:S(2)}) %collective-permute-start.64) | collective-permute-done | bytes 409632 | tf_op jit(solution)/shard_map/ppermute | solution.py:1104
  501.1 10.7 %collective-permute-done.66.refs_6_ = bf16[80,2560]{1,0:T(8,128)(2,1)S(1)} collective-permute-done((bf16[80,2560]{1,0:T(8,128)(2,1)S(1)}, bf16[80,2560]{1,0:T(8,128)(2,1)S(1)}, u32[]{:S(2)}, u32[]{:S(2)}) %collective-permute-start.66) | collective-permute-done | bytes 409632 | tf_op jit(solution)/shard_map/ppermute | solution.py:1104
  519.0 6.1 %collective-permute-done.67.refs_6_ = bf16[80,2560]{1,0:T(8,128)(2,1)S(1)} collective-permute-done((bf16[80,2560]{1,0:T(8,128)(2,1)}, bf16[80,2560]{1,0:T(8,128)(2,1)S(1)}, u32[]{:S(2)}, u32[]{:S(2)}) %collective-permute-start.67) | collective-permute-done | bytes 409632 | tf_op jit(solution)/shard_map/ppermute | solution.py:1104
  541.5 4.4 collective-permute-done.72
  (583 shorter events, 261.4 us)
Async XLA Ops:
  2.6 27.7 %collective-permute-start.5 = (bf16[80,2560]{1,0:T(8,128)(2,1)}, bf16[80,2560]{1,0:T(8,128)(2,1)}, u32[]{:S(2)}, u32[]{:S(2)}) collective-permute-start(bf16[80,2560]{1,0:T(8,128)(2,1)} %bitcast_convert_fusion.refs_0_), channel_id=1, source_target_pairs={{0,1},{1,0},{2,3},{3,2},{4,5},{5,4},{6,7},{7,6},{8,9},{9,8},{10,11... | collective-permute-start | bytes 1228808 | tf_op jit(solution)/shard_map/ppermute | solution.py:1092
  5.5 42.0 %collective-permute-start.6 = (bf16[80,2560]{1,0:T(8,128)(2,1)}, bf16[80,2560]{1,0:T(8,128)(2,1)}, u32[]{:S(2)}, u32[]{:S(2)}) collective-permute-start(bf16[80,2560]{1,0:T(8,128)(2,1)} %bitcast_convert_fusion.refs_0_), channel_id=1, source_target_pairs={{0,4},{2,6},{4,0},{6,2},{8,12},{10,14},{12,8},{14,10},{16,20},{18,... | collective-permute-start | bytes 1228808 | tf_op jit(solution)/shard_map/ppermute | solution.py:1098
  12.9 37.9 %collective-permute-start = (bf16[2,288,1280]{2,1,0:T(8,128)(2,1)}, bf16[2,288,1280]{2,1,0:T(8,128)(2,1)}, u32[]{:S(2)}, u32[]{:S(2)}) collective-permute-start(bf16[2,288,1280]{2,1,0:T(8,128)(2,1)} %pad_maximum_fusion), channel_id=1, source_target_pairs={{0,1},{1,0},{2,3},{3,2},{4,5},{5,4},{6,7},{7,6},{8,9},{9,8},{10,11... | collective-permute-start | bytes 4423688 | tf_op jit(solution)/shard_map/ppermute | solution.py:1092
  18.7 37.2 %collective-permute-start.1 = (bf16[80,3200]{1,0:T(8,128)(2,1)}, bf16[80,3200]{1,0:T(8,128)(2,1)}, u32[]{:S(2)}, u32[]{:S(2)}) collective-permute-start(bf16[80,3200]{1,0:T(8,128)(2,1)} %shard_map.363.refs_8_.refs_0_), channel_id=1, source_target_pairs={{0,24},{2,26},{4,28},{6,30},{8,0},{10,2},{12,4},{14,6},{16,8},{18,... | collective-permute-start | bytes 1536008 | tf_op jit(solution)/shard_map/ppermute | solution.py:1101
  53.9 31.0 %collective-permute-start.11 = (bf16[320,1920]{1,0:T(8,128)(2,1)}, bf16[320,1920]{1,0:T(8,128)(2,1)}, u32[]{:S(2)}, u32[]{:S(2)}) collective-permute-start(bf16[320,1920]{1,0:T(8,128)(2,1)} %shard_map.364.refs_1_), channel_id=1, source_target_pairs={{0,1},{1,0},{2,3},{3,2},{4,5},{5,4},{6,7},{7,6},{8,9},{9,8},{10,11... | collective-permute-start | bytes 3686408 | tf_op jit(solution)/shard_map/ppermute | solution.py:1092
  55.4 29.5 %collective-permute-start.8 = (bf16[320,1920]{1,0:T(8,128)(2,1)}, bf16[320,1920]{1,0:T(8,128)(2,1)}, u32[]{:S(2)}, u32[]{:S(2)}) collective-permute-start(bf16[320,1920]{1,0:T(8,128)(2,1)} %shard_map.364.refs_1_), channel_id=1, source_target_pairs={{0,4},{2,6},{4,0},{6,2},{8,12},{10,14},{12,8},{14,10},{16,20},{18,... | collective-permute-start | bytes 3686408 | tf_op jit(solution)/shard_map/ppermute | solution.py:1098
  55.9 29.0 %collective-permute-start.9 = (bf16[320,1920]{1,0:T(8,128)(2,1)}, bf16[320,1920]{1,0:T(8,128)(2,1)}, u32[]{:S(2)}, u32[]{:S(2)}) collective-permute-start(bf16[320,1920]{1,0:T(8,128)(2,1)} %shard_map.364.refs_1_), channel_id=1, source_target_pairs={{0,2},{2,0},{4,6},{6,4},{8,10},{10,8},{12,14},{14,12},{16,18},{18,... | collective-permute-start | bytes 3686408 | tf_op jit(solution)/shard_map/ppermute | solution.py:1095
  57.0 23.7 %collective-permute-start.18 = (bf16[80,3200]{1,0:T(8,128)(2,1)S(1)}, bf16[80,3200]{1,0:T(8,128)(2,1)S(1)}, u32[]{:S(2)}, u32[]{:S(2)}) collective-permute-start(bf16[80,3200]{1,0:T(8,128)(2,1)S(1)} %shard_map.365.refs_4_.refs_1_), channel_id=1, source_target_pairs={{0,24},{2,26},{4,28},{6,30},{8,0},{10,2},{12,4},{14,6},{16,8},{18,... | collective-permute-start | bytes 1536008 | tf_op jit(solution)/shard_map/ppermute | solution.py:1101
  95.0 35.7 %collective-permute-start.22 = (bf16[160,5120]{1,0:T(8,128)(2,1)}, bf16[160,5120]{1,0:T(8,128)(2,1)}, u32[]{:S(2)}, u32[]{:S(2)}) collective-permute-start(bf16[160,5120]{1,0:T(8,128)(2,1)} %shard_map.370.refs_8_.refs_1_), channel_id=1, source_target_pairs={{0,24},{2,26},{4,28},{6,30},{8,0},{10,2},{12,4},{14,6},{16,8},{18,... | collective-permute-start | bytes 4915208 | tf_op jit(solution)/shard_map/ppermute | solution.py:1101
  99.7 33.6 %collective-permute-start.21 = (bf16[160,5120]{1,0:T(8,128)(2,1)}, bf16[160,5120]{1,0:T(8,128)(2,1)}, u32[]{:S(2)}, u32[]{:S(2)}) collective-permute-start(bf16[160,5120]{1,0:T(8,128)(2,1)} %shard_map.370.refs_8_.refs_1_), channel_id=1, source_target_pairs={{0,2},{2,0},{4,6},{6,4},{8,10},{10,8},{12,14},{14,12},{16,18},{18,... | collective-permute-start | bytes 4915208 | tf_op jit(solution)/shard_map/ppermute | solution.py:1095
  107.5 30.1 %collective-permute-start.20 = (bf16[320,3200]{1,0:T(8,128)(2,1)}, bf16[320,3200]{1,0:T(8,128)(2,1)S(1)}, u32[]{:S(2)}, u32[]{:S(2)}) collective-permute-start(bf16[320,3200]{1,0:T(8,128)(2,1)} %shard_map.371.refs_14_.refs_1_), channel_id=1, source_target_pairs={{0,2},{2,0},{4,6},{6,4},{8,10},{10,8},{12,14},{14,12},{16,18},{18,... | collective-permute-start | bytes 6144008 | tf_op jit(solution)/shard_map/ppermute | solution.py:1095
  107.6 47.8 %collective-permute-start.23 = (bf16[320,3200]{1,0:T(8,128)(2,1)}, bf16[320,3200]{1,0:T(8,128)(2,1)}, u32[]{:S(2)}, u32[]{:S(2)}) collective-permute-start(bf16[320,3200]{1,0:T(8,128)(2,1)} %shard_map.371.refs_14_.refs_1_), channel_id=1, source_target_pairs={{0,4},{2,6},{4,0},{6,2},{8,12},{10,14},{12,8},{14,10},{16,20},{18,... | collective-permute-start | bytes 6144008 | tf_op jit(solution)/shard_map/ppermute | solution.py:1098
  108.1 47.3 %collective-permute-start.25 = (bf16[320,3200]{1,0:T(8,128)(2,1)}, bf16[320,3200]{1,0:T(8,128)(2,1)}, u32[]{:S(2)}, u32[]{:S(2)}) collective-permute-start(bf16[320,3200]{1,0:T(8,128)(2,1)} %shard_map.371.refs_14_.refs_1_), channel_id=1, source_target_pairs={{0,1},{1,0},{2,3},{3,2},{4,5},{5,4},{6,7},{7,6},{8,9},{9,8},{10,11... | collective-permute-start | bytes 6144008 | tf_op jit(solution)/shard_map/ppermute | solution.py:1092
  133.4 40.3 %collective-permute-start.32 = (bf16[160,5120]{1,0:T(8,128)(2,1)}, bf16[160,5120]{1,0:T(8,128)(2,1)}, u32[]{:S(2)}, u32[]{:S(2)}) collective-permute-start(bf16[160,5120]{1,0:T(8,128)(2,1)} %shard_map.373.refs_7_.refs_2_), channel_id=1, source_target_pairs={{0,24},{2,26},{4,28},{6,30},{8,0},{10,2},{12,4},{14,6},{16,8},{18,... | collective-permute-start | bytes 4915208 | tf_op jit(solution)/shard_map/ppermute | solution.py:1101
  159.3 29.2 %collective-permute-start.27 = (bf16[320,1920]{1,0:T(8,128)(2,1)S(1)}, bf16[320,1920]{1,0:T(8,128)(2,1)S(1)}, u32[]{:S(2)}, u32[]{:S(2)}) collective-permute-start(bf16[320,1920]{1,0:T(8,128)(2,1)S(1)} %get-tuple-element.113.refs_3_), channel_id=1, source_target_pairs={{0,4},{2,6},{4,0},{6,2},{8,12},{10,14},{12,8},{14,10},{16,20},{18,... | collective-permute-start | bytes 3686408 | tf_op jit(solution)/shard_map/ppermute | solution.py:1098
  161.4 27.2 %collective-permute-start.24 = (bf16[320,3200]{1,0:T(8,128)(2,1)}, bf16[320,3200]{1,0:T(8,128)(2,1)S(1)}, u32[]{:S(2)}, u32[]{:S(2)}) collective-permute-start(bf16[320,3200]{1,0:T(8,128)(2,1)} %collective-permute-done.23.refs_1_.refs_2_), channel_id=1, source_target_pairs={{0,2},{2,0},{4,6},{6,4},{8,10},{10,8},{12,14},{14,12},{16,18},{18,... | collective-permute-start | bytes 6144008 | tf_op jit(solution)/shard_map/ppermute | solution.py:1095
  161.5 27.7 %collective-permute-start.28 = (bf16[320,3200]{1,0:T(8,128)(2,1)}, bf16[320,3200]{1,0:T(8,128)(2,1)S(1)}, u32[]{:S(2)}, u32[]{:S(2)}) collective-permute-start(bf16[320,3200]{1,0:T(8,128)(2,1)} %collective-permute-done.25.refs_0_.refs_5_.refs_9_), channel_id=1, source_target_pairs={{0,2},{2,0},{4,6},{6,4},{8,10},{10,8},{12,14},{14,12},{16,18},{18,... | collective-permute-start | bytes 6144008 | tf_op jit(solution)/shard_map/ppermute | solution.py:1095
  173.7 53.4 %collective-permute-start.33 = (bf16[160,5120]{1,0:T(8,128)(2,1)}, bf16[160,5120]{1,0:T(8,128)(2,1)}, u32[]{:S(2)}, u32[]{:S(2)}) collective-permute-start(bf16[160,5120]{1,0:T(8,128)(2,1)} %collective-permute-done.32.refs_3_), channel_id=1, source_target_pairs={{0,24},{2,26},{4,28},{6,30},{8,0},{10,2},{12,4},{14,6},{16,8},{18,... | collective-permute-start | bytes 4915208 | tf_op jit(solution)/shard_map/ppermute | solution.py:1101
  180.0 49.4 %collective-permute-start.34 = (bf16[160,5120]{1,0:T(8,128)(2,1)}, bf16[160,5120]{1,0:T(8,128)(2,1)}, u32[]{:S(2)}, u32[]{:S(2)}) collective-permute-start(bf16[160,5120]{1,0:T(8,128)(2,1)} %collective-permute-done.32.refs_3_), channel_id=1, source_target_pairs={{0,2},{2,0},{4,6},{6,4},{8,10},{10,8},{12,14},{14,12},{16,18},{18,... | collective-permute-start | bytes 4915208 | tf_op jit(solution)/shard_map/ppermute | solution.py:1095
  258.7 46.6 %collective-permute-start.39 = (bf16[640,1280]{1,0:T(8,128)(2,1)}, bf16[640,1280]{1,0:T(8,128)(2,1)}, u32[]{:S(2)}, u32[]{:S(2)}) collective-permute-start(bf16[640,1280]{1,0:T(8,128)(2,1)} %get-tuple-element.126), channel_id=1, source_target_pairs={{0,1},{1,0},{2,3},{3,2},{4,5},{5,4},{6,7},{7,6},{8,9},{9,8},{10,11... | collective-permute-start | bytes 4915208 | tf_op jit(solution)/shard_map/ppermute | solution.py:1092
  260.2 45.1 %collective-permute-start.38 = (bf16[640,1280]{1,0:T(8,128)(2,1)}, bf16[640,1280]{1,0:T(8,128)(2,1)}, u32[]{:S(2)}, u32[]{:S(2)}) collective-permute-start(bf16[640,1280]{1,0:T(8,128)(2,1)} %get-tuple-element.125), channel_id=1, source_target_pairs={{0,4},{2,6},{4,0},{6,2},{8,12},{10,14},{12,8},{14,10},{16,20},{18,... | collective-permute-start | bytes 4915208 | tf_op jit(solution)/shard_map/ppermute | solution.py:1098
  285.4 34.5 %collective-permute-start.42 = (bf16[640,5120]{1,0:T(8,128)(2,1)}, bf16[640,5120]{1,0:T(8,128)(2,1)}, u32[]{:S(2)}, u32[]{:S(2)}) collective-permute-start(bf16[640,5120]{1,0:T(8,128)(2,1)} %shard_map.386.refs_17_), channel_id=1, source_target_pairs={{0,2},{2,0},{4,6},{6,4},{8,10},{10,8},{12,14},{14,12},{16,18},{18,... | collective-permute-start | bytes 19660808 | tf_op jit(solution)/shard_map/ppermute | solution.py:1095
  285.4 51.5 %collective-permute-start.37 = (bf16[288,1280]{1,0:T(8,128)(2,1)}, bf16[288,1280]{1,0:T(8,128)(2,1)}, u32[]{:S(2)}, u32[]{:S(2)}) collective-permute-start(bf16[288,1280]{1,0:T(8,128)(2,1)} %get-tuple-element.124), channel_id=1, source_target_pairs={{0,1},{1,0},{2,3},{3,2},{4,5},{5,4},{6,7},{7,6},{8,9},{9,8},{10,11... | collective-permute-start | bytes 2211848 | tf_op jit(solution)/shard_map/ppermute | solution.py:1092
  332.0 37.7 %collective-permute-start.45 = (bf16[640,1280]{1,0:T(8,128)(2,1)}, bf16[640,1280]{1,0:T(8,128)(2,1)}, u32[]{:S(2)}, u32[]{:S(2)}) collective-permute-start(bf16[640,1280]{1,0:T(8,128)(2,1)} %get-tuple-element.140), channel_id=1, source_target_pairs={{0,1},{1,0},{2,3},{3,2},{4,5},{5,4},{6,7},{7,6},{8,9},{9,8},{10,11... | collective-permute-start | bytes 4915208 | tf_op jit(solution)/shard_map/ppermute | solution.py:1092
  332.6 37.4 %collective-permute-start.44 = (bf16[640,1280]{1,0:T(8,128)(2,1)}, bf16[640,1280]{1,0:T(8,128)(2,1)}, u32[]{:S(2)}, u32[]{:S(2)}) collective-permute-start(bf16[640,1280]{1,0:T(8,128)(2,1)} %get-tuple-element.139), channel_id=1, source_target_pairs={{0,4},{2,6},{4,0},{6,2},{8,12},{10,14},{12,8},{14,10},{16,20},{18,... | collective-permute-start | bytes 4915208 | tf_op jit(solution)/shard_map/ppermute | solution.py:1098
  336.9 35.0 %collective-permute-start.43 = (bf16[80,2560]{1,0:T(8,128)(2,1)}, bf16[80,2560]{1,0:T(8,128)(2,1)}, u32[]{:S(2)}, u32[]{:S(2)}) collective-permute-start(bf16[80,2560]{1,0:T(8,128)(2,1)} %shard_map.392.refs_3_), channel_id=1, source_target_pairs={{0,8},{2,10},{4,12},{6,14},{8,16},{10,18},{12,20},{14,22},{16,24},... | collective-permute-start | bytes 1228808 | tf_op jit(solution)/shard_map/ppermute | solution.py:1104
  381.5 23.2 %collective-permute-start.50 = (bf16[320,1280]{1,0:T(8,128)(2,1)}, bf16[320,1280]{1,0:T(8,128)(2,1)S(1)}, u32[]{:S(2)}, u32[]{:S(2)}) collective-permute-start(bf16[320,1280]{1,0:T(8,128)(2,1)} %copy-done.84), channel_id=1, source_target_pairs={{0,1},{1,0},{2,3},{3,2},{4,5},{5,4},{6,7},{7,6},{8,9},{9,8},{10,11... | collective-permute-start | bytes 2457608 | tf_op jit(solution)/shard_map/ppermute | solution.py:1092
  407.3 34.1 %collective-permute-start.54 = (bf16[80,2560]{1,0:T(8,128)(2,1)}, bf16[80,2560]{1,0:T(8,128)(2,1)}, u32[]{:S(2)}, u32[]{:S(2)}) collective-permute-start(bf16[80,2560]{1,0:T(8,128)(2,1)} %shard_map.401.refs_5_), channel_id=1, source_target_pairs={{0,8},{2,10},{4,12},{6,14},{8,16},{10,18},{12,20},{14,22},{16,24},... | collective-permute-start | bytes 1228808 | tf_op jit(solution)/shard_map/ppermute | solution.py:1104
  415.1 37.8 %collective-permute-start.53 = (bf16[640,1280]{1,0:T(8,128)(2,1)}, bf16[640,1280]{1,0:T(8,128)(2,1)}, u32[]{:S(2)}, u32[]{:S(2)}) collective-permute-start(bf16[640,1280]{1,0:T(8,128)(2,1)} %get-tuple-element.148), channel_id=1, source_target_pairs={{0,1},{1,0},{2,3},{3,2},{4,5},{5,4},{6,7},{7,6},{8,9},{9,8},{10,11... | collective-permute-start | bytes 4915208 | tf_op jit(solution)/shard_map/ppermute | solution.py:1092
  416.6 37.5 %collective-permute-start.52 = (bf16[640,1280]{1,0:T(8,128)(2,1)}, bf16[640,1280]{1,0:T(8,128)(2,1)}, u32[]{:S(2)}, u32[]{:S(2)}) collective-permute-start(bf16[640,1280]{1,0:T(8,128)(2,1)} %get-tuple-element.147), channel_id=1, source_target_pairs={{0,4},{2,6},{4,0},{6,2},{8,12},{10,14},{12,8},{14,10},{16,20},{18,... | collective-permute-start | bytes 4915208 | tf_op jit(solution)/shard_map/ppermute | solution.py:1098
  458.3 22.3 %collective-permute-start.55 = (bf16[320,1280]{1,0:T(8,128)(2,1)S(1)}, bf16[320,1280]{1,0:T(8,128)(2,1)S(1)}, u32[]{:S(2)}, u32[]{:S(2)}) collective-permute-start(bf16[320,1280]{1,0:T(8,128)(2,1)S(1)} %get-tuple-element.151.refs_7_), channel_id=1, source_target_pairs={{0,1},{1,0},{2,3},{3,2},{4,5},{5,4},{6,7},{7,6},{8,9},{9,8},{10,11... | collective-permute-start | bytes 2457608 | tf_op jit(solution)/shard_map/ppermute | solution.py:1092
  491.5 23.9 %collective-permute-start.61 = (bf16[288,1280]{1,0:T(8,128)(2,1)}, bf16[288,1280]{1,0:T(8,128)(2,1)}, u32[]{:S(2)}, u32[]{:S(2)}) collective-permute-start(bf16[288,1280]{1,0:T(8,128)(2,1)} %get-tuple-element.159), channel_id=1, source_target_pairs={{0,1},{1,0},{2,3},{3,2},{4,5},{5,4},{6,7},{7,6},{8,9},{9,8},{10,11... | collective-permute-start | bytes 2211848 | tf_op jit(solution)/shard_map/ppermute | solution.py:1092
  (211 other events, 2146.9 us)
